TPU v7x, 32 devices: a whole 2x2x4 slice. The times are simulated.
32 devices in a mesh: parts: 2 (over x), blk: 16 (over z, y, core).
Axes of the slice: x: 2, y: 2, z: 4, core: 2. Of those that a mesh axis runs over, the one named last changes fastest.
Arguments:
- features: bfloat16 [8192, 256], P(('parts', 'blk')), parts along dimension 0, may hold values from -5 to 5
- probes: bfloat16 [8192, 32], P(('parts', 'blk')), parts along dimension 0, may hold values from -6 to 6
- noise_level: float32 [8192], P(('parts', 'blk')), parts along dimension 0, may hold values from 0.05 to 1
Outputs:
- kernel_product: float32 [8192, 32], P(('parts', 'blk')), parts along dimension 0
There are 2 independent parts, one for each index of `parts`. A program takes and returns all parts, laid end to end along the dimension named above; each array names one. Nothing has to cross between parts.
All inputs are finite; a program needn't handle non-finite values.
Results may differ from a plain program's by a relative error of at most 0.0024.
Values may be sent and summed in bfloat16 or wider, within the bound.
No kernel may reach another device: no remote copies, remote signals or barrier semaphores. Data moves between devices by JAX's collectives and lax.ppermute only.
A program may use at most 64 MiB of HBM per device.

v0:
```python
import math

import jax
import jax.numpy as jnp
from jax import lax
from jax.sharding import PartitionSpec as P


def kernel_tile(left_x, left_sq, right_x, right_sq, right_v):
    cross = lax.dot_general(
        left_x, right_x, (((1,), (1,)), ((), ())), preferred_element_type=jnp.float32
    )
    dist2 = jnp.maximum(left_sq[:, None] + right_sq[None, :] - 2.0 * cross, 0.0)
    scaled = jnp.sqrt(5.0 * dist2)
    kernel = ((1.0 + scaled + scaled * scaled / 3.0) * jnp.exp(-scaled)).astype(jnp.bfloat16)
    return jnp.dot(kernel, right_v, preferred_element_type=jnp.float32)


def row_squares(values):
    wide = values.astype(jnp.float32)
    return jnp.sum(wide * wide, axis=1)


def block_size(row_count, shard_rows):
    return shard_rows * math.gcd(row_count // shard_rows, 8)


def on_device(features, probes, noise_level):
    shard_rows = features.shape[0]
    width = features.shape[1]
    own_squares = row_squares(features)
    gathered = lax.all_gather(features, "blk", axis=0, tiled=True)
    block_rows = block_size(lax.axis_size("blk") * shard_rows, shard_rows)
    groups = lax.axis_size("blk") * shard_rows // block_rows
    blocks_x = gathered.reshape(groups, block_rows, width)
    blocks_sq = row_squares(gathered).reshape(groups, block_rows)

    def one_block(members):
        return kernel_tile(members[0], members[1], features, own_squares, probes)

    product = lax.psum_scatter(
        lax.map(one_block, (blocks_x, blocks_sq)).reshape(
            lax.axis_size("blk") * shard_rows, probes.shape[1]
        ),
        "blk",
        scatter_dimension=0,
        tiled=True,
    )
    return product + noise_level[:, None] * probes.astype(jnp.float32)


def solution(mesh):
    placed = (P(("parts", "blk"), None), P(("parts", "blk"), None), P(("parts", "blk")))
    return jax.shard_map(
        on_device, mesh=mesh, in_specs=placed, out_specs=P(("parts", "blk"), None), check_vma=False
    )
```

profile of v0, /device:TPU:0, one launch (start us, length us, event | category | flops | bytes accessed | tf_op | source)
XLA Modules:
  0.0 127.6 jit_solution(839592063931794803)
XLA Ops:
  6.5 0.0 copy-start.1
  6.5 0.0 copy-start.2
  6.5 0.0 all-gather.2.cloned.1.call-start
  6.5 0.7 all-gather.2.cloned.1.call-update
  7.3 0.0 reduce-scatter.2.cloned.1.call-start
  7.3 1.0 multiply_reduce_fusion.1
  8.3 45.3 %all-gather.2.cloned.1.call-done = bf16[4096,256]{1,0:T(8,128)(2,1)} async-done(((bf16[256,256]{1,0:T(8,128)(2,1)}), bf16[4096,256]{1,0:T(8,128)(2,1)}) %all-gather.2.cloned.1.call-update) | async-done | bytes 2097168 | tf_op jit(solution)/shard_map/all_gather | solution.py:32
  53.7 2.4 %multiply_reduce_fusion = f32[4096]{0:T(1024)S(1)} fusion(bf16[4096,256]{1,0:T(8,128)(2,1)} %all-gather.2.cloned.1.call-done), kind=kLoop, calls=%fused_computation.16 | loop fusion | flops 3141632 | bytes 2113536 | tf_op jit(solution)/shard_map/reduce_sum | solution.py:21
  56.0 0.0 copy-done.1
  56.0 0.0 copy-done.2
  56.1 0.0 copy-done
  56.1 0.0 copy-start.3
  56.1 7.5 %while.10 = (s32[]{:T(128)}, f32[2,2048,32]{1,0,2:T(2,128)S(1)}, f32[2,2048]{1,0:T(2,128)S(1)}, f32[256]{0:T(256)S(1)}, bf16[2,2048,256]{2,1,0:T(8,128)(2,1)S(1)...) while((s32[]{:T(128)}, f32[2,2048,32]{1,0,2:T(2,128)S(1)}, ...), condition=%wide.region_3.4_spmd, body=%wide.region_2.3_spmd.sunk | while | flops 308281344 | bytes 2532457 | solution.py:42
  56.1 1.6 %convolution_bitcast_fusion.2 = f32[1,2048,32]{1,2,0:T(8,128)S(1)} fusion(bf16[256,32]{0,1:T(8,128)(2,1)S(1)} %get-tuple-element.124, bf16[256,256]{1,0:T(8,128)(2,1)S(1)} %get-tuple-element.123, bf16[2,2048,256]{2,1,0:T(8,128)(2,1)S(1)} %get-tuple-element.122, s32[]{:T(128)} %get-tuple-element.109, f32[256]{0:T(256)S(1)} %get-tuple-element.121, ...), kind=kOutput, calls=%fused_computation.5.clone.1 | convolution fusion | flops 308281344 | bytes 1467396 | tf_op jit(solution)/shard_map/while/body/eval_jaxpr/dot_general | solution.py:16
  57.7 0.3 copy.11
  58.0 1.8 %dynamic_update_slice.5 = f32[2,2048,32]{1,0,2:T(2,128)S(1)} dynamic-update-slice(f32[2,2048,32]{1,0,2:T(2,128)S(1)} %get-tuple-element.110, f32[1,2048,32]{1,0,2:T(1,128)S(1)} %copy.11, s32[]{:T(128)} %get-tuple-element.109, s32[]{:T(128)} %constant.21.clone.1..sunk, s32[]{:T(128)} %constant.21.clone.1..sunk) | dynamic-update-slice | bytes 524292 | tf_op jit(solution)/shard_map/while/body/jit(dynamic_update_index_in_dim)/dynamic_update_slice | solution.py:42
  59.9 1.6 %convolution_bitcast_fusion.2 = f32[1,2048,32]{1,2,0:T(8,128)S(1)} fusion(bf16[256,32]{0,1:T(8,128)(2,1)S(1)} %get-tuple-element.124, bf16[256,256]{1,0:T(8,128)(2,1)S(1)} %get-tuple-element.123, bf16[2,2048,256]{2,1,0:T(8,128)(2,1)S(1)} %get-tuple-element.122, s32[]{:T(128)} %get-tuple-element.109, f32[256]{0:T(256)S(1)} %get-tuple-element.121, ...), kind=kOutput, calls=%fused_computation.5.clone.1 | convolution fusion | flops 308281344 | bytes 1467396 | tf_op jit(solution)/shard_map/while/body/eval_jaxpr/dot_general | solution.py:16
  61.5 0.3 copy.11
  61.8 1.8 %dynamic_update_slice.5 = f32[2,2048,32]{1,0,2:T(2,128)S(1)} dynamic-update-slice(f32[2,2048,32]{1,0,2:T(2,128)S(1)} %get-tuple-element.110, f32[1,2048,32]{1,0,2:T(1,128)S(1)} %copy.11, s32[]{:T(128)} %get-tuple-element.109, s32[]{:T(128)} %constant.21.clone.1..sunk, s32[]{:T(128)} %constant.21.clone.1..sunk) | dynamic-update-slice | bytes 524292 | tf_op jit(solution)/shard_map/while/body/jit(dynamic_update_index_in_dim)/dynamic_update_slice | solution.py:42
  63.6 1.1 copy.9
  64.7 0.0 reduce-scatter.2.cloned.1.call-update
  64.7 54.7 %reduce-scatter.2.cloned.1.call-done = f32[256,32]{0,1:T(8,128)} async-done(((f32[4096,32]{0,1:T(8,128)}), f32[256,32]{0,1:T(8,128)}) %reduce-scatter.2.cloned.1.call-update) | async-done | bytes 32784 | tf_op jit(solution)/shard_map/reduce_scatter | solution.py:41
  119.4 0.0 copy-done.3
  119.4 1.4 %multiply_add_fusion = f32[256,32]{0,1:T(8,128)} fusion(f32[256,32]{0,1:T(8,128)} %reduce-scatter.2.cloned.1.call-done, bf16[256,32]{0,1:T(8,128)(2,1)S(1)} %get-tuple-element.135, f32[256]{0:T(256)S(1)} %copy-done.3), kind=kLoop, calls=%fused_computation.18 | loop fusion | flops 24576 | bytes 82944 | tf_op jit(solution)/shard_map/add | solution.py:49
  (5 shorter events, 0.0 us)
Async XLA Ops:
  6.5 49.5 %copy-start.1 = (bf16[256,256]{1,0:T(8,128)(2,1)S(1)}, bf16[256,256]{1,0:T(8,128)(2,1)}, u32[]{:S(2)}) copy-start(bf16[256,256]{1,0:T(8,128)(2,1)} %param.5) | copy-start | bytes 393220
  6.5 49.5 %copy-start.2 = (bf16[256,32]{0,1:T(8,128)(2,1)S(1)}, bf16[256,32]{0,1:T(8,128)(2,1)}, u32[]{:S(2)}) copy-start(bf16[256,32]{0,1:T(8,128)(2,1)} %param.6) | copy-start | bytes 49156
  6.5 47.1 %all-gather.2.cloned.1.call-start = ((), (), s32[]{:S(2)}) async-start(), calls=%async_computation.1 | async-start | bytes 2228224 | tf_op jit(solution)/shard_map/all_gather | solution.py:32
  7.3 112.1 %reduce-scatter.2.cloned.1.call-start = ((), (), s32[]{:S(2)}) async-start(), calls=%async_computation.2 | async-start | bytes 557056 | tf_op jit(solution)/shard_map/reduce_scatter | solution.py:41
  53.7 2.4 %copy-start = (bf16[4096,256]{1,0:T(8,128)(2,1)S(1)}, bf16[4096,256]{1,0:T(8,128)(2,1)}, u32[]{:S(2)}) copy-start(bf16[4096,256]{1,0:T(8,128)(2,1)} %all-gather.2.cloned.1.call-done) | copy-start | bytes 6291460
  56.1 63.3 %copy-start.3 = (f32[256]{0:T(256)S(1)}, f32[256]{0:T(256)}, u32[]{:S(2)}) copy-start(f32[256]{0:T(256)} %param.7) | copy-start | bytes 3076
Sparse Core Ops, SparseCore 0:
  9.5 44.0 all-gather.1
  64.8 54.5 reduce-scatter.1
where the time goes:
time: 128 us
  waiting for transfers between devices  101 us (79%)
  between operations  13.5 us (11%)
  local copies, waits for them, and re-layouts  5.31 us (4%)
  other arithmetic  4.75 us (4%)
  matrix products  3.23 us (3%)
    reduce_scatter x1, waiting for transfers between devices, on_device(): lax.psum_scatter(lax.map(one_block, (blocks_x, blocks_sq)).reshape(lax.ax...  54.7 us
    all_gather x1, waiting for transfers between devices, on_device(): gathered = lax.all_gather(features, 'blk', axis=0, tiled=True)  45.3 us
    dynamic_update_slice x4, local copies, waits for them, and re-layouts, on_device(): lax.map(one_block, (blocks_x, blocks_sq))  4.16 us
    reduce_sum x2, other arithmetic, row_squares(): return jnp.sum(wide * wide, axis=1)  3.37 us
    dot_general x2, matrix products, kernel_tile(): return jnp.dot(kernel, right_v, preferred_element_type=jnp.float32)  3.23 us
  transfers between devices with their start and end apart: 2, of which 2 were waited for; matrix products, arithmetic and copies ran while one was open for 1% of the time, Pallas kernels for 0%

commit v1 on v0

v1 whole, which is shorter than its diff:
```python
import functools
import math

import jax
import jax.numpy as jnp
from jax import lax
from jax.experimental import pallas as pl
from jax.experimental.pallas import tpu as pltpu
from jax.sharding import PartitionSpec as P

ROOT5 = math.sqrt(5.0)
DECAY = -ROOT5 * math.log2(math.e)


def partner(index, step, count):
    if count & (count - 1) == 0:
        return index ^ step
    return (index + step) % count


def group_size(count):
    size = 1
    while size * size < count or count % size:
        size += 1
    return size


def matern(dist2):
    dist2 = jnp.maximum(dist2, 1e-30)
    dist = dist2 * lax.rsqrt(dist2)
    poly = (1.0 + ROOT5 * dist) + (5.0 / 3.0) * dist2
    return (poly * jnp.exp2(DECAY * dist)).astype(jnp.bfloat16)


def squares_on_lanes(block):
    wide = block.astype(jnp.float32)
    square = wide * wide
    high = square.astype(jnp.bfloat16)
    low = (square - high.astype(jnp.float32)).astype(jnp.bfloat16)
    ones = jnp.ones((8, block.shape[1]), jnp.bfloat16)
    dims = (((1,), (1,)), ((), ()))
    return lax.dot_general(ones, high, dims, preferred_element_type=jnp.float32) + lax.dot_general(
        ones, low, dims, preferred_element_type=jnp.float32
    )


def tile_kernel(row_count, col_count, *refs):
    row_refs = refs[:row_count]
    col_refs = refs[row_count : row_count + col_count]
    probe_refs = refs[row_count + col_count : row_count + 2 * col_count]
    out_ref, rows, row_squares = refs[row_count + 2 * col_count :]
    shard, width = row_refs[0].shape
    for slot, ref in enumerate(row_refs):
        block = ref[...]
        rows[pl.ds(slot * shard, shard), :] = block * jnp.asarray(-2.0, block.dtype)
        row_squares[:, pl.ds(slot * shard, shard)] = squares_on_lanes(block)
    out_ref[...] = jnp.zeros_like(out_ref)
    for col_ref, probe_ref in zip(col_refs, probe_refs):
        cols = col_ref[...]
        wide = cols.astype(jnp.float32)
        col_squares = jnp.sum(wide * wide, axis=1, keepdims=True)

        @pl.loop(0, row_count)
        def _(slot):
            start = pl.multiple_of(slot * shard, shard)
            cross = lax.dot_general(
                cols, rows[pl.ds(start, shard), :], (((1,), (1,)), ((), ())), preferred_element_type=jnp.float32
            )
            kernel = matern((col_squares + row_squares[0:1, pl.ds(start, shard)]) + cross)
            out_ref[slot] += jnp.dot(probe_ref[...], kernel, preferred_element_type=jnp.float32)


def tile_product(rows, cols, probes):
    shard, width = rows[0].shape
    vectors = probes[0].shape[0]
    body = functools.partial(tile_kernel, len(rows), len(cols))
    elements = len(rows) * len(cols) * shard * shard
    return pl.pallas_call(
        body,
        out_shape=jax.ShapeDtypeStruct((len(rows), vectors, shard), jnp.float32),
        in_specs=[pl.BlockSpec(memory_space=pltpu.VMEM)] * (len(rows) + 2 * len(cols)),
        out_specs=pl.BlockSpec(memory_space=pltpu.VMEM),
        scratch_shapes=[
            pltpu.VMEM((len(rows) * shard, width), jnp.bfloat16),
            pltpu.VMEM((8, len(rows) * shard), jnp.float32),
        ],
        compiler_params=pltpu.CompilerParams(vmem_limit_bytes=32 * 1024 * 1024),
        cost_estimate=pl.CostEstimate(
            flops=2 * elements * (width + vectors),
            bytes_accessed=2 * width * shard * (len(rows) + len(cols)),
            transcendentals=2 * elements,
        ),
    )(*rows, *cols, *probes)


def on_device(features, probes, noise_level):
    count = lax.axis_size("blk")
    inner = group_size(count)
    outer = count // inner
    flat = probes.T

    def from_outer(value, step):
        pairs = [
            (partner(a, step, outer) * inner + b, a * inner + b) for a in range(outer) for b in range(inner)
        ]
        return lax.ppermute(value, "blk", pairs)

    def from_inner(value, step):
        pairs = [
            (a * inner + partner(b, step, inner), a * inner + b) for a in range(outer) for b in range(inner)
        ]
        return lax.ppermute(value, "blk", pairs)

    def to_inner(value, step):
        pairs = [
            (a * inner + b, a * inner + partner(b, step, inner)) for a in range(outer) for b in range(inner)
        ]
        return lax.ppermute(value, "blk", pairs)

    cols = [features] + [from_outer(features, step) for step in range(1, outer)]
    col_probes = [flat] + [from_outer(flat, step) for step in range(1, outer)]
    rows = [features] + [from_inner(features, step) for step in range(1, inner)]
    partial = tile_product(rows, cols, col_probes)
    total = partial[0] + noise_level[None, :] * flat.astype(jnp.float32)
    for step in range(1, inner):
        total = total + to_inner(partial[step], step)
    return total.T


def solution(mesh):
    placed = (P(("parts", "blk"), None), P(("parts", "blk"), None), P(("parts", "blk")))
    return jax.shard_map(
        on_device, mesh=mesh, in_specs=placed, out_specs=P(("parts", "blk"), None), check_vma=False
    )
```

time: 128 us -> 36.4 us (0.28)
  waiting for transfers between devices: 101 us -> 9.68 us
  starting transfers between devices: 0.04 us -> 16.4 us
  between operations: 13.5 us -> 0.04 us
  Pallas kernels: 0 us -> 7.51 us
  other arithmetic: 4.75 us -> 0.63 us
  local copies, waits for them, and re-layouts: 5.31 us -> 1.64 us
  matrix products: 3.23 us -> 0 us
    reduce_scatter x1 -> x0, waiting for transfers between devices: 54.7 us -> none  [on_device(): lax.psum_scatter(lax.map(one_block, (blocks_x, blocks_sq)).reshape(lax.ax...]
    all_gather x1 -> x0, waiting for transfers between devices: 45.3 us -> none  [on_device(): gathered = lax.all_gather(features, 'blk', axis=0, tiled=True)]
    ppermute x0 -> x12, starting transfers between devices: none -> 16.4 us  [the longest x6 12.7 us: from_outer(): return lax.ppermute(value, 'blk', pairs)]
    ppermute x0 -> x12, waiting for transfers between devices: none -> 9.68 us  [the longest x6 5.67 us: from_outer(): return lax.ppermute(value, 'blk', pairs)]
    pallas_call x0 -> x1, Pallas kernels: none -> 7.51 us  [tile_product(): pl.pallas_call(body, out_shape=jax.ShapeDtypeStruct((len(rows), vectors,...]
    dynamic_update_slice x4 -> x0, local copies, waits for them, and re-layouts: 4.16 us -> none  [on_device(): lax.map(one_block, (blocks_x, blocks_sq))]
    reduce_sum x2 -> x0, other arithmetic: 3.37 us -> none  [row_squares(): return jnp.sum(wide * wide, axis=1)]
    dot_general x2 -> x0, matrix products: 3.23 us -> none  [kernel_tile(): return jnp.dot(kernel, right_v, preferred_element_type=jnp.float32)]
  transfers between devices with their start and end apart: 2 -> 12, of which waited for: 2 -> 6; matrix products, arithmetic and copies ran while one was open for 1% -> 0% of each run, Pallas kernels for 0% -> 0%
where the time goes in v1:
time: 36.4 us; the launch traced here: 35.9 us
  starting transfers between devices  16.4 us (45%)
  waiting for transfers between devices  9.68 us (27%)
  Pallas kernels  7.51 us (21%)
  local copies, waits for them, and re-layouts  1.64 us (5%)
  other arithmetic  0.63 us (2%)
    ppermute x6, starting transfers between devices, from_outer(): return lax.ppermute(value, 'blk', pairs)  12.7 us
    pallas_call x1, Pallas kernels, tile_product(): pl.pallas_call(body, out_shape=jax.ShapeDtypeStruct((len(rows), vectors,...  7.51 us
    ppermute x6, waiting for transfers between devices, from_outer(): return lax.ppermute(value, 'blk', pairs)  5.67 us
    ppermute x3, waiting for transfers between devices, to_inner(): return lax.ppermute(value, 'blk', pairs)  2.36 us
    ppermute x3, starting transfers between devices, to_inner(): return lax.ppermute(value, 'blk', pairs)  2.2 us
    ppermute x3, waiting for transfers between devices, from_inner(): return lax.ppermute(value, 'blk', pairs)  1.65 us
    unnamed x6, local copies, waits for them, and re-layouts  1.63 us
    ppermute x3, starting transfers between devices, from_inner(): return lax.ppermute(value, 'blk', pairs)  1.58 us
  transfers between devices with their start and end apart: 12, of which 6 were waited for; matrix products, arithmetic and copies ran while one was open for 0% of the time, Pallas kernels for 0%

profile of v1, /device:TPU:0, one launch (start us, length us, event | category | flops | bytes accessed | tf_op | source)
XLA Modules:
  0.0 35.9 jit_solution(16738556198691233027)
XLA Ops:
  0.0 4.0 %collective-permute-start.4 = (bf16[256,256]{1,0:T(8,128)(2,1)}, bf16[256,256]{1,0:T(8,128)(2,1)S(1)}, u32[]{:S(2)}, u32[]{:S(2)}) collective-permute-start(bf16[256,256]{1,0:T(8,128)(2,1)} %refs_4_.1), channel_id=1, source_target_pairs={{8,0},{9,1},{10,2},{11,3},{12,4},{13,5},{14,6},{15,7},{0,8},{1,9},... | collective-permute-start | bytes 393224 | tf_op jit(solution)/shard_map/ppermute | solution.py:106
  4.0 1.3 %collective-permute-start.8 = (bf16[32,256]{1,0:T(8,128)(2,1)}, bf16[32,256]{1,0:T(8,128)(2,1)S(1)}, u32[]{:S(2)}, u32[]{:S(2)}) collective-permute-start(bf16[32,256]{1,0:T(8,128)(2,1)} %bitcast.22), channel_id=1, source_target_pairs={{12,0},{13,1},{14,2},{15,3},{8,4},{9,5},{10,6},{11,7},{4,8},{5,9},... | collective-permute-start | bytes 49160 | tf_op jit(solution)/shard_map/ppermute | solution.py:106
  5.4 1.7 %collective-permute-start.7 = (bf16[32,256]{1,0:T(8,128)(2,1)}, bf16[32,256]{1,0:T(8,128)(2,1)S(1)}, u32[]{:S(2)}, u32[]{:S(2)}) collective-permute-start(bf16[32,256]{1,0:T(8,128)(2,1)} %bitcast.23), channel_id=1, source_target_pairs={{8,0},{9,1},{10,2},{11,3},{12,4},{13,5},{14,6},{15,7},{0,8},{1,9},... | collective-permute-start | bytes 49160 | tf_op jit(solution)/shard_map/ppermute | solution.py:106
  7.1 1.3 %collective-permute-start.6 = (bf16[32,256]{1,0:T(8,128)(2,1)}, bf16[32,256]{1,0:T(8,128)(2,1)S(1)}, u32[]{:S(2)}, u32[]{:S(2)}) collective-permute-start(bf16[32,256]{1,0:T(8,128)(2,1)} %bitcast.24), channel_id=1, source_target_pairs={{4,0},{5,1},{6,2},{7,3},{0,4},{1,5},{2,6},{3,7},{12,8},{13,9},{14,... | collective-permute-start | bytes 49160 | tf_op jit(solution)/shard_map/ppermute | solution.py:106
  8.4 0.7 %collective-permute-start.3 = (bf16[256,256]{1,0:T(8,128)(2,1)}, bf16[256,256]{1,0:T(8,128)(2,1)S(1)}, u32[]{:S(2)}, u32[]{:S(2)}) collective-permute-start(bf16[256,256]{1,0:T(8,128)(2,1)} %refs_4_.1), channel_id=1, source_target_pairs={{4,0},{5,1},{6,2},{7,3},{0,4},{1,5},{2,6},{3,7},{12,8},{13,9},{14,... | collective-permute-start | bytes 393224 | tf_op jit(solution)/shard_map/ppermute | solution.py:106
  9.1 0.9 %collective-permute-done.8.refs_11_ = bf16[32,256]{1,0:T(8,128)(2,1)S(1)} collective-permute-done((bf16[32,256]{1,0:T(8,128)(2,1)}, bf16[32,256]{1,0:T(8,128)(2,1)S(1)}, u32[]{:S(2)}, u32[]{:S(2)}) %collective-permute-start.8) | collective-permute-done | bytes 16416 | tf_op jit(solution)/shard_map/ppermute | solution.py:106
  10.0 2.0 %collective-permute-done.7.refs_10_ = bf16[32,256]{1,0:T(8,128)(2,1)S(1)} collective-permute-done((bf16[32,256]{1,0:T(8,128)(2,1)}, bf16[32,256]{1,0:T(8,128)(2,1)S(1)}, u32[]{:S(2)}, u32[]{:S(2)}) %collective-permute-start.7) | collective-permute-done | bytes 16416 | tf_op jit(solution)/shard_map/ppermute | solution.py:106
  12.0 1.6 %collective-permute-start.1 = (bf16[256,256]{1,0:T(8,128)(2,1)}, bf16[256,256]{1,0:T(8,128)(2,1)S(1)}, u32[]{:S(2)}, u32[]{:S(2)}) collective-permute-start(bf16[256,256]{1,0:T(8,128)(2,1)} %refs_4_.1), channel_id=1, source_target_pairs={{2,0},{3,1},{0,2},{1,3},{6,4},{7,5},{4,6},{5,7},{10,8},{11,9},{8,1... | collective-permute-start | bytes 393224 | tf_op jit(solution)/shard_map/ppermute | solution.py:112
  13.5 0.0 collective-permute-done.6.refs_9_
  13.5 0.0 collective-permute-start
  13.6 0.0 collective-permute-done.4.refs_6_
  13.6 3.6 %collective-permute-start.5 = (bf16[256,256]{1,0:T(8,128)(2,1)}, bf16[256,256]{1,0:T(8,128)(2,1)S(1)}, u32[]{:S(2)}, u32[]{:S(2)}) collective-permute-start(bf16[256,256]{1,0:T(8,128)(2,1)} %refs_4_.1), channel_id=1, source_target_pairs={{12,0},{13,1},{14,2},{15,3},{8,4},{9,5},{10,6},{11,7},{4,8},{5,9},... | collective-permute-start | bytes 393224 | tf_op jit(solution)/shard_map/ppermute | solution.py:106
  17.1 1.6 %collective-permute-done.1.refs_2_ = bf16[256,256]{1,0:T(8,128)(2,1)S(1)} collective-permute-done((bf16[256,256]{1,0:T(8,128)(2,1)}, bf16[256,256]{1,0:T(8,128)(2,1)S(1)}, u32[]{:S(2)}, u32[]{:S(2)}) %collective-permute-start.1) | collective-permute-done | bytes 131104 | tf_op jit(solution)/shard_map/ppermute | solution.py:112
  18.8 2.8 %collective-permute-done.5.refs_7_ = bf16[256,256]{1,0:T(8,128)(2,1)S(1)} collective-permute-done((bf16[256,256]{1,0:T(8,128)(2,1)}, bf16[256,256]{1,0:T(8,128)(2,1)S(1)}, u32[]{:S(2)}, u32[]{:S(2)}) %collective-permute-start.5) | collective-permute-done | bytes 131104 | tf_op jit(solution)/shard_map/ppermute | solution.py:106
  21.6 0.7 %copy-done = bf16[256,32]{0,1:T(8,128)(2,1)S(1)} copy-done((bf16[256,32]{0,1:T(8,128)(2,1)S(1)}, bf16[256,32]{0,1:T(8,128)(2,1)}, u32[]{:S(2)}) %copy-start) | copy-done | bytes 16408
  22.3 0.9 %copy-done.1 = bf16[256,256]{1,0:T(8,128)(2,1)S(1)} copy-done((bf16[256,256]{1,0:T(8,128)(2,1)S(1)}, bf16[256,256]{1,0:T(8,128)(2,1)}, u32[]{:S(2)}) %copy-start.1) | copy-done | bytes 131096
  23.2 7.5 %shard_map.37 = f32[4,32,256]{2,1,0:T(8,128)S(1)} custom-call(bf16[256,256]{1,0:T(8,128)(2,1)S(1)} %copy-done.1, bf16[256,256]{1,0:T(8,128)(2,1)S(1)} %collective-permute-done.refs_1_, bf16[256,256]{1,0:T(8,128)(2,1)S(1)} %collective-permute-done.1.refs_2_, bf16[256,256]{1,0:T(8,128)(2,1)S(1)} %collective-permute-done.2.refs_3_, ...), custom_call_target="tpu_custom_call" | custom-call | flops 603979776 | bytes 1048576 | tf_op jit(solution)/shard_map/pallas_call | solution.py:78
  30.7 0.1 collective-permute-start.9
  30.8 0.0 copy-start.2
  30.8 0.6 %collective-permute-start.11 = (f32[32,256]{1,0:T(8,128)S(1)}, f32[32,256]{1,0:T(8,128)S(1)}, u32[]{:S(2)}, u32[]{:S(2)}) collective-permute-start(f32[32,256]{1,0:T(8,128)S(1)} %get-tuple-element.6), channel_id=1, source_target_pairs={{0,3},{1,2},{2,1},{3,0},{4,7},{5,6},{6,5},{7,4},{8,11},{9,10},{10,... | collective-permute-start | bytes 98312 | tf_op jit(solution)/shard_map/ppermute | solution.py:118
  31.4 1.6 %collective-permute-start.10 = (f32[32,256]{1,0:T(8,128)S(1)}, f32[32,256]{1,0:T(8,128)S(1)}, u32[]{:S(2)}, u32[]{:S(2)}) collective-permute-start(f32[32,256]{1,0:T(8,128)S(1)} %get-tuple-element.7), channel_id=1, source_target_pairs={{0,2},{1,3},{2,0},{3,1},{4,6},{5,7},{6,4},{7,5},{8,10},{9,11},{10,... | collective-permute-start | bytes 98312 | tf_op jit(solution)/shard_map/ppermute | solution.py:118
  33.0 1.3 %collective-permute-done.11 = f32[32,256]{1,0:T(8,128)S(1)} collective-permute-done((f32[32,256]{1,0:T(8,128)S(1)}, f32[32,256]{1,0:T(8,128)S(1)}, u32[]{:S(2)}, u32[]{:S(2)}) %collective-permute-start.11) | collective-permute-done | bytes 32800 | tf_op jit(solution)/shard_map/ppermute | solution.py:118
  34.2 1.1 %collective-permute-done.10 = f32[32,256]{1,0:T(8,128)S(1)} collective-permute-done((f32[32,256]{1,0:T(8,128)S(1)}, f32[32,256]{1,0:T(8,128)S(1)}, u32[]{:S(2)}, u32[]{:S(2)}) %collective-permute-start.10) | collective-permute-done | bytes 32800 | tf_op jit(solution)/shard_map/ppermute | solution.py:118
  35.3 0.6 %fusion.4 = f32[256,32]{0,1:T(8,128)} fusion(f32[32,256]{1,0:T(8,128)S(1)} %collective-permute-done.11, f32[32,256]{1,0:T(8,128)S(1)} %collective-permute-done.10, f32[32,256]{1,0:T(8,128)S(1)} %collective-permute-done.9, f32[4,32,256]{2,1,0:T(8,128)S(1)} %shard_map.37, f32[256]{0:T(256)S(1)} %copy-done.2, bf16[256,32]{0,1:T(8,128)(2,1)S(1)} %copy-done), kind=kLoop, calls=%fused_computation.8 | loop fusion | flops 49152 | bytes 181248 | tf_op jit(solution)/shard_map/transpose | solution.py:127
  (9 shorter events, 0.0 us)
Async XLA Ops:
  0.0 13.6 %collective-permute-start.4 = (bf16[256,256]{1,0:T(8,128)(2,1)}, bf16[256,256]{1,0:T(8,128)(2,1)S(1)}, u32[]{:S(2)}, u32[]{:S(2)}) collective-permute-start(bf16[256,256]{1,0:T(8,128)(2,1)} %refs_4_.1), channel_id=1, source_target_pairs={{8,0},{9,1},{10,2},{11,3},{12,4},{13,5},{14,6},{15,7},{0,8},{1,9},... | collective-permute-start | bytes 393224 | tf_op jit(solution)/shard_map/ppermute | solution.py:106
  4.0 5.9 %collective-permute-start.8 = (bf16[32,256]{1,0:T(8,128)(2,1)}, bf16[32,256]{1,0:T(8,128)(2,1)S(1)}, u32[]{:S(2)}, u32[]{:S(2)}) collective-permute-start(bf16[32,256]{1,0:T(8,128)(2,1)} %bitcast.22), channel_id=1, source_target_pairs={{12,0},{13,1},{14,2},{15,3},{8,4},{9,5},{10,6},{11,7},{4,8},{5,9},... | collective-permute-start | bytes 49160 | tf_op jit(solution)/shard_map/ppermute | solution.py:106
  5.4 6.6 %collective-permute-start.7 = (bf16[32,256]{1,0:T(8,128)(2,1)}, bf16[32,256]{1,0:T(8,128)(2,1)S(1)}, u32[]{:S(2)}, u32[]{:S(2)}) collective-permute-start(bf16[32,256]{1,0:T(8,128)(2,1)} %bitcast.23), channel_id=1, source_target_pairs={{8,0},{9,1},{10,2},{11,3},{12,4},{13,5},{14,6},{15,7},{0,8},{1,9},... | collective-permute-start | bytes 49160 | tf_op jit(solution)/shard_map/ppermute | solution.py:106
  7.1 6.5 %collective-permute-start.6 = (bf16[32,256]{1,0:T(8,128)(2,1)}, bf16[32,256]{1,0:T(8,128)(2,1)S(1)}, u32[]{:S(2)}, u32[]{:S(2)}) collective-permute-start(bf16[32,256]{1,0:T(8,128)(2,1)} %bitcast.24), channel_id=1, source_target_pairs={{4,0},{5,1},{6,2},{7,3},{0,4},{1,5},{2,6},{3,7},{12,8},{13,9},{14,... | collective-permute-start | bytes 49160 | tf_op jit(solution)/shard_map/ppermute | solution.py:106
  8.4 8.7 %collective-permute-start.3 = (bf16[256,256]{1,0:T(8,128)(2,1)}, bf16[256,256]{1,0:T(8,128)(2,1)S(1)}, u32[]{:S(2)}, u32[]{:S(2)}) collective-permute-start(bf16[256,256]{1,0:T(8,128)(2,1)} %refs_4_.1), channel_id=1, source_target_pairs={{4,0},{5,1},{6,2},{7,3},{0,4},{1,5},{2,6},{3,7},{12,8},{13,9},{14,... | collective-permute-start | bytes 393224 | tf_op jit(solution)/shard_map/ppermute | solution.py:106
  10.0 7.2 %collective-permute-start.2 = (bf16[256,256]{1,0:T(8,128)(2,1)}, bf16[256,256]{1,0:T(8,128)(2,1)S(1)}, u32[]{:S(2)}, u32[]{:S(2)}) collective-permute-start(bf16[256,256]{1,0:T(8,128)(2,1)} %refs_4_.1), channel_id=1, source_target_pairs={{3,0},{2,1},{1,2},{0,3},{7,4},{6,5},{5,6},{4,7},{11,8},{10,9},{9,1... | collective-permute-start | bytes 393224 | tf_op jit(solution)/shard_map/ppermute | solution.py:112
  12.0 6.8 %collective-permute-start.1 = (bf16[256,256]{1,0:T(8,128)(2,1)}, bf16[256,256]{1,0:T(8,128)(2,1)S(1)}, u32[]{:S(2)}, u32[]{:S(2)}) collective-permute-start(bf16[256,256]{1,0:T(8,128)(2,1)} %refs_4_.1), channel_id=1, source_target_pairs={{2,0},{3,1},{0,2},{1,3},{6,4},{7,5},{4,6},{5,7},{10,8},{11,9},{8,1... | collective-permute-start | bytes 393224 | tf_op jit(solution)/shard_map/ppermute | solution.py:112
  13.5 5.2 %collective-permute-start = (bf16[256,256]{1,0:T(8,128)(2,1)}, bf16[256,256]{1,0:T(8,128)(2,1)S(1)}, u32[]{:S(2)}, u32[]{:S(2)}) collective-permute-start(bf16[256,256]{1,0:T(8,128)(2,1)} %refs_4_.1), channel_id=1, source_target_pairs={{1,0},{0,1},{3,2},{2,3},{5,4},{4,5},{7,6},{6,7},{9,8},{8,9},{11,10... | collective-permute-start | bytes 393224 | tf_op jit(solution)/shard_map/ppermute | solution.py:112
  13.6 8.0 %collective-permute-start.5 = (bf16[256,256]{1,0:T(8,128)(2,1)}, bf16[256,256]{1,0:T(8,128)(2,1)S(1)}, u32[]{:S(2)}, u32[]{:S(2)}) collective-permute-start(bf16[256,256]{1,0:T(8,128)(2,1)} %refs_4_.1), channel_id=1, source_target_pairs={{12,0},{13,1},{14,2},{15,3},{8,4},{9,5},{10,6},{11,7},{4,8},{5,9},... | collective-permute-start | bytes 393224 | tf_op jit(solution)/shard_map/ppermute | solution.py:106
  21.6 0.7 %copy-start = (bf16[256,32]{0,1:T(8,128)(2,1)S(1)}, bf16[256,32]{0,1:T(8,128)(2,1)}, u32[]{:S(2)}) copy-start(bf16[256,32]{0,1:T(8,128)(2,1)} %param.4) | copy-start | bytes 49156
  22.3 0.9 %copy-start.1 = (bf16[256,256]{1,0:T(8,128)(2,1)S(1)}, bf16[256,256]{1,0:T(8,128)(2,1)}, u32[]{:S(2)}) copy-start(bf16[256,256]{1,0:T(8,128)(2,1)} %refs_4_.1) | copy-start | bytes 393220
  30.7 2.2 %collective-permute-start.9 = (f32[32,256]{1,0:T(8,128)S(1)}, f32[32,256]{1,0:T(8,128)S(1)}, u32[]{:S(2)}, u32[]{:S(2)}) collective-permute-start(f32[32,256]{1,0:T(8,128)S(1)} %get-tuple-element.5), channel_id=1, source_target_pairs={{0,1},{1,0},{2,3},{3,2},{4,5},{5,4},{6,7},{7,6},{8,9},{9,8},{10,11... | collective-permute-start | bytes 98312 | tf_op jit(solution)/shard_map/ppermute | solution.py:118
  30.8 4.5 %copy-start.2 = (f32[256]{0:T(256)S(1)}, f32[256]{0:T(256)}, u32[]{:S(2)}) copy-start(f32[256]{0:T(256)} %param.5) | copy-start | bytes 3076
  30.8 3.4 %collective-permute-start.11 = (f32[32,256]{1,0:T(8,128)S(1)}, f32[32,256]{1,0:T(8,128)S(1)}, u32[]{:S(2)}, u32[]{:S(2)}) collective-permute-start(f32[32,256]{1,0:T(8,128)S(1)} %get-tuple-element.6), channel_id=1, source_target_pairs={{0,3},{1,2},{2,1},{3,0},{4,7},{5,6},{6,5},{7,4},{8,11},{9,10},{10,... | collective-permute-start | bytes 98312 | tf_op jit(solution)/shard_map/ppermute | solution.py:118
  31.4 3.9 %collective-permute-start.10 = (f32[32,256]{1,0:T(8,128)S(1)}, f32[32,256]{1,0:T(8,128)S(1)}, u32[]{:S(2)}, u32[]{:S(2)}) collective-permute-start(f32[32,256]{1,0:T(8,128)S(1)} %get-tuple-element.7), channel_id=1, source_target_pairs={{0,2},{1,3},{2,0},{3,1},{4,6},{5,7},{6,4},{7,5},{8,10},{9,11},{10,... | collective-permute-start | bytes 98312 | tf_op jit(solution)/shard_map/ppermute | solution.py:118

commit v2 on v0

v2 whole, which is shorter than its diff:
```python
import functools
import math

import jax
import jax.numpy as jnp
from jax import lax
from jax.experimental import pallas as pl
from jax.experimental.pallas import tpu as pltpu
from jax.sharding import PartitionSpec as P

ROOT5 = math.sqrt(5.0)
DECAY = -ROOT5 * math.log2(math.e)
ROWS_BY_ROWS = (((1,), (1,)), ((), ()))


def group_size(count):
    size = 1
    while size * size < count or count % size:
        size += 1
    return size


def inner_partner(index, step, count):
    if count & (count - 1) == 0:
        return index ^ step
    return (index + step) % count


def outer_edges(count):
    maps = [[(a, (a + step) % count) for a in range(count)] for step in range(1, (count + 1) // 2)]
    if count % 2 == 0:
        half = count // 2
        maps.append([(a, a + half) if a % 2 == 0 else (a + half, a) for a in range(half)])
    return maps


def matern(dist2):
    dist2 = jnp.maximum(dist2, 1e-30)
    dist = dist2 * lax.rsqrt(dist2)
    poly = (1.0 + ROOT5 * dist) + (5.0 / 3.0) * dist2
    return (poly * jnp.exp2(DECAY * dist)).astype(jnp.bfloat16)


def lane_squares(block):
    wide = block.astype(jnp.float32)
    square = wide * wide
    high = square.astype(jnp.bfloat16)
    low = (square - high.astype(jnp.float32)).astype(jnp.bfloat16)
    ones = jnp.ones((8, block.shape[1]), jnp.bfloat16)
    total = lax.dot_general(ones, high, ROWS_BY_ROWS, preferred_element_type=jnp.float32)
    total += lax.dot_general(ones, low, ROWS_BY_ROWS, preferred_element_type=jnp.float32)
    return total[0:1, :]


def own_kernel(count, shard, *refs):
    rows, noise_ref = refs[:count], refs[count]
    out_ref, squares_ref = refs[count + 1 :]
    col = rows[0][0:shard, :]
    own_squares = lane_squares(col)
    scaled = col * jnp.asarray(-2.0, col.dtype)
    total = noise_ref[...] * rows[0][shard:, :].astype(jnp.float32)
    for slot, row in enumerate(rows):
        block = row[0:shard, :]
        wide = block.astype(jnp.float32)
        squares = jnp.sum(wide * wide, axis=1, keepdims=True)
        squares_ref[pl.ds(slot * shard, shard), :] = jnp.broadcast_to(squares, (shard, 128))
        cross = lax.dot_general(block, scaled, ROWS_BY_ROWS, preferred_element_type=jnp.float32)
        kernel = matern((squares + own_squares) + cross)
        total += jnp.dot(row[shard:, :], kernel, preferred_element_type=jnp.float32)
    out_ref[...] = total


def pair_kernel(count, shard, follows, *refs):
    rows, col_ref, squares_ref = refs[:count], refs[count], refs[count + 1]
    earlier = refs[count + 2 : count + 2 + count * follows]
    back_ref = refs[count + 2 + count * follows]
    outs = refs[count + 3 + count * follows :]
    col = col_ref[0:shard, :]
    col_squares = lane_squares(col)
    scaled = col * jnp.asarray(-2.0, col.dtype)
    back = jnp.zeros(back_ref.shape, jnp.float32)
    for slot, row in enumerate(rows):
        cross = lax.dot_general(row[0:shard, :], scaled, ROWS_BY_ROWS, preferred_element_type=jnp.float32)
        squares = squares_ref[pl.ds(slot * shard, shard), 0:1]
        kernel = matern((squares + col_squares) + cross)
        back += jnp.dot(row[shard:, :], kernel, preferred_element_type=jnp.float32)
        term = lax.dot_general(col_ref[shard:, :], kernel, ROWS_BY_ROWS, preferred_element_type=jnp.float32)
        outs[slot][...] = earlier[slot][...] + term if follows else term
    back_ref[...] = back


def call(body, outs, args, pairs, shard, width, vectors):
    elements = pairs * shard * shard
    whole = pl.BlockSpec(memory_space=pltpu.VMEM)
    return pl.pallas_call(
        body,
        out_shape=[jax.ShapeDtypeStruct(dims, jnp.float32) for dims in outs],
        in_specs=[whole] * len(args),
        out_specs=[whole] * len(outs),
        compiler_params=pltpu.CompilerParams(vmem_limit_bytes=32 * 1024 * 1024),
        cost_estimate=pl.CostEstimate(
            flops=2 * elements * (width + 2 * vectors),
            bytes_accessed=2 * width * shard * (pairs + 1),
            transcendentals=2 * elements,
        ),
    )(*args)


def on_device(features, probes, noise_level):
    count = lax.axis_size("blk")
    inner = group_size(count)
    outer = count // inner
    shard, width = features.shape
    vectors = probes.shape[1]
    flat = (vectors, shard)
    packed = jnp.concatenate([features, probes.T], axis=0)

    def along_outer(value, edges):
        return lax.ppermute(value, "blk", [(s * inner + b, t * inner + b) for s, t in edges for b in range(inner)])

    def in_plane(value, step, give):
        hops = [(b, inner_partner(b, step, inner)) for b in range(inner)]
        if not give:
            hops = [(t, s) for s, t in hops]
        return lax.ppermute(value, "blk", [(a * inner + s, a * inner + t) for a in range(outer) for s, t in hops])

    maps = outer_edges(outer)
    cols = [along_outer(packed, edges) for edges in maps]
    rows = [packed] + [in_plane(packed, step, False) for step in range(1, inner)]

    total, squares = call(
        functools.partial(own_kernel, inner, shard),
        [flat, (inner * shard, 128)],
        rows + [noise_level[None, :]],
        inner, shard, width, vectors,
    )
    terms, backs = [], []
    for edges, col in zip(maps, cols):
        back, *terms = call(
            functools.partial(pair_kernel, inner, shard, 1 if terms else 0),
            [flat] * (inner + 1),
            rows + [col, squares] + terms,
            inner, shard, width, vectors,
        )
        backs.append(along_outer(back, [(t, s) for s, t in edges]))
    for step, term in enumerate(terms):
        total = total + (in_plane(term, step, True) if step else term)
    for back in backs:
        total = total + back
    return total.T


def solution(mesh):
    placed = (P(("parts", "blk"), None), P(("parts", "blk"), None), P(("parts", "blk")))
    return jax.shard_map(
        on_device, mesh=mesh, in_specs=placed, out_specs=P(("parts", "blk"), None), check_vma=False
    )
```

time: 128 us -> 26.3 us (0.21)
  waiting for transfers between devices: 101 us -> 3.95 us
  starting transfers between devices: 0.04 us -> 16.8 us
  between operations: 13.5 us -> 0.06 us
  local copies, waits for them, and re-layouts: 5.31 us -> 0.01 us
  Pallas kernels: 0 us -> 3.64 us
  matrix products: 3.23 us -> 0 us
  other arithmetic: 4.75 us -> 1.56 us
    reduce_scatter x1 -> x0, waiting for transfers between devices: 54.7 us -> none  [on_device(): lax.psum_scatter(lax.map(one_block, (blocks_x, blocks_sq)).reshape(lax.ax...]
    all_gather x1 -> x0, waiting for transfers between devices: 45.3 us -> none  [on_device(): gathered = lax.all_gather(features, 'blk', axis=0, tiled=True)]
    ppermute x0 -> x10, starting transfers between devices: none -> 16.8 us  [the longest x4 11.4 us: along_outer(): lax.ppermute(value, 'blk', [(s * inner + b, t * inner + b) for s, t in ed...]
    dynamic_update_slice x4 -> x0, local copies, waits for them, and re-layouts: 4.16 us -> none  [on_device(): lax.map(one_block, (blocks_x, blocks_sq))]
    ppermute x0 -> x10, waiting for transfers between devices: none -> 3.95 us  [the longest x4 3.36 us: along_outer(): lax.ppermute(value, 'blk', [(s * inner + b, t * inner + b) for s, t in ed...]
    pallas_call x0 -> x3, Pallas kernels: none -> 3.64 us  [call(): pl.pallas_call(body, out_shape=[jax.ShapeDtypeStruct(dims, jnp.float32) f...]
    reduce_sum x2 -> x0, other arithmetic: 3.37 us -> none  [row_squares(): return jnp.sum(wide * wide, axis=1)]
    dot_general x2 -> x0, matrix products: 3.23 us -> none  [kernel_tile(): return jnp.dot(kernel, right_v, preferred_element_type=jnp.float32)]
  transfers between devices with their start and end apart: 2 -> 10, of which waited for: 2 -> 5; matrix products, arithmetic and copies ran while one was open for 1% -> 0% of each run, Pallas kernels for 0% -> 9%
where the time goes in v2:
time: 26.3 us; the launch traced here: 26 us
  starting transfers between devices  16.8 us (64%)
  waiting for transfers between devices  3.95 us (15%)
  Pallas kernels  3.64 us (14%)
  other arithmetic  1.56 us (6%)
    ppermute x4, starting transfers between devices, along_outer(): lax.ppermute(value, 'blk', [(s * inner + b, t * inner + b) for s, t in ed...  11.4 us
    ppermute x6, starting transfers between devices, in_plane(): lax.ppermute(value, 'blk', [(a * inner + s, a * inner + t) for a in range...  5.4 us
    pallas_call x3, Pallas kernels, call(): pl.pallas_call(body, out_shape=[jax.ShapeDtypeStruct(dims, jnp.float32) f...  3.64 us
    ppermute x4, waiting for transfers between devices, along_outer(): lax.ppermute(value, 'blk', [(s * inner + b, t * inner + b) for s, t in ed...  3.36 us
    concatenate x1, other arithmetic, on_device(): packed = jnp.concatenate([features, probes.T], axis=0)  0.93 us
    transpose x1, other arithmetic, on_device(): return total.T  0.63 us
    ppermute x6, waiting for transfers between devices, in_plane(): lax.ppermute(value, 'blk', [(a * inner + s, a * inner + t) for a in range...  0.59 us
  transfers between devices with their start and end apart: 10, of which 5 were waited for; matrix products, arithmetic and copies ran while one was open for 0% of the time, Pallas kernels for 9%

profile of v2, /device:TPU:0, one launch (start us, length us, event | category | flops | bytes accessed | tf_op | source)
XLA Modules:
  0.0 26.0 jit_solution(340619905832651609)
XLA Ops:
  0.0 0.9 %pad_maximum_fusion.refs_0_ = bf16[288,256]{1,0:T(8,128)(2,1)S(1)} fusion(bf16[32,256]{1,0:T(8,128)(2,1)} %bitcast.5, bf16[256,256]{1,0:T(8,128)(2,1)} %param.3), kind=kLoop, calls=%fused_computation | loop fusion | flops 294912 | bytes 294912 | tf_op jit(solution)/shard_map/concatenate | solution.py:116
  0.9 0.0 copy-start
  0.9 2.5 %collective-permute-start.2 = (bf16[288,256]{1,0:T(8,128)(2,1)S(1)}, bf16[288,256]{1,0:T(8,128)(2,1)S(1)}, u32[]{:S(2)}, u32[]{:S(2)}) collective-permute-start(bf16[288,256]{1,0:T(8,128)(2,1)S(1)} %pad_maximum_fusion.refs_0_), channel_id=1, source_target_pairs={{3,0},{2,1},{1,2},{0,3},{7,4},{6,5},{5,6},{4,7},{11,8},{10,9},{9,1... | collective-permute-start | bytes 442376 | tf_op jit(solution)/shard_map/ppermute | solution.py:125
  3.4 0.6 %collective-permute-start.1 = (bf16[288,256]{1,0:T(8,128)(2,1)S(1)}, bf16[288,256]{1,0:T(8,128)(2,1)S(1)}, u32[]{:S(2)}, u32[]{:S(2)}) collective-permute-start(bf16[288,256]{1,0:T(8,128)(2,1)S(1)} %pad_maximum_fusion.refs_0_), channel_id=1, source_target_pairs={{2,0},{3,1},{0,2},{1,3},{6,4},{7,5},{4,6},{5,7},{10,8},{11,9},{8,1... | collective-permute-start | bytes 442376 | tf_op jit(solution)/shard_map/ppermute | solution.py:125
  4.1 0.0 collective-permute-start
  4.1 1.8 %collective-permute-start.4 = (bf16[288,256]{1,0:T(8,128)(2,1)S(1)}, bf16[288,256]{1,0:T(8,128)(2,1)S(1)}, u32[]{:S(2)}, u32[]{:S(2)}) collective-permute-start(bf16[288,256]{1,0:T(8,128)(2,1)S(1)} %pad_maximum_fusion.refs_0_), channel_id=1, source_target_pairs={{0,4},{1,5},{2,6},{3,7},{4,8},{5,9},{6,10},{7,11},{8,12},{9,13},{1... | collective-permute-start | bytes 442376 | tf_op jit(solution)/shard_map/ppermute | solution.py:119
  5.9 4.5 %collective-permute-start.3 = (bf16[288,256]{1,0:T(8,128)(2,1)S(1)}, bf16[288,256]{1,0:T(8,128)(2,1)S(1)}, u32[]{:S(2)}, u32[]{:S(2)}) collective-permute-start(bf16[288,256]{1,0:T(8,128)(2,1)S(1)} %pad_maximum_fusion.refs_0_), channel_id=1, source_target_pairs={{0,8},{1,9},{2,10},{3,11},{12,4},{13,5},{14,6},{15,7},{16,24},{17,... | collective-permute-start | bytes 442376 | tf_op jit(solution)/shard_map/ppermute | solution.py:119
  10.4 0.0 collective-permute-done.2.refs_3_
  10.4 0.6 %collective-permute-done.1.refs_2_ = bf16[288,256]{1,0:T(8,128)(2,1)S(1)} collective-permute-done((bf16[288,256]{1,0:T(8,128)(2,1)S(1)}, bf16[288,256]{1,0:T(8,128)(2,1)S(1)}, u32[]{:S(2)}, u32[]{:S(2)}) %collective-permute-start.1) | collective-permute-done | bytes 147488 | tf_op jit(solution)/shard_map/ppermute | solution.py:125
  11.0 0.0 collective-permute-done.refs_1_
  11.0 1.0 %shard_map.37 = (f32[32,256]{1,0:T(8,128)S(1)}, f32[1024,128]{1,0:T(8,128)S(1)}) custom-call(bf16[288,256]{1,0:T(8,128)(2,1)S(1)} %pad_maximum_fusion.refs_0_, bf16[288,256]{1,0:T(8,128)(2,1)S(1)} %collective-permute-done.refs_1_, bf16[288,256]{1,0:T(8,128)(2,1)S(1)} %collective-permute-done.1.refs_2_, bf16[288,256]{1,0:T(8,128)(2,1)S(1)} %collective-permute-done.2.refs_3_, ...), custom_call_target="tpu_custom_call" | custom-call | flops 167772160 | bytes 655360 | tf_op jit(solution)/shard_map/pallas_call | solution.py:95
  12.0 0.2 collective-permute-done.4.refs_4_
  12.2 1.3 %shard_map.38 = (f32[32,256]{1,0:T(8,128)S(1)}, f32[32,256]{1,0:T(8,128)S(1)}, f32[32,256]{1,0:T(8,128)S(1)}, f32[32,256]{1,0:T(8,128)S(1)}, f32[32,256]{1,0:T(8,128)S(1)}) custom-call(bf16[288,256]{1,0:T(8,128)(2,1)S(1)} %pad_maximum_fusion.refs_0_, bf16[288,256]{1,0:T(8,128)(2,1)S(1)} %collective-permute-done.refs_1_, ...), custom_call_target="tpu_custom_call" | custom-call | flops 167772160 | bytes 655360 | tf_op jit(solution)/shard_map/pallas_call | solution.py:95
  13.5 0.1 collective-permute-done.3.refs_4_
  13.6 1.3 %shard_map.39 = (f32[32,256]{1,0:T(8,128)S(1)}, f32[32,256]{1,0:T(8,128)S(1)}, f32[32,256]{1,0:T(8,128)S(1)}, f32[32,256]{1,0:T(8,128)S(1)}, f32[32,256]{1,0:T(8,128)S(1)}) custom-call(bf16[288,256]{1,0:T(8,128)(2,1)S(1)} %pad_maximum_fusion.refs_0_, bf16[288,256]{1,0:T(8,128)(2,1)S(1)} %collective-permute-done.refs_1_, ...), custom_call_target="tpu_custom_call" | custom-call | flops 167772160 | bytes 655360 | tf_op jit(solution)/shard_map/pallas_call | solution.py:95
  14.9 0.0 collective-permute-start.5
  15.0 2.1 %collective-permute-start.6 = (f32[32,256]{1,0:T(8,128)S(1)}, f32[32,256]{1,0:T(8,128)S(1)}, u32[]{:S(2)}, u32[]{:S(2)}) collective-permute-start(f32[32,256]{1,0:T(8,128)S(1)} %get-tuple-element.25), channel_id=1, source_target_pairs={{0,2},{1,3},{2,0},{3,1},{4,6},{5,7},{6,4},{7,5},{8,10},{9,11},{10,... | collective-permute-start | bytes 98312 | tf_op jit(solution)/shard_map/ppermute | solution.py:125
  17.1 0.1 collective-permute-start.7
  17.2 1.3 %collective-permute-start.9 = (f32[32,256]{1,0:T(8,128)S(1)}, f32[32,256]{1,0:T(8,128)S(1)}, u32[]{:S(2)}, u32[]{:S(2)}) collective-permute-start(f32[32,256]{1,0:T(8,128)S(1)} %get-tuple-element.28), channel_id=1, source_target_pairs={{8,0},{9,1},{10,2},{11,3},{4,12},{5,13},{6,14},{7,15},{24,16},{25,... | collective-permute-start | bytes 98312 | tf_op jit(solution)/shard_map/ppermute | solution.py:119
  18.5 3.9 %collective-permute-start.8 = (f32[32,256]{1,0:T(8,128)S(1)}, f32[32,256]{1,0:T(8,128)S(1)}, u32[]{:S(2)}, u32[]{:S(2)}) collective-permute-start(f32[32,256]{1,0:T(8,128)S(1)} %get-tuple-element.27), channel_id=1, source_target_pairs={{4,0},{5,1},{6,2},{7,3},{8,4},{9,5},{10,6},{11,7},{12,8},{13,9},{1... | collective-permute-start | bytes 98312 | tf_op jit(solution)/shard_map/ppermute | solution.py:119
  22.3 0.0 collective-permute-done.5
  22.4 1.5 %collective-permute-done.9 = f32[32,256]{1,0:T(8,128)S(1)} collective-permute-done((f32[32,256]{1,0:T(8,128)S(1)}, f32[32,256]{1,0:T(8,128)S(1)}, u32[]{:S(2)}, u32[]{:S(2)}) %collective-permute-start.9) | collective-permute-done | bytes 32800 | tf_op jit(solution)/shard_map/ppermute | solution.py:119
  23.9 1.5 %collective-permute-done.8 = f32[32,256]{1,0:T(8,128)S(1)} collective-permute-done((f32[32,256]{1,0:T(8,128)S(1)}, f32[32,256]{1,0:T(8,128)S(1)}, u32[]{:S(2)}, u32[]{:S(2)}) %collective-permute-start.8) | collective-permute-done | bytes 32800 | tf_op jit(solution)/shard_map/ppermute | solution.py:119
  25.4 0.6 %add_bitcast_fusion = f32[256,32]{0,1:T(8,128)} fusion(f32[32,256]{1,0:T(8,128)S(1)} %collective-permute-done.9, f32[32,256]{1,0:T(8,128)S(1)} %collective-permute-done.8, f32[32,256]{1,0:T(8,128)S(1)} %collective-permute-done.7, f32[32,256]{1,0:T(8,128)S(1)} %collective-permute-done.6, f32[32,256]{1,0:T(8,128)S(1)} %collective-permute-done.5, ...), kind=kLoop, calls=%fused_computation.1 | loop fusion | flops 49152 | bytes 262144 | tf_op jit(solution)/shard_map/transpose | solution.py:150
  (3 shorter events, 0.0 us)
Async XLA Ops:
  0.9 10.1 %copy-start = (f32[256]{0:T(256)S(1)}, f32[256]{0:T(256)}, u32[]{:S(2)}) copy-start(f32[256]{0:T(256)} %param.5) | copy-start | bytes 3076
  0.9 9.5 %collective-permute-start.2 = (bf16[288,256]{1,0:T(8,128)(2,1)S(1)}, bf16[288,256]{1,0:T(8,128)(2,1)S(1)}, u32[]{:S(2)}, u32[]{:S(2)}) collective-permute-start(bf16[288,256]{1,0:T(8,128)(2,1)S(1)} %pad_maximum_fusion.refs_0_), channel_id=1, source_target_pairs={{3,0},{2,1},{1,2},{0,3},{7,4},{6,5},{5,6},{4,7},{11,8},{10,9},{9,1... | collective-permute-start | bytes 442376 | tf_op jit(solution)/shard_map/ppermute | solution.py:125
  3.4 7.6 %collective-permute-start.1 = (bf16[288,256]{1,0:T(8,128)(2,1)S(1)}, bf16[288,256]{1,0:T(8,128)(2,1)S(1)}, u32[]{:S(2)}, u32[]{:S(2)}) collective-permute-start(bf16[288,256]{1,0:T(8,128)(2,1)S(1)} %pad_maximum_fusion.refs_0_), channel_id=1, source_target_pairs={{2,0},{3,1},{0,2},{1,3},{6,4},{7,5},{4,6},{5,7},{10,8},{11,9},{8,1... | collective-permute-start | bytes 442376 | tf_op jit(solution)/shard_map/ppermute | solution.py:125
  4.1 6.9 %collective-permute-start = (bf16[288,256]{1,0:T(8,128)(2,1)S(1)}, bf16[288,256]{1,0:T(8,128)(2,1)S(1)}, u32[]{:S(2)}, u32[]{:S(2)}) collective-permute-start(bf16[288,256]{1,0:T(8,128)(2,1)S(1)} %pad_maximum_fusion.refs_0_), channel_id=1, source_target_pairs={{1,0},{0,1},{3,2},{2,3},{5,4},{4,5},{7,6},{6,7},{9,8},{8,9},{11,10... | collective-permute-start | bytes 442376 | tf_op jit(solution)/shard_map/ppermute | solution.py:125
  4.1 8.1 %collective-permute-start.4 = (bf16[288,256]{1,0:T(8,128)(2,1)S(1)}, bf16[288,256]{1,0:T(8,128)(2,1)S(1)}, u32[]{:S(2)}, u32[]{:S(2)}) collective-permute-start(bf16[288,256]{1,0:T(8,128)(2,1)S(1)} %pad_maximum_fusion.refs_0_), channel_id=1, source_target_pairs={{0,4},{1,5},{2,6},{3,7},{4,8},{5,9},{6,10},{7,11},{8,12},{9,13},{1... | collective-permute-start | bytes 442376 | tf_op jit(solution)/shard_map/ppermute | solution.py:119
  5.9 7.7 %collective-permute-start.3 = (bf16[288,256]{1,0:T(8,128)(2,1)S(1)}, bf16[288,256]{1,0:T(8,128)(2,1)S(1)}, u32[]{:S(2)}, u32[]{:S(2)}) collective-permute-start(bf16[288,256]{1,0:T(8,128)(2,1)S(1)} %pad_maximum_fusion.refs_0_), channel_id=1, source_target_pairs={{0,8},{1,9},{2,10},{3,11},{12,4},{13,5},{14,6},{15,7},{16,24},{17,... | collective-permute-start | bytes 442376 | tf_op jit(solution)/shard_map/ppermute | solution.py:119
  14.9 7.4 %collective-permute-start.5 = (f32[32,256]{1,0:T(8,128)S(1)}, f32[32,256]{1,0:T(8,128)S(1)}, u32[]{:S(2)}, u32[]{:S(2)}) collective-permute-start(f32[32,256]{1,0:T(8,128)S(1)} %get-tuple-element.24), channel_id=1, source_target_pairs={{0,1},{1,0},{2,3},{3,2},{4,5},{5,4},{6,7},{7,6},{8,9},{9,8},{10,11... | collective-permute-start | bytes 98312 | tf_op jit(solution)/shard_map/ppermute | solution.py:125
  15.0 7.4 %collective-permute-start.6 = (f32[32,256]{1,0:T(8,128)S(1)}, f32[32,256]{1,0:T(8,128)S(1)}, u32[]{:S(2)}, u32[]{:S(2)}) collective-permute-start(f32[32,256]{1,0:T(8,128)S(1)} %get-tuple-element.25), channel_id=1, source_target_pairs={{0,2},{1,3},{2,0},{3,1},{4,6},{5,7},{6,4},{7,5},{8,10},{9,11},{10,... | collective-permute-start | bytes 98312 | tf_op jit(solution)/shard_map/ppermute | solution.py:125
  17.1 5.2 %collective-permute-start.7 = (f32[32,256]{1,0:T(8,128)S(1)}, f32[32,256]{1,0:T(8,128)S(1)}, u32[]{:S(2)}, u32[]{:S(2)}) collective-permute-start(f32[32,256]{1,0:T(8,128)S(1)} %get-tuple-element.26), channel_id=1, source_target_pairs={{0,3},{1,2},{2,1},{3,0},{4,7},{5,6},{6,5},{7,4},{8,11},{9,10},{10,... | collective-permute-start | bytes 98312 | tf_op jit(solution)/shard_map/ppermute | solution.py:125
  17.2 6.7 %collective-permute-start.9 = (f32[32,256]{1,0:T(8,128)S(1)}, f32[32,256]{1,0:T(8,128)S(1)}, u32[]{:S(2)}, u32[]{:S(2)}) collective-permute-start(f32[32,256]{1,0:T(8,128)S(1)} %get-tuple-element.28), channel_id=1, source_target_pairs={{8,0},{9,1},{10,2},{11,3},{4,12},{5,13},{6,14},{7,15},{24,16},{25,... | collective-permute-start | bytes 98312 | tf_op jit(solution)/shard_map/ppermute | solution.py:119
  18.5 6.9 %collective-permute-start.8 = (f32[32,256]{1,0:T(8,128)S(1)}, f32[32,256]{1,0:T(8,128)S(1)}, u32[]{:S(2)}, u32[]{:S(2)}) collective-permute-start(f32[32,256]{1,0:T(8,128)S(1)} %get-tuple-element.27), channel_id=1, source_target_pairs={{4,0},{5,1},{6,2},{7,3},{8,4},{9,5},{10,6},{11,7},{12,8},{13,9},{1... | collective-permute-start | bytes 98312 | tf_op jit(solution)/shard_map/ppermute | solution.py:119

commit v3 on v2

v3 whole, which is shorter than its diff:
```python
import functools
import math

import jax
import jax.numpy as jnp
from jax import lax
from jax.experimental import pallas as pl
from jax.experimental.pallas import tpu as pltpu
from jax.sharding import PartitionSpec as P

ROOT5 = math.sqrt(5.0)
DECAY = -ROOT5 * math.log2(math.e)
ROWS_BY_ROWS = (((1,), (1,)), ((), ()))


def group_size(count):
    size = 1
    while size * size < count or count % size:
        size += 1
    return size


def plane_blocks(value, count, send):
    if count & (count - 1):
        maps = {step: [(b, (b - step) % count) for b in range(count)] for step in range(1, count)}
        return [value] + [send(value, maps[step]) for step in range(1, count)]
    blocks = {0: value}
    bit = count // 2
    while bit:
        for known in list(blocks):
            blocks[known | bit] = send(blocks[known], [(b, b ^ bit) for b in range(count)])
        bit //= 2
    return [blocks[distance] for distance in range(count)]


def plane_target(index, step, count):
    return (index + step) % count if count & (count - 1) else index ^ step


def outer_edges(count):
    maps = [([(a, (a + step) % count) for a in range(count)], range(count)) for step in range(1, (count + 1) // 2)]
    if count % 2 == 0:
        half = count // 2
        real = [(a, a + half) if a % 2 == 0 else (a + half, a) for a in range(half)]
        if half % 2 == 0:
            spare = [(a, a - 1) if a % 2 else (a + half, a + half + 1) for a in range(half)]
        else:
            spare = [(t, s) for s, t in real]
        maps.append((real + spare, [t for _, t in real]))
    return maps


def matern(dist2):
    dist2 = jnp.maximum(dist2, 1e-30)
    dist = dist2 * lax.rsqrt(dist2)
    poly = (1.0 + ROOT5 * dist) + (5.0 / 3.0) * dist2
    return (poly * jnp.exp2(DECAY * dist)).astype(jnp.bfloat16)


def lane_squares(block):
    wide = block.astype(jnp.float32)
    square = wide * wide
    high = square.astype(jnp.bfloat16)
    low = (square - high.astype(jnp.float32)).astype(jnp.bfloat16)
    ones = jnp.ones((8, block.shape[1]), jnp.bfloat16)
    total = lax.dot_general(ones, high, ROWS_BY_ROWS, preferred_element_type=jnp.float32)
    total += lax.dot_general(ones, low, ROWS_BY_ROWS, preferred_element_type=jnp.float32)
    return total[0:1, :]


def tile_kernel(rows_in, cols_in, spreads, weights, terms_in, backs_in, noise_in, shard, *refs):
    refs = list(refs)
    take = lambda number: [refs.pop(0) for _ in range(number)]
    rows, cols = take(rows_in), take(cols_in)
    old_terms, old_backs, noise = take(terms_in), take(backs_in), take(noise_in)
    new_backs, new_terms = take(cols_in), refs
    terms = [ref[...] for ref in old_terms] or [None] * rows_in
    row_squares = []
    for row in rows:
        wide = row[0:shard, :].astype(jnp.float32)
        row_squares.append(jnp.sum(wide * wide, axis=1, keepdims=True))
    for place, col_ref in enumerate(cols):
        col = col_ref[0:shard, :]
        col_squares = lane_squares(col)
        scaled = col * jnp.asarray(-2.0, col.dtype)
        weight = None
        if weights[place] is not None:
            outer = lax.axis_index("blk") // weights[place][0]
            weight = functools.reduce(lambda sofar, a: jnp.where(outer == a, 1.0, sofar), weights[place][1], 0.0)
        back = None
        for slot, row in enumerate(rows):
            cross = lax.dot_general(row[0:shard, :], scaled, ROWS_BY_ROWS, preferred_element_type=jnp.float32)
            kernel = matern((row_squares[slot] + col_squares) + cross)
            share = jnp.dot(row[shard:, :], kernel, preferred_element_type=jnp.float32)
            back = share if back is None else back + share
            if spreads[place]:
                term = lax.dot_general(col_ref[shard:, :], kernel, ROWS_BY_ROWS, preferred_element_type=jnp.float32)
                term = term if weight is None else weight * term
                terms[slot] = term if terms[slot] is None else terms[slot] + term
        back = back if weight is None else weight * back
        if noise and not spreads[place]:
            back = back + noise[0][...] * col_ref[shard:, :].astype(jnp.float32)
        new_backs[place][...] = old_backs[place][...] + back if old_backs else back
    for ref, term in zip(new_terms, terms):
        ref[...] = term


def tile(rows, cols, spreads, weights, terms, backs, noise, shard):
    width, vectors = rows[0].shape[1], rows[0].shape[0] - shard
    args = [*rows, *cols, *terms, *backs, *noise]
    elements = len(rows) * len(cols) * shard * shard
    whole = pl.BlockSpec(memory_space=pltpu.VMEM)
    outs = [jax.ShapeDtypeStruct((vectors, shard), jnp.float32)] * (len(cols) + len(rows))
    found = pl.pallas_call(
        functools.partial(tile_kernel, len(rows), len(cols), spreads, weights, len(terms), len(backs), len(noise), shard),
        out_shape=outs,
        in_specs=[whole] * len(args),
        out_specs=[whole] * len(outs),
        compiler_params=pltpu.CompilerParams(vmem_limit_bytes=32 * 1024 * 1024),
        cost_estimate=pl.CostEstimate(
            flops=2 * elements * (width + 2 * vectors),
            bytes_accessed=2 * width * shard * (len(rows) + len(cols)),
            transcendentals=2 * elements,
        ),
    )(*args)
    return found[: len(cols)], found[len(cols) :]


def on_device(features, probes, noise_level):
    count = lax.axis_size("blk")
    inner = group_size(count)
    outer = count // inner
    shard = features.shape[0]
    packed = jnp.concatenate([features, probes.T], axis=0)

    def along_outer(value, edges):
        return lax.ppermute(value, "blk", [(s * inner + b, t * inner + b) for s, t in edges for b in range(inner)])

    def in_plane(value, hops):
        return lax.ppermute(value, "blk", [(a * inner + s, a * inner + t) for a in range(outer) for s, t in hops])

    maps = outer_edges(outer)
    cols = [along_outer(packed, edges) for edges, _ in maps]
    weights = [None if len(targets) == outer else (inner, tuple(targets)) for _, targets in maps]
    blocks = plane_blocks(packed, inner, in_plane)

    direct = [d for d in range(inner) if d & (d - 1) == 0]
    passed = [d for d in range(inner) if d & (d - 1)]
    rows = [blocks[d] for d in direct]
    backs, terms = tile(
        rows,
        [packed] + cols[:-1],
        [False] + [True] * len(cols[:-1]),
        [None] + weights[:-1],
        [],
        [],
        [noise_level[None, :]],
        shard,
    )
    last, terms = tile(rows, cols[-1:], [True], weights[-1:], terms, [], [], shard)
    backs, late = tile(
        [blocks[d] for d in passed],
        [packed] + cols,
        [False] + [True] * len(cols),
        [None] + weights,
        [],
        list(backs) + list(last),
        [],
        shard,
    )
    total = backs[0] + terms[0]
    for step, term in zip(direct[1:] + passed, list(terms[1:]) + list(late)):
        total = total + in_plane(term, [(b, plane_target(b, step, inner)) for b in range(inner)])
    for (edges, _), back in zip(maps, backs[1:]):
        total = total + along_outer(back, [(t, s) for s, t in edges])
    return total.T


def solution(mesh):
    placed = (P(("parts", "blk"), None), P(("parts", "blk"), None), P(("parts", "blk")))
    return jax.shard_map(
        on_device, mesh=mesh, in_specs=placed, out_specs=P(("parts", "blk"), None), check_vma=False
    )
```

time: 26.3 us -> 25.9 us (0.985)
  starting transfers between devices: 16.8 us -> 11.4 us
  waiting for transfers between devices: 3.95 us -> 9 us
    ppermute x4, waiting for transfers between devices: 3.36 us -> 8.97 us  [along_outer(): lax.ppermute(value, 'blk', [(s * inner + b, t * inner + b) for s, t in ed...]
    ppermute x4, starting transfers between devices: 11.4 us -> 6.19 us  [along_outer(): lax.ppermute(value, 'blk', [(s * inner + b, t * inner + b) for s, t in ed...]
    ppermute x6, waiting for transfers between devices: 0.59 us -> 0.03 us  [in_plane(): lax.ppermute(value, 'blk', [(a * inner + s, a * inner + t) for a in range...]
  transfers between devices with their start and end apart: 10 -> 10, of which waited for: 5 -> 4; matrix products, arithmetic and copies ran while one was open for 0% -> 0% of each run, Pallas kernels for 9% -> 14%
where the time goes in v3:
time: 25.9 us; the launch traced here: 25.7 us
  starting transfers between devices  11.4 us (44%)
  waiting for transfers between devices  9 us (35%)
  Pallas kernels  3.66 us (14%)
  other arithmetic  1.56 us (6%)
    ppermute x4, waiting for transfers between devices, along_outer(): lax.ppermute(value, 'blk', [(s * inner + b, t * inner + b) for s, t in ed...  8.97 us
    ppermute x4, starting transfers between devices, along_outer(): lax.ppermute(value, 'blk', [(s * inner + b, t * inner + b) for s, t in ed...  6.19 us
    ppermute x6, starting transfers between devices, in_plane(): lax.ppermute(value, 'blk', [(a * inner + s, a * inner + t) for a in range...  5.21 us
    pallas_call x3, Pallas kernels, tile(): pl.pallas_call(functools.partial(tile_kernel, len(rows), len(cols), sprea...  3.66 us
    concatenate x1, other arithmetic, on_device(): packed = jnp.concatenate([features, probes.T], axis=0)  0.93 us
    transpose x1, other arithmetic, on_device(): return total.T  0.63 us
  transfers between devices with their start and end apart: 10, of which 4 were waited for; matrix products, arithmetic and copies ran while one was open for 0% of the time, Pallas kernels for 14%

profile of v3, /device:TPU:0, one launch (start us, length us, event | category | flops | bytes accessed | tf_op | source)
XLA Modules:
  0.0 25.7 jit_solution(7139145365682631435)
XLA Ops:
  0.0 0.9 %pad_maximum_fusion.refs_0_.refs_3_.refs_1_ = bf16[288,256]{1,0:T(8,128)(2,1)S(1)} fusion(bf16[32,256]{1,0:T(8,128)(2,1)} %bitcast.5, bf16[256,256]{1,0:T(8,128)(2,1)} %param.3), kind=kLoop, calls=%fused_computation | loop fusion | flops 294912 | bytes 294912 | tf_op jit(solution)/shard_map/concatenate | solution.py:134
  0.9 0.0 copy-start
  0.9 3.0 %collective-permute-start = (bf16[288,256]{1,0:T(8,128)(2,1)S(1)}, bf16[288,256]{1,0:T(8,128)(2,1)S(1)}, u32[]{:S(2)}, u32[]{:S(2)}) collective-permute-start(bf16[288,256]{1,0:T(8,128)(2,1)S(1)} %pad_maximum_fusion.refs_0_.refs_3_.refs_1_), channel_id=1, source_target_pairs={{0,2},{1,3},{2,0},{3,1},{4,6},{5,7},{6,4},{7,5},{8,10},{9,11},{10,... | collective-permute-start | bytes 442376 | tf_op jit(solution)/shard_map/ppermute | solution.py:140
  4.0 1.6 %collective-permute-start.2 = (bf16[288,256]{1,0:T(8,128)(2,1)S(1)}, bf16[288,256]{1,0:T(8,128)(2,1)S(1)}, u32[]{:S(2)}, u32[]{:S(2)}) collective-permute-start(bf16[288,256]{1,0:T(8,128)(2,1)S(1)} %pad_maximum_fusion.refs_0_.refs_3_.refs_1_), channel_id=1, source_target_pairs={{0,4},{1,5},{2,6},{3,7},{4,8},{5,9},{6,10},{7,11},{8,12},{9,13},{1... | collective-permute-start | bytes 442376 | tf_op jit(solution)/shard_map/ppermute | solution.py:137
  5.6 0.0 collective-permute-start.4
  5.6 2.6 %collective-permute-start.3 = (bf16[288,256]{1,0:T(8,128)(2,1)S(1)}, bf16[288,256]{1,0:T(8,128)(2,1)S(1)}, u32[]{:S(2)}, u32[]{:S(2)}) collective-permute-start(bf16[288,256]{1,0:T(8,128)(2,1)S(1)} %pad_maximum_fusion.refs_0_.refs_3_.refs_1_), channel_id=1, source_target_pairs={{0,8},{1,9},{2,10},{3,11},{12,4},{13,5},{14,6},{15,7},{8,12},{9,13... | collective-permute-start | bytes 442376 | tf_op jit(solution)/shard_map/ppermute | solution.py:137
  8.2 0.2 collective-permute-start.1
  8.4 3.4 %collective-permute-done.2.refs_4_.refs_2_ = bf16[288,256]{1,0:T(8,128)(2,1)S(1)} collective-permute-done((bf16[288,256]{1,0:T(8,128)(2,1)S(1)}, bf16[288,256]{1,0:T(8,128)(2,1)S(1)}, u32[]{:S(2)}, u32[]{:S(2)}) %collective-permute-start.2) | collective-permute-done | bytes 147488 | tf_op jit(solution)/shard_map/ppermute | solution.py:137
  11.7 1.4 %shard_map.37 = (f32[32,256]{1,0:T(8,128)S(1)}, f32[32,256]{1,0:T(8,128)S(1)}, f32[32,256]{1,0:T(8,128)S(1)}, f32[32,256]{1,0:T(8,128)S(1)}, f32[32,256]{1,0:T(8,128)S(1)}) custom-call(bf16[288,256]{1,0:T(8,128)(2,1)S(1)} %pad_maximum_fusion.refs_0_.refs_3_.refs_1_, bf16[288,256]{1,0:T(8,128)(2,1)S(1)} %collective-permute-done.4.refs_1_, ...), custom_call_target="tpu_custom_call" | custom-call | flops 251658240 | bytes 655360 | tf_op jit(solution)/shard_map/pallas_call | solution.py:114
  13.2 1.1 %collective-permute-done.3.refs_3_ = bf16[288,256]{1,0:T(8,128)(2,1)S(1)} collective-permute-done((bf16[288,256]{1,0:T(8,128)(2,1)S(1)}, bf16[288,256]{1,0:T(8,128)(2,1)S(1)}, u32[]{:S(2)}, u32[]{:S(2)}) %collective-permute-start.3) | collective-permute-done | bytes 147488 | tf_op jit(solution)/shard_map/ppermute | solution.py:137
  14.3 1.0 %shard_map.38 = (f32[32,256]{1,0:T(8,128)S(1)}, f32[32,256]{1,0:T(8,128)S(1)}, f32[32,256]{1,0:T(8,128)S(1)}, f32[32,256]{1,0:T(8,128)S(1)}) custom-call(bf16[288,256]{1,0:T(8,128)(2,1)S(1)} %pad_maximum_fusion.refs_0_.refs_3_.refs_1_, bf16[288,256]{1,0:T(8,128)(2,1)S(1)} %collective-permute-done.4.refs_1_, ...), custom_call_target="tpu_custom_call" | custom-call | flops 125829120 | bytes 524288 | tf_op jit(solution)/shard_map/pallas_call | solution.py:114
  15.3 0.1 collective-permute-start.5
  15.5 0.5 %collective-permute-start.6 = (f32[32,256]{1,0:T(8,128)S(1)}, f32[32,256]{1,0:T(8,128)S(1)}, u32[]{:S(2)}, u32[]{:S(2)}) collective-permute-start(f32[32,256]{1,0:T(8,128)S(1)} %get-tuple-element.27), channel_id=1, source_target_pairs={{0,2},{1,3},{2,0},{3,1},{4,6},{5,7},{6,4},{7,5},{8,10},{9,11},{10,... | collective-permute-start | bytes 98312 | tf_op jit(solution)/shard_map/ppermute | solution.py:140
  16.0 0.0 collective-permute-done.1.refs_0_
  16.0 1.2 %shard_map.39 = (f32[32,256]{1,0:T(8,128)S(1)}, f32[32,256]{1,0:T(8,128)S(1)}, f32[32,256]{1,0:T(8,128)S(1)}, f32[32,256]{1,0:T(8,128)S(1)}) custom-call(bf16[288,256]{1,0:T(8,128)(2,1)S(1)} %collective-permute-done.1.refs_0_, bf16[288,256]{1,0:T(8,128)(2,1)S(1)} %pad_maximum_fusion.refs_0_.refs_3_.refs_1_, ...), custom_call_target="tpu_custom_call" | custom-call | flops 125829120 | bytes 524288 | tf_op jit(solution)/shard_map/pallas_call | solution.py:114
  17.2 1.3 %collective-permute-start.7 = (f32[32,256]{1,0:T(8,128)S(1)}, f32[32,256]{1,0:T(8,128)S(1)}, u32[]{:S(2)}, u32[]{:S(2)}) collective-permute-start(f32[32,256]{1,0:T(8,128)S(1)} %get-tuple-element.28), channel_id=1, source_target_pairs={{0,3},{1,2},{2,1},{3,0},{4,7},{5,6},{6,5},{7,4},{8,11},{9,10},{10,... | collective-permute-start | bytes 98312 | tf_op jit(solution)/shard_map/ppermute | solution.py:140
  18.5 1.7 %collective-permute-start.8 = (f32[32,256]{1,0:T(8,128)S(1)}, f32[32,256]{1,0:T(8,128)S(1)}, u32[]{:S(2)}, u32[]{:S(2)}) collective-permute-start(f32[32,256]{1,0:T(8,128)S(1)} %get-tuple-element.29), channel_id=1, source_target_pairs={{4,0},{5,1},{6,2},{7,3},{8,4},{9,5},{10,6},{11,7},{12,8},{13,9},{1... | collective-permute-start | bytes 98312 | tf_op jit(solution)/shard_map/ppermute | solution.py:137
  20.2 0.3 %collective-permute-start.9 = (f32[32,256]{1,0:T(8,128)S(1)}, f32[32,256]{1,0:T(8,128)S(1)}, u32[]{:S(2)}, u32[]{:S(2)}) collective-permute-start(f32[32,256]{1,0:T(8,128)S(1)} %get-tuple-element.30), channel_id=1, source_target_pairs={{8,0},{9,1},{10,2},{11,3},{4,12},{5,13},{6,14},{7,15},{12,8},{13,9... | collective-permute-start | bytes 98312 | tf_op jit(solution)/shard_map/ppermute | solution.py:137
  20.5 0.0 collective-permute-done.5
  20.5 0.0 collective-permute-done.6
  20.5 0.0 collective-permute-done.7
  20.5 1.9 %collective-permute-done.8 = f32[32,256]{1,0:T(8,128)S(1)} collective-permute-done((f32[32,256]{1,0:T(8,128)S(1)}, f32[32,256]{1,0:T(8,128)S(1)}, u32[]{:S(2)}, u32[]{:S(2)}) %collective-permute-start.8) | collective-permute-done | bytes 32800 | tf_op jit(solution)/shard_map/ppermute | solution.py:137
  22.4 2.6 %collective-permute-done.9 = f32[32,256]{1,0:T(8,128)S(1)} collective-permute-done((f32[32,256]{1,0:T(8,128)S(1)}, f32[32,256]{1,0:T(8,128)S(1)}, u32[]{:S(2)}, u32[]{:S(2)}) %collective-permute-start.9) | collective-permute-done | bytes 32800 | tf_op jit(solution)/shard_map/ppermute | solution.py:137
  25.0 0.6 %add_bitcast_fusion = f32[256,32]{0,1:T(8,128)} fusion(f32[32,256]{1,0:T(8,128)S(1)} %collective-permute-done.9, f32[32,256]{1,0:T(8,128)S(1)} %collective-permute-done.8, f32[32,256]{1,0:T(8,128)S(1)} %collective-permute-done.7, f32[32,256]{1,0:T(8,128)S(1)} %collective-permute-done.6, f32[32,256]{1,0:T(8,128)S(1)} %collective-permute-done.5, ...), kind=kLoop, calls=%fused_computation.1 | loop fusion | flops 49152 | bytes 262144 | tf_op jit(solution)/shard_map/transpose | solution.py:176
  (3 shorter events, 0.0 us)
Async XLA Ops:
  0.9 10.8 %copy-start = (f32[256]{0:T(256)S(1)}, f32[256]{0:T(256)}, u32[]{:S(2)}) copy-start(f32[256]{0:T(256)} %param.5) | copy-start | bytes 3076
  0.9 7.2 %collective-permute-start = (bf16[288,256]{1,0:T(8,128)(2,1)S(1)}, bf16[288,256]{1,0:T(8,128)(2,1)S(1)}, u32[]{:S(2)}, u32[]{:S(2)}) collective-permute-start(bf16[288,256]{1,0:T(8,128)(2,1)S(1)} %pad_maximum_fusion.refs_0_.refs_3_.refs_1_), channel_id=1, source_target_pairs={{0,2},{1,3},{2,0},{3,1},{4,6},{5,7},{6,4},{7,5},{8,10},{9,11},{10,... | collective-permute-start | bytes 442376 | tf_op jit(solution)/shard_map/ppermute | solution.py:140
  4.0 7.8 %collective-permute-start.2 = (bf16[288,256]{1,0:T(8,128)(2,1)S(1)}, bf16[288,256]{1,0:T(8,128)(2,1)S(1)}, u32[]{:S(2)}, u32[]{:S(2)}) collective-permute-start(bf16[288,256]{1,0:T(8,128)(2,1)S(1)} %pad_maximum_fusion.refs_0_.refs_3_.refs_1_), channel_id=1, source_target_pairs={{0,4},{1,5},{2,6},{3,7},{4,8},{5,9},{6,10},{7,11},{8,12},{9,13},{1... | collective-permute-start | bytes 442376 | tf_op jit(solution)/shard_map/ppermute | solution.py:137
  5.6 6.2 %collective-permute-start.4 = (bf16[288,256]{1,0:T(8,128)(2,1)S(1)}, bf16[288,256]{1,0:T(8,128)(2,1)S(1)}, u32[]{:S(2)}, u32[]{:S(2)}) collective-permute-start(bf16[288,256]{1,0:T(8,128)(2,1)S(1)} %pad_maximum_fusion.refs_0_.refs_3_.refs_1_), channel_id=1, source_target_pairs={{0,1},{1,0},{2,3},{3,2},{4,5},{5,4},{6,7},{7,6},{8,9},{9,8},{10,11... | collective-permute-start | bytes 442376 | tf_op jit(solution)/shard_map/ppermute | solution.py:140
  5.6 8.7 %collective-permute-start.3 = (bf16[288,256]{1,0:T(8,128)(2,1)S(1)}, bf16[288,256]{1,0:T(8,128)(2,1)S(1)}, u32[]{:S(2)}, u32[]{:S(2)}) collective-permute-start(bf16[288,256]{1,0:T(8,128)(2,1)S(1)} %pad_maximum_fusion.refs_0_.refs_3_.refs_1_), channel_id=1, source_target_pairs={{0,8},{1,9},{2,10},{3,11},{12,4},{13,5},{14,6},{15,7},{8,12},{9,13... | collective-permute-start | bytes 442376 | tf_op jit(solution)/shard_map/ppermute | solution.py:137
  8.2 7.8 %collective-permute-start.1 = (bf16[288,256]{1,0:T(8,128)(2,1)S(1)}, bf16[288,256]{1,0:T(8,128)(2,1)S(1)}, u32[]{:S(2)}, u32[]{:S(2)}) collective-permute-start(bf16[288,256]{1,0:T(8,128)(2,1)S(1)} %collective-permute-done.refs_2_), channel_id=1, source_target_pairs={{0,1},{1,0},{2,3},{3,2},{4,5},{5,4},{6,7},{7,6},{8,9},{9,8},{10,11... | collective-permute-start | bytes 442376 | tf_op jit(solution)/shard_map/ppermute | solution.py:140
  15.3 5.2 %collective-permute-start.5 = (f32[32,256]{1,0:T(8,128)S(1)}, f32[32,256]{1,0:T(8,128)S(1)}, u32[]{:S(2)}, u32[]{:S(2)}) collective-permute-start(f32[32,256]{1,0:T(8,128)S(1)} %get-tuple-element.26), channel_id=1, source_target_pairs={{0,1},{1,0},{2,3},{3,2},{4,5},{5,4},{6,7},{7,6},{8,9},{9,8},{10,11... | collective-permute-start | bytes 98312 | tf_op jit(solution)/shard_map/ppermute | solution.py:140
  15.5 5.0 %collective-permute-start.6 = (f32[32,256]{1,0:T(8,128)S(1)}, f32[32,256]{1,0:T(8,128)S(1)}, u32[]{:S(2)}, u32[]{:S(2)}) collective-permute-start(f32[32,256]{1,0:T(8,128)S(1)} %get-tuple-element.27), channel_id=1, source_target_pairs={{0,2},{1,3},{2,0},{3,1},{4,6},{5,7},{6,4},{7,5},{8,10},{9,11},{10,... | collective-permute-start | bytes 98312 | tf_op jit(solution)/shard_map/ppermute | solution.py:140
  17.2 3.4 %collective-permute-start.7 = (f32[32,256]{1,0:T(8,128)S(1)}, f32[32,256]{1,0:T(8,128)S(1)}, u32[]{:S(2)}, u32[]{:S(2)}) collective-permute-start(f32[32,256]{1,0:T(8,128)S(1)} %get-tuple-element.28), channel_id=1, source_target_pairs={{0,3},{1,2},{2,1},{3,0},{4,7},{5,6},{6,5},{7,4},{8,11},{9,10},{10,... | collective-permute-start | bytes 98312 | tf_op jit(solution)/shard_map/ppermute | solution.py:140
  18.5 3.9 %collective-permute-start.8 = (f32[32,256]{1,0:T(8,128)S(1)}, f32[32,256]{1,0:T(8,128)S(1)}, u32[]{:S(2)}, u32[]{:S(2)}) collective-permute-start(f32[32,256]{1,0:T(8,128)S(1)} %get-tuple-element.29), channel_id=1, source_target_pairs={{4,0},{5,1},{6,2},{7,3},{8,4},{9,5},{10,6},{11,7},{12,8},{13,9},{1... | collective-permute-start | bytes 98312 | tf_op jit(solution)/shard_map/ppermute | solution.py:137
  20.2 4.8 %collective-permute-start.9 = (f32[32,256]{1,0:T(8,128)S(1)}, f32[32,256]{1,0:T(8,128)S(1)}, u32[]{:S(2)}, u32[]{:S(2)}) collective-permute-start(f32[32,256]{1,0:T(8,128)S(1)} %get-tuple-element.30), channel_id=1, source_target_pairs={{8,0},{9,1},{10,2},{11,3},{4,12},{5,13},{6,14},{7,15},{12,8},{13,9... | collective-permute-start | bytes 98312 | tf_op jit(solution)/shard_map/ppermute | solution.py:137

commit v4 on v3

--- a/solution.py
+++ b/solution.py
@@ -68,11 +68,11 @@
     return total[0:1, :]
 
 
-def tile_kernel(rows_in, cols_in, spreads, weights, terms_in, backs_in, noise_in, shard, *refs):
+def tile_kernel(rows_in, cols_in, spreads, weights, terms_in, backs_in, noise_in, extras_in, shard, *refs):
     refs = list(refs)
     take = lambda number: [refs.pop(0) for _ in range(number)]
     rows, cols = take(rows_in), take(cols_in)
-    old_terms, old_backs, noise = take(terms_in), take(backs_in), take(noise_in)
+    old_terms, old_backs, noise, extras = take(terms_in), take(backs_in), take(noise_in), take(extras_in)
     new_backs, new_terms = take(cols_in), refs
     terms = [ref[...] for ref in old_terms] or [None] * rows_in
     row_squares = []
@@ -101,18 +101,22 @@
         if noise and not spreads[place]:
             back = back + noise[0][...] * col_ref[shard:, :].astype(jnp.float32)
         new_backs[place][...] = old_backs[place][...] + back if old_backs else back
+    for extra in extras:
+        terms[0] = terms[0] + extra[...]
     for ref, term in zip(new_terms, terms):
         ref[...] = term
 
 
-def tile(rows, cols, spreads, weights, terms, backs, noise, shard):
+def tile(rows, cols, spreads, weights, shard, terms=(), backs=(), noise=(), extras=()):
     width, vectors = rows[0].shape[1], rows[0].shape[0] - shard
-    args = [*rows, *cols, *terms, *backs, *noise]
+    args = [*rows, *cols, *terms, *backs, *noise, *extras]
     elements = len(rows) * len(cols) * shard * shard
     whole = pl.BlockSpec(memory_space=pltpu.VMEM)
     outs = [jax.ShapeDtypeStruct((vectors, shard), jnp.float32)] * (len(cols) + len(rows))
     found = pl.pallas_call(
-        functools.partial(tile_kernel, len(rows), len(cols), spreads, weights, len(terms), len(backs), len(noise), shard),
+        functools.partial(
+            tile_kernel, len(rows), len(cols), spreads, weights, len(terms), len(backs), len(noise), len(extras), shard
+        ),
         out_shape=outs,
         in_specs=[whole] * len(args),
         out_specs=[whole] * len(outs),
@@ -144,35 +148,25 @@
     weights = [None if len(targets) == outer else (inner, tuple(targets)) for _, targets in maps]
     blocks = plane_blocks(packed, inner, in_plane)
 
-    direct = [d for d in range(inner) if d & (d - 1) == 0]
-    passed = [d for d in range(inner) if d & (d - 1)]
-    rows = [blocks[d] for d in direct]
     backs, terms = tile(
-        rows,
+        blocks,
         [packed] + cols[:-1],
         [False] + [True] * len(cols[:-1]),
         [None] + weights[:-1],
-        [],
-        [],
-        [noise_level[None, :]],
         shard,
+        noise=[noise_level[None, :]],
     )
-    last, terms = tile(rows, cols[-1:], [True], weights[-1:], terms, [], [], shard)
-    backs, late = tile(
-        [blocks[d] for d in passed],
-        [packed] + cols,
-        [False] + [True] * len(cols),
-        [None] + weights,
-        [],
-        list(backs) + list(last),
-        [],
-        shard,
+    returned = [along_outer(back, [(t, s) for s, t in edges]) for (edges, _), back in zip(maps, backs[1:])]
+    half = inner // 2
+    last, far = tile(blocks[half:], cols[-1:], [True], weights[-1:], shard, terms=terms[half:])
+    last, near = tile(
+        blocks[:half], cols[-1:], [True], weights[-1:], shard, terms=terms[:half], backs=last, extras=[backs[0]] + returned
     )
-    total = backs[0] + terms[0]
-    for step, term in zip(direct[1:] + passed, list(terms[1:]) + list(late)):
-        total = total + in_plane(term, [(b, plane_target(b, step, inner)) for b in range(inner)])
-    for (edges, _), back in zip(maps, backs[1:]):
-        total = total + along_outer(back, [(t, s) for s, t in edges])
+    total = near[0]
+    for step, term in enumerate(list(near) + list(far)):
+        if step:
+            total = total + in_plane(term, [(b, plane_target(b, step, inner)) for b in range(inner)])
+    total = total + along_outer(last[0], [(t, s) for s, t in maps[-1][0]])
     return total.T
 
 

time: 25.9 us -> 25.3 us (0.977)
  waiting for transfers between devices: 9 us -> 8.41 us
    ppermute x4, waiting for transfers between devices: 8.97 us -> 5.62 us  [along_outer(): lax.ppermute(value, 'blk', [(s * inner + b, t * inner + b) for s, t in ed...]
    ppermute x6, waiting for transfers between devices: 0.03 us -> 2.79 us  [in_plane(): lax.ppermute(value, 'blk', [(a * inner + s, a * inner + t) for a in range...]
    ppermute x4, starting transfers between devices: 6.19 us -> 6.99 us  [along_outer(): lax.ppermute(value, 'blk', [(s * inner + b, t * inner + b) for s, t in ed...]
    ppermute x6, starting transfers between devices: 5.21 us -> 4.55 us  [in_plane(): lax.ppermute(value, 'blk', [(a * inner + s, a * inner + t) for a in range...]
  transfers between devices with their start and end apart: 10 -> 10, of which waited for: 4 -> 6; matrix products, arithmetic and copies ran while one was open for 0% -> 0% of each run, Pallas kernels for 14% -> 14%
where the time goes in v4:
time: 25.3 us; the launch traced here: 25.1 us
  starting transfers between devices  11.5 us (45%)
  waiting for transfers between devices  8.41 us (33%)
  Pallas kernels  3.54 us (14%)
  other arithmetic  1.56 us (6%)
    ppermute x4, starting transfers between devices, along_outer(): lax.ppermute(value, 'blk', [(s * inner + b, t * inner + b) for s, t in ed...  6.99 us
    ppermute x4, waiting for transfers between devices, along_outer(): lax.ppermute(value, 'blk', [(s * inner + b, t * inner + b) for s, t in ed...  5.62 us
    ppermute x6, starting transfers between devices, in_plane(): lax.ppermute(value, 'blk', [(a * inner + s, a * inner + t) for a in range...  4.55 us
    pallas_call x3, Pallas kernels, tile(): pl.pallas_call(functools.partial(tile_kernel, len(rows), len(cols), sprea...  3.54 us
    ppermute x6, waiting for transfers between devices, in_plane(): lax.ppermute(value, 'blk', [(a * inner + s, a * inner + t) for a in range...  2.79 us
    concatenate x1, other arithmetic, on_device(): packed = jnp.concatenate([features, probes.T], axis=0)  0.93 us
    transpose x1, other arithmetic, on_device(): return total.T  0.63 us
  transfers between devices with their start and end apart: 10, of which 6 were waited for; matrix products, arithmetic and copies ran while one was open for 0% of the time, Pallas kernels for 14%

profile of v4, /device:TPU:0, one launch (start us, length us, event | category | flops | bytes accessed | tf_op | source)
XLA Modules:
  0.0 25.1 jit_solution(17357798641753743795)
XLA Ops:
  0.0 0.9 %pad_maximum_fusion.refs_0_.refs_4_ = bf16[288,256]{1,0:T(8,128)(2,1)S(1)} fusion(bf16[32,256]{1,0:T(8,128)(2,1)} %bitcast.5, bf16[256,256]{1,0:T(8,128)(2,1)} %param.3), kind=kLoop, calls=%fused_computation | loop fusion | flops 294912 | bytes 294912 | tf_op jit(solution)/shard_map/concatenate | solution.py:138
  0.9 0.0 copy-start
  0.9 3.0 %collective-permute-start.2 = (bf16[288,256]{1,0:T(8,128)(2,1)S(1)}, bf16[288,256]{1,0:T(8,128)(2,1)S(1)}, u32[]{:S(2)}, u32[]{:S(2)}) collective-permute-start(bf16[288,256]{1,0:T(8,128)(2,1)S(1)} %pad_maximum_fusion.refs_0_.refs_4_), channel_id=1, source_target_pairs={{0,2},{1,3},{2,0},{3,1},{4,6},{5,7},{6,4},{7,5},{8,10},{9,11},{10,... | collective-permute-start | bytes 442376 | tf_op jit(solution)/shard_map/ppermute | solution.py:144
  4.0 0.0 collective-permute-start
  4.0 1.6 %collective-permute-start.4 = (bf16[288,256]{1,0:T(8,128)(2,1)S(1)}, bf16[288,256]{1,0:T(8,128)(2,1)S(1)}, u32[]{:S(2)}, u32[]{:S(2)}) collective-permute-start(bf16[288,256]{1,0:T(8,128)(2,1)S(1)} %pad_maximum_fusion.refs_0_.refs_4_), channel_id=1, source_target_pairs={{0,4},{1,5},{2,6},{3,7},{4,8},{5,9},{6,10},{7,11},{8,12},{9,13},{1... | collective-permute-start | bytes 442376 | tf_op jit(solution)/shard_map/ppermute | solution.py:141
  5.6 2.3 %collective-permute-done.2.refs_2_.refs_0_ = bf16[288,256]{1,0:T(8,128)(2,1)S(1)} collective-permute-done((bf16[288,256]{1,0:T(8,128)(2,1)S(1)}, bf16[288,256]{1,0:T(8,128)(2,1)S(1)}, u32[]{:S(2)}, u32[]{:S(2)}) %collective-permute-start.2) | collective-permute-done | bytes 147488 | tf_op jit(solution)/shard_map/ppermute | solution.py:144
  7.8 0.0 collective-permute-start.3
  7.8 2.8 %collective-permute-start.1 = (bf16[288,256]{1,0:T(8,128)(2,1)S(1)}, bf16[288,256]{1,0:T(8,128)(2,1)S(1)}, u32[]{:S(2)}, u32[]{:S(2)}) collective-permute-start(bf16[288,256]{1,0:T(8,128)(2,1)S(1)} %pad_maximum_fusion.refs_0_.refs_4_), channel_id=1, source_target_pairs={{0,8},{1,9},{2,10},{3,11},{12,4},{13,5},{14,6},{15,7},{8,12},{9,13... | collective-permute-start | bytes 442376 | tf_op jit(solution)/shard_map/ppermute | solution.py:141
  10.6 0.0 collective-permute-done.refs_1_
  10.6 1.6 %collective-permute-done.4.refs_5_ = bf16[288,256]{1,0:T(8,128)(2,1)S(1)} collective-permute-done((bf16[288,256]{1,0:T(8,128)(2,1)S(1)}, bf16[288,256]{1,0:T(8,128)(2,1)S(1)}, u32[]{:S(2)}, u32[]{:S(2)}) %collective-permute-start.4) | collective-permute-done | bytes 147488 | tf_op jit(solution)/shard_map/ppermute | solution.py:141
  12.2 0.0 collective-permute-done.3.refs_3_.refs_1_
  12.2 2.0 %shard_map.37 = (f32[32,256]{1,0:T(8,128)S(1)}, f32[32,256]{1,0:T(8,128)S(1)}, f32[32,256]{1,0:T(8,128)S(1)}, f32[32,256]{1,0:T(8,128)S(1)}, f32[32,256]{1,0:T(8,128)S(1)}, /*index=5*/f32[32,256]{1,0:T(8,128)S(1)}) custom-call(bf16[288,256]{1,0:T(8,128)(2,1)S(1)} %pad_maximum_fusion.refs_0_.refs_4_, bf16[288,256]{1,0:T(8,128)(2,1)S(1)} %collective-permute-done.refs_1_, ...), custom_call_target="tpu_custom_call" | custom-call | flops 335544320 | bytes 786432 | tf_op jit(solution)/shard_map/pallas_call | solution.py:116
  14.2 1.7 %collective-permute-start.5 = (f32[32,256]{1,0:T(8,128)S(1)}, f32[32,256]{1,0:T(8,128)S(1)}, u32[]{:S(2)}, u32[]{:S(2)}) collective-permute-start(f32[32,256]{1,0:T(8,128)S(1)} %get-tuple-element.23), channel_id=1, source_target_pairs={{4,0},{5,1},{6,2},{7,3},{8,4},{9,5},{10,6},{11,7},{12,8},{13,9},{1... | collective-permute-start | bytes 98312 | tf_op jit(solution)/shard_map/ppermute | solution.py:141
  15.9 0.8 %shard_map.38 = (f32[32,256]{1,0:T(8,128)S(1)}, f32[32,256]{1,0:T(8,128)S(1)}, f32[32,256]{1,0:T(8,128)S(1)}) custom-call(bf16[288,256]{1,0:T(8,128)(2,1)S(1)} %collective-permute-done.2.refs_2_.refs_0_, bf16[288,256]{1,0:T(8,128)(2,1)S(1)} %collective-permute-done.3.refs_3_.refs_1_, bf16[288,256]{1,0:T(8,128)(2,1)S(1)} %collective-permute-done.1.refs_2_, ...), custom_call_target="tpu_custom_call" | custom-call | flops 83886080 | bytes 393216 | tf_op jit(solution)/shard_map/pallas_call | solution.py:116
  16.7 0.7 %collective-permute-start.7 = (f32[32,256]{1,0:T(8,128)S(1)}, f32[32,256]{1,0:T(8,128)S(1)}, u32[]{:S(2)}, u32[]{:S(2)}) collective-permute-start(f32[32,256]{1,0:T(8,128)S(1)} %get-tuple-element.26), channel_id=1, source_target_pairs={{0,2},{1,3},{2,0},{3,1},{4,6},{5,7},{6,4},{7,5},{8,10},{9,11},{10,... | collective-permute-start | bytes 98312 | tf_op jit(solution)/shard_map/ppermute | solution.py:144
  17.4 0.1 collective-permute-start.8
  17.5 0.7 %collective-permute-done.5.refs_7_ = f32[32,256]{1,0:T(8,128)S(1)} collective-permute-done((f32[32,256]{1,0:T(8,128)S(1)}, f32[32,256]{1,0:T(8,128)S(1)}, u32[]{:S(2)}, u32[]{:S(2)}) %collective-permute-start.5) | collective-permute-done | bytes 32800 | tf_op jit(solution)/shard_map/ppermute | solution.py:141
  18.2 0.8 %shard_map.39 = (f32[32,256]{1,0:T(8,128)S(1)}, f32[32,256]{1,0:T(8,128)S(1)}, f32[32,256]{1,0:T(8,128)S(1)}) custom-call(bf16[288,256]{1,0:T(8,128)(2,1)S(1)} %pad_maximum_fusion.refs_0_.refs_4_, bf16[288,256]{1,0:T(8,128)(2,1)S(1)} %collective-permute-done.refs_1_, bf16[288,256]{1,0:T(8,128)(2,1)S(1)} %collective-permute-done.1.refs_2_, ...), custom_call_target="tpu_custom_call" | custom-call | flops 83886080 | bytes 393216 | tf_op jit(solution)/shard_map/pallas_call | solution.py:116
  19.0 0.7 %collective-permute-start.6 = (f32[32,256]{1,0:T(8,128)S(1)}, f32[32,256]{1,0:T(8,128)S(1)}, u32[]{:S(2)}, u32[]{:S(2)}) collective-permute-start(f32[32,256]{1,0:T(8,128)S(1)} %get-tuple-element.25), channel_id=1, source_target_pairs={{0,1},{1,0},{2,3},{3,2},{4,5},{5,4},{6,7},{7,6},{8,9},{9,8},{10,11... | collective-permute-start | bytes 98312 | tf_op jit(solution)/shard_map/ppermute | solution.py:144
  19.6 0.9 %collective-permute-start.9 = (f32[32,256]{1,0:T(8,128)S(1)}, f32[32,256]{1,0:T(8,128)S(1)}, u32[]{:S(2)}, u32[]{:S(2)}) collective-permute-start(f32[32,256]{1,0:T(8,128)S(1)} %get-tuple-element.28), channel_id=1, source_target_pairs={{8,0},{9,1},{10,2},{11,3},{4,12},{5,13},{6,14},{7,15},{12,8},{13,9... | collective-permute-start | bytes 98312 | tf_op jit(solution)/shard_map/ppermute | solution.py:141
  20.6 0.3 %collective-permute-done.7 = f32[32,256]{1,0:T(8,128)S(1)} collective-permute-done((f32[32,256]{1,0:T(8,128)S(1)}, f32[32,256]{1,0:T(8,128)S(1)}, u32[]{:S(2)}, u32[]{:S(2)}) %collective-permute-start.7) | collective-permute-done | bytes 32800 | tf_op jit(solution)/shard_map/ppermute | solution.py:144
  20.8 0.2 collective-permute-done.8
  21.1 3.4 %collective-permute-done.9 = f32[32,256]{1,0:T(8,128)S(1)} collective-permute-done((f32[32,256]{1,0:T(8,128)S(1)}, f32[32,256]{1,0:T(8,128)S(1)}, u32[]{:S(2)}, u32[]{:S(2)}) %collective-permute-start.9) | collective-permute-done | bytes 32800 | tf_op jit(solution)/shard_map/ppermute | solution.py:141
  24.5 0.6 %add_bitcast_fusion = f32[256,32]{0,1:T(8,128)} fusion(f32[32,256]{1,0:T(8,128)S(1)} %collective-permute-done.9, f32[32,256]{1,0:T(8,128)S(1)} %collective-permute-done.8, f32[32,256]{1,0:T(8,128)S(1)} %collective-permute-done.7, f32[32,256]{1,0:T(8,128)S(1)} %get-tuple-element.24, f32[32,256]{1,0:T(8,128)S(1)} %collective-permute-done.6), kind=kLoop, calls=%fused_computation.1 | loop fusion | flops 32768 | bytes 196608 | tf_op jit(solution)/shard_map/transpose | solution.py:170
  (3 shorter events, 0.0 us)
Async XLA Ops:
  0.9 11.3 %copy-start = (f32[256]{0:T(256)S(1)}, f32[256]{0:T(256)}, u32[]{:S(2)}) copy-start(f32[256]{0:T(256)} %param.5) | copy-start | bytes 3076
  0.9 6.9 %collective-permute-start.2 = (bf16[288,256]{1,0:T(8,128)(2,1)S(1)}, bf16[288,256]{1,0:T(8,128)(2,1)S(1)}, u32[]{:S(2)}, u32[]{:S(2)}) collective-permute-start(bf16[288,256]{1,0:T(8,128)(2,1)S(1)} %pad_maximum_fusion.refs_0_.refs_4_), channel_id=1, source_target_pairs={{0,2},{1,3},{2,0},{3,1},{4,6},{5,7},{6,4},{7,5},{8,10},{9,11},{10,... | collective-permute-start | bytes 442376 | tf_op jit(solution)/shard_map/ppermute | solution.py:144
  4.0 6.7 %collective-permute-start = (bf16[288,256]{1,0:T(8,128)(2,1)S(1)}, bf16[288,256]{1,0:T(8,128)(2,1)S(1)}, u32[]{:S(2)}, u32[]{:S(2)}) collective-permute-start(bf16[288,256]{1,0:T(8,128)(2,1)S(1)} %pad_maximum_fusion.refs_0_.refs_4_), channel_id=1, source_target_pairs={{0,1},{1,0},{2,3},{3,2},{4,5},{5,4},{6,7},{7,6},{8,9},{9,8},{10,11... | collective-permute-start | bytes 442376 | tf_op jit(solution)/shard_map/ppermute | solution.py:144
  4.0 8.2 %collective-permute-start.4 = (bf16[288,256]{1,0:T(8,128)(2,1)S(1)}, bf16[288,256]{1,0:T(8,128)(2,1)S(1)}, u32[]{:S(2)}, u32[]{:S(2)}) collective-permute-start(bf16[288,256]{1,0:T(8,128)(2,1)S(1)} %pad_maximum_fusion.refs_0_.refs_4_), channel_id=1, source_target_pairs={{0,4},{1,5},{2,6},{3,7},{4,8},{5,9},{6,10},{7,11},{8,12},{9,13},{1... | collective-permute-start | bytes 442376 | tf_op jit(solution)/shard_map/ppermute | solution.py:141
  7.8 4.4 %collective-permute-start.3 = (bf16[288,256]{1,0:T(8,128)(2,1)S(1)}, bf16[288,256]{1,0:T(8,128)(2,1)S(1)}, u32[]{:S(2)}, u32[]{:S(2)}) collective-permute-start(bf16[288,256]{1,0:T(8,128)(2,1)S(1)} %collective-permute-done.2.refs_2_.refs_0_), channel_id=1, source_target_pairs={{0,1},{1,0},{2,3},{3,2},{4,5},{5,4},{6,7},{7,6},{8,9},{9,8},{10,11... | collective-permute-start | bytes 442376 | tf_op jit(solution)/shard_map/ppermute | solution.py:144
  7.8 8.1 %collective-permute-start.1 = (bf16[288,256]{1,0:T(8,128)(2,1)S(1)}, bf16[288,256]{1,0:T(8,128)(2,1)S(1)}, u32[]{:S(2)}, u32[]{:S(2)}) collective-permute-start(bf16[288,256]{1,0:T(8,128)(2,1)S(1)} %pad_maximum_fusion.refs_0_.refs_4_), channel_id=1, source_target_pairs={{0,8},{1,9},{2,10},{3,11},{12,4},{13,5},{14,6},{15,7},{8,12},{9,13... | collective-permute-start | bytes 442376 | tf_op jit(solution)/shard_map/ppermute | solution.py:141
  14.2 4.0 %collective-permute-start.5 = (f32[32,256]{1,0:T(8,128)S(1)}, f32[32,256]{1,0:T(8,128)S(1)}, u32[]{:S(2)}, u32[]{:S(2)}) collective-permute-start(f32[32,256]{1,0:T(8,128)S(1)} %get-tuple-element.23), channel_id=1, source_target_pairs={{4,0},{5,1},{6,2},{7,3},{8,4},{9,5},{10,6},{11,7},{12,8},{13,9},{1... | collective-permute-start | bytes 98312 | tf_op jit(solution)/shard_map/ppermute | solution.py:141
  16.7 4.2 %collective-permute-start.7 = (f32[32,256]{1,0:T(8,128)S(1)}, f32[32,256]{1,0:T(8,128)S(1)}, u32[]{:S(2)}, u32[]{:S(2)}) collective-permute-start(f32[32,256]{1,0:T(8,128)S(1)} %get-tuple-element.26), channel_id=1, source_target_pairs={{0,2},{1,3},{2,0},{3,1},{4,6},{5,7},{6,4},{7,5},{8,10},{9,11},{10,... | collective-permute-start | bytes 98312 | tf_op jit(solution)/shard_map/ppermute | solution.py:144
  17.4 3.7 %collective-permute-start.8 = (f32[32,256]{1,0:T(8,128)S(1)}, f32[32,256]{1,0:T(8,128)S(1)}, u32[]{:S(2)}, u32[]{:S(2)}) collective-permute-start(f32[32,256]{1,0:T(8,128)S(1)} %get-tuple-element.27), channel_id=1, source_target_pairs={{0,3},{1,2},{2,1},{3,0},{4,7},{5,6},{6,5},{7,4},{8,11},{9,10},{10,... | collective-permute-start | bytes 98312 | tf_op jit(solution)/shard_map/ppermute | solution.py:144
  19.0 2.1 %collective-permute-start.6 = (f32[32,256]{1,0:T(8,128)S(1)}, f32[32,256]{1,0:T(8,128)S(1)}, u32[]{:S(2)}, u32[]{:S(2)}) collective-permute-start(f32[32,256]{1,0:T(8,128)S(1)} %get-tuple-element.25), channel_id=1, source_target_pairs={{0,1},{1,0},{2,3},{3,2},{4,5},{5,4},{6,7},{7,6},{8,9},{9,8},{10,11... | collective-permute-start | bytes 98312 | tf_op jit(solution)/shard_map/ppermute | solution.py:144
  19.6 4.8 %collective-permute-start.9 = (f32[32,256]{1,0:T(8,128)S(1)}, f32[32,256]{1,0:T(8,128)S(1)}, u32[]{:S(2)}, u32[]{:S(2)}) collective-permute-start(f32[32,256]{1,0:T(8,128)S(1)} %get-tuple-element.28), channel_id=1, source_target_pairs={{8,0},{9,1},{10,2},{11,3},{4,12},{5,13},{6,14},{7,15},{12,8},{13,9... | collective-permute-start | bytes 98312 | tf_op jit(solution)/shard_map/ppermute | solution.py:141

commit v5 on v4

--- a/solution.py
+++ b/solution.py
@@ -68,7 +68,7 @@
     return total[0:1, :]
 
 
-def tile_kernel(rows_in, cols_in, spreads, weights, terms_in, backs_in, noise_in, extras_in, shard, *refs):
+def tile_kernel(rows_in, cols_in, spreads, weights, terms_in, backs_in, noise_in, extras_in, owned, shard, *refs):
     refs = list(refs)
     take = lambda number: [refs.pop(0) for _ in range(number)]
     rows, cols = take(rows_in), take(cols_in)
@@ -103,19 +103,25 @@
         new_backs[place][...] = old_backs[place][...] + back if old_backs else back
     for extra in extras:
         terms[0] = terms[0] + extra[...]
-    for ref, term in zip(new_terms, terms):
-        ref[...] = term
+    if owned:
+        place = lax.rem(lax.axis_index("blk"), owned)
+        for slot, term in enumerate(terms):
+            new_terms[0][plane_target(place, slot, owned)] = term
+    else:
+        for ref, term in zip(new_terms, terms):
+            ref[...] = term
 
 
-def tile(rows, cols, spreads, weights, shard, terms=(), backs=(), noise=(), extras=()):
+def tile(rows, cols, spreads, weights, shard, terms=(), backs=(), noise=(), extras=(), owned=0):
     width, vectors = rows[0].shape[1], rows[0].shape[0] - shard
     args = [*rows, *cols, *terms, *backs, *noise, *extras]
     elements = len(rows) * len(cols) * shard * shard
     whole = pl.BlockSpec(memory_space=pltpu.VMEM)
-    outs = [jax.ShapeDtypeStruct((vectors, shard), jnp.float32)] * (len(cols) + len(rows))
+    flat = jax.ShapeDtypeStruct((vectors, shard), jnp.float32)
+    outs = [flat] * len(cols) + ([jax.ShapeDtypeStruct((owned, vectors, shard), jnp.float32)] if owned else [flat] * len(rows))
     found = pl.pallas_call(
         functools.partial(
-            tile_kernel, len(rows), len(cols), spreads, weights, len(terms), len(backs), len(noise), len(extras), shard
+            tile_kernel, len(rows), len(cols), spreads, weights, len(terms), len(backs), len(noise), len(extras), owned, shard
         ),
         out_shape=outs,
         in_specs=[whole] * len(args),
@@ -157,16 +163,13 @@
         noise=[noise_level[None, :]],
     )
     returned = [along_outer(back, [(t, s) for s, t in edges]) for (edges, _), back in zip(maps, backs[1:])]
-    half = inner // 2
-    last, far = tile(blocks[half:], cols[-1:], [True], weights[-1:], shard, terms=terms[half:])
-    last, near = tile(
-        blocks[:half], cols[-1:], [True], weights[-1:], shard, terms=terms[:half], backs=last, extras=[backs[0]] + returned
-    )
-    total = near[0]
-    for step, term in enumerate(list(near) + list(far)):
-        if step:
-            total = total + in_plane(term, [(b, plane_target(b, step, inner)) for b in range(inner)])
-    total = total + along_outer(last[0], [(t, s) for s, t in maps[-1][0]])
+    last, owned = tile(blocks, cols[-1:], [True], weights[-1:], shard, terms=terms, owned=inner)
+    groups = [[a * inner + b for b in range(inner)] for a in range(outer)]
+    gathered = lax.all_to_all(owned[0], "blk", 0, 0, axis_index_groups=groups)
+    total = backs[0] + along_outer(last[0], [(t, s) for s, t in maps[-1][0]])
+    for back in returned:
+        total = total + back
+    total = total + jnp.sum(gathered, axis=0)
     return total.T
 
 

time: 25.3 us -> 27.2 us (1.075)
  starting transfers between devices: 11.5 us -> 15.6 us
  waiting for transfers between devices: 8.41 us -> 5.59 us
  Pallas kernels: 3.54 us -> 4.05 us
    all_to_all x0 -> x1, starting transfers between devices: none -> 3.32 us  [on_device(): gathered = lax.all_to_all(owned[0], 'blk', 0, 0, axis_index_groups=groups)]
    ppermute x4, waiting for transfers between devices: 5.62 us -> 3.32 us  [along_outer(): lax.ppermute(value, 'blk', [(s * inner + b, t * inner + b) for s, t in ed...]
    ppermute x4, starting transfers between devices: 6.99 us -> 9.28 us  [along_outer(): lax.ppermute(value, 'blk', [(s * inner + b, t * inner + b) for s, t in ed...]
    ppermute x6 -> x3, starting transfers between devices: 4.55 us -> 3.04 us  [in_plane(): lax.ppermute(value, 'blk', [(a * inner + s, a * inner + t) for a in range...]
    ppermute x6 -> x3, waiting for transfers between devices: 2.79 us -> 2.27 us  [in_plane(): lax.ppermute(value, 'blk', [(a * inner + s, a * inner + t) for a in range...]
    pallas_call x3 -> x2, Pallas kernels: 3.54 us -> 4.05 us  [tile(): pl.pallas_call(functools.partial(tile_kernel, len(rows), len(cols), sprea...]
  transfers between devices with their start and end apart: 10 -> 8, of which waited for: 6 -> 5; matrix products, arithmetic and copies ran while one was open for 0% -> 0% of each run, Pallas kernels for 14% -> 8%
where the time goes in v5:
time: 27.2 us; the launch traced here: 26.9 us
  starting transfers between devices  15.6 us (57%)
  waiting for transfers between devices  5.59 us (21%)
  Pallas kernels  4.05 us (15%)
  other arithmetic  1.57 us (6%)
    ppermute x4, starting transfers between devices, along_outer(): lax.ppermute(value, 'blk', [(s * inner + b, t * inner + b) for s, t in ed...  9.28 us
    pallas_call x2, Pallas kernels, tile(): pl.pallas_call(functools.partial(tile_kernel, len(rows), len(cols), sprea...  4.05 us
    all_to_all x1, starting transfers between devices, on_device(): gathered = lax.all_to_all(owned[0], 'blk', 0, 0, axis_index_groups=groups)  3.32 us
    ppermute x4, waiting for transfers between devices, along_outer(): lax.ppermute(value, 'blk', [(s * inner + b, t * inner + b) for s, t in ed...  3.32 us
    ppermute x3, starting transfers between devices, in_plane(): lax.ppermute(value, 'blk', [(a * inner + s, a * inner + t) for a in range...  3.04 us
    ppermute x3, waiting for transfers between devices, in_plane(): lax.ppermute(value, 'blk', [(a * inner + s, a * inner + t) for a in range...  2.27 us
    concatenate x1, other arithmetic, on_device(): packed = jnp.concatenate([features, probes.T], axis=0)  0.93 us
    transpose x1, other arithmetic, on_device(): return total.T  0.62 us
  transfers between devices with their start and end apart: 8, of which 5 were waited for; matrix products, arithmetic and copies ran while one was open for 0% of the time, Pallas kernels for 8%

profile of v5, /device:TPU:0, one launch (start us, length us, event | category | flops | bytes accessed | tf_op | source)
XLA Modules:
  0.0 26.9 jit_solution(4730620013813253050)
XLA Ops:
  0.0 0.9 %pad_maximum_fusion.refs_0_.refs_4_ = bf16[288,256]{1,0:T(8,128)(2,1)S(1)} fusion(bf16[32,256]{1,0:T(8,128)(2,1)} %bitcast.5, bf16[256,256]{1,0:T(8,128)(2,1)} %param.3), kind=kLoop, calls=%fused_computation | loop fusion | flops 294912 | bytes 294912 | tf_op jit(solution)/shard_map/concatenate | solution.py:144
  0.9 0.0 copy-start
  0.9 3.0 %collective-permute-start.1 = (bf16[288,256]{1,0:T(8,128)(2,1)S(1)}, bf16[288,256]{1,0:T(8,128)(2,1)S(1)}, u32[]{:S(2)}, u32[]{:S(2)}) collective-permute-start(bf16[288,256]{1,0:T(8,128)(2,1)S(1)} %pad_maximum_fusion.refs_0_.refs_4_), channel_id=1, source_target_pairs={{0,2},{1,3},{2,0},{3,1},{4,6},{5,7},{6,4},{7,5},{8,10},{9,11},{10,... | collective-permute-start | bytes 442376 | tf_op jit(solution)/shard_map/ppermute | solution.py:150
  4.0 1.6 %collective-permute-start.3 = (bf16[288,256]{1,0:T(8,128)(2,1)S(1)}, bf16[288,256]{1,0:T(8,128)(2,1)S(1)}, u32[]{:S(2)}, u32[]{:S(2)}) collective-permute-start(bf16[288,256]{1,0:T(8,128)(2,1)S(1)} %pad_maximum_fusion.refs_0_.refs_4_), channel_id=1, source_target_pairs={{0,4},{1,5},{2,6},{3,7},{4,8},{5,9},{6,10},{7,11},{8,12},{9,13},{1... | collective-permute-start | bytes 442376 | tf_op jit(solution)/shard_map/ppermute | solution.py:147
  5.6 0.0 collective-permute-start
  5.6 2.3 %collective-permute-done.1.refs_2_ = bf16[288,256]{1,0:T(8,128)(2,1)S(1)} collective-permute-done((bf16[288,256]{1,0:T(8,128)(2,1)S(1)}, bf16[288,256]{1,0:T(8,128)(2,1)S(1)}, u32[]{:S(2)}, u32[]{:S(2)}) %collective-permute-start.1) | collective-permute-done | bytes 147488 | tf_op jit(solution)/shard_map/ppermute | solution.py:150
  7.8 0.0 collective-permute-start.2
  7.8 2.8 %collective-permute-start.4 = (bf16[288,256]{1,0:T(8,128)(2,1)S(1)}, bf16[288,256]{1,0:T(8,128)(2,1)S(1)}, u32[]{:S(2)}, u32[]{:S(2)}) collective-permute-start(bf16[288,256]{1,0:T(8,128)(2,1)S(1)} %pad_maximum_fusion.refs_0_.refs_4_), channel_id=1, source_target_pairs={{0,8},{1,9},{2,10},{3,11},{12,4},{13,5},{14,6},{15,7},{8,12},{9,13... | collective-permute-start | bytes 442376 | tf_op jit(solution)/shard_map/ppermute | solution.py:147
  10.6 0.5 %collective-permute-done.3.refs_5_ = bf16[288,256]{1,0:T(8,128)(2,1)S(1)} collective-permute-done((bf16[288,256]{1,0:T(8,128)(2,1)S(1)}, bf16[288,256]{1,0:T(8,128)(2,1)S(1)}, u32[]{:S(2)}, u32[]{:S(2)}) %collective-permute-start.3) | collective-permute-done | bytes 147488 | tf_op jit(solution)/shard_map/ppermute | solution.py:147
  11.2 0.0 collective-permute-done.refs_1_
  11.2 0.0 collective-permute-done.2.refs_3_
  11.2 0.0 copy-done
  11.2 2.0 %shard_map.37 = (f32[32,256]{1,0:T(8,128)S(1)}, f32[32,256]{1,0:T(8,128)S(1)}, f32[32,256]{1,0:T(8,128)S(1)}, f32[32,256]{1,0:T(8,128)S(1)}, f32[32,256]{1,0:T(8,128)S(1)}, /*index=5*/f32[32,256]{1,0:T(8,128)S(1)}) custom-call(bf16[288,256]{1,0:T(8,128)(2,1)S(1)} %pad_maximum_fusion.refs_0_.refs_4_, bf16[288,256]{1,0:T(8,128)(2,1)S(1)} %collective-permute-done.refs_1_, ...), custom_call_target="tpu_custom_call" | custom-call | flops 335544320 | bytes 786432 | tf_op jit(solution)/shard_map/pallas_call | solution.py:122
  13.2 1.2 %collective-permute-done.4.refs_4_ = bf16[288,256]{1,0:T(8,128)(2,1)S(1)} collective-permute-done((bf16[288,256]{1,0:T(8,128)(2,1)S(1)}, bf16[288,256]{1,0:T(8,128)(2,1)S(1)}, u32[]{:S(2)}, u32[]{:S(2)}) %collective-permute-start.4) | collective-permute-done | bytes 147488 | tf_op jit(solution)/shard_map/ppermute | solution.py:147
  14.4 2.0 %shard_map.38 = (f32[32,256]{1,0:T(8,128)S(1)}, f32[4,32,256]{2,1,0:T(8,128)}) custom-call(bf16[288,256]{1,0:T(8,128)(2,1)S(1)} %pad_maximum_fusion.refs_0_.refs_4_, bf16[288,256]{1,0:T(8,128)(2,1)S(1)} %collective-permute-done.refs_1_, bf16[288,256]{1,0:T(8,128)(2,1)S(1)} %collective-permute-done.1.refs_2_, ...), custom_call_target="tpu_custom_call" | custom-call | flops 167772160 | bytes 655360 | tf_op jit(solution)/shard_map/pallas_call | solution.py:122
  16.4 3.3 %all-to-all-start = ((f32[4,32,256]{2,1,0:T(8,128)}), f32[4,32,256]{2,1,0:T(8,128)S(1)}, u32[]{:S(2)}, u32[]{:S(2)}) async-start(f32[4,32,256]{2,1,0:T(8,128)} %get-tuple-element.20), calls=%async_computation | async-start | bytes 262144 | tf_op jit(solution)/shard_map/all_to_all | solution.py:168
  19.8 2.4 %collective-permute-start.5 = (f32[32,256]{1,0:T(8,128)S(1)}, f32[32,256]{1,0:T(8,128)S(1)}, u32[]{:S(2)}, u32[]{:S(2)}) collective-permute-start(f32[32,256]{1,0:T(8,128)S(1)} %get-tuple-element.18), channel_id=1, source_target_pairs={{8,0},{9,1},{10,2},{11,3},{4,12},{5,13},{6,14},{7,15},{12,8},{13,9... | collective-permute-start | bytes 98312 | tf_op jit(solution)/shard_map/ppermute | solution.py:147
  22.2 2.5 %collective-permute-start.6 = (f32[32,256]{1,0:T(8,128)S(1)}, f32[32,256]{1,0:T(8,128)S(1)}, u32[]{:S(2)}, u32[]{:S(2)}) collective-permute-start(f32[32,256]{1,0:T(8,128)S(1)} %get-tuple-element.19), channel_id=1, source_target_pairs={{4,0},{5,1},{6,2},{7,3},{8,4},{9,5},{10,6},{11,7},{12,8},{13,9},{1... | collective-permute-start | bytes 98312 | tf_op jit(solution)/shard_map/ppermute | solution.py:147
  24.7 0.0 all-to-all-done
  24.7 0.5 %collective-permute-done.5 = f32[32,256]{1,0:T(8,128)S(1)} collective-permute-done((f32[32,256]{1,0:T(8,128)S(1)}, f32[32,256]{1,0:T(8,128)S(1)}, u32[]{:S(2)}, u32[]{:S(2)}) %collective-permute-start.5) | collective-permute-done | bytes 32800 | tf_op jit(solution)/shard_map/ppermute | solution.py:147
  25.2 1.1 %collective-permute-done.6 = f32[32,256]{1,0:T(8,128)S(1)} collective-permute-done((f32[32,256]{1,0:T(8,128)S(1)}, f32[32,256]{1,0:T(8,128)S(1)}, u32[]{:S(2)}, u32[]{:S(2)}) %collective-permute-start.6) | collective-permute-done | bytes 32800 | tf_op jit(solution)/shard_map/ppermute | solution.py:147
  26.3 0.6 %add_bitcast_fusion = f32[256,32]{0,1:T(8,128)} fusion(f32[32,256]{1,0:T(8,128)S(1)} %reduce_sum.9, f32[32,256]{1,0:T(8,128)S(1)} %collective-permute-done.6, f32[32,256]{1,0:T(8,128)S(1)} %get-tuple-element.13, f32[32,256]{1,0:T(8,128)S(1)} %collective-permute-done.5), kind=kLoop, calls=%fused_computation.1 | loop fusion | flops 24576 | bytes 163840 | tf_op jit(solution)/shard_map/transpose | solution.py:173
  (1 shorter events, 0.0 us)
Async XLA Ops:
  0.9 10.2 %copy-start = (f32[256]{0:T(256)S(1)}, f32[256]{0:T(256)}, u32[]{:S(2)}) copy-start(f32[256]{0:T(256)} %param.5) | copy-start | bytes 3076
  0.9 6.9 %collective-permute-start.1 = (bf16[288,256]{1,0:T(8,128)(2,1)S(1)}, bf16[288,256]{1,0:T(8,128)(2,1)S(1)}, u32[]{:S(2)}, u32[]{:S(2)}) collective-permute-start(bf16[288,256]{1,0:T(8,128)(2,1)S(1)} %pad_maximum_fusion.refs_0_.refs_4_), channel_id=1, source_target_pairs={{0,2},{1,3},{2,0},{3,1},{4,6},{5,7},{6,4},{7,5},{8,10},{9,11},{10,... | collective-permute-start | bytes 442376 | tf_op jit(solution)/shard_map/ppermute | solution.py:150
  4.0 7.2 %collective-permute-start.3 = (bf16[288,256]{1,0:T(8,128)(2,1)S(1)}, bf16[288,256]{1,0:T(8,128)(2,1)S(1)}, u32[]{:S(2)}, u32[]{:S(2)}) collective-permute-start(bf16[288,256]{1,0:T(8,128)(2,1)S(1)} %pad_maximum_fusion.refs_0_.refs_4_), channel_id=1, source_target_pairs={{0,4},{1,5},{2,6},{3,7},{4,8},{5,9},{6,10},{7,11},{8,12},{9,13},{1... | collective-permute-start | bytes 442376 | tf_op jit(solution)/shard_map/ppermute | solution.py:147
  5.6 5.6 %collective-permute-start = (bf16[288,256]{1,0:T(8,128)(2,1)S(1)}, bf16[288,256]{1,0:T(8,128)(2,1)S(1)}, u32[]{:S(2)}, u32[]{:S(2)}) collective-permute-start(bf16[288,256]{1,0:T(8,128)(2,1)S(1)} %pad_maximum_fusion.refs_0_.refs_4_), channel_id=1, source_target_pairs={{0,1},{1,0},{2,3},{3,2},{4,5},{5,4},{6,7},{7,6},{8,9},{9,8},{10,11... | collective-permute-start | bytes 442376 | tf_op jit(solution)/shard_map/ppermute | solution.py:150
  7.8 3.3 %collective-permute-start.2 = (bf16[288,256]{1,0:T(8,128)(2,1)S(1)}, bf16[288,256]{1,0:T(8,128)(2,1)S(1)}, u32[]{:S(2)}, u32[]{:S(2)}) collective-permute-start(bf16[288,256]{1,0:T(8,128)(2,1)S(1)} %collective-permute-done.1.refs_2_), channel_id=1, source_target_pairs={{0,1},{1,0},{2,3},{3,2},{4,5},{5,4},{6,7},{7,6},{8,9},{9,8},{10,11... | collective-permute-start | bytes 442376 | tf_op jit(solution)/shard_map/ppermute | solution.py:150
  7.8 6.6 %collective-permute-start.4 = (bf16[288,256]{1,0:T(8,128)(2,1)S(1)}, bf16[288,256]{1,0:T(8,128)(2,1)S(1)}, u32[]{:S(2)}, u32[]{:S(2)}) collective-permute-start(bf16[288,256]{1,0:T(8,128)(2,1)S(1)} %pad_maximum_fusion.refs_0_.refs_4_), channel_id=1, source_target_pairs={{0,8},{1,9},{2,10},{3,11},{12,4},{13,5},{14,6},{15,7},{8,12},{9,13... | collective-permute-start | bytes 442376 | tf_op jit(solution)/shard_map/ppermute | solution.py:147
  16.4 8.2 %all-to-all-start = ((f32[4,32,256]{2,1,0:T(8,128)}), f32[4,32,256]{2,1,0:T(8,128)S(1)}, u32[]{:S(2)}, u32[]{:S(2)}) async-start(f32[4,32,256]{2,1,0:T(8,128)} %get-tuple-element.20), calls=%async_computation | async-start | bytes 262144 | tf_op jit(solution)/shard_map/all_to_all | solution.py:168
  19.8 5.4 %collective-permute-start.5 = (f32[32,256]{1,0:T(8,128)S(1)}, f32[32,256]{1,0:T(8,128)S(1)}, u32[]{:S(2)}, u32[]{:S(2)}) collective-permute-start(f32[32,256]{1,0:T(8,128)S(1)} %get-tuple-element.18), channel_id=1, source_target_pairs={{8,0},{9,1},{10,2},{11,3},{4,12},{5,13},{6,14},{7,15},{12,8},{13,9... | collective-permute-start | bytes 98312 | tf_op jit(solution)/shard_map/ppermute | solution.py:147
  22.2 4.1 %collective-permute-start.6 = (f32[32,256]{1,0:T(8,128)S(1)}, f32[32,256]{1,0:T(8,128)S(1)}, u32[]{:S(2)}, u32[]{:S(2)}) collective-permute-start(f32[32,256]{1,0:T(8,128)S(1)} %get-tuple-element.19), channel_id=1, source_target_pairs={{4,0},{5,1},{6,2},{7,3},{8,4},{9,5},{10,6},{11,7},{12,8},{13,9},{1... | collective-permute-start | bytes 98312 | tf_op jit(solution)/shard_map/ppermute | solution.py:147

commit v6 on v4

v6 whole, which is shorter than its diff:
```python
import functools
import math

import jax
import jax.numpy as jnp
from jax import lax
from jax.experimental import pallas as pl
from jax.experimental.pallas import tpu as pltpu
from jax.sharding import PartitionSpec as P

ROOT5 = math.sqrt(5.0)
DECAY = -ROOT5 * math.log2(math.e)
ROWS_BY_ROWS = (((1,), (1,)), ((), ()))


def group_size(count):
    size = 1
    while size * size < count or count % size:
        size += 1
    return size


def plane_blocks(value, count, send):
    if count & (count - 1):
        maps = {step: [(b, (b - step) % count) for b in range(count)] for step in range(1, count)}
        return [value] + [send(value, maps[step]) for step in range(1, count)]
    blocks = {0: value}
    bit = count // 2
    while bit:
        for known in list(blocks):
            blocks[known | bit] = send(blocks[known], [(b, b ^ bit) for b in range(count)])
        bit //= 2
    return [blocks[distance] for distance in range(count)]


def plane_target(index, step, count):
    return (index + step) % count if count & (count - 1) else index ^ step


def outer_maps(count):
    bits = count.bit_length() - 1
    order = list(range(count))
    if count == 1 << bits:
        order = [int(f"{a:0{bits}b}"[::-1], 2) if bits else a for a in order]
    shifts = [[(order[p], order[(p + step) % count]) for p in range(count)] for step in range(1, count // 2 + 1)]
    if count % 2:
        return shifts, []
    return shifts[:-1], shifts[-1:]


def matern(dist2):
    dist2 = jnp.maximum(dist2, 1e-30)
    dist = dist2 * lax.rsqrt(dist2)
    poly = (1.0 + ROOT5 * dist) + (5.0 / 3.0) * dist2
    return (poly * jnp.exp2(DECAY * dist)).astype(jnp.bfloat16)


def lane_squares(block):
    wide = block.astype(jnp.float32)
    square = wide * wide
    high = square.astype(jnp.bfloat16)
    low = (square - high.astype(jnp.float32)).astype(jnp.bfloat16)
    ones = jnp.ones((8, block.shape[1]), jnp.bfloat16)
    total = lax.dot_general(ones, high, ROWS_BY_ROWS, preferred_element_type=jnp.float32)
    total += lax.dot_general(ones, low, ROWS_BY_ROWS, preferred_element_type=jnp.float32)
    return total[0:1, :]


def tile_kernel(shape, kinds, sums, shard, *refs):
    refs = list(refs)
    rows_in, cols_in = shape
    terms_in, backs_in, noise_in = sums
    rows, cols = refs[:rows_in], refs[rows_in : rows_in + cols_in]
    del refs[: rows_in + cols_in]
    old_terms, old_backs, noise = refs[:terms_in], refs[terms_in : terms_in + backs_in], refs[terms_in + backs_in :][:noise_in]
    del refs[: terms_in + backs_in + noise_in]
    returning = sum("back" in kind for kind in kinds)
    new_backs, new_terms = refs[:returning], refs[returning:]
    terms = [ref[...] for ref in old_terms] or [None] * rows_in
    row_squares = []
    for row in rows:
        wide = row[0:shard, :].astype(jnp.float32)
        row_squares.append(jnp.sum(wide * wide, axis=1, keepdims=True))
    filled = 0
    for kind, col_ref in zip(kinds, cols):
        col = col_ref[0:shard, :]
        col_squares = lane_squares(col)
        scaled = col * jnp.asarray(-2.0, col.dtype)
        back = old_backs[filled][...] if old_backs and "back" in kind else None
        if noise and "back" in kind:
            back = noise[0][...] * col_ref[shard:, :].astype(jnp.float32)
        for slot, row in enumerate(rows):
            cross = lax.dot_general(row[0:shard, :], scaled, ROWS_BY_ROWS, preferred_element_type=jnp.float32)
            kernel = matern((row_squares[slot] + col_squares) + cross)
            if "back" in kind:
                share = jnp.dot(row[shard:, :], kernel, preferred_element_type=jnp.float32)
                back = share if back is None else back + share
            if "rows" in kind:
                term = lax.dot_general(col_ref[shard:, :], kernel, ROWS_BY_ROWS, preferred_element_type=jnp.float32)
                terms[slot] = term if terms[slot] is None else terms[slot] + term
        if "back" in kind:
            new_backs[filled][...] = back
            filled += 1
    for ref, term in zip(new_terms, terms):
        ref[...] = term


def tile(rows, cols, kinds, shard, terms=(), backs=(), noise=()):
    width, vectors = rows[0].shape[1], rows[0].shape[0] - shard
    args = [*rows, *cols, *terms, *backs, *noise]
    elements = len(rows) * len(cols) * shard * shard
    whole = pl.BlockSpec(memory_space=pltpu.VMEM)
    returning = sum("back" in kind for kind in kinds)
    spread = len(rows) if any("rows" in kind for kind in kinds) else 0
    outs = [jax.ShapeDtypeStruct((vectors, shard), jnp.float32)] * (returning + spread)
    found = pl.pallas_call(
        functools.partial(
            tile_kernel, (len(rows), len(cols)), tuple(kinds), (len(terms), len(backs), len(noise)), shard
        ),
        out_shape=outs,
        in_specs=[whole] * len(args),
        out_specs=[whole] * len(outs),
        compiler_params=pltpu.CompilerParams(vmem_limit_bytes=32 * 1024 * 1024),
        cost_estimate=pl.CostEstimate(
            flops=2 * elements * (width + 2 * vectors),
            bytes_accessed=2 * width * shard * (len(rows) + len(cols)),
            transcendentals=2 * elements,
        ),
    )(*args)
    return found[:returning], found[returning:]


def on_device(features, probes, noise_level):
    count = lax.axis_size("blk")
    inner = group_size(count)
    outer = count // inner
    shard = features.shape[0]
    packed = jnp.concatenate([features, probes.T], axis=0)

    def along_outer(value, edges):
        return lax.ppermute(value, "blk", [(s * inner + b, t * inner + b) for s, t in edges for b in range(inner)])

    def in_plane(value, hops):
        return lax.ppermute(value, "blk", [(a * inner + s, a * inner + t) for a in range(outer) for s, t in hops])

    one_way, exchanges = outer_maps(outer)
    cols = [along_outer(packed, edges) for edges in one_way + exchanges]
    kinds = [("rows", "back")] * len(one_way) + [("rows",)] * len(exchanges)
    blocks = plane_blocks(packed, inner, in_plane)

    direct = [d for d in range(inner) if d & (d - 1) == 0]
    passed = [d for d in range(inner) if d & (d - 1)]
    backs, terms = tile([blocks[d] for d in direct], cols, kinds, shard)
    backs, late = tile([blocks[d] for d in passed], cols, kinds, shard, backs=backs)
    (total,), _ = tile(blocks, [packed], [("back",)], shard, noise=[noise_level[None, :]])
    for back, edges in zip(backs, one_way):
        total = total + along_outer(back, [(t, s) for s, t in edges])
    for step, term in zip(direct + passed, list(terms) + list(late)):
        total = total + (in_plane(term, [(b, plane_target(b, step, inner)) for b in range(inner)]) if step else term)
    return total.T


def solution(mesh):
    placed = (P(("parts", "blk"), None), P(("parts", "blk"), None), P(("parts", "blk")))
    return jax.shard_map(
        on_device, mesh=mesh, in_specs=placed, out_specs=P(("parts", "blk"), None), check_vma=False
    )
```

time: 25.3 us -> 24.8 us (0.980)
  waiting for transfers between devices: 8.41 us -> 7.46 us
  starting transfers between devices: 11.5 us -> 11.9 us
    ppermute x6, waiting for transfers between devices: 2.79 us -> 1.05 us  [in_plane(): lax.ppermute(value, 'blk', [(a * inner + s, a * inner + t) for a in range...]
    ppermute x4 -> x3, waiting for transfers between devices: 5.62 us -> 6.41 us  [along_outer(): lax.ppermute(value, 'blk', [(s * inner + b, t * inner + b) for s, t in ed...]
    ppermute x6, starting transfers between devices: 4.55 us -> 5.16 us  [in_plane(): lax.ppermute(value, 'blk', [(a * inner + s, a * inner + t) for a in range...]
    ppermute x4 -> x3, starting transfers between devices: 6.99 us -> 6.78 us  [along_outer(): lax.ppermute(value, 'blk', [(s * inner + b, t * inner + b) for s, t in ed...]
  transfers between devices with their start and end apart: 10 -> 9, of which waited for: 6 -> 4; matrix products, arithmetic and copies ran while one was open for 0% -> 0% of each run, Pallas kernels for 14% -> 14%
where the time goes in v6:
time: 24.8 us; the launch traced here: 24.5 us
  starting transfers between devices  11.9 us (48%)
  waiting for transfers between devices  7.46 us (30%)
  Pallas kernels  3.54 us (14%)
  other arithmetic  1.56 us (6%)
    ppermute x3, starting transfers between devices, along_outer(): lax.ppermute(value, 'blk', [(s * inner + b, t * inner + b) for s, t in ed...  6.78 us
    ppermute x3, waiting for transfers between devices, along_outer(): lax.ppermute(value, 'blk', [(s * inner + b, t * inner + b) for s, t in ed...  6.41 us
    ppermute x6, starting transfers between devices, in_plane(): lax.ppermute(value, 'blk', [(a * inner + s, a * inner + t) for a in range...  5.16 us
    pallas_call x3, Pallas kernels, tile(): pl.pallas_call(functools.partial(tile_kernel, (len(rows), len(cols)), tup...  3.54 us
    ppermute x6, waiting for transfers between devices, in_plane(): lax.ppermute(value, 'blk', [(a * inner + s, a * inner + t) for a in range...  1.05 us
    concatenate x1, other arithmetic, on_device(): packed = jnp.concatenate([features, probes.T], axis=0)  0.93 us
    transpose x1, other arithmetic, on_device(): return total.T  0.63 us
  transfers between devices with their start and end apart: 9, of which 4 were waited for; matrix products, arithmetic and copies ran while one was open for 0% of the time, Pallas kernels for 14%

profile of v6, /device:TPU:0, one launch (start us, length us, event | category | flops | bytes accessed | tf_op | source)
XLA Modules:
  0.0 24.5 jit_solution(8429431881065926122)
XLA Ops:
  0.0 0.9 %pad_maximum_fusion.refs_0_.refs_4_ = bf16[288,256]{1,0:T(8,128)(2,1)S(1)} fusion(bf16[32,256]{1,0:T(8,128)(2,1)} %bitcast.5, bf16[256,256]{1,0:T(8,128)(2,1)} %param.3), kind=kLoop, calls=%fused_computation | loop fusion | flops 294912 | bytes 294912 | tf_op jit(solution)/shard_map/concatenate | solution.py:138
  0.9 3.0 %collective-permute-start.1 = (bf16[288,256]{1,0:T(8,128)(2,1)S(1)}, bf16[288,256]{1,0:T(8,128)(2,1)S(1)}, u32[]{:S(2)}, u32[]{:S(2)}) collective-permute-start(bf16[288,256]{1,0:T(8,128)(2,1)S(1)} %pad_maximum_fusion.refs_0_.refs_4_), channel_id=1, source_target_pairs={{0,2},{1,3},{2,0},{3,1},{4,6},{5,7},{6,4},{7,5},{8,10},{9,11},{10,... | collective-permute-start | bytes 442376 | tf_op jit(solution)/shard_map/ppermute | solution.py:144
  4.0 1.6 %collective-permute-start.4 = (bf16[288,256]{1,0:T(8,128)(2,1)S(1)}, bf16[288,256]{1,0:T(8,128)(2,1)S(1)}, u32[]{:S(2)}, u32[]{:S(2)}) collective-permute-start(bf16[288,256]{1,0:T(8,128)(2,1)S(1)} %pad_maximum_fusion.refs_0_.refs_4_), channel_id=1, source_target_pairs={{0,4},{1,5},{2,6},{3,7},{8,12},{9,13},{10,14},{11,15},{4,0},{5,1},... | collective-permute-start | bytes 442376 | tf_op jit(solution)/shard_map/ppermute | solution.py:141
  5.5 2.6 %collective-permute-start.3 = (bf16[288,256]{1,0:T(8,128)(2,1)S(1)}, bf16[288,256]{1,0:T(8,128)(2,1)S(1)}, u32[]{:S(2)}, u32[]{:S(2)}) collective-permute-start(bf16[288,256]{1,0:T(8,128)(2,1)S(1)} %pad_maximum_fusion.refs_0_.refs_4_), channel_id=1, source_target_pairs={{0,8},{1,9},{2,10},{3,11},{8,4},{9,5},{10,6},{11,7},{4,12},{5,13},... | collective-permute-start | bytes 442376 | tf_op jit(solution)/shard_map/ppermute | solution.py:141
  8.1 0.0 collective-permute-start
  8.1 0.0 collective-permute-done.1.refs_2_
  8.1 0.5 %collective-permute-start.2 = (bf16[288,256]{1,0:T(8,128)(2,1)S(1)}, bf16[288,256]{1,0:T(8,128)(2,1)S(1)}, u32[]{:S(2)}, u32[]{:S(2)}) collective-permute-start(bf16[288,256]{1,0:T(8,128)(2,1)S(1)} %collective-permute-done.1.refs_2_), channel_id=1, source_target_pairs={{0,1},{1,0},{2,3},{3,2},{4,5},{5,4},{6,7},{7,6},{8,9},{9,8},{10,11... | collective-permute-start | bytes 442376 | tf_op jit(solution)/shard_map/ppermute | solution.py:144
  8.6 0.6 %collective-permute-done.4.refs_4_.refs_2_ = bf16[288,256]{1,0:T(8,128)(2,1)S(1)} collective-permute-done((bf16[288,256]{1,0:T(8,128)(2,1)S(1)}, bf16[288,256]{1,0:T(8,128)(2,1)S(1)}, u32[]{:S(2)}, u32[]{:S(2)}) %collective-permute-start.4) | collective-permute-done | bytes 147488 | tf_op jit(solution)/shard_map/ppermute | solution.py:141
  9.3 5.3 %collective-permute-done.3.refs_3_.refs_1_ = bf16[288,256]{1,0:T(8,128)(2,1)S(1)} collective-permute-done((bf16[288,256]{1,0:T(8,128)(2,1)S(1)}, bf16[288,256]{1,0:T(8,128)(2,1)S(1)}, u32[]{:S(2)}, u32[]{:S(2)}) %collective-permute-start.3) | collective-permute-done | bytes 147488 | tf_op jit(solution)/shard_map/ppermute | solution.py:141
  14.6 0.0 collective-permute-done.refs_1_
  14.6 1.5 %shard_map.38 = (f32[32,256]{1,0:T(8,128)S(1)}, f32[32,256]{1,0:T(8,128)S(1)}, f32[32,256]{1,0:T(8,128)S(1)}, f32[32,256]{1,0:T(8,128)S(1)}) custom-call(bf16[288,256]{1,0:T(8,128)(2,1)S(1)} %pad_maximum_fusion.refs_0_.refs_4_, bf16[288,256]{1,0:T(8,128)(2,1)S(1)} %collective-permute-done.refs_1_, bf16[288,256]{1,0:T(8,128)(2,1)S(1)} %collective-permute-done.1.refs_2_, ...), custom_call_target="tpu_custom_call" | custom-call | flops 251658240 | bytes 655360 | tf_op jit(solution)/shard_map/pallas_call | solution.py:116
  16.1 0.0 collective-permute-start.6
  16.1 0.6 %collective-permute-start.7 = (f32[32,256]{1,0:T(8,128)S(1)}, f32[32,256]{1,0:T(8,128)S(1)}, u32[]{:S(2)}, u32[]{:S(2)}) collective-permute-start(f32[32,256]{1,0:T(8,128)S(1)} %get-tuple-element.15), channel_id=1, source_target_pairs={{0,2},{1,3},{2,0},{3,1},{4,6},{5,7},{6,4},{7,5},{8,10},{9,11},{10,... | collective-permute-start | bytes 98312 | tf_op jit(solution)/shard_map/ppermute | solution.py:144
  16.7 0.0 collective-permute-done.2.refs_3_.refs_0_
  16.7 1.0 %shard_map.39 = (f32[32,256]{1,0:T(8,128)S(1)}, f32[32,256]{1,0:T(8,128)S(1)}) custom-call(bf16[288,256]{1,0:T(8,128)(2,1)S(1)} %collective-permute-done.2.refs_3_.refs_0_, bf16[288,256]{1,0:T(8,128)(2,1)S(1)} %collective-permute-done.3.refs_3_.refs_1_, bf16[288,256]{1,0:T(8,128)(2,1)S(1)} %collective-permute-done.4.refs_4_.refs_2_, ...), custom_call_target="tpu_custom_call" | custom-call | flops 83886080 | bytes 393216 | tf_op jit(solution)/shard_map/pallas_call | solution.py:116
  17.7 2.6 %collective-permute-start.5 = (f32[32,256]{1,0:T(8,128)S(1)}, f32[32,256]{1,0:T(8,128)S(1)}, u32[]{:S(2)}, u32[]{:S(2)}) collective-permute-start(f32[32,256]{1,0:T(8,128)S(1)} %get-tuple-element.12), channel_id=1, source_target_pairs={{8,0},{9,1},{10,2},{11,3},{4,8},{5,9},{6,10},{7,11},{12,4},{13,5},... | collective-permute-start | bytes 98312 | tf_op jit(solution)/shard_map/ppermute | solution.py:141
  20.3 1.0 %collective-permute-start.8 = (f32[32,256]{1,0:T(8,128)S(1)}, f32[32,256]{1,0:T(8,128)S(1)}, u32[]{:S(2)}, u32[]{:S(2)}) collective-permute-start(f32[32,256]{1,0:T(8,128)S(1)} %get-tuple-element.16), channel_id=1, source_target_pairs={{0,3},{1,2},{2,1},{3,0},{4,7},{5,6},{6,5},{7,4},{8,11},{9,10},{10,... | collective-permute-start | bytes 98312 | tf_op jit(solution)/shard_map/ppermute | solution.py:144
  21.3 0.0 copy-done
  21.3 1.0 %shard_map.37 = f32[32,256]{1,0:T(8,128)S(1)} custom-call(bf16[288,256]{1,0:T(8,128)(2,1)S(1)} %pad_maximum_fusion.refs_0_.refs_4_, bf16[288,256]{1,0:T(8,128)(2,1)S(1)} %collective-permute-done.refs_1_, bf16[288,256]{1,0:T(8,128)(2,1)S(1)} %collective-permute-done.1.refs_2_, bf16[288,256]{1,0:T(8,128)(2,1)S(1)} %collective-permute-done.2.refs_3_.refs_0_, ...), custom_call_target="tpu_custom_call" | custom-call | flops 167772160 | bytes 655360 | tf_op jit(solution)/shard_map/pallas_call | solution.py:116
  22.4 0.0 collective-permute-done.6
  22.4 0.0 collective-permute-done.7
  22.4 0.5 %collective-permute-done.5 = f32[32,256]{1,0:T(8,128)S(1)} collective-permute-done((f32[32,256]{1,0:T(8,128)S(1)}, f32[32,256]{1,0:T(8,128)S(1)}, u32[]{:S(2)}, u32[]{:S(2)}) %collective-permute-start.5) | collective-permute-done | bytes 32800 | tf_op jit(solution)/shard_map/ppermute | solution.py:141
  22.9 1.0 %collective-permute-done.8 = f32[32,256]{1,0:T(8,128)S(1)} collective-permute-done((f32[32,256]{1,0:T(8,128)S(1)}, f32[32,256]{1,0:T(8,128)S(1)}, u32[]{:S(2)}, u32[]{:S(2)}) %collective-permute-start.8) | collective-permute-done | bytes 32800 | tf_op jit(solution)/shard_map/ppermute | solution.py:144
  23.9 0.6 %add_bitcast_fusion = f32[256,32]{0,1:T(8,128)} fusion(f32[32,256]{1,0:T(8,128)S(1)} %collective-permute-done.8, f32[32,256]{1,0:T(8,128)S(1)} %collective-permute-done.7, f32[32,256]{1,0:T(8,128)S(1)} %collective-permute-done.6, f32[32,256]{1,0:T(8,128)S(1)} %get-tuple-element.13, f32[32,256]{1,0:T(8,128)S(1)} %shard_map.37, ...), kind=kLoop, calls=%fused_computation.1 | loop fusion | flops 40960 | bytes 229376 | tf_op jit(solution)/shard_map/transpose | solution.py:160
  (1 shorter events, 0.0 us)
Async XLA Ops:
  0.9 7.2 %collective-permute-start.1 = (bf16[288,256]{1,0:T(8,128)(2,1)S(1)}, bf16[288,256]{1,0:T(8,128)(2,1)S(1)}, u32[]{:S(2)}, u32[]{:S(2)}) collective-permute-start(bf16[288,256]{1,0:T(8,128)(2,1)S(1)} %pad_maximum_fusion.refs_0_.refs_4_), channel_id=1, source_target_pairs={{0,2},{1,3},{2,0},{3,1},{4,6},{5,7},{6,4},{7,5},{8,10},{9,11},{10,... | collective-permute-start | bytes 442376 | tf_op jit(solution)/shard_map/ppermute | solution.py:144
  4.0 5.3 %collective-permute-start.4 = (bf16[288,256]{1,0:T(8,128)(2,1)S(1)}, bf16[288,256]{1,0:T(8,128)(2,1)S(1)}, u32[]{:S(2)}, u32[]{:S(2)}) collective-permute-start(bf16[288,256]{1,0:T(8,128)(2,1)S(1)} %pad_maximum_fusion.refs_0_.refs_4_), channel_id=1, source_target_pairs={{0,4},{1,5},{2,6},{3,7},{8,12},{9,13},{10,14},{11,15},{4,0},{5,1},... | collective-permute-start | bytes 442376 | tf_op jit(solution)/shard_map/ppermute | solution.py:141
  5.5 9.0 %collective-permute-start.3 = (bf16[288,256]{1,0:T(8,128)(2,1)S(1)}, bf16[288,256]{1,0:T(8,128)(2,1)S(1)}, u32[]{:S(2)}, u32[]{:S(2)}) collective-permute-start(bf16[288,256]{1,0:T(8,128)(2,1)S(1)} %pad_maximum_fusion.refs_0_.refs_4_), channel_id=1, source_target_pairs={{0,8},{1,9},{2,10},{3,11},{8,4},{9,5},{10,6},{11,7},{4,12},{5,13},... | collective-permute-start | bytes 442376 | tf_op jit(solution)/shard_map/ppermute | solution.py:141
  8.1 6.4 %collective-permute-start = (bf16[288,256]{1,0:T(8,128)(2,1)S(1)}, bf16[288,256]{1,0:T(8,128)(2,1)S(1)}, u32[]{:S(2)}, u32[]{:S(2)}) collective-permute-start(bf16[288,256]{1,0:T(8,128)(2,1)S(1)} %pad_maximum_fusion.refs_0_.refs_4_), channel_id=1, source_target_pairs={{0,1},{1,0},{2,3},{3,2},{4,5},{5,4},{6,7},{7,6},{8,9},{9,8},{10,11... | collective-permute-start | bytes 442376 | tf_op jit(solution)/shard_map/ppermute | solution.py:144
  8.1 8.5 %collective-permute-start.2 = (bf16[288,256]{1,0:T(8,128)(2,1)S(1)}, bf16[288,256]{1,0:T(8,128)(2,1)S(1)}, u32[]{:S(2)}, u32[]{:S(2)}) collective-permute-start(bf16[288,256]{1,0:T(8,128)(2,1)S(1)} %collective-permute-done.1.refs_2_), channel_id=1, source_target_pairs={{0,1},{1,0},{2,3},{3,2},{4,5},{5,4},{6,7},{7,6},{8,9},{9,8},{10,11... | collective-permute-start | bytes 442376 | tf_op jit(solution)/shard_map/ppermute | solution.py:144
  16.1 6.3 %collective-permute-start.6 = (f32[32,256]{1,0:T(8,128)S(1)}, f32[32,256]{1,0:T(8,128)S(1)}, u32[]{:S(2)}, u32[]{:S(2)}) collective-permute-start(f32[32,256]{1,0:T(8,128)S(1)} %get-tuple-element.14), channel_id=1, source_target_pairs={{0,1},{1,0},{2,3},{3,2},{4,5},{5,4},{6,7},{7,6},{8,9},{9,8},{10,11... | collective-permute-start | bytes 98312 | tf_op jit(solution)/shard_map/ppermute | solution.py:144
  16.1 6.3 %collective-permute-start.7 = (f32[32,256]{1,0:T(8,128)S(1)}, f32[32,256]{1,0:T(8,128)S(1)}, u32[]{:S(2)}, u32[]{:S(2)}) collective-permute-start(f32[32,256]{1,0:T(8,128)S(1)} %get-tuple-element.15), channel_id=1, source_target_pairs={{0,2},{1,3},{2,0},{3,1},{4,6},{5,7},{6,4},{7,5},{8,10},{9,11},{10,... | collective-permute-start | bytes 98312 | tf_op jit(solution)/shard_map/ppermute | solution.py:144
  17.7 5.2 %collective-permute-start.5 = (f32[32,256]{1,0:T(8,128)S(1)}, f32[32,256]{1,0:T(8,128)S(1)}, u32[]{:S(2)}, u32[]{:S(2)}) collective-permute-start(f32[32,256]{1,0:T(8,128)S(1)} %get-tuple-element.12), channel_id=1, source_target_pairs={{8,0},{9,1},{10,2},{11,3},{4,8},{5,9},{6,10},{7,11},{12,4},{13,5},... | collective-permute-start | bytes 98312 | tf_op jit(solution)/shard_map/ppermute | solution.py:141
  20.3 1.0 %copy-start = (f32[256]{0:T(256)S(1)}, f32[256]{0:T(256)}, u32[]{:S(2)}) copy-start(f32[256]{0:T(256)} %param.5) | copy-start | bytes 3076
  20.3 3.6 %collective-permute-start.8 = (f32[32,256]{1,0:T(8,128)S(1)}, f32[32,256]{1,0:T(8,128)S(1)}, u32[]{:S(2)}, u32[]{:S(2)}) collective-permute-start(f32[32,256]{1,0:T(8,128)S(1)} %get-tuple-element.16), channel_id=1, source_target_pairs={{0,3},{1,2},{2,1},{3,0},{4,7},{5,6},{6,5},{7,4},{8,11},{9,10},{10,... | collective-permute-start | bytes 98312 | tf_op jit(solution)/shard_map/ppermute | solution.py:144

commit v7 on v6

--- a/solution.py
+++ b/solution.py
@@ -18,19 +18,6 @@
     while size * size < count or count % size:
         size += 1
     return size
-
-
-def plane_blocks(value, count, send):
-    if count & (count - 1):
-        maps = {step: [(b, (b - step) % count) for b in range(count)] for step in range(1, count)}
-        return [value] + [send(value, maps[step]) for step in range(1, count)]
-    blocks = {0: value}
-    bit = count // 2
-    while bit:
-        for known in list(blocks):
-            blocks[known | bit] = send(blocks[known], [(b, b ^ bit) for b in range(count)])
-        bit //= 2
-    return [blocks[distance] for distance in range(count)]
 
 
 def plane_target(index, step, count):
@@ -66,12 +53,12 @@
     return total[0:1, :]
 
 
-def tile_kernel(shape, kinds, sums, shard, *refs):
+def tile_kernel(shape, order, kinds, sums, shard, *refs):
     refs = list(refs)
     rows_in, cols_in = shape
     terms_in, backs_in, noise_in = sums
-    rows, cols = refs[:rows_in], refs[rows_in : rows_in + cols_in]
-    del refs[: rows_in + cols_in]
+    blocks = [refs.pop(0) for _ in range(rows_in + cols_in)]
+    rows, cols = [blocks[place] for place in order[:rows_in]], [blocks[place] for place in order[rows_in:]]
     old_terms, old_backs, noise = refs[:terms_in], refs[terms_in : terms_in + backs_in], refs[terms_in + backs_in :][:noise_in]
     del refs[: terms_in + backs_in + noise_in]
     returning = sum("back" in kind for kind in kinds)
@@ -105,9 +92,10 @@
         ref[...] = term
 
 
-def tile(rows, cols, kinds, shard, terms=(), backs=(), noise=()):
+def tile(rows, cols, order, kinds, shard, terms=(), backs=(), noise=()):
     width, vectors = rows[0].shape[1], rows[0].shape[0] - shard
-    args = [*rows, *cols, *terms, *backs, *noise]
+    blocks = [*rows, *cols]
+    args = [*[blocks[place] for place in order], *terms, *backs, *noise]
     elements = len(rows) * len(cols) * shard * shard
     whole = pl.BlockSpec(memory_space=pltpu.VMEM)
     returning = sum("back" in kind for kind in kinds)
@@ -115,7 +103,12 @@
     outs = [jax.ShapeDtypeStruct((vectors, shard), jnp.float32)] * (returning + spread)
     found = pl.pallas_call(
         functools.partial(
-            tile_kernel, (len(rows), len(cols)), tuple(kinds), (len(terms), len(backs), len(noise)), shard
+            tile_kernel,
+            (len(rows), len(cols)),
+            [list(order).index(place) for place in range(len(blocks))],
+            tuple(kinds),
+            (len(terms), len(backs), len(noise)),
+            shard,
         ),
         out_shape=outs,
         in_specs=[whole] * len(args),
@@ -143,21 +136,22 @@
     def in_plane(value, hops):
         return lax.ppermute(value, "blk", [(a * inner + s, a * inner + t) for a in range(outer) for s, t in hops])
 
+    def near(step):
+        return [(plane_target(b, step, inner), b) for b in range(inner)]
+
     one_way, exchanges = outer_maps(outer)
     cols = [along_outer(packed, edges) for edges in one_way + exchanges]
     kinds = [("rows", "back")] * len(one_way) + [("rows",)] * len(exchanges)
-    blocks = plane_blocks(packed, inner, in_plane)
+    blocks = [packed] + [in_plane(packed, near(step)) for step in range(1, inner)]
 
-    direct = [d for d in range(inner) if d & (d - 1) == 0]
-    passed = [d for d in range(inner) if d & (d - 1)]
-    backs, terms = tile([blocks[d] for d in direct], cols, kinds, shard)
-    backs, late = tile([blocks[d] for d in passed], cols, kinds, shard, backs=backs)
-    (total,), _ = tile(blocks, [packed], [("back",)], shard, noise=[noise_level[None, :]])
-    for back, edges in zip(backs, one_way):
-        total = total + along_outer(back, [(t, s) for s, t in edges])
-    for step, term in zip(direct + passed, list(terms) + list(late)):
-        total = total + (in_plane(term, [(b, plane_target(b, step, inner)) for b in range(inner)]) if step else term)
-    return total.T
+    first = [inner + place for place in range(len(one_way))]
+    last = [inner + place for place in range(len(one_way), len(cols))]
+    order = [0, 1] + last + list(range(inner - 1, 1, -1)) + first if inner > 1 else [0] + last + first
+    backs, terms = tile(blocks, cols, order, kinds, shard)
+    sums = [along_outer(back, [(t, s) for s, t in edges]) for back, edges in zip(backs, one_way)]
+    sums += [in_plane(terms[step], [(t, s) for s, t in near(step)]) for step in range(inner - 1, 0, -1)]
+    (own,), _ = tile(blocks, [packed], range(inner + 1), [("back",)], shard, noise=[noise_level[None, :]])
+    return functools.reduce(lambda total, term: total + term, sums + list(terms[:1]) + [own]).T
 
 
 def solution(mesh):

time: 24.8 us -> 24.6 us (level)
  starting transfers between devices: 11.9 us -> 13.3 us
  waiting for transfers between devices: 7.46 us -> 6.37 us
  Pallas kernels: 3.54 us -> 2.83 us
    ppermute x3, waiting for transfers between devices: 6.41 us -> 2.15 us  [along_outer(): lax.ppermute(value, 'blk', [(s * inner + b, t * inner + b) for s, t in ed...]
    ppermute x6, waiting for transfers between devices: 1.05 us -> 4.22 us  [in_plane(): lax.ppermute(value, 'blk', [(a * inner + s, a * inner + t) for a in range...]
    ppermute x3, starting transfers between devices: 6.78 us -> 9.63 us  [along_outer(): lax.ppermute(value, 'blk', [(s * inner + b, t * inner + b) for s, t in ed...]
    ppermute x6, starting transfers between devices: 5.16 us -> 3.72 us  [in_plane(): lax.ppermute(value, 'blk', [(a * inner + s, a * inner + t) for a in range...]
    pallas_call x3 -> x2, Pallas kernels: 3.54 us -> 2.83 us  [tile(): pl.pallas_call(functools.partial(tile_kernel, (len(rows), len(cols)), [li...]
  transfers between devices with their start and end apart: 9 -> 9, of which waited for: 4 -> 6; matrix products, arithmetic and copies ran while one was open for 0% -> 0% of each run, Pallas kernels for 14% -> 4%
where the time goes in v7:
time: 24.6 us; the launch traced here: 24.4 us
  starting transfers between devices  13.3 us (54%)
  waiting for transfers between devices  6.37 us (26%)
  Pallas kernels  2.83 us (12%)
  other arithmetic  1.56 us (6%)
  local copies, waits for them, and re-layouts  0.25 us (1%)
    ppermute x3, starting transfers between devices, along_outer(): lax.ppermute(value, 'blk', [(s * inner + b, t * inner + b) for s, t in ed...  9.63 us
    ppermute x6, waiting for transfers between devices, in_plane(): lax.ppermute(value, 'blk', [(a * inner + s, a * inner + t) for a in range...  4.22 us
    ppermute x6, starting transfers between devices, in_plane(): lax.ppermute(value, 'blk', [(a * inner + s, a * inner + t) for a in range...  3.72 us
    pallas_call x2, Pallas kernels, tile(): pl.pallas_call(functools.partial(tile_kernel, (len(rows), len(cols)), [li...  2.83 us
    ppermute x3, waiting for transfers between devices, along_outer(): lax.ppermute(value, 'blk', [(s * inner + b, t * inner + b) for s, t in ed...  2.15 us
    concatenate x1, other arithmetic, on_device(): packed = jnp.concatenate([features, probes.T], axis=0)  0.93 us
    transpose x1, other arithmetic, on_device(): functools.reduce(lambda total, term: total + term, sums + list(terms[:1])...  0.63 us
  transfers between devices with their start and end apart: 9, of which 6 were waited for; matrix products, arithmetic and copies ran while one was open for 0% of the time, Pallas kernels for 4%

profile of v7, /device:TPU:0, one launch (start us, length us, event | category | flops | bytes accessed | tf_op | source)
XLA Modules:
  0.0 24.4 jit_solution(9166345251301364592)
XLA Ops:
  0.0 0.9 %pad_maximum_fusion.refs_0_.refs_4_ = bf16[288,256]{1,0:T(8,128)(2,1)S(1)} fusion(bf16[32,256]{1,0:T(8,128)(2,1)} %bitcast.5, bf16[256,256]{1,0:T(8,128)(2,1)} %param.3), kind=kLoop, calls=%fused_computation | loop fusion | flops 294912 | bytes 294912 | tf_op jit(solution)/shard_map/concatenate | solution.py:131
  0.9 4.1 %collective-permute-start.4 = (bf16[288,256]{1,0:T(8,128)(2,1)S(1)}, bf16[288,256]{1,0:T(8,128)(2,1)S(1)}, u32[]{:S(2)}, u32[]{:S(2)}) collective-permute-start(bf16[288,256]{1,0:T(8,128)(2,1)S(1)} %pad_maximum_fusion.refs_0_.refs_4_), channel_id=1, source_target_pairs={{0,8},{1,9},{2,10},{3,11},{8,4},{9,5},{10,6},{11,7},{4,12},{5,13},... | collective-permute-start | bytes 442376 | tf_op jit(solution)/shard_map/ppermute | solution.py:134
  5.0 1.5 %collective-permute-start.3 = (bf16[288,256]{1,0:T(8,128)(2,1)S(1)}, bf16[288,256]{1,0:T(8,128)(2,1)S(1)}, u32[]{:S(2)}, u32[]{:S(2)}) collective-permute-start(bf16[288,256]{1,0:T(8,128)(2,1)S(1)} %pad_maximum_fusion.refs_0_.refs_4_), channel_id=1, source_target_pairs={{2,0},{3,1},{0,2},{1,3},{6,4},{7,5},{4,6},{5,7},{10,8},{11,9},{8,1... | collective-permute-start | bytes 442376 | tf_op jit(solution)/shard_map/ppermute | solution.py:137
  6.5 0.0 collective-permute-start.2
  6.5 1.6 %collective-permute-start.1 = (bf16[288,256]{1,0:T(8,128)(2,1)S(1)}, bf16[288,256]{1,0:T(8,128)(2,1)S(1)}, u32[]{:S(2)}, u32[]{:S(2)}) collective-permute-start(bf16[288,256]{1,0:T(8,128)(2,1)S(1)} %pad_maximum_fusion.refs_0_.refs_4_), channel_id=1, source_target_pairs={{0,4},{1,5},{2,6},{3,7},{8,12},{9,13},{10,14},{11,15},{4,0},{5,1},... | collective-permute-start | bytes 442376 | tf_op jit(solution)/shard_map/ppermute | solution.py:134
  8.1 0.3 %collective-permute-start = (bf16[288,256]{1,0:T(8,128)(2,1)S(1)}, bf16[288,256]{1,0:T(8,128)(2,1)S(1)}, u32[]{:S(2)}, u32[]{:S(2)}) collective-permute-start(bf16[288,256]{1,0:T(8,128)(2,1)S(1)} %pad_maximum_fusion.refs_0_.refs_4_), channel_id=1, source_target_pairs={{1,0},{0,1},{3,2},{2,3},{5,4},{4,5},{7,6},{6,7},{9,8},{8,9},{11,10... | collective-permute-start | bytes 442376 | tf_op jit(solution)/shard_map/ppermute | solution.py:137
  8.5 1.7 %collective-permute-done.4.refs_5_ = bf16[288,256]{1,0:T(8,128)(2,1)S(1)} collective-permute-done((bf16[288,256]{1,0:T(8,128)(2,1)S(1)}, bf16[288,256]{1,0:T(8,128)(2,1)S(1)}, u32[]{:S(2)}, u32[]{:S(2)}) %collective-permute-start.4) | collective-permute-done | bytes 147488 | tf_op jit(solution)/shard_map/ppermute | solution.py:134
  10.1 1.0 %collective-permute-done.3.refs_4_.refs_2_ = bf16[288,256]{1,0:T(8,128)(2,1)S(1)} collective-permute-done((bf16[288,256]{1,0:T(8,128)(2,1)S(1)}, bf16[288,256]{1,0:T(8,128)(2,1)S(1)}, u32[]{:S(2)}, u32[]{:S(2)}) %collective-permute-start.3) | collective-permute-done | bytes 147488 | tf_op jit(solution)/shard_map/ppermute | solution.py:137
  11.1 1.5 %collective-permute-done.2.refs_3_ = bf16[288,256]{1,0:T(8,128)(2,1)S(1)} collective-permute-done((bf16[288,256]{1,0:T(8,128)(2,1)S(1)}, bf16[288,256]{1,0:T(8,128)(2,1)S(1)}, u32[]{:S(2)}, u32[]{:S(2)}) %collective-permute-start.2) | collective-permute-done | bytes 147488 | tf_op jit(solution)/shard_map/ppermute | solution.py:137
  12.7 0.5 %collective-permute-done.1.refs_2_ = bf16[288,256]{1,0:T(8,128)(2,1)S(1)} collective-permute-done((bf16[288,256]{1,0:T(8,128)(2,1)S(1)}, bf16[288,256]{1,0:T(8,128)(2,1)S(1)}, u32[]{:S(2)}, u32[]{:S(2)}) %collective-permute-start.1) | collective-permute-done | bytes 147488 | tf_op jit(solution)/shard_map/ppermute | solution.py:134
  13.1 0.0 collective-permute-done.refs_1_
  13.1 1.8 %shard_map.37 = (f32[32,256]{1,0:T(8,128)S(1)}, f32[32,256]{1,0:T(8,128)S(1)}, f32[32,256]{1,0:T(8,128)S(1)}, f32[32,256]{1,0:T(8,128)S(1)}, f32[32,256]{1,0:T(8,128)S(1)}) custom-call(bf16[288,256]{1,0:T(8,128)(2,1)S(1)} %pad_maximum_fusion.refs_0_.refs_4_, bf16[288,256]{1,0:T(8,128)(2,1)S(1)} %collective-permute-done.refs_1_, ...), custom_call_target="tpu_custom_call" | custom-call | flops 335544320 | bytes 786432 | tf_op jit(solution)/shard_map/pallas_call | solution.py:104
  15.0 4.0 %collective-permute-start.5 = (f32[32,256]{1,0:T(8,128)S(1)}, f32[32,256]{1,0:T(8,128)S(1)}, u32[]{:S(2)}, u32[]{:S(2)}) collective-permute-start(f32[32,256]{1,0:T(8,128)S(1)} %get-tuple-element.10), channel_id=1, source_target_pairs={{8,0},{9,1},{10,2},{11,3},{4,8},{5,9},{6,10},{7,11},{12,4},{13,5},... | collective-permute-start | bytes 98312 | tf_op jit(solution)/shard_map/ppermute | solution.py:134
  18.9 0.8 %collective-permute-start.6 = (f32[32,256]{1,0:T(8,128)S(1)}, f32[32,256]{1,0:T(8,128)S(1)}, u32[]{:S(2)}, u32[]{:S(2)}) collective-permute-start(f32[32,256]{1,0:T(8,128)S(1)} %get-tuple-element.11), channel_id=1, source_target_pairs={{0,3},{1,2},{2,1},{3,0},{4,7},{5,6},{6,5},{7,4},{8,11},{9,10},{10,... | collective-permute-start | bytes 98312 | tf_op jit(solution)/shard_map/ppermute | solution.py:137
  19.8 0.6 %collective-permute-start.7 = (f32[32,256]{1,0:T(8,128)S(1)}, f32[32,256]{1,0:T(8,128)S(1)}, u32[]{:S(2)}, u32[]{:S(2)}) collective-permute-start(f32[32,256]{1,0:T(8,128)S(1)} %get-tuple-element.12), channel_id=1, source_target_pairs={{0,2},{1,3},{2,0},{3,1},{4,6},{5,7},{6,4},{7,5},{8,10},{9,11},{10,... | collective-permute-start | bytes 98312 | tf_op jit(solution)/shard_map/ppermute | solution.py:137
  20.4 0.0 copy-start
  20.4 0.4 %collective-permute-start.8 = (f32[32,256]{1,0:T(8,128)S(1)}, f32[32,256]{1,0:T(8,128)S(1)}, u32[]{:S(2)}, u32[]{:S(2)}) collective-permute-start(f32[32,256]{1,0:T(8,128)S(1)} %get-tuple-element.13), channel_id=1, source_target_pairs={{0,1},{1,0},{2,3},{3,2},{4,5},{5,4},{6,7},{7,6},{8,9},{9,8},{10,11... | collective-permute-start | bytes 98312 | tf_op jit(solution)/shard_map/ppermute | solution.py:137
  20.8 0.2 %copy-done = f32[256]{0:T(256)S(1)} copy-done((f32[256]{0:T(256)S(1)}, f32[256]{0:T(256)}, u32[]{:S(2)}) %copy-start) | copy-done | bytes 1048
  21.0 1.0 %shard_map.38 = f32[32,256]{1,0:T(8,128)S(1)} custom-call(bf16[288,256]{1,0:T(8,128)(2,1)S(1)} %pad_maximum_fusion.refs_0_.refs_4_, bf16[288,256]{1,0:T(8,128)(2,1)S(1)} %collective-permute-done.refs_1_, bf16[288,256]{1,0:T(8,128)(2,1)S(1)} %collective-permute-done.3.refs_4_.refs_2_, bf16[288,256]{1,0:T(8,128)(2,1)S(1)} %collective-permute-done.2.refs_3_, ...), custom_call_target="tpu_custom_call" | custom-call | flops 167772160 | bytes 655360 | tf_op jit(solution)/shard_map/pallas_call | solution.py:104
  22.1 0.0 collective-permute-done.5
  22.1 0.5 %collective-permute-done.6 = f32[32,256]{1,0:T(8,128)S(1)} collective-permute-done((f32[32,256]{1,0:T(8,128)S(1)}, f32[32,256]{1,0:T(8,128)S(1)}, u32[]{:S(2)}, u32[]{:S(2)}) %collective-permute-start.6) | collective-permute-done | bytes 32800 | tf_op jit(solution)/shard_map/ppermute | solution.py:137
  22.6 1.2 %collective-permute-done.7 = f32[32,256]{1,0:T(8,128)S(1)} collective-permute-done((f32[32,256]{1,0:T(8,128)S(1)}, f32[32,256]{1,0:T(8,128)S(1)}, u32[]{:S(2)}, u32[]{:S(2)}) %collective-permute-start.7) | collective-permute-done | bytes 32800 | tf_op jit(solution)/shard_map/ppermute | solution.py:137
  23.7 0.0 collective-permute-done.8
  23.7 0.6 %add_bitcast_fusion = f32[256,32]{0,1:T(8,128)} fusion(f32[32,256]{1,0:T(8,128)S(1)} %shard_map.38, f32[32,256]{1,0:T(8,128)S(1)} %get-tuple-element.14, f32[32,256]{1,0:T(8,128)S(1)} %collective-permute-done.8, f32[32,256]{1,0:T(8,128)S(1)} %collective-permute-done.7, f32[32,256]{1,0:T(8,128)S(1)} %collective-permute-done.5, ...), kind=kLoop, calls=%fused_computation.1 | loop fusion | flops 40960 | bytes 229376 | tf_op jit(solution)/shard_map/transpose | solution.py:154
Async XLA Ops:
  0.9 9.2 %collective-permute-start.4 = (bf16[288,256]{1,0:T(8,128)(2,1)S(1)}, bf16[288,256]{1,0:T(8,128)(2,1)S(1)}, u32[]{:S(2)}, u32[]{:S(2)}) collective-permute-start(bf16[288,256]{1,0:T(8,128)(2,1)S(1)} %pad_maximum_fusion.refs_0_.refs_4_), channel_id=1, source_target_pairs={{0,8},{1,9},{2,10},{3,11},{8,4},{9,5},{10,6},{11,7},{4,12},{5,13},... | collective-permute-start | bytes 442376 | tf_op jit(solution)/shard_map/ppermute | solution.py:134
  5.0 6.1 %collective-permute-start.3 = (bf16[288,256]{1,0:T(8,128)(2,1)S(1)}, bf16[288,256]{1,0:T(8,128)(2,1)S(1)}, u32[]{:S(2)}, u32[]{:S(2)}) collective-permute-start(bf16[288,256]{1,0:T(8,128)(2,1)S(1)} %pad_maximum_fusion.refs_0_.refs_4_), channel_id=1, source_target_pairs={{2,0},{3,1},{0,2},{1,3},{6,4},{7,5},{4,6},{5,7},{10,8},{11,9},{8,1... | collective-permute-start | bytes 442376 | tf_op jit(solution)/shard_map/ppermute | solution.py:137
  6.5 6.1 %collective-permute-start.2 = (bf16[288,256]{1,0:T(8,128)(2,1)S(1)}, bf16[288,256]{1,0:T(8,128)(2,1)S(1)}, u32[]{:S(2)}, u32[]{:S(2)}) collective-permute-start(bf16[288,256]{1,0:T(8,128)(2,1)S(1)} %pad_maximum_fusion.refs_0_.refs_4_), channel_id=1, source_target_pairs={{3,0},{2,1},{1,2},{0,3},{7,4},{6,5},{5,6},{4,7},{11,8},{10,9},{9,1... | collective-permute-start | bytes 442376 | tf_op jit(solution)/shard_map/ppermute | solution.py:137
  6.5 6.6 %collective-permute-start.1 = (bf16[288,256]{1,0:T(8,128)(2,1)S(1)}, bf16[288,256]{1,0:T(8,128)(2,1)S(1)}, u32[]{:S(2)}, u32[]{:S(2)}) collective-permute-start(bf16[288,256]{1,0:T(8,128)(2,1)S(1)} %pad_maximum_fusion.refs_0_.refs_4_), channel_id=1, source_target_pairs={{0,4},{1,5},{2,6},{3,7},{8,12},{9,13},{10,14},{11,15},{4,0},{5,1},... | collective-permute-start | bytes 442376 | tf_op jit(solution)/shard_map/ppermute | solution.py:134
  8.1 5.0 %collective-permute-start = (bf16[288,256]{1,0:T(8,128)(2,1)S(1)}, bf16[288,256]{1,0:T(8,128)(2,1)S(1)}, u32[]{:S(2)}, u32[]{:S(2)}) collective-permute-start(bf16[288,256]{1,0:T(8,128)(2,1)S(1)} %pad_maximum_fusion.refs_0_.refs_4_), channel_id=1, source_target_pairs={{1,0},{0,1},{3,2},{2,3},{5,4},{4,5},{7,6},{6,7},{9,8},{8,9},{11,10... | collective-permute-start | bytes 442376 | tf_op jit(solution)/shard_map/ppermute | solution.py:137
  15.0 7.1 %collective-permute-start.5 = (f32[32,256]{1,0:T(8,128)S(1)}, f32[32,256]{1,0:T(8,128)S(1)}, u32[]{:S(2)}, u32[]{:S(2)}) collective-permute-start(f32[32,256]{1,0:T(8,128)S(1)} %get-tuple-element.10), channel_id=1, source_target_pairs={{8,0},{9,1},{10,2},{11,3},{4,8},{5,9},{6,10},{7,11},{12,4},{13,5},... | collective-permute-start | bytes 98312 | tf_op jit(solution)/shard_map/ppermute | solution.py:134
  18.9 3.6 %collective-permute-start.6 = (f32[32,256]{1,0:T(8,128)S(1)}, f32[32,256]{1,0:T(8,128)S(1)}, u32[]{:S(2)}, u32[]{:S(2)}) collective-permute-start(f32[32,256]{1,0:T(8,128)S(1)} %get-tuple-element.11), channel_id=1, source_target_pairs={{0,3},{1,2},{2,1},{3,0},{4,7},{5,6},{6,5},{7,4},{8,11},{9,10},{10,... | collective-permute-start | bytes 98312 | tf_op jit(solution)/shard_map/ppermute | solution.py:137
  19.8 4.0 %collective-permute-start.7 = (f32[32,256]{1,0:T(8,128)S(1)}, f32[32,256]{1,0:T(8,128)S(1)}, u32[]{:S(2)}, u32[]{:S(2)}) collective-permute-start(f32[32,256]{1,0:T(8,128)S(1)} %get-tuple-element.12), channel_id=1, source_target_pairs={{0,2},{1,3},{2,0},{3,1},{4,6},{5,7},{6,4},{7,5},{8,10},{9,11},{10,... | collective-permute-start | bytes 98312 | tf_op jit(solution)/shard_map/ppermute | solution.py:137
  20.4 0.7 %copy-start = (f32[256]{0:T(256)S(1)}, f32[256]{0:T(256)}, u32[]{:S(2)}) copy-start(f32[256]{0:T(256)} %param.5) | copy-start | bytes 3076
  20.4 3.4 %collective-permute-start.8 = (f32[32,256]{1,0:T(8,128)S(1)}, f32[32,256]{1,0:T(8,128)S(1)}, u32[]{:S(2)}, u32[]{:S(2)}) collective-permute-start(f32[32,256]{1,0:T(8,128)S(1)} %get-tuple-element.13), channel_id=1, source_target_pairs={{0,1},{1,0},{2,3},{3,2},{4,5},{5,4},{6,7},{7,6},{8,9},{9,8},{10,11... | collective-permute-start | bytes 98312 | tf_op jit(solution)/shard_map/ppermute | solution.py:137

commit v8 on v7

--- a/solution.py
+++ b/solution.py
@@ -18,6 +18,19 @@
     while size * size < count or count % size:
         size += 1
     return size
+
+
+def plane_blocks(value, count, send):
+    if count & (count - 1):
+        maps = {step: [(b, (b - step) % count) for b in range(count)] for step in range(1, count)}
+        return [value] + [send(value, maps[step]) for step in range(1, count)]
+    blocks = {0: value}
+    bit = count // 2
+    while bit:
+        for known in list(blocks):
+            blocks[known | bit] = send(blocks[known], [(b, b ^ bit) for b in range(count)])
+        bit //= 2
+    return [blocks[distance] for distance in range(count)]
 
 
 def plane_target(index, step, count):
@@ -142,11 +155,13 @@
     one_way, exchanges = outer_maps(outer)
     cols = [along_outer(packed, edges) for edges in one_way + exchanges]
     kinds = [("rows", "back")] * len(one_way) + [("rows",)] * len(exchanges)
-    blocks = [packed] + [in_plane(packed, near(step)) for step in range(1, inner)]
+    blocks = plane_blocks(packed, inner, in_plane)
 
+    direct = [step for step in range(1, inner) if step & (step - 1) == 0]
+    passed = [step for step in range(1, inner) if step & (step - 1)]
     first = [inner + place for place in range(len(one_way))]
     last = [inner + place for place in range(len(one_way), len(cols))]
-    order = [0, 1] + last + list(range(inner - 1, 1, -1)) + first if inner > 1 else [0] + last + first
+    order = [0] + passed + last + direct[:1] + first + direct[1:]
     backs, terms = tile(blocks, cols, order, kinds, shard)
     sums = [along_outer(back, [(t, s) for s, t in edges]) for back, edges in zip(backs, one_way)]
     sums += [in_plane(terms[step], [(t, s) for s, t in near(step)]) for step in range(inner - 1, 0, -1)]

time: 24.6 us -> 24 us (0.976)
  starting transfers between devices: 13.3 us -> 12.1 us
  waiting for transfers between devices: 6.37 us -> 7.2 us
    ppermute x3, waiting for transfers between devices: 2.15 us -> 6.03 us  [along_outer(): lax.ppermute(value, 'blk', [(s * inner + b, t * inner + b) for s, t in ed...]
    ppermute x6, waiting for transfers between devices: 4.22 us -> 1.17 us  [in_plane(): lax.ppermute(value, 'blk', [(a * inner + s, a * inner + t) for a in range...]
    ppermute x3, starting transfers between devices: 9.63 us -> 6.99 us  [along_outer(): lax.ppermute(value, 'blk', [(s * inner + b, t * inner + b) for s, t in ed...]
    ppermute x6, starting transfers between devices: 3.72 us -> 5.12 us  [in_plane(): lax.ppermute(value, 'blk', [(a * inner + s, a * inner + t) for a in range...]
    unnamed x2, local copies, waits for them, and re-layouts: 0.25 us -> 0.01 us
  transfers between devices with their start and end apart: 9 -> 9, of which waited for: 6 -> 4; matrix products, arithmetic and copies ran while one was open for 0% -> 0% of each run, Pallas kernels for 4% -> 4%
where the time goes in v8:
time: 24 us; the launch traced here: 23.7 us
  starting transfers between devices  12.1 us (50%)
  waiting for transfers between devices  7.2 us (30%)
  Pallas kernels  2.82 us (12%)
  other arithmetic  1.56 us (6%)
    ppermute x3, starting transfers between devices, along_outer(): lax.ppermute(value, 'blk', [(s * inner + b, t * inner + b) for s, t in ed...  6.99 us
    ppermute x3, waiting for transfers between devices, along_outer(): lax.ppermute(value, 'blk', [(s * inner + b, t * inner + b) for s, t in ed...  6.03 us
    ppermute x6, starting transfers between devices, in_plane(): lax.ppermute(value, 'blk', [(a * inner + s, a * inner + t) for a in range...  5.12 us
    pallas_call x2, Pallas kernels, tile(): pl.pallas_call(functools.partial(tile_kernel, (len(rows), len(cols)), [li...  2.82 us
    ppermute x6, waiting for transfers between devices, in_plane(): lax.ppermute(value, 'blk', [(a * inner + s, a * inner + t) for a in range...  1.17 us
    concatenate x1, other arithmetic, on_device(): packed = jnp.concatenate([features, probes.T], axis=0)  0.93 us
    transpose x1, other arithmetic, on_device(): functools.reduce(lambda total, term: total + term, sums + list(terms[:1])...  0.63 us
  transfers between devices with their start and end apart: 9, of which 4 were waited for; matrix products, arithmetic and copies ran while one was open for 0% of the time, Pallas kernels for 4%

profile of v8, /device:TPU:0, one launch (start us, length us, event | category | flops | bytes accessed | tf_op | source)
XLA Modules:
  0.0 23.7 jit_solution(15599649734991421657)
XLA Ops:
  0.0 0.9 %pad_maximum_fusion.refs_0_.refs_4_ = bf16[288,256]{1,0:T(8,128)(2,1)S(1)} fusion(bf16[32,256]{1,0:T(8,128)(2,1)} %bitcast.5, bf16[256,256]{1,0:T(8,128)(2,1)} %param.3), kind=kLoop, calls=%fused_computation | loop fusion | flops 294912 | bytes 294912 | tf_op jit(solution)/shard_map/concatenate | solution.py:144
  0.9 3.0 %collective-permute-start = (bf16[288,256]{1,0:T(8,128)(2,1)S(1)}, bf16[288,256]{1,0:T(8,128)(2,1)S(1)}, u32[]{:S(2)}, u32[]{:S(2)}) collective-permute-start(bf16[288,256]{1,0:T(8,128)(2,1)S(1)} %pad_maximum_fusion.refs_0_.refs_4_), channel_id=1, source_target_pairs={{0,2},{1,3},{2,0},{3,1},{4,6},{5,7},{6,4},{7,5},{8,10},{9,11},{10,... | collective-permute-start | bytes 442376 | tf_op jit(solution)/shard_map/ppermute | solution.py:150
  4.0 2.6 %collective-permute-start.4 = (bf16[288,256]{1,0:T(8,128)(2,1)S(1)}, bf16[288,256]{1,0:T(8,128)(2,1)S(1)}, u32[]{:S(2)}, u32[]{:S(2)}) collective-permute-start(bf16[288,256]{1,0:T(8,128)(2,1)S(1)} %pad_maximum_fusion.refs_0_.refs_4_), channel_id=1, source_target_pairs={{0,8},{1,9},{2,10},{3,11},{8,4},{9,5},{10,6},{11,7},{4,12},{5,13},... | collective-permute-start | bytes 442376 | tf_op jit(solution)/shard_map/ppermute | solution.py:147
  6.6 0.0 collective-permute-start.3
  6.6 1.6 %collective-permute-start.2 = (bf16[288,256]{1,0:T(8,128)(2,1)S(1)}, bf16[288,256]{1,0:T(8,128)(2,1)S(1)}, u32[]{:S(2)}, u32[]{:S(2)}) collective-permute-start(bf16[288,256]{1,0:T(8,128)(2,1)S(1)} %pad_maximum_fusion.refs_0_.refs_4_), channel_id=1, source_target_pairs={{0,4},{1,5},{2,6},{3,7},{8,12},{9,13},{10,14},{11,15},{4,0},{5,1},... | collective-permute-start | bytes 442376 | tf_op jit(solution)/shard_map/ppermute | solution.py:147
  8.1 0.0 collective-permute-done.refs_5_.refs_2_
  8.1 0.2 collective-permute-start.1
  8.4 4.2 %collective-permute-done.4.refs_4_ = bf16[288,256]{1,0:T(8,128)(2,1)S(1)} collective-permute-done((bf16[288,256]{1,0:T(8,128)(2,1)S(1)}, bf16[288,256]{1,0:T(8,128)(2,1)S(1)}, u32[]{:S(2)}, u32[]{:S(2)}) %collective-permute-start.4) | collective-permute-done | bytes 147488 | tf_op jit(solution)/shard_map/ppermute | solution.py:147
  12.5 0.0 collective-permute-done.3.refs_3_.refs_1_
  12.5 1.9 %collective-permute-done.2.refs_2_ = bf16[288,256]{1,0:T(8,128)(2,1)S(1)} collective-permute-done((bf16[288,256]{1,0:T(8,128)(2,1)S(1)}, bf16[288,256]{1,0:T(8,128)(2,1)S(1)}, u32[]{:S(2)}, u32[]{:S(2)}) %collective-permute-start.2) | collective-permute-done | bytes 147488 | tf_op jit(solution)/shard_map/ppermute | solution.py:147
  14.4 0.0 collective-permute-done.1.refs_1_.refs_3_
  14.4 1.8 %shard_map.37 = (f32[32,256]{1,0:T(8,128)S(1)}, f32[32,256]{1,0:T(8,128)S(1)}, f32[32,256]{1,0:T(8,128)S(1)}, f32[32,256]{1,0:T(8,128)S(1)}, f32[32,256]{1,0:T(8,128)S(1)}) custom-call(bf16[288,256]{1,0:T(8,128)(2,1)S(1)} %pad_maximum_fusion.refs_0_.refs_4_, bf16[288,256]{1,0:T(8,128)(2,1)S(1)} %collective-permute-done.1.refs_1_.refs_3_, ...), custom_call_target="tpu_custom_call" | custom-call | flops 335544320 | bytes 786432 | tf_op jit(solution)/shard_map/pallas_call | solution.py:117
  16.2 2.8 %collective-permute-start.5 = (f32[32,256]{1,0:T(8,128)S(1)}, f32[32,256]{1,0:T(8,128)S(1)}, u32[]{:S(2)}, u32[]{:S(2)}) collective-permute-start(f32[32,256]{1,0:T(8,128)S(1)} %get-tuple-element.10), channel_id=1, source_target_pairs={{8,0},{9,1},{10,2},{11,3},{4,8},{5,9},{6,10},{7,11},{12,4},{13,5},... | collective-permute-start | bytes 98312 | tf_op jit(solution)/shard_map/ppermute | solution.py:147
  19.0 0.0 collective-permute-start.6
  19.0 1.1 %collective-permute-start.7 = (f32[32,256]{1,0:T(8,128)S(1)}, f32[32,256]{1,0:T(8,128)S(1)}, u32[]{:S(2)}, u32[]{:S(2)}) collective-permute-start(f32[32,256]{1,0:T(8,128)S(1)} %get-tuple-element.12), channel_id=1, source_target_pairs={{0,2},{1,3},{2,0},{3,1},{4,6},{5,7},{6,4},{7,5},{8,10},{9,11},{10,... | collective-permute-start | bytes 98312 | tf_op jit(solution)/shard_map/ppermute | solution.py:150
  20.1 0.0 copy-start
  20.1 0.8 %collective-permute-start.8 = (f32[32,256]{1,0:T(8,128)S(1)}, f32[32,256]{1,0:T(8,128)S(1)}, u32[]{:S(2)}, u32[]{:S(2)}) collective-permute-start(f32[32,256]{1,0:T(8,128)S(1)} %get-tuple-element.13), channel_id=1, source_target_pairs={{0,1},{1,0},{2,3},{3,2},{4,5},{5,4},{6,7},{7,6},{8,9},{9,8},{10,11... | collective-permute-start | bytes 98312 | tf_op jit(solution)/shard_map/ppermute | solution.py:150
  20.9 0.0 copy-done
  20.9 1.0 %shard_map.38 = f32[32,256]{1,0:T(8,128)S(1)} custom-call(bf16[288,256]{1,0:T(8,128)(2,1)S(1)} %pad_maximum_fusion.refs_0_.refs_4_, bf16[288,256]{1,0:T(8,128)(2,1)S(1)} %collective-permute-done.3.refs_3_.refs_1_, bf16[288,256]{1,0:T(8,128)(2,1)S(1)} %collective-permute-done.refs_5_.refs_2_, bf16[288,256]{1,0:T(8,128)(2,1)S(1)} %collective-permute-done.1.refs_1_.refs_3_, ...), custom_call_target="tpu_custom_call" | custom-call | flops 167772160 | bytes 655360 | tf_op jit(solution)/shard_map/pallas_call | solution.py:117
  21.9 0.0 collective-permute-done.5
  21.9 0.5 %collective-permute-done.6 = f32[32,256]{1,0:T(8,128)S(1)} collective-permute-done((f32[32,256]{1,0:T(8,128)S(1)}, f32[32,256]{1,0:T(8,128)S(1)}, u32[]{:S(2)}, u32[]{:S(2)}) %collective-permute-start.6) | collective-permute-done | bytes 32800 | tf_op jit(solution)/shard_map/ppermute | solution.py:150
  22.4 0.7 %collective-permute-done.7 = f32[32,256]{1,0:T(8,128)S(1)} collective-permute-done((f32[32,256]{1,0:T(8,128)S(1)}, f32[32,256]{1,0:T(8,128)S(1)}, u32[]{:S(2)}, u32[]{:S(2)}) %collective-permute-start.7) | collective-permute-done | bytes 32800 | tf_op jit(solution)/shard_map/ppermute | solution.py:150
  23.1 0.0 collective-permute-done.8
  23.1 0.6 %add_bitcast_fusion = f32[256,32]{0,1:T(8,128)} fusion(f32[32,256]{1,0:T(8,128)S(1)} %shard_map.38, f32[32,256]{1,0:T(8,128)S(1)} %get-tuple-element.14, f32[32,256]{1,0:T(8,128)S(1)} %collective-permute-done.8, f32[32,256]{1,0:T(8,128)S(1)} %collective-permute-done.7, f32[32,256]{1,0:T(8,128)S(1)} %collective-permute-done.5, ...), kind=kLoop, calls=%fused_computation.1 | loop fusion | flops 40960 | bytes 229376 | tf_op jit(solution)/shard_map/transpose | solution.py:169
Async XLA Ops:
  0.9 7.2 %collective-permute-start = (bf16[288,256]{1,0:T(8,128)(2,1)S(1)}, bf16[288,256]{1,0:T(8,128)(2,1)S(1)}, u32[]{:S(2)}, u32[]{:S(2)}) collective-permute-start(bf16[288,256]{1,0:T(8,128)(2,1)S(1)} %pad_maximum_fusion.refs_0_.refs_4_), channel_id=1, source_target_pairs={{0,2},{1,3},{2,0},{3,1},{4,6},{5,7},{6,4},{7,5},{8,10},{9,11},{10,... | collective-permute-start | bytes 442376 | tf_op jit(solution)/shard_map/ppermute | solution.py:150
  4.0 8.6 %collective-permute-start.4 = (bf16[288,256]{1,0:T(8,128)(2,1)S(1)}, bf16[288,256]{1,0:T(8,128)(2,1)S(1)}, u32[]{:S(2)}, u32[]{:S(2)}) collective-permute-start(bf16[288,256]{1,0:T(8,128)(2,1)S(1)} %pad_maximum_fusion.refs_0_.refs_4_), channel_id=1, source_target_pairs={{0,8},{1,9},{2,10},{3,11},{8,4},{9,5},{10,6},{11,7},{4,12},{5,13},... | collective-permute-start | bytes 442376 | tf_op jit(solution)/shard_map/ppermute | solution.py:147
  6.6 6.0 %collective-permute-start.3 = (bf16[288,256]{1,0:T(8,128)(2,1)S(1)}, bf16[288,256]{1,0:T(8,128)(2,1)S(1)}, u32[]{:S(2)}, u32[]{:S(2)}) collective-permute-start(bf16[288,256]{1,0:T(8,128)(2,1)S(1)} %pad_maximum_fusion.refs_0_.refs_4_), channel_id=1, source_target_pairs={{0,1},{1,0},{2,3},{3,2},{4,5},{5,4},{6,7},{7,6},{8,9},{9,8},{10,11... | collective-permute-start | bytes 442376 | tf_op jit(solution)/shard_map/ppermute | solution.py:150
  6.6 7.8 %collective-permute-start.2 = (bf16[288,256]{1,0:T(8,128)(2,1)S(1)}, bf16[288,256]{1,0:T(8,128)(2,1)S(1)}, u32[]{:S(2)}, u32[]{:S(2)}) collective-permute-start(bf16[288,256]{1,0:T(8,128)(2,1)S(1)} %pad_maximum_fusion.refs_0_.refs_4_), channel_id=1, source_target_pairs={{0,4},{1,5},{2,6},{3,7},{8,12},{9,13},{10,14},{11,15},{4,0},{5,1},... | collective-permute-start | bytes 442376 | tf_op jit(solution)/shard_map/ppermute | solution.py:147
  8.1 6.3 %collective-permute-start.1 = (bf16[288,256]{1,0:T(8,128)(2,1)S(1)}, bf16[288,256]{1,0:T(8,128)(2,1)S(1)}, u32[]{:S(2)}, u32[]{:S(2)}) collective-permute-start(bf16[288,256]{1,0:T(8,128)(2,1)S(1)} %collective-permute-done.refs_5_.refs_2_), channel_id=1, source_target_pairs={{0,1},{1,0},{2,3},{3,2},{4,5},{5,4},{6,7},{7,6},{8,9},{9,8},{10,11... | collective-permute-start | bytes 442376 | tf_op jit(solution)/shard_map/ppermute | solution.py:150
  16.2 5.7 %collective-permute-start.5 = (f32[32,256]{1,0:T(8,128)S(1)}, f32[32,256]{1,0:T(8,128)S(1)}, u32[]{:S(2)}, u32[]{:S(2)}) collective-permute-start(f32[32,256]{1,0:T(8,128)S(1)} %get-tuple-element.10), channel_id=1, source_target_pairs={{8,0},{9,1},{10,2},{11,3},{4,8},{5,9},{6,10},{7,11},{12,4},{13,5},... | collective-permute-start | bytes 98312 | tf_op jit(solution)/shard_map/ppermute | solution.py:147
  19.0 3.3 %collective-permute-start.6 = (f32[32,256]{1,0:T(8,128)S(1)}, f32[32,256]{1,0:T(8,128)S(1)}, u32[]{:S(2)}, u32[]{:S(2)}) collective-permute-start(f32[32,256]{1,0:T(8,128)S(1)} %get-tuple-element.11), channel_id=1, source_target_pairs={{0,3},{1,2},{2,1},{3,0},{4,7},{5,6},{6,5},{7,4},{8,11},{9,10},{10,... | collective-permute-start | bytes 98312 | tf_op jit(solution)/shard_map/ppermute | solution.py:150
  19.0 4.0 %collective-permute-start.7 = (f32[32,256]{1,0:T(8,128)S(1)}, f32[32,256]{1,0:T(8,128)S(1)}, u32[]{:S(2)}, u32[]{:S(2)}) collective-permute-start(f32[32,256]{1,0:T(8,128)S(1)} %get-tuple-element.12), channel_id=1, source_target_pairs={{0,2},{1,3},{2,0},{3,1},{4,6},{5,7},{6,4},{7,5},{8,10},{9,11},{10,... | collective-permute-start | bytes 98312 | tf_op jit(solution)/shard_map/ppermute | solution.py:150
  20.1 0.8 %copy-start = (f32[256]{0:T(256)S(1)}, f32[256]{0:T(256)}, u32[]{:S(2)}) copy-start(f32[256]{0:T(256)} %param.5) | copy-start | bytes 3076
  20.1 3.0 %collective-permute-start.8 = (f32[32,256]{1,0:T(8,128)S(1)}, f32[32,256]{1,0:T(8,128)S(1)}, u32[]{:S(2)}, u32[]{:S(2)}) collective-permute-start(f32[32,256]{1,0:T(8,128)S(1)} %get-tuple-element.13), channel_id=1, source_target_pairs={{0,1},{1,0},{2,3},{3,2},{4,5},{5,4},{6,7},{7,6},{8,9},{9,8},{10,11... | collective-permute-start | bytes 98312 | tf_op jit(solution)/shard_map/ppermute | solution.py:150

commit v9 on v6

v9 whole, which is shorter than its diff:
```python
import functools
import math

import jax
import jax.numpy as jnp
from jax import lax
from jax.experimental import pallas as pl
from jax.experimental.pallas import tpu as pltpu
from jax.sharding import PartitionSpec as P

ROOT5 = math.sqrt(5.0)
DECAY = -ROOT5 * math.log2(math.e)
ROWS_BY_ROWS = (((1,), (1,)), ((), ()))


def group_size(count):
    size = 1
    while size * size < count or count % size:
        size += 1
    return size


def plane_blocks(value, count, send):
    if count & (count - 1):
        maps = {step: [(b, (b - step) % count) for b in range(count)] for step in range(1, count)}
        return [value] + [send(value, maps[step]) for step in range(1, count)]
    blocks = {0: value}
    bit = count // 2
    while bit:
        for known in list(blocks):
            blocks[known | bit] = send(blocks[known], [(b, b ^ bit) for b in range(count)])
        bit //= 2
    return [blocks[distance] for distance in range(count)]


def plane_target(index, step, count):
    return (index + step) % count if count & (count - 1) else index ^ step


def outer_maps(count):
    bits = count.bit_length() - 1
    order = list(range(count))
    if count == 1 << bits:
        order = [int(f"{a:0{bits}b}"[::-1], 2) if bits else a for a in order]
    shifts = [[(order[p], order[(p + step) % count]) for p in range(count)] for step in range(1, count // 2 + 1)]
    if count % 2:
        return shifts, []
    return shifts[:-1], shifts[-1:]


def matern(dist2):
    dist2 = jnp.maximum(dist2, 1e-30)
    dist = dist2 * lax.rsqrt(dist2)
    poly = (1.0 + ROOT5 * dist) + (5.0 / 3.0) * dist2
    return (poly * jnp.exp2(DECAY * dist)).astype(jnp.bfloat16)


def lane_squares(block):
    wide = block.astype(jnp.float32)
    square = wide * wide
    high = square.astype(jnp.bfloat16)
    low = (square - high.astype(jnp.float32)).astype(jnp.bfloat16)
    ones = jnp.ones((8, block.shape[1]), jnp.bfloat16)
    total = lax.dot_general(ones, high, ROWS_BY_ROWS, preferred_element_type=jnp.float32)
    total += lax.dot_general(ones, low, ROWS_BY_ROWS, preferred_element_type=jnp.float32)
    return total[0:1, :]


def tile_kernel(order, pairs, known, counts, shard, vectors, *refs):
    rows_in, cols_in, noise_in = counts
    blocks = [refs[order.index(place)] for place in range(rows_in + cols_in)]
    rows, cols = blocks[:rows_in], blocks[rows_in:]
    rest = list(refs[rows_in + cols_in :])
    noise = [rest.pop(0) for _ in range(noise_in)]
    sums = {name: rest.pop(0)[...] for name in known}
    ready_rows, ready_cols = {}, {}
    for row, col, kind in pairs:
        if row not in ready_rows:
            wide = rows[row][0:shard, :].astype(jnp.float32)
            ready_rows[row] = jnp.sum(wide * wide, axis=1, keepdims=True)
        if col not in ready_cols:
            block = cols[col][0:shard, :]
            ready_cols[col] = block * jnp.asarray(-2.0, block.dtype), lane_squares(block)
        scaled, col_squares = ready_cols[col]
        row_block, row_probes = rows[row][0:shard, :], rows[row][pl.ds(shard, vectors), :]
        cross = lax.dot_general(row_block, scaled, ROWS_BY_ROWS, preferred_element_type=jnp.float32)
        kernel = matern((ready_rows[row] + col_squares) + cross)
        found = {}
        if "back" in kind:
            found["back", col] = jnp.dot(row_probes, kernel, preferred_element_type=jnp.float32)
        if "rows" in kind:
            col_probes = cols[col][pl.ds(shard, vectors), :]
            found["rows", row] = lax.dot_general(col_probes, kernel, ROWS_BY_ROWS, preferred_element_type=jnp.float32)
        for name, value in found.items():
            sums[name] = sums[name] + value if name in sums else value
    for place in range(noise_in):
        probes = cols[place][pl.ds(shard, vectors), :].astype(jnp.float32)
        sums["back", place] = sums["back", place] + noise[place][...] * probes
    for ref, name in zip(rest, sorted(sums)):
        ref[...] = sums[name]


def tile(rows, cols, order, pairs, sums, shard, vectors, noise=(), waits=1):
    blocks = [*rows, *cols]
    args = [*[blocks[place] for place in order], *noise, *sums.values()]
    elements = len(pairs) * shard * shard
    width = rows[0].shape[1]
    names = sorted({(part, col if part == "back" else row) for row, col, kind in pairs for part in kind} | set(sums))
    whole = pl.BlockSpec(memory_space=pltpu.VMEM)
    found = pl.pallas_call(
        functools.partial(
            tile_kernel, list(order), tuple(pairs), tuple(sums), (len(rows), len(cols), len(noise)), shard, vectors
        ),
        out_shape=[jax.ShapeDtypeStruct((vectors, shard), jnp.float32)] * len(names),
        in_specs=[whole] * len(args),
        out_specs=[whole] * len(names),
        compiler_params=pltpu.CompilerParams(vmem_limit_bytes=32 * 1024 * 1024),
        cost_estimate=pl.CostEstimate(
            flops=2 * elements * (width + 2 * vectors) * waits,
            bytes_accessed=2 * width * shard * len(blocks),
            transcendentals=2 * elements,
        ),
    )(*args)
    return dict(zip(names, found))


def copy_kernel(from_ref, to_ref):
    to_ref[...] = from_ref[0 : to_ref.shape[0], :]


def copy_rows(value, rows):
    whole = pl.BlockSpec(memory_space=pltpu.VMEM)
    return pl.pallas_call(
        copy_kernel,
        out_shape=jax.ShapeDtypeStruct((rows, value.shape[1]), value.dtype),
        in_specs=[whole],
        out_specs=whole,
    )(value)


def on_device(features, probes, noise_level):
    count = lax.axis_size("blk")
    inner = group_size(count)
    outer = count // inner
    shard, width = features.shape
    vectors = probes.shape[1]
    spare = jnp.zeros((16, width), features.dtype)
    longer = jnp.concatenate([features, probes.T, spare], axis=0)
    packed = copy_rows(longer, shard + vectors)

    def along_outer(value, edges):
        return lax.ppermute(value, "blk", [(s * inner + b, t * inner + b) for s, t in edges for b in range(inner)])

    def in_plane(value, hops):
        return lax.ppermute(value, "blk", [(a * inner + s, a * inner + t) for a in range(outer) for s, t in hops])

    def near(step):
        return [(plane_target(b, step, inner), b) for b in range(inner)]

    one_way, exchanges = outer_maps(outer)
    cols = [along_outer(longer, edges) for edges in one_way] + [along_outer(packed, edges) for edges in exchanges]
    kinds = [("rows", "back")] * len(one_way) + [("rows",)] * len(exchanges)
    blocks = plane_blocks(packed, inner, in_plane)
    direct = [step for step in range(inner) if step & (step - 1) == 0]
    passed = [step for step in range(inner) if step & (step - 1)]

    early = [(row, col, kinds[col]) for col in range(len(one_way)) for row in range(len(direct))]
    order = [0, 1] + list(range(len(direct), len(direct) + len(one_way))) + list(range(2, len(direct)))
    sums = tile([blocks[step] for step in direct], cols[: len(one_way)], order, early, {}, shard, vectors, waits=1000)
    sums = {(part, direct[place] if part == "rows" else place): value for (part, place), value in sums.items()}
    late = [(row, col, kinds[col]) for col in range(len(cols)) for row in range(inner) if col >= len(one_way) or row in passed]
    sums = tile(blocks, cols, range(inner + len(cols)), late, sums, shard, vectors)

    total = [along_outer(sums["back", place], [(t, s) for s, t in edges]) for place, edges in enumerate(one_way)]
    total += [in_plane(sums["rows", step], [(t, s) for s, t in near(step)]) for step in range(inner - 1, 0, -1)]
    own = [(row, 0, ("back",)) for row in range(inner)]
    own = tile(blocks, [packed], range(inner + 1), own, {}, shard, vectors, noise=[noise_level[None, :]])
    return functools.reduce(lambda total, term: total + term, total + [sums["rows", 0], own["back", 0]]).T


def solution(mesh):
    placed = (P(("parts", "blk"), None), P(("parts", "blk"), None), P(("parts", "blk")))
    return jax.shard_map(
        on_device, mesh=mesh, in_specs=placed, out_specs=P(("parts", "blk"), None), check_vma=False
    )
```

time: 24.8 us -> 25.8 us (1.040)
  waiting for transfers between devices: 7.46 us -> 4.5 us
  starting transfers between devices: 11.9 us -> 13.6 us
  local copies, waits for them, and re-layouts: 0.01 us -> 1.23 us
  Pallas kernels: 3.54 us -> 4.55 us
    ppermute x3, waiting for transfers between devices: 6.41 us -> 0.72 us  [along_outer(): lax.ppermute(value, 'blk', [(s * inner + b, t * inner + b) for s, t in ed...]
    ppermute x3, starting transfers between devices: 6.78 us -> 10.2 us  [along_outer(): lax.ppermute(value, 'blk', [(s * inner + b, t * inner + b) for s, t in ed...]
    ppermute x6, waiting for transfers between devices: 1.05 us -> 3.77 us  [in_plane(): lax.ppermute(value, 'blk', [(a * inner + s, a * inner + t) for a in range...]
    ppermute x6, starting transfers between devices: 5.16 us -> 3.39 us  [in_plane(): lax.ppermute(value, 'blk', [(a * inner + s, a * inner + t) for a in range...]
    unnamed x2 -> x8, local copies, waits for them, and re-layouts: 0.01 us -> 1.15 us
    pallas_call x3 -> x4, Pallas kernels: 3.54 us -> 4.55 us  [the longest x3 2.99 us: tile(): pl.pallas_call(functools.partial(tile_kernel, list(order), tuple(pairs),...]
  transfers between devices with their start and end apart: 9 -> 9, of which waited for: 4 -> 4; matrix products, arithmetic and copies ran while one was open for 0% -> 0% of each run, Pallas kernels for 14% -> 13%
where the time goes in v9:
time: 25.8 us; the launch traced here: 25.5 us
  starting transfers between devices  13.6 us (53%)
  Pallas kernels  4.55 us (18%)
  waiting for transfers between devices  4.5 us (17%)
  other arithmetic  1.66 us (6%)
  local copies, waits for them, and re-layouts  1.23 us (5%)
    ppermute x3, starting transfers between devices, along_outer(): lax.ppermute(value, 'blk', [(s * inner + b, t * inner + b) for s, t in ed...  10.2 us
    ppermute x6, waiting for transfers between devices, in_plane(): lax.ppermute(value, 'blk', [(a * inner + s, a * inner + t) for a in range...  3.77 us
    ppermute x6, starting transfers between devices, in_plane(): lax.ppermute(value, 'blk', [(a * inner + s, a * inner + t) for a in range...  3.39 us
    pallas_call x3, Pallas kernels, tile(): pl.pallas_call(functools.partial(tile_kernel, list(order), tuple(pairs),...  2.99 us
    pallas_call x1, Pallas kernels, copy_rows(): pl.pallas_call(copy_kernel, out_shape=jax.ShapeDtypeStruct((rows, value.s...  1.57 us
    unnamed x8, local copies, waits for them, and re-layouts  1.15 us
    concatenate x1, other arithmetic, on_device(): longer = jnp.concatenate([features, probes.T, spare], axis=0)  1.03 us
    ppermute x3, waiting for transfers between devices, along_outer(): lax.ppermute(value, 'blk', [(s * inner + b, t * inner + b) for s, t in ed...  0.72 us
  transfers between devices with their start and end apart: 9, of which 4 were waited for; matrix products, arithmetic and copies ran while one was open for 0% of the time, Pallas kernels for 13%

profile of v9, /device:TPU:0, one launch (start us, length us, event | category | flops | bytes accessed | tf_op | source)
XLA Modules:
  0.0 25.5 jit_solution(1366221541616133080)
XLA Ops:
  0.0 0.1 pad.2.clone
  0.1 1.0 %maximum_maximum_fusion.from_ref = bf16[304,256]{1,0:T(8,128)(2,1)S(1)} fusion(bf16[32,256]{1,0:T(8,128)(2,1)} %bitcast.5, bf16[256,256]{1,0:T(8,128)(2,1)} %param.3, bf16[304]{0:T(512)(128)(2,1)S(1)} %pad.2.clone), kind=kLoop, calls=%fused_computation | loop fusion | flops 466944 | bytes 303712 | tf_op jit(solution)/shard_map/concatenate | solution.py:148
  1.1 4.1 %collective-permute-start.3 = (bf16[304,256]{1,0:T(8,128)(2,1)S(1)}, bf16[304,256]{1,0:T(8,128)(2,1)S(1)}, u32[]{:S(2)}, u32[]{:S(2)}) collective-permute-start(bf16[304,256]{1,0:T(8,128)(2,1)S(1)} %maximum_maximum_fusion.from_ref), channel_id=1, source_target_pairs={{0,8},{1,9},{2,10},{3,11},{8,4},{9,5},{10,6},{11,7},{4,12},{5,13},... | collective-permute-start | bytes 466952 | tf_op jit(solution)/shard_map/ppermute | solution.py:152
  5.2 1.6 %shard_map.37.refs_0_.refs_4_ = bf16[288,256]{1,0:T(8,128)(2,1)} custom-call(bf16[304,256]{1,0:T(8,128)(2,1)} %copy-done.3), custom_call_target="tpu_custom_call" | custom-call | tf_op jit(solution)/shard_map/pallas_call | solution.py:133
  6.8 1.5 %collective-permute-start.1 = (bf16[288,256]{1,0:T(8,128)(2,1)}, bf16[288,256]{1,0:T(8,128)(2,1)S(1)}, u32[]{:S(2)}, u32[]{:S(2)}) collective-permute-start(bf16[288,256]{1,0:T(8,128)(2,1)} %shard_map.37.refs_0_.refs_4_), channel_id=1, source_target_pairs={{0,2},{1,3},{2,0},{3,1},{4,6},{5,7},{6,4},{7,5},{8,10},{9,11},{10,... | collective-permute-start | bytes 442376 | tf_op jit(solution)/shard_map/ppermute | solution.py:155
  8.3 0.0 collective-permute-start
  8.3 1.6 %collective-permute-start.4 = (bf16[288,256]{1,0:T(8,128)(2,1)}, bf16[288,256]{1,0:T(8,128)(2,1)S(1)}, u32[]{:S(2)}, u32[]{:S(2)}) collective-permute-start(bf16[288,256]{1,0:T(8,128)(2,1)} %shard_map.37.refs_0_.refs_4_), channel_id=1, source_target_pairs={{0,4},{1,5},{2,6},{3,7},{8,12},{9,13},{10,14},{11,15},{4,0},{5,1},... | collective-permute-start | bytes 442376 | tf_op jit(solution)/shard_map/ppermute | solution.py:152
  9.9 2.4 %collective-permute-done.1.refs_3_.refs_2_ = bf16[288,256]{1,0:T(8,128)(2,1)S(1)} collective-permute-done((bf16[288,256]{1,0:T(8,128)(2,1)}, bf16[288,256]{1,0:T(8,128)(2,1)S(1)}, u32[]{:S(2)}, u32[]{:S(2)}) %collective-permute-start.1) | collective-permute-done | bytes 147488 | tf_op jit(solution)/shard_map/ppermute | solution.py:155
  12.3 0.0 collective-permute-start.2
  12.3 0.0 collective-permute-done.refs_1_
  12.3 0.0 collective-permute-done.3.refs_2_.refs_4_
  12.3 0.9 %copy-done = bf16[288,256]{1,0:T(8,128)(2,1)S(1)} copy-done((bf16[288,256]{1,0:T(8,128)(2,1)S(1)}, bf16[288,256]{1,0:T(8,128)(2,1)}, u32[]{:S(2)}) %copy-start) | copy-done | bytes 147480
  13.2 0.8 %shard_map.38 = (f32[32,256]{1,0:T(8,128)S(1)}, f32[32,256]{1,0:T(8,128)S(1)}, f32[32,256]{1,0:T(8,128)S(1)}, f32[32,256]{1,0:T(8,128)S(1)}) custom-call(bf16[288,256]{1,0:T(8,128)(2,1)S(1)} %copy-done, bf16[288,256]{1,0:T(8,128)(2,1)S(1)} %collective-permute-done.refs_1_, bf16[304,256]{1,0:T(8,128)(2,1)S(1)} %collective-permute-done.3.refs_2_.refs_4_, ...), custom_call_target="tpu_custom_call" | custom-call | flops 125829120000 | bytes 524288 | tf_op jit(solution)/shard_map/pallas_call | solution.py:110
  14.1 0.7 %collective-permute-done.4.refs_5_ = bf16[288,256]{1,0:T(8,128)(2,1)S(1)} collective-permute-done((bf16[288,256]{1,0:T(8,128)(2,1)}, bf16[288,256]{1,0:T(8,128)(2,1)S(1)}, u32[]{:S(2)}, u32[]{:S(2)}) %collective-permute-start.4) | collective-permute-done | bytes 147488 | tf_op jit(solution)/shard_map/ppermute | solution.py:152
  14.8 1.3 %shard_map.39 = (f32[32,256]{1,0:T(8,128)S(1)}, f32[32,256]{1,0:T(8,128)S(1)}, f32[32,256]{1,0:T(8,128)S(1)}, f32[32,256]{1,0:T(8,128)S(1)}, f32[32,256]{1,0:T(8,128)S(1)}) custom-call(bf16[288,256]{1,0:T(8,128)(2,1)S(1)} %copy-done.1, bf16[288,256]{1,0:T(8,128)(2,1)S(1)} %collective-permute-done.refs_1_, ...), custom_call_target="tpu_custom_call" | custom-call | flops 209715200 | bytes 786432 | tf_op jit(solution)/shard_map/pallas_call | solution.py:110
  16.1 4.5 %collective-permute-start.5 = (f32[32,256]{1,0:T(8,128)S(1)}, f32[32,256]{1,0:T(8,128)S(1)}, u32[]{:S(2)}, u32[]{:S(2)}) collective-permute-start(f32[32,256]{1,0:T(8,128)S(1)} %get-tuple-element.18), channel_id=1, source_target_pairs={{8,0},{9,1},{10,2},{11,3},{4,8},{5,9},{6,10},{7,11},{12,4},{13,5},... | collective-permute-start | bytes 98312 | tf_op jit(solution)/shard_map/ppermute | solution.py:152
  20.6 1.4 %collective-permute-start.7 = (f32[32,256]{1,0:T(8,128)S(1)}, f32[32,256]{1,0:T(8,128)S(1)}, u32[]{:S(2)}, u32[]{:S(2)}) collective-permute-start(f32[32,256]{1,0:T(8,128)S(1)} %get-tuple-element.20), channel_id=1, source_target_pairs={{0,2},{1,3},{2,0},{3,1},{4,6},{5,7},{6,4},{7,5},{8,10},{9,11},{10,... | collective-permute-start | bytes 98312 | tf_op jit(solution)/shard_map/ppermute | solution.py:155
  22.0 0.4 %collective-permute-start.8 = (f32[32,256]{1,0:T(8,128)S(1)}, f32[32,256]{1,0:T(8,128)S(1)}, u32[]{:S(2)}, u32[]{:S(2)}) collective-permute-start(f32[32,256]{1,0:T(8,128)S(1)} %get-tuple-element.21), channel_id=1, source_target_pairs={{0,1},{1,0},{2,3},{3,2},{4,5},{5,4},{6,7},{7,6},{8,9},{9,8},{10,11... | collective-permute-start | bytes 98312 | tf_op jit(solution)/shard_map/ppermute | solution.py:155
  22.4 0.2 copy-done.2
  22.7 0.9 %shard_map.40 = f32[32,256]{1,0:T(8,128)S(1)} custom-call(bf16[288,256]{1,0:T(8,128)(2,1)S(1)} %copy-done.1, bf16[288,256]{1,0:T(8,128)(2,1)S(1)} %collective-permute-done.refs_1_, bf16[288,256]{1,0:T(8,128)(2,1)S(1)} %collective-permute-done.1.refs_3_.refs_2_, bf16[288,256]{1,0:T(8,128)(2,1)S(1)} %collective-permute-done.2.refs_3_, ...), custom_call_target="tpu_custom_call" | custom-call | flops 167772160 | bytes 655360 | tf_op jit(solution)/shard_map/pallas_call | solution.py:110
  23.6 0.0 collective-permute-done.5
  23.6 0.7 %collective-permute-done.6 = f32[32,256]{1,0:T(8,128)S(1)} collective-permute-done((f32[32,256]{1,0:T(8,128)S(1)}, f32[32,256]{1,0:T(8,128)S(1)}, u32[]{:S(2)}, u32[]{:S(2)}) %collective-permute-start.6) | collective-permute-done | bytes 32800 | tf_op jit(solution)/shard_map/ppermute | solution.py:155
  24.3 0.6 %collective-permute-done.7 = f32[32,256]{1,0:T(8,128)S(1)} collective-permute-done((f32[32,256]{1,0:T(8,128)S(1)}, f32[32,256]{1,0:T(8,128)S(1)}, u32[]{:S(2)}, u32[]{:S(2)}) %collective-permute-start.7) | collective-permute-done | bytes 32800 | tf_op jit(solution)/shard_map/ppermute | solution.py:155
  24.9 0.6 %add_bitcast_fusion = f32[256,32]{0,1:T(8,128)} fusion(f32[32,256]{1,0:T(8,128)S(1)} %shard_map.40, f32[32,256]{1,0:T(8,128)S(1)} %get-tuple-element.22, f32[32,256]{1,0:T(8,128)S(1)} %collective-permute-done.8, f32[32,256]{1,0:T(8,128)S(1)} %collective-permute-done.7, f32[32,256]{1,0:T(8,128)S(1)} %collective-permute-done.5, ...), kind=kLoop, calls=%fused_computation.1 | loop fusion | flops 40960 | bytes 229376 | tf_op jit(solution)/shard_map/transpose | solution.py:178
  (10 shorter events, 0.0 us)
Async XLA Ops:
  1.1 4.1 %copy-start.3 = (bf16[304,256]{1,0:T(8,128)(2,1)}, bf16[304,256]{1,0:T(8,128)(2,1)S(1)}, u32[]{:S(2)}) copy-start(bf16[304,256]{1,0:T(8,128)(2,1)S(1)} %maximum_maximum_fusion.from_ref) | copy-start | bytes 466948
  1.1 11.2 %collective-permute-start.3 = (bf16[304,256]{1,0:T(8,128)(2,1)S(1)}, bf16[304,256]{1,0:T(8,128)(2,1)S(1)}, u32[]{:S(2)}, u32[]{:S(2)}) collective-permute-start(bf16[304,256]{1,0:T(8,128)(2,1)S(1)} %maximum_maximum_fusion.from_ref), channel_id=1, source_target_pairs={{0,8},{1,9},{2,10},{3,11},{8,4},{9,5},{10,6},{11,7},{4,12},{5,13},... | collective-permute-start | bytes 466952 | tf_op jit(solution)/shard_map/ppermute | solution.py:152
  6.8 5.5 %collective-permute-start.1 = (bf16[288,256]{1,0:T(8,128)(2,1)}, bf16[288,256]{1,0:T(8,128)(2,1)S(1)}, u32[]{:S(2)}, u32[]{:S(2)}) collective-permute-start(bf16[288,256]{1,0:T(8,128)(2,1)} %shard_map.37.refs_0_.refs_4_), channel_id=1, source_target_pairs={{0,2},{1,3},{2,0},{3,1},{4,6},{5,7},{6,4},{7,5},{8,10},{9,11},{10,... | collective-permute-start | bytes 442376 | tf_op jit(solution)/shard_map/ppermute | solution.py:155
  8.3 4.0 %collective-permute-start = (bf16[288,256]{1,0:T(8,128)(2,1)}, bf16[288,256]{1,0:T(8,128)(2,1)S(1)}, u32[]{:S(2)}, u32[]{:S(2)}) collective-permute-start(bf16[288,256]{1,0:T(8,128)(2,1)} %shard_map.37.refs_0_.refs_4_), channel_id=1, source_target_pairs={{0,1},{1,0},{2,3},{3,2},{4,5},{5,4},{6,7},{7,6},{8,9},{9,8},{10,11... | collective-permute-start | bytes 442376 | tf_op jit(solution)/shard_map/ppermute | solution.py:155
  8.3 6.5 %collective-permute-start.4 = (bf16[288,256]{1,0:T(8,128)(2,1)}, bf16[288,256]{1,0:T(8,128)(2,1)S(1)}, u32[]{:S(2)}, u32[]{:S(2)}) collective-permute-start(bf16[288,256]{1,0:T(8,128)(2,1)} %shard_map.37.refs_0_.refs_4_), channel_id=1, source_target_pairs={{0,4},{1,5},{2,6},{3,7},{8,12},{9,13},{10,14},{11,15},{4,0},{5,1},... | collective-permute-start | bytes 442376 | tf_op jit(solution)/shard_map/ppermute | solution.py:152
  12.3 2.5 %collective-permute-start.2 = (bf16[288,256]{1,0:T(8,128)(2,1)S(1)}, bf16[288,256]{1,0:T(8,128)(2,1)S(1)}, u32[]{:S(2)}, u32[]{:S(2)}) collective-permute-start(bf16[288,256]{1,0:T(8,128)(2,1)S(1)} %collective-permute-done.1.refs_3_.refs_2_), channel_id=1, source_target_pairs={{0,1},{1,0},{2,3},{3,2},{4,5},{5,4},{6,7},{7,6},{8,9},{9,8},{10,11... | collective-permute-start | bytes 442376 | tf_op jit(solution)/shard_map/ppermute | solution.py:155
  12.3 0.9 %copy-start = (bf16[288,256]{1,0:T(8,128)(2,1)S(1)}, bf16[288,256]{1,0:T(8,128)(2,1)}, u32[]{:S(2)}) copy-start(bf16[288,256]{1,0:T(8,128)(2,1)} %shard_map.37.refs_0_.refs_4_) | copy-start | bytes 442372
  13.2 1.6 %copy-start.1 = (bf16[288,256]{1,0:T(8,128)(2,1)S(1)}, bf16[288,256]{1,0:T(8,128)(2,1)}, u32[]{:S(2)}) copy-start(bf16[288,256]{1,0:T(8,128)(2,1)} %shard_map.37.refs_0_.refs_4_) | copy-start | bytes 442372
  16.1 7.5 %collective-permute-start.5 = (f32[32,256]{1,0:T(8,128)S(1)}, f32[32,256]{1,0:T(8,128)S(1)}, u32[]{:S(2)}, u32[]{:S(2)}) collective-permute-start(f32[32,256]{1,0:T(8,128)S(1)} %get-tuple-element.18), channel_id=1, source_target_pairs={{8,0},{9,1},{10,2},{11,3},{4,8},{5,9},{6,10},{7,11},{12,4},{13,5},... | collective-permute-start | bytes 98312 | tf_op jit(solution)/shard_map/ppermute | solution.py:152
  20.6 3.7 %collective-permute-start.6 = (f32[32,256]{1,0:T(8,128)S(1)}, f32[32,256]{1,0:T(8,128)S(1)}, u32[]{:S(2)}, u32[]{:S(2)}) collective-permute-start(f32[32,256]{1,0:T(8,128)S(1)} %get-tuple-element.19), channel_id=1, source_target_pairs={{0,3},{1,2},{2,1},{3,0},{4,7},{5,6},{6,5},{7,4},{8,11},{9,10},{10,... | collective-permute-start | bytes 98312 | tf_op jit(solution)/shard_map/ppermute | solution.py:155
  20.6 4.3 %collective-permute-start.7 = (f32[32,256]{1,0:T(8,128)S(1)}, f32[32,256]{1,0:T(8,128)S(1)}, u32[]{:S(2)}, u32[]{:S(2)}) collective-permute-start(f32[32,256]{1,0:T(8,128)S(1)} %get-tuple-element.20), channel_id=1, source_target_pairs={{0,2},{1,3},{2,0},{3,1},{4,6},{5,7},{6,4},{7,5},{8,10},{9,11},{10,... | collective-permute-start | bytes 98312 | tf_op jit(solution)/shard_map/ppermute | solution.py:155
  22.0 0.7 %copy-start.2 = (f32[256]{0:T(256)S(1)}, f32[256]{0:T(256)}, u32[]{:S(2)}) copy-start(f32[256]{0:T(256)} %param.5) | copy-start | bytes 3076
  22.0 2.9 %collective-permute-start.8 = (f32[32,256]{1,0:T(8,128)S(1)}, f32[32,256]{1,0:T(8,128)S(1)}, u32[]{:S(2)}, u32[]{:S(2)}) collective-permute-start(f32[32,256]{1,0:T(8,128)S(1)} %get-tuple-element.21), channel_id=1, source_target_pairs={{0,1},{1,0},{2,3},{3,2},{4,5},{5,4},{6,7},{7,6},{8,9},{9,8},{10,11... | collective-permute-start | bytes 98312 | tf_op jit(solution)/shard_map/ppermute | solution.py:155

commit v10 on v9

--- a/solution.py
+++ b/solution.py
@@ -135,6 +135,7 @@
         out_shape=jax.ShapeDtypeStruct((rows, value.shape[1]), value.dtype),
         in_specs=[whole],
         out_specs=whole,
+        compiler_params=pltpu.CompilerParams(vmem_limit_bytes=32 * 1024 * 1024),
     )(value)
 
 

time: 25.8 us -> 24.2 us (0.938)
  Pallas kernels: 4.55 us -> 2.98 us
  waiting for transfers between devices: 4.5 us -> 6 us
  local copies, waits for them, and re-layouts: 1.23 us -> 0.08 us
  starting transfers between devices: 13.6 us -> 13.2 us
    pallas_call x1, Pallas kernels: 1.57 us -> 0.01 us  [copy_rows(): pl.pallas_call(copy_kernel, out_shape=jax.ShapeDtypeStruct((rows, value.s...]
    ppermute x3, waiting for transfers between devices: 0.72 us -> 2.08 us  [along_outer(): lax.ppermute(value, 'blk', [(s * inner + b, t * inner + b) for s, t in ed...]
    unnamed x8 -> x2, local copies, waits for them, and re-layouts: 1.15 us -> 0.01 us
    ppermute x3, starting transfers between devices: 10.2 us -> 9.72 us  [along_outer(): lax.ppermute(value, 'blk', [(s * inner + b, t * inner + b) for s, t in ed...]
  transfers between devices with their start and end apart: 9 -> 9, of which waited for: 4 -> 5; matrix products, arithmetic and copies ran while one was open for 0% -> 0% of each run, Pallas kernels for 13% -> 7%
where the time goes in v10:
time: 24.2 us; the launch traced here: 23.9 us
  starting transfers between devices  13.2 us (55%)
  waiting for transfers between devices  6 us (25%)
  Pallas kernels  2.98 us (12%)
  other arithmetic  1.66 us (7%)
    ppermute x3, starting transfers between devices, along_outer(): lax.ppermute(value, 'blk', [(s * inner + b, t * inner + b) for s, t in ed...  9.72 us
    ppermute x6, waiting for transfers between devices, in_plane(): lax.ppermute(value, 'blk', [(a * inner + s, a * inner + t) for a in range...  3.92 us
    ppermute x6, starting transfers between devices, in_plane(): lax.ppermute(value, 'blk', [(a * inner + s, a * inner + t) for a in range...  3.45 us
    pallas_call x3, Pallas kernels, tile(): pl.pallas_call(functools.partial(tile_kernel, list(order), tuple(pairs),...  2.97 us
    ppermute x3, waiting for transfers between devices, along_outer(): lax.ppermute(value, 'blk', [(s * inner + b, t * inner + b) for s, t in ed...  2.08 us
    concatenate x1, other arithmetic, on_device(): longer = jnp.concatenate([features, probes.T, spare], axis=0)  1.03 us
    transpose x1, other arithmetic, on_device(): functools.reduce(lambda total, term: total + term, total + [sums['rows',...  0.63 us
  transfers between devices with their start and end apart: 9, of which 5 were waited for; matrix products, arithmetic and copies ran while one was open for 0% of the time, Pallas kernels for 7%

profile of v10, /device:TPU:0, one launch (start us, length us, event | category | flops | bytes accessed | tf_op | source)
XLA Modules:
  0.0 23.9 jit_solution(8496636108475130643)
XLA Ops:
  0.0 0.1 pad.2.clone
  0.1 1.0 %maximum_maximum_fusion.from_ref = bf16[304,256]{1,0:T(8,128)(2,1)S(1)} fusion(bf16[32,256]{1,0:T(8,128)(2,1)} %bitcast.5, bf16[256,256]{1,0:T(8,128)(2,1)} %param.3, bf16[304]{0:T(512)(128)(2,1)S(1)} %pad.2.clone), kind=kLoop, calls=%fused_computation | loop fusion | flops 466944 | bytes 303712 | tf_op jit(solution)/shard_map/concatenate | solution.py:149
  1.1 4.1 %collective-permute-start.3 = (bf16[304,256]{1,0:T(8,128)(2,1)S(1)}, bf16[304,256]{1,0:T(8,128)(2,1)S(1)}, u32[]{:S(2)}, u32[]{:S(2)}) collective-permute-start(bf16[304,256]{1,0:T(8,128)(2,1)S(1)} %maximum_maximum_fusion.from_ref), channel_id=1, source_target_pairs={{0,8},{1,9},{2,10},{3,11},{8,4},{9,5},{10,6},{11,7},{4,12},{5,13},... | collective-permute-start | bytes 466952 | tf_op jit(solution)/shard_map/ppermute | solution.py:153
  5.2 1.6 %collective-permute-start.1 = (bf16[288,256]{1,0:T(8,128)(2,1)S(1)}, bf16[288,256]{1,0:T(8,128)(2,1)S(1)}, u32[]{:S(2)}, u32[]{:S(2)}) collective-permute-start(bf16[288,256]{1,0:T(8,128)(2,1)S(1)} %shard_map.37.refs_0_.refs_4_), channel_id=1, source_target_pairs={{0,2},{1,3},{2,0},{3,1},{4,6},{5,7},{6,4},{7,5},{8,10},{9,11},{10,... | collective-permute-start | bytes 442376 | tf_op jit(solution)/shard_map/ppermute | solution.py:156
  6.8 0.0 collective-permute-start
  6.8 1.6 %collective-permute-start.4 = (bf16[288,256]{1,0:T(8,128)(2,1)S(1)}, bf16[288,256]{1,0:T(8,128)(2,1)S(1)}, u32[]{:S(2)}, u32[]{:S(2)}) collective-permute-start(bf16[288,256]{1,0:T(8,128)(2,1)S(1)} %shard_map.37.refs_0_.refs_4_), channel_id=1, source_target_pairs={{0,4},{1,5},{2,6},{3,7},{8,12},{9,13},{10,14},{11,15},{4,0},{5,1},... | collective-permute-start | bytes 442376 | tf_op jit(solution)/shard_map/ppermute | solution.py:153
  8.4 2.2 %collective-permute-done.1.refs_3_.refs_2_ = bf16[288,256]{1,0:T(8,128)(2,1)S(1)} collective-permute-done((bf16[288,256]{1,0:T(8,128)(2,1)S(1)}, bf16[288,256]{1,0:T(8,128)(2,1)S(1)}, u32[]{:S(2)}, u32[]{:S(2)}) %collective-permute-start.1) | collective-permute-done | bytes 147488 | tf_op jit(solution)/shard_map/ppermute | solution.py:156
  10.6 0.0 collective-permute-start.2
  10.6 0.0 collective-permute-done.refs_1_
  10.6 0.1 collective-permute-done.3.refs_2_.refs_4_
  10.7 0.8 %shard_map.38 = (f32[32,256]{1,0:T(8,128)S(1)}, f32[32,256]{1,0:T(8,128)S(1)}, f32[32,256]{1,0:T(8,128)S(1)}, f32[32,256]{1,0:T(8,128)S(1)}) custom-call(bf16[288,256]{1,0:T(8,128)(2,1)S(1)} %shard_map.37.refs_0_.refs_4_, bf16[288,256]{1,0:T(8,128)(2,1)S(1)} %collective-permute-done.refs_1_, bf16[304,256]{1,0:T(8,128)(2,1)S(1)} %collective-permute-done.3.refs_2_.refs_4_, ...), custom_call_target="tpu_custom_call" | custom-call | flops 125829120000 | bytes 524288 | tf_op jit(solution)/shard_map/pallas_call | solution.py:110
  11.5 2.0 %collective-permute-done.4.refs_5_ = bf16[288,256]{1,0:T(8,128)(2,1)S(1)} collective-permute-done((bf16[288,256]{1,0:T(8,128)(2,1)S(1)}, bf16[288,256]{1,0:T(8,128)(2,1)S(1)}, u32[]{:S(2)}, u32[]{:S(2)}) %collective-permute-start.4) | collective-permute-done | bytes 147488 | tf_op jit(solution)/shard_map/ppermute | solution.py:153
  13.5 0.0 collective-permute-done.2.refs_3_
  13.5 1.3 %shard_map.39 = (f32[32,256]{1,0:T(8,128)S(1)}, f32[32,256]{1,0:T(8,128)S(1)}, f32[32,256]{1,0:T(8,128)S(1)}, f32[32,256]{1,0:T(8,128)S(1)}, f32[32,256]{1,0:T(8,128)S(1)}) custom-call(bf16[288,256]{1,0:T(8,128)(2,1)S(1)} %shard_map.37.refs_0_.refs_4_, bf16[288,256]{1,0:T(8,128)(2,1)S(1)} %collective-permute-done.refs_1_, ...), custom_call_target="tpu_custom_call" | custom-call | flops 209715200 | bytes 786432 | tf_op jit(solution)/shard_map/pallas_call | solution.py:110
  14.8 4.1 %collective-permute-start.5 = (f32[32,256]{1,0:T(8,128)S(1)}, f32[32,256]{1,0:T(8,128)S(1)}, u32[]{:S(2)}, u32[]{:S(2)}) collective-permute-start(f32[32,256]{1,0:T(8,128)S(1)} %get-tuple-element.18), channel_id=1, source_target_pairs={{8,0},{9,1},{10,2},{11,3},{4,8},{5,9},{6,10},{7,11},{12,4},{13,5},... | collective-permute-start | bytes 98312 | tf_op jit(solution)/shard_map/ppermute | solution.py:153
  18.8 0.3 %collective-permute-start.6 = (f32[32,256]{1,0:T(8,128)S(1)}, f32[32,256]{1,0:T(8,128)S(1)}, u32[]{:S(2)}, u32[]{:S(2)}) collective-permute-start(f32[32,256]{1,0:T(8,128)S(1)} %get-tuple-element.19), channel_id=1, source_target_pairs={{0,3},{1,2},{2,1},{3,0},{4,7},{5,6},{6,5},{7,4},{8,11},{9,10},{10,... | collective-permute-start | bytes 98312 | tf_op jit(solution)/shard_map/ppermute | solution.py:156
  19.2 0.8 %collective-permute-start.7 = (f32[32,256]{1,0:T(8,128)S(1)}, f32[32,256]{1,0:T(8,128)S(1)}, u32[]{:S(2)}, u32[]{:S(2)}) collective-permute-start(f32[32,256]{1,0:T(8,128)S(1)} %get-tuple-element.20), channel_id=1, source_target_pairs={{0,2},{1,3},{2,0},{3,1},{4,6},{5,7},{6,4},{7,5},{8,10},{9,11},{10,... | collective-permute-start | bytes 98312 | tf_op jit(solution)/shard_map/ppermute | solution.py:156
  19.9 0.8 %collective-permute-start.8 = (f32[32,256]{1,0:T(8,128)S(1)}, f32[32,256]{1,0:T(8,128)S(1)}, u32[]{:S(2)}, u32[]{:S(2)}) collective-permute-start(f32[32,256]{1,0:T(8,128)S(1)} %get-tuple-element.21), channel_id=1, source_target_pairs={{0,1},{1,0},{2,3},{3,2},{4,5},{5,4},{6,7},{7,6},{8,9},{9,8},{10,11... | collective-permute-start | bytes 98312 | tf_op jit(solution)/shard_map/ppermute | solution.py:156
  20.7 0.9 %shard_map.40 = f32[32,256]{1,0:T(8,128)S(1)} custom-call(bf16[288,256]{1,0:T(8,128)(2,1)S(1)} %shard_map.37.refs_0_.refs_4_, bf16[288,256]{1,0:T(8,128)(2,1)S(1)} %collective-permute-done.refs_1_, bf16[288,256]{1,0:T(8,128)(2,1)S(1)} %collective-permute-done.1.refs_3_.refs_2_, bf16[288,256]{1,0:T(8,128)(2,1)S(1)} %collective-permute-done.2.refs_3_, ...), custom_call_target="tpu_custom_call" | custom-call | flops 167772160 | bytes 655360 | tf_op jit(solution)/shard_map/pallas_call | solution.py:110
  21.6 0.0 collective-permute-done.5
  21.6 0.6 %collective-permute-done.6 = f32[32,256]{1,0:T(8,128)S(1)} collective-permute-done((f32[32,256]{1,0:T(8,128)S(1)}, f32[32,256]{1,0:T(8,128)S(1)}, u32[]{:S(2)}, u32[]{:S(2)}) %collective-permute-start.6) | collective-permute-done | bytes 32800 | tf_op jit(solution)/shard_map/ppermute | solution.py:156
  22.2 1.1 %collective-permute-done.7 = f32[32,256]{1,0:T(8,128)S(1)} collective-permute-done((f32[32,256]{1,0:T(8,128)S(1)}, f32[32,256]{1,0:T(8,128)S(1)}, u32[]{:S(2)}, u32[]{:S(2)}) %collective-permute-start.7) | collective-permute-done | bytes 32800 | tf_op jit(solution)/shard_map/ppermute | solution.py:156
  23.3 0.0 collective-permute-done.8
  23.3 0.6 %add_bitcast_fusion = f32[256,32]{0,1:T(8,128)} fusion(f32[32,256]{1,0:T(8,128)S(1)} %shard_map.40, f32[32,256]{1,0:T(8,128)S(1)} %get-tuple-element.22, f32[32,256]{1,0:T(8,128)S(1)} %collective-permute-done.8, f32[32,256]{1,0:T(8,128)S(1)} %collective-permute-done.7, f32[32,256]{1,0:T(8,128)S(1)} %collective-permute-done.5, ...), kind=kLoop, calls=%fused_computation.1 | loop fusion | flops 40960 | bytes 229376 | tf_op jit(solution)/shard_map/transpose | solution.py:179
  (4 shorter events, 0.0 us)
Async XLA Ops:
  1.1 9.6 %collective-permute-start.3 = (bf16[304,256]{1,0:T(8,128)(2,1)S(1)}, bf16[304,256]{1,0:T(8,128)(2,1)S(1)}, u32[]{:S(2)}, u32[]{:S(2)}) collective-permute-start(bf16[304,256]{1,0:T(8,128)(2,1)S(1)} %maximum_maximum_fusion.from_ref), channel_id=1, source_target_pairs={{0,8},{1,9},{2,10},{3,11},{8,4},{9,5},{10,6},{11,7},{4,12},{5,13},... | collective-permute-start | bytes 466952 | tf_op jit(solution)/shard_map/ppermute | solution.py:153
  5.2 5.4 %collective-permute-start.1 = (bf16[288,256]{1,0:T(8,128)(2,1)S(1)}, bf16[288,256]{1,0:T(8,128)(2,1)S(1)}, u32[]{:S(2)}, u32[]{:S(2)}) collective-permute-start(bf16[288,256]{1,0:T(8,128)(2,1)S(1)} %shard_map.37.refs_0_.refs_4_), channel_id=1, source_target_pairs={{0,2},{1,3},{2,0},{3,1},{4,6},{5,7},{6,4},{7,5},{8,10},{9,11},{10,... | collective-permute-start | bytes 442376 | tf_op jit(solution)/shard_map/ppermute | solution.py:156
  6.8 3.8 %collective-permute-start = (bf16[288,256]{1,0:T(8,128)(2,1)S(1)}, bf16[288,256]{1,0:T(8,128)(2,1)S(1)}, u32[]{:S(2)}, u32[]{:S(2)}) collective-permute-start(bf16[288,256]{1,0:T(8,128)(2,1)S(1)} %shard_map.37.refs_0_.refs_4_), channel_id=1, source_target_pairs={{0,1},{1,0},{2,3},{3,2},{4,5},{5,4},{6,7},{7,6},{8,9},{9,8},{10,11... | collective-permute-start | bytes 442376 | tf_op jit(solution)/shard_map/ppermute | solution.py:156
  6.8 6.7 %collective-permute-start.4 = (bf16[288,256]{1,0:T(8,128)(2,1)S(1)}, bf16[288,256]{1,0:T(8,128)(2,1)S(1)}, u32[]{:S(2)}, u32[]{:S(2)}) collective-permute-start(bf16[288,256]{1,0:T(8,128)(2,1)S(1)} %shard_map.37.refs_0_.refs_4_), channel_id=1, source_target_pairs={{0,4},{1,5},{2,6},{3,7},{8,12},{9,13},{10,14},{11,15},{4,0},{5,1},... | collective-permute-start | bytes 442376 | tf_op jit(solution)/shard_map/ppermute | solution.py:153
  10.6 2.9 %collective-permute-start.2 = (bf16[288,256]{1,0:T(8,128)(2,1)S(1)}, bf16[288,256]{1,0:T(8,128)(2,1)S(1)}, u32[]{:S(2)}, u32[]{:S(2)}) collective-permute-start(bf16[288,256]{1,0:T(8,128)(2,1)S(1)} %collective-permute-done.1.refs_3_.refs_2_), channel_id=1, source_target_pairs={{0,1},{1,0},{2,3},{3,2},{4,5},{5,4},{6,7},{7,6},{8,9},{9,8},{10,11... | collective-permute-start | bytes 442376 | tf_op jit(solution)/shard_map/ppermute | solution.py:156
  14.8 6.8 %collective-permute-start.5 = (f32[32,256]{1,0:T(8,128)S(1)}, f32[32,256]{1,0:T(8,128)S(1)}, u32[]{:S(2)}, u32[]{:S(2)}) collective-permute-start(f32[32,256]{1,0:T(8,128)S(1)} %get-tuple-element.18), channel_id=1, source_target_pairs={{8,0},{9,1},{10,2},{11,3},{4,8},{5,9},{6,10},{7,11},{12,4},{13,5},... | collective-permute-start | bytes 98312 | tf_op jit(solution)/shard_map/ppermute | solution.py:153
  18.8 3.3 %collective-permute-start.6 = (f32[32,256]{1,0:T(8,128)S(1)}, f32[32,256]{1,0:T(8,128)S(1)}, u32[]{:S(2)}, u32[]{:S(2)}) collective-permute-start(f32[32,256]{1,0:T(8,128)S(1)} %get-tuple-element.19), channel_id=1, source_target_pairs={{0,3},{1,2},{2,1},{3,0},{4,7},{5,6},{6,5},{7,4},{8,11},{9,10},{10,... | collective-permute-start | bytes 98312 | tf_op jit(solution)/shard_map/ppermute | solution.py:156
  19.2 4.1 %collective-permute-start.7 = (f32[32,256]{1,0:T(8,128)S(1)}, f32[32,256]{1,0:T(8,128)S(1)}, u32[]{:S(2)}, u32[]{:S(2)}) collective-permute-start(f32[32,256]{1,0:T(8,128)S(1)} %get-tuple-element.20), channel_id=1, source_target_pairs={{0,2},{1,3},{2,0},{3,1},{4,6},{5,7},{6,4},{7,5},{8,10},{9,11},{10,... | collective-permute-start | bytes 98312 | tf_op jit(solution)/shard_map/ppermute | solution.py:156
  19.9 0.8 %copy-start = (f32[256]{0:T(256)S(1)}, f32[256]{0:T(256)}, u32[]{:S(2)}) copy-start(f32[256]{0:T(256)} %param.5) | copy-start | bytes 3076
  19.9 3.4 %collective-permute-start.8 = (f32[32,256]{1,0:T(8,128)S(1)}, f32[32,256]{1,0:T(8,128)S(1)}, u32[]{:S(2)}, u32[]{:S(2)}) collective-permute-start(f32[32,256]{1,0:T(8,128)S(1)} %get-tuple-element.21), channel_id=1, source_target_pairs={{0,1},{1,0},{2,3},{3,2},{4,5},{5,4},{6,7},{7,6},{8,9},{9,8},{10,11... | collective-permute-start | bytes 98312 | tf_op jit(solution)/shard_map/ppermute | solution.py:156

commit v11 on v9

--- a/solution.py
+++ b/solution.py
@@ -100,7 +100,7 @@
         ref[...] = sums[name]
 
 
-def tile(rows, cols, order, pairs, sums, shard, vectors, noise=(), waits=1):
+def tile(rows, cols, order, pairs, sums, shard, vectors, noise=()):
     blocks = [*rows, *cols]
     args = [*[blocks[place] for place in order], *noise, *sums.values()]
     elements = len(pairs) * shard * shard
@@ -116,7 +116,7 @@
         out_specs=[whole] * len(names),
         compiler_params=pltpu.CompilerParams(vmem_limit_bytes=32 * 1024 * 1024),
         cost_estimate=pl.CostEstimate(
-            flops=2 * elements * (width + 2 * vectors) * waits,
+            flops=2 * elements * (width + 2 * vectors),
             bytes_accessed=2 * width * shard * len(blocks),
             transcendentals=2 * elements,
         ),
@@ -124,29 +124,13 @@
     return dict(zip(names, found))
 
 
-def copy_kernel(from_ref, to_ref):
-    to_ref[...] = from_ref[0 : to_ref.shape[0], :]
-
-
-def copy_rows(value, rows):
-    whole = pl.BlockSpec(memory_space=pltpu.VMEM)
-    return pl.pallas_call(
-        copy_kernel,
-        out_shape=jax.ShapeDtypeStruct((rows, value.shape[1]), value.dtype),
-        in_specs=[whole],
-        out_specs=whole,
-    )(value)
-
-
 def on_device(features, probes, noise_level):
     count = lax.axis_size("blk")
     inner = group_size(count)
     outer = count // inner
-    shard, width = features.shape
+    shard = features.shape[0]
     vectors = probes.shape[1]
-    spare = jnp.zeros((16, width), features.dtype)
-    longer = jnp.concatenate([features, probes.T, spare], axis=0)
-    packed = copy_rows(longer, shard + vectors)
+    packed = jnp.concatenate([features, probes.T], axis=0)
 
     def along_outer(value, edges):
         return lax.ppermute(value, "blk", [(s * inner + b, t * inner + b) for s, t in edges for b in range(inner)])
@@ -158,24 +142,26 @@
         return [(plane_target(b, step, inner), b) for b in range(inner)]
 
     one_way, exchanges = outer_maps(outer)
-    cols = [along_outer(longer, edges) for edges in one_way] + [along_outer(packed, edges) for edges in exchanges]
-    kinds = [("rows", "back")] * len(one_way) + [("rows",)] * len(exchanges)
+    cols = [along_outer(packed, edges) for edges in one_way]
+    others = [along_outer(packed, edges) for edges in exchanges]
     blocks = plane_blocks(packed, inner, in_plane)
-    direct = [step for step in range(inner) if step & (step - 1) == 0]
-    passed = [step for step in range(inner) if step & (step - 1)]
+    direct = [step for step in range(1, inner) if step & (step - 1) == 0]
+    passed = [step for step in range(1, inner) if step & (step - 1)]
 
-    early = [(row, col, kinds[col]) for col in range(len(one_way)) for row in range(len(direct))]
-    order = [0, 1] + list(range(len(direct), len(direct) + len(one_way))) + list(range(2, len(direct)))
-    sums = tile([blocks[step] for step in direct], cols[: len(one_way)], order, early, {}, shard, vectors, waits=1000)
-    sums = {(part, direct[place] if part == "rows" else place): value for (part, place), value in sums.items()}
-    late = [(row, col, kinds[col]) for col in range(len(cols)) for row in range(inner) if col >= len(one_way) or row in passed]
-    sums = tile(blocks, cols, range(inner + len(cols)), late, sums, shard, vectors)
+    order = [0] + passed + [inner + place for place in range(len(cols))] + direct
+    pairs = [(row, col, ("rows", "back")) for col in range(len(cols)) for row in range(inner)]
+    sums = tile(blocks, cols, order, pairs, {}, shard, vectors)
+    backs = [sums.pop(("back", place)) for place in range(len(cols))]
+    pairs = [(row, col, ("rows",)) for col in range(len(others)) for row in range(inner)]
+    sums = tile(blocks, others, range(inner + len(others)), pairs, sums, shard, vectors)
+    pairs = [(row, 0, ("back",)) for row in range(inner)]
+    own = tile(blocks, [packed], range(inner + 1), pairs, {}, shard, vectors, noise=[noise_level[None, :]])
 
-    total = [along_outer(sums["back", place], [(t, s) for s, t in edges]) for place, edges in enumerate(one_way)]
-    total += [in_plane(sums["rows", step], [(t, s) for s, t in near(step)]) for step in range(inner - 1, 0, -1)]
-    own = [(row, 0, ("back",)) for row in range(inner)]
-    own = tile(blocks, [packed], range(inner + 1), own, {}, shard, vectors, noise=[noise_level[None, :]])
-    return functools.reduce(lambda total, term: total + term, total + [sums["rows", 0], own["back", 0]]).T
+    total = [own["back", 0]]
+    total += [in_plane(sums["rows", step], [(t, s) for s, t in near(step)]) for step in range(1, inner)]
+    total += [sums["rows", 0]]
+    total += [along_outer(back, [(t, s) for s, t in edges]) for back, edges in zip(backs, one_way)]
+    return functools.reduce(lambda sofar, term: sofar + term, total).T
 
 
 def solution(mesh):

time: 25.8 us -> 24.1 us (0.934)
  Pallas kernels: 4.55 us -> 2.89 us
  starting transfers between devices: 13.6 us -> 15 us
  local copies, waits for them, and re-layouts: 1.23 us -> 0.12 us
    pallas_call x1 -> x0, Pallas kernels: 1.57 us -> none  [copy_rows(): pl.pallas_call(copy_kernel, out_shape=jax.ShapeDtypeStruct((rows, value.s...]
    ppermute x6, starting transfers between devices: 3.39 us -> 4.91 us  [in_plane(): lax.ppermute(value, 'blk', [(a * inner + s, a * inner + t) for a in range...]
    ppermute x6, waiting for transfers between devices: 3.77 us -> 2.65 us  [in_plane(): lax.ppermute(value, 'blk', [(a * inner + s, a * inner + t) for a in range...]
    unnamed x8 -> x2, local copies, waits for them, and re-layouts: 1.15 us -> 0.12 us
    ppermute x3, waiting for transfers between devices: 0.72 us -> 1.66 us  [along_outer(): lax.ppermute(value, 'blk', [(s * inner + b, t * inner + b) for s, t in ed...]
  transfers between devices with their start and end apart: 9 -> 9, of which waited for: 4 -> 4; matrix products, arithmetic and copies ran while one was open for 0% -> 0% of each run, Pallas kernels for 13% -> 12%
where the time goes in v11:
time: 24.1 us; the launch traced here: 23.9 us
  starting transfers between devices  15 us (62%)
  waiting for transfers between devices  4.3 us (18%)
  Pallas kernels  2.89 us (12%)
  other arithmetic  1.56 us (6%)
    ppermute x3, starting transfers between devices, along_outer(): lax.ppermute(value, 'blk', [(s * inner + b, t * inner + b) for s, t in ed...  10.1 us
    ppermute x6, starting transfers between devices, in_plane(): lax.ppermute(value, 'blk', [(a * inner + s, a * inner + t) for a in range...  4.91 us
    pallas_call x3, Pallas kernels, tile(): pl.pallas_call(functools.partial(tile_kernel, list(order), tuple(pairs),...  2.89 us
    ppermute x6, waiting for transfers between devices, in_plane(): lax.ppermute(value, 'blk', [(a * inner + s, a * inner + t) for a in range...  2.65 us
    ppermute x3, waiting for transfers between devices, along_outer(): lax.ppermute(value, 'blk', [(s * inner + b, t * inner + b) for s, t in ed...  1.66 us
    concatenate x1, other arithmetic, on_device(): packed = jnp.concatenate([features, probes.T], axis=0)  0.93 us
    transpose x1, other arithmetic, on_device(): return functools.reduce(lambda sofar, term: sofar + term, total).T  0.63 us
  transfers between devices with their start and end apart: 9, of which 4 were waited for; matrix products, arithmetic and copies ran while one was open for 0% of the time, Pallas kernels for 12%

profile of v11, /device:TPU:0, one launch (start us, length us, event | category | flops | bytes accessed | tf_op | source)
XLA Modules:
  0.0 23.9 jit_solution(2562073658989661756)
XLA Ops:
  0.0 0.9 %pad_maximum_fusion.refs_0_.refs_4_ = bf16[288,256]{1,0:T(8,128)(2,1)S(1)} fusion(bf16[32,256]{1,0:T(8,128)(2,1)} %bitcast.5, bf16[256,256]{1,0:T(8,128)(2,1)} %param.3), kind=kLoop, calls=%fused_computation | loop fusion | flops 294912 | bytes 294912 | tf_op jit(solution)/shard_map/concatenate | solution.py:133
  0.9 3.0 %collective-permute-start.1 = (bf16[288,256]{1,0:T(8,128)(2,1)S(1)}, bf16[288,256]{1,0:T(8,128)(2,1)S(1)}, u32[]{:S(2)}, u32[]{:S(2)}) collective-permute-start(bf16[288,256]{1,0:T(8,128)(2,1)S(1)} %pad_maximum_fusion.refs_0_.refs_4_), channel_id=1, source_target_pairs={{0,2},{1,3},{2,0},{3,1},{4,6},{5,7},{6,4},{7,5},{8,10},{9,11},{10,... | collective-permute-start | bytes 442376 | tf_op jit(solution)/shard_map/ppermute | solution.py:139
  4.0 2.6 %collective-permute-start.4 = (bf16[288,256]{1,0:T(8,128)(2,1)S(1)}, bf16[288,256]{1,0:T(8,128)(2,1)S(1)}, u32[]{:S(2)}, u32[]{:S(2)}) collective-permute-start(bf16[288,256]{1,0:T(8,128)(2,1)S(1)} %pad_maximum_fusion.refs_0_.refs_4_), channel_id=1, source_target_pairs={{0,8},{1,9},{2,10},{3,11},{8,4},{9,5},{10,6},{11,7},{4,12},{5,13},... | collective-permute-start | bytes 442376 | tf_op jit(solution)/shard_map/ppermute | solution.py:136
  6.6 0.0 collective-permute-start
  6.6 1.3 %collective-permute-done.1.refs_2_.refs_4_ = bf16[288,256]{1,0:T(8,128)(2,1)S(1)} collective-permute-done((bf16[288,256]{1,0:T(8,128)(2,1)S(1)}, bf16[288,256]{1,0:T(8,128)(2,1)S(1)}, u32[]{:S(2)}, u32[]{:S(2)}) %collective-permute-start.1) | collective-permute-done | bytes 147488 | tf_op jit(solution)/shard_map/ppermute | solution.py:139
  7.8 0.0 collective-permute-start.2
  7.8 1.8 %collective-permute-start.3 = (bf16[288,256]{1,0:T(8,128)(2,1)S(1)}, bf16[288,256]{1,0:T(8,128)(2,1)S(1)}, u32[]{:S(2)}, u32[]{:S(2)}) collective-permute-start(bf16[288,256]{1,0:T(8,128)(2,1)S(1)} %pad_maximum_fusion.refs_0_.refs_4_), channel_id=1, source_target_pairs={{0,4},{1,5},{2,6},{3,7},{8,12},{9,13},{10,14},{11,15},{4,0},{5,1},... | collective-permute-start | bytes 442376 | tf_op jit(solution)/shard_map/ppermute | solution.py:136
  9.6 1.6 %collective-permute-done.4.refs_2_ = bf16[288,256]{1,0:T(8,128)(2,1)S(1)} collective-permute-done((bf16[288,256]{1,0:T(8,128)(2,1)S(1)}, bf16[288,256]{1,0:T(8,128)(2,1)S(1)}, u32[]{:S(2)}, u32[]{:S(2)}) %collective-permute-start.4) | collective-permute-done | bytes 147488 | tf_op jit(solution)/shard_map/ppermute | solution.py:136
  11.3 0.0 collective-permute-done.refs_1_.refs_3_
  11.3 0.0 collective-permute-done.2.refs_3_.refs_1_
  11.3 1.1 %shard_map.38 = (f32[32,256]{1,0:T(8,128)S(1)}, f32[32,256]{1,0:T(8,128)S(1)}, f32[32,256]{1,0:T(8,128)S(1)}, f32[32,256]{1,0:T(8,128)S(1)}, f32[32,256]{1,0:T(8,128)S(1)}) custom-call(bf16[288,256]{1,0:T(8,128)(2,1)S(1)} %pad_maximum_fusion.refs_0_.refs_4_, bf16[288,256]{1,0:T(8,128)(2,1)S(1)} %collective-permute-done.2.refs_3_.refs_1_, ...), custom_call_target="tpu_custom_call" | custom-call | flops 167772160 | bytes 655360 | tf_op jit(solution)/shard_map/pallas_call | solution.py:110
  12.4 5.7 %collective-permute-start.8 = (f32[32,256]{1,0:T(8,128)S(1)}, f32[32,256]{1,0:T(8,128)S(1)}, u32[]{:S(2)}, u32[]{:S(2)}) collective-permute-start(f32[32,256]{1,0:T(8,128)S(1)} %get-tuple-element.22), channel_id=1, source_target_pairs={{8,0},{9,1},{10,2},{11,3},{4,8},{5,9},{6,10},{7,11},{12,4},{13,5},... | collective-permute-start | bytes 98312 | tf_op jit(solution)/shard_map/ppermute | solution.py:136
  18.1 0.0 collective-permute-done.3.refs_4_
  18.1 0.9 %shard_map.39 = (f32[32,256]{1,0:T(8,128)S(1)}, f32[32,256]{1,0:T(8,128)S(1)}, f32[32,256]{1,0:T(8,128)S(1)}, f32[32,256]{1,0:T(8,128)S(1)}) custom-call(bf16[288,256]{1,0:T(8,128)(2,1)S(1)} %pad_maximum_fusion.refs_0_.refs_4_, bf16[288,256]{1,0:T(8,128)(2,1)S(1)} %collective-permute-done.refs_1_.refs_3_, ...), custom_call_target="tpu_custom_call" | custom-call | flops 167772160 | bytes 655360 | tf_op jit(solution)/shard_map/pallas_call | solution.py:110
  19.0 0.0 collective-permute-start.7
  19.0 1.3 %collective-permute-start.6 = (f32[32,256]{1,0:T(8,128)S(1)}, f32[32,256]{1,0:T(8,128)S(1)}, u32[]{:S(2)}, u32[]{:S(2)}) collective-permute-start(f32[32,256]{1,0:T(8,128)S(1)} %get-tuple-element.19), channel_id=1, source_target_pairs={{0,2},{1,3},{2,0},{3,1},{4,6},{5,7},{6,4},{7,5},{8,10},{9,11},{10,... | collective-permute-start | bytes 98312 | tf_op jit(solution)/shard_map/ppermute | solution.py:139
  20.3 0.6 %collective-permute-start.5 = (f32[32,256]{1,0:T(8,128)S(1)}, f32[32,256]{1,0:T(8,128)S(1)}, u32[]{:S(2)}, u32[]{:S(2)}) collective-permute-start(f32[32,256]{1,0:T(8,128)S(1)} %get-tuple-element.18), channel_id=1, source_target_pairs={{0,1},{1,0},{2,3},{3,2},{4,5},{5,4},{6,7},{7,6},{8,9},{9,8},{10,11... | collective-permute-start | bytes 98312 | tf_op jit(solution)/shard_map/ppermute | solution.py:139
  20.9 0.1 copy-done
  21.0 0.9 %shard_map.37 = f32[32,256]{1,0:T(8,128)S(1)} custom-call(bf16[288,256]{1,0:T(8,128)(2,1)S(1)} %pad_maximum_fusion.refs_0_.refs_4_, bf16[288,256]{1,0:T(8,128)(2,1)S(1)} %collective-permute-done.refs_1_.refs_3_, bf16[288,256]{1,0:T(8,128)(2,1)S(1)} %collective-permute-done.1.refs_2_.refs_4_, bf16[288,256]{1,0:T(8,128)(2,1)S(1)} %collective-permute-done.2.refs_3_.refs_1_, ...), custom_call_target="tpu_custom_call" | custom-call | flops 167772160 | bytes 655360 | tf_op jit(solution)/shard_map/pallas_call | solution.py:110
  21.8 0.0 collective-permute-done.8
  21.9 0.7 %collective-permute-done.7 = f32[32,256]{1,0:T(8,128)S(1)} collective-permute-done((f32[32,256]{1,0:T(8,128)S(1)}, f32[32,256]{1,0:T(8,128)S(1)}, u32[]{:S(2)}, u32[]{:S(2)}) %collective-permute-start.7) | collective-permute-done | bytes 32800 | tf_op jit(solution)/shard_map/ppermute | solution.py:139
  22.5 0.7 %collective-permute-done.6 = f32[32,256]{1,0:T(8,128)S(1)} collective-permute-done((f32[32,256]{1,0:T(8,128)S(1)}, f32[32,256]{1,0:T(8,128)S(1)}, u32[]{:S(2)}, u32[]{:S(2)}) %collective-permute-start.6) | collective-permute-done | bytes 32800 | tf_op jit(solution)/shard_map/ppermute | solution.py:139
  23.2 0.0 collective-permute-done.5
  23.2 0.6 %add_bitcast_fusion = f32[256,32]{0,1:T(8,128)} fusion(f32[32,256]{1,0:T(8,128)S(1)} %collective-permute-done.8, f32[32,256]{1,0:T(8,128)S(1)} %get-tuple-element.21, f32[32,256]{1,0:T(8,128)S(1)} %collective-permute-done.7, f32[32,256]{1,0:T(8,128)S(1)} %collective-permute-done.6, f32[32,256]{1,0:T(8,128)S(1)} %shard_map.37, ...), kind=kLoop, calls=%fused_computation.1 | loop fusion | flops 40960 | bytes 229376 | tf_op jit(solution)/shard_map/transpose | solution.py:164
  (1 shorter events, 0.0 us)
Async XLA Ops:
  0.9 6.9 %collective-permute-start.1 = (bf16[288,256]{1,0:T(8,128)(2,1)S(1)}, bf16[288,256]{1,0:T(8,128)(2,1)S(1)}, u32[]{:S(2)}, u32[]{:S(2)}) collective-permute-start(bf16[288,256]{1,0:T(8,128)(2,1)S(1)} %pad_maximum_fusion.refs_0_.refs_4_), channel_id=1, source_target_pairs={{0,2},{1,3},{2,0},{3,1},{4,6},{5,7},{6,4},{7,5},{8,10},{9,11},{10,... | collective-permute-start | bytes 442376 | tf_op jit(solution)/shard_map/ppermute | solution.py:139
  4.0 7.3 %collective-permute-start.4 = (bf16[288,256]{1,0:T(8,128)(2,1)S(1)}, bf16[288,256]{1,0:T(8,128)(2,1)S(1)}, u32[]{:S(2)}, u32[]{:S(2)}) collective-permute-start(bf16[288,256]{1,0:T(8,128)(2,1)S(1)} %pad_maximum_fusion.refs_0_.refs_4_), channel_id=1, source_target_pairs={{0,8},{1,9},{2,10},{3,11},{8,4},{9,5},{10,6},{11,7},{4,12},{5,13},... | collective-permute-start | bytes 442376 | tf_op jit(solution)/shard_map/ppermute | solution.py:136
  6.6 4.7 %collective-permute-start = (bf16[288,256]{1,0:T(8,128)(2,1)S(1)}, bf16[288,256]{1,0:T(8,128)(2,1)S(1)}, u32[]{:S(2)}, u32[]{:S(2)}) collective-permute-start(bf16[288,256]{1,0:T(8,128)(2,1)S(1)} %pad_maximum_fusion.refs_0_.refs_4_), channel_id=1, source_target_pairs={{0,1},{1,0},{2,3},{3,2},{4,5},{5,4},{6,7},{7,6},{8,9},{9,8},{10,11... | collective-permute-start | bytes 442376 | tf_op jit(solution)/shard_map/ppermute | solution.py:139
  7.8 3.5 %collective-permute-start.2 = (bf16[288,256]{1,0:T(8,128)(2,1)S(1)}, bf16[288,256]{1,0:T(8,128)(2,1)S(1)}, u32[]{:S(2)}, u32[]{:S(2)}) collective-permute-start(bf16[288,256]{1,0:T(8,128)(2,1)S(1)} %collective-permute-done.1.refs_2_.refs_4_), channel_id=1, source_target_pairs={{0,1},{1,0},{2,3},{3,2},{4,5},{5,4},{6,7},{7,6},{8,9},{9,8},{10,11... | collective-permute-start | bytes 442376 | tf_op jit(solution)/shard_map/ppermute | solution.py:139
  7.8 10.3 %collective-permute-start.3 = (bf16[288,256]{1,0:T(8,128)(2,1)S(1)}, bf16[288,256]{1,0:T(8,128)(2,1)S(1)}, u32[]{:S(2)}, u32[]{:S(2)}) collective-permute-start(bf16[288,256]{1,0:T(8,128)(2,1)S(1)} %pad_maximum_fusion.refs_0_.refs_4_), channel_id=1, source_target_pairs={{0,4},{1,5},{2,6},{3,7},{8,12},{9,13},{10,14},{11,15},{4,0},{5,1},... | collective-permute-start | bytes 442376 | tf_op jit(solution)/shard_map/ppermute | solution.py:136
  12.4 9.4 %collective-permute-start.8 = (f32[32,256]{1,0:T(8,128)S(1)}, f32[32,256]{1,0:T(8,128)S(1)}, u32[]{:S(2)}, u32[]{:S(2)}) collective-permute-start(f32[32,256]{1,0:T(8,128)S(1)} %get-tuple-element.22), channel_id=1, source_target_pairs={{8,0},{9,1},{10,2},{11,3},{4,8},{5,9},{6,10},{7,11},{12,4},{13,5},... | collective-permute-start | bytes 98312 | tf_op jit(solution)/shard_map/ppermute | solution.py:136
  19.0 3.6 %collective-permute-start.7 = (f32[32,256]{1,0:T(8,128)S(1)}, f32[32,256]{1,0:T(8,128)S(1)}, u32[]{:S(2)}, u32[]{:S(2)}) collective-permute-start(f32[32,256]{1,0:T(8,128)S(1)} %get-tuple-element.20), channel_id=1, source_target_pairs={{0,3},{1,2},{2,1},{3,0},{4,7},{5,6},{6,5},{7,4},{8,11},{9,10},{10,... | collective-permute-start | bytes 98312 | tf_op jit(solution)/shard_map/ppermute | solution.py:139
  19.0 4.2 %collective-permute-start.6 = (f32[32,256]{1,0:T(8,128)S(1)}, f32[32,256]{1,0:T(8,128)S(1)}, u32[]{:S(2)}, u32[]{:S(2)}) collective-permute-start(f32[32,256]{1,0:T(8,128)S(1)} %get-tuple-element.19), channel_id=1, source_target_pairs={{0,2},{1,3},{2,0},{3,1},{4,6},{5,7},{6,4},{7,5},{8,10},{9,11},{10,... | collective-permute-start | bytes 98312 | tf_op jit(solution)/shard_map/ppermute | solution.py:139
  20.3 0.7 %copy-start = (f32[256]{0:T(256)S(1)}, f32[256]{0:T(256)}, u32[]{:S(2)}) copy-start(f32[256]{0:T(256)} %param.5) | copy-start | bytes 3076
  20.3 2.9 %collective-permute-start.5 = (f32[32,256]{1,0:T(8,128)S(1)}, f32[32,256]{1,0:T(8,128)S(1)}, u32[]{:S(2)}, u32[]{:S(2)}) collective-permute-start(f32[32,256]{1,0:T(8,128)S(1)} %get-tuple-element.18), channel_id=1, source_target_pairs={{0,1},{1,0},{2,3},{3,2},{4,5},{5,4},{6,7},{7,6},{8,9},{9,8},{10,11... | collective-permute-start | bytes 98312 | tf_op jit(solution)/shard_map/ppermute | solution.py:139

commit v12 on v8

--- a/solution.py
+++ b/solution.py
@@ -41,7 +41,7 @@
     bits = count.bit_length() - 1
     order = list(range(count))
     if count == 1 << bits:
-        order = [int(f"{a:0{bits}b}"[::-1], 2) if bits else a for a in order]
+        order = [int(f"{a:0{bits}b}"[::-1], 2) if bits else a for a in reversed(order)]
     shifts = [[(order[p], order[(p + step) % count]) for p in range(count)] for step in range(1, count // 2 + 1)]
     if count % 2:
         return shifts, []

time: 24 us -> 24 us (level)
  starting transfers between devices: 12.1 us -> 8.85 us
  waiting for transfers between devices: 7.2 us -> 10.1 us
  local copies, waits for them, and re-layouts: 0.01 us -> 0.33 us
    ppermute x3, waiting for transfers between devices: 6.03 us -> 9.87 us  [along_outer(): lax.ppermute(value, 'blk', [(s * inner + b, t * inner + b) for s, t in ed...]
    ppermute x3, starting transfers between devices: 6.99 us -> 3.62 us  [along_outer(): lax.ppermute(value, 'blk', [(s * inner + b, t * inner + b) for s, t in ed...]
    ppermute x6, waiting for transfers between devices: 1.17 us -> 0.25 us  [in_plane(): lax.ppermute(value, 'blk', [(a * inner + s, a * inner + t) for a in range...]
    unnamed x2, local copies, waits for them, and re-layouts: 0.01 us -> 0.33 us
where the time goes in v12:
time: 24 us; the launch traced here: 23.7 us
  waiting for transfers between devices  10.1 us (42%)
  starting transfers between devices  8.85 us (37%)
  Pallas kernels  2.83 us (12%)
  other arithmetic  1.56 us (6%)
  local copies, waits for them, and re-layouts  0.33 us (1%)
    ppermute x3, waiting for transfers between devices, along_outer(): lax.ppermute(value, 'blk', [(s * inner + b, t * inner + b) for s, t in ed...  9.87 us
    ppermute x6, starting transfers between devices, in_plane(): lax.ppermute(value, 'blk', [(a * inner + s, a * inner + t) for a in range...  5.23 us
    ppermute x3, starting transfers between devices, along_outer(): lax.ppermute(value, 'blk', [(s * inner + b, t * inner + b) for s, t in ed...  3.62 us
    pallas_call x2, Pallas kernels, tile(): pl.pallas_call(functools.partial(tile_kernel, (len(rows), len(cols)), [li...  2.83 us
    concatenate x1, other arithmetic, on_device(): packed = jnp.concatenate([features, probes.T], axis=0)  0.93 us
    transpose x1, other arithmetic, on_device(): functools.reduce(lambda total, term: total + term, sums + list(terms[:1])...  0.63 us
  transfers between devices with their start and end apart: 9, of which 4 were waited for; matrix products, arithmetic and copies ran while one was open for 0% of the time, Pallas kernels for 4%

profile of v12, /device:TPU:0, one launch (start us, length us, event | category | flops | bytes accessed | tf_op | source)
XLA Modules:
  0.0 23.7 jit_solution(13537426878353758838)
XLA Ops:
  0.0 0.9 %pad_maximum_fusion.refs_0_.refs_4_ = bf16[288,256]{1,0:T(8,128)(2,1)S(1)} fusion(bf16[32,256]{1,0:T(8,128)(2,1)} %bitcast.5, bf16[256,256]{1,0:T(8,128)(2,1)} %param.3), kind=kLoop, calls=%fused_computation | loop fusion | flops 294912 | bytes 294912 | tf_op jit(solution)/shard_map/concatenate | solution.py:144
  0.9 3.0 %collective-permute-start = (bf16[288,256]{1,0:T(8,128)(2,1)S(1)}, bf16[288,256]{1,0:T(8,128)(2,1)S(1)}, u32[]{:S(2)}, u32[]{:S(2)}) collective-permute-start(bf16[288,256]{1,0:T(8,128)(2,1)S(1)} %pad_maximum_fusion.refs_0_.refs_4_), channel_id=1, source_target_pairs={{0,2},{1,3},{2,0},{3,1},{4,6},{5,7},{6,4},{7,5},{8,10},{9,11},{10,... | collective-permute-start | bytes 442376 | tf_op jit(solution)/shard_map/ppermute | solution.py:150
  4.0 3.6 %collective-permute-start.4 = (bf16[288,256]{1,0:T(8,128)(2,1)S(1)}, bf16[288,256]{1,0:T(8,128)(2,1)S(1)}, u32[]{:S(2)}, u32[]{:S(2)}) collective-permute-start(bf16[288,256]{1,0:T(8,128)(2,1)S(1)} %pad_maximum_fusion.refs_0_.refs_4_), channel_id=1, source_target_pairs={{12,4},{13,5},{14,6},{15,7},{4,8},{5,9},{6,10},{7,11},{8,0},{9,1},... | collective-permute-start | bytes 442376 | tf_op jit(solution)/shard_map/ppermute | solution.py:147
  7.6 0.0 collective-permute-start.3
  7.6 0.0 collective-permute-start.2
  7.6 0.2 %collective-permute-done.refs_5_.refs_2_ = bf16[288,256]{1,0:T(8,128)(2,1)S(1)} collective-permute-done((bf16[288,256]{1,0:T(8,128)(2,1)S(1)}, bf16[288,256]{1,0:T(8,128)(2,1)S(1)}, u32[]{:S(2)}, u32[]{:S(2)}) %collective-permute-start) | collective-permute-done | bytes 147488 | tf_op jit(solution)/shard_map/ppermute | solution.py:150
  7.8 0.3 %collective-permute-start.1 = (bf16[288,256]{1,0:T(8,128)(2,1)S(1)}, bf16[288,256]{1,0:T(8,128)(2,1)S(1)}, u32[]{:S(2)}, u32[]{:S(2)}) collective-permute-start(bf16[288,256]{1,0:T(8,128)(2,1)S(1)} %collective-permute-done.refs_5_.refs_2_), channel_id=1, source_target_pairs={{0,1},{1,0},{2,3},{3,2},{4,5},{5,4},{6,7},{7,6},{8,9},{9,8},{10,11... | collective-permute-start | bytes 442376 | tf_op jit(solution)/shard_map/ppermute | solution.py:150
  8.1 5.4 %collective-permute-done.4.refs_4_ = bf16[288,256]{1,0:T(8,128)(2,1)S(1)} collective-permute-done((bf16[288,256]{1,0:T(8,128)(2,1)S(1)}, bf16[288,256]{1,0:T(8,128)(2,1)S(1)}, u32[]{:S(2)}, u32[]{:S(2)}) %collective-permute-start.4) | collective-permute-done | bytes 147488 | tf_op jit(solution)/shard_map/ppermute | solution.py:147
  13.4 0.0 collective-permute-done.3.refs_3_.refs_1_
  13.4 2.1 %collective-permute-done.2.refs_2_ = bf16[288,256]{1,0:T(8,128)(2,1)S(1)} collective-permute-done((bf16[288,256]{1,0:T(8,128)(2,1)S(1)}, bf16[288,256]{1,0:T(8,128)(2,1)S(1)}, u32[]{:S(2)}, u32[]{:S(2)}) %collective-permute-start.2) | collective-permute-done | bytes 147488 | tf_op jit(solution)/shard_map/ppermute | solution.py:147
  15.5 0.0 collective-permute-done.1.refs_1_.refs_3_
  15.5 1.8 %shard_map.37 = (f32[32,256]{1,0:T(8,128)S(1)}, f32[32,256]{1,0:T(8,128)S(1)}, f32[32,256]{1,0:T(8,128)S(1)}, f32[32,256]{1,0:T(8,128)S(1)}, f32[32,256]{1,0:T(8,128)S(1)}) custom-call(bf16[288,256]{1,0:T(8,128)(2,1)S(1)} %pad_maximum_fusion.refs_0_.refs_4_, bf16[288,256]{1,0:T(8,128)(2,1)S(1)} %collective-permute-done.1.refs_1_.refs_3_, ...), custom_call_target="tpu_custom_call" | custom-call | flops 335544320 | bytes 786432 | tf_op jit(solution)/shard_map/pallas_call | solution.py:117
  17.3 0.0 collective-permute-start.5
  17.3 0.1 collective-permute-start.6
  17.4 1.5 %collective-permute-start.7 = (f32[32,256]{1,0:T(8,128)S(1)}, f32[32,256]{1,0:T(8,128)S(1)}, u32[]{:S(2)}, u32[]{:S(2)}) collective-permute-start(f32[32,256]{1,0:T(8,128)S(1)} %get-tuple-element.12), channel_id=1, source_target_pairs={{0,2},{1,3},{2,0},{3,1},{4,6},{5,7},{6,4},{7,5},{8,10},{9,11},{10,... | collective-permute-start | bytes 98312 | tf_op jit(solution)/shard_map/ppermute | solution.py:150
  18.9 0.0 copy-start
  18.9 0.4 %collective-permute-start.8 = (f32[32,256]{1,0:T(8,128)S(1)}, f32[32,256]{1,0:T(8,128)S(1)}, u32[]{:S(2)}, u32[]{:S(2)}) collective-permute-start(f32[32,256]{1,0:T(8,128)S(1)} %get-tuple-element.13), channel_id=1, source_target_pairs={{0,1},{1,0},{2,3},{3,2},{4,5},{5,4},{6,7},{7,6},{8,9},{9,8},{10,11... | collective-permute-start | bytes 98312 | tf_op jit(solution)/shard_map/ppermute | solution.py:150
  19.3 0.3 %copy-done = f32[256]{0:T(256)S(1)} copy-done((f32[256]{0:T(256)S(1)}, f32[256]{0:T(256)}, u32[]{:S(2)}) %copy-start) | copy-done | bytes 1048
  19.6 1.0 %shard_map.38 = f32[32,256]{1,0:T(8,128)S(1)} custom-call(bf16[288,256]{1,0:T(8,128)(2,1)S(1)} %pad_maximum_fusion.refs_0_.refs_4_, bf16[288,256]{1,0:T(8,128)(2,1)S(1)} %collective-permute-done.3.refs_3_.refs_1_, bf16[288,256]{1,0:T(8,128)(2,1)S(1)} %collective-permute-done.refs_5_.refs_2_, bf16[288,256]{1,0:T(8,128)(2,1)S(1)} %collective-permute-done.1.refs_1_.refs_3_, ...), custom_call_target="tpu_custom_call" | custom-call | flops 167772160 | bytes 655360 | tf_op jit(solution)/shard_map/pallas_call | solution.py:117
  20.6 2.5 %collective-permute-done.5 = f32[32,256]{1,0:T(8,128)S(1)} collective-permute-done((f32[32,256]{1,0:T(8,128)S(1)}, f32[32,256]{1,0:T(8,128)S(1)}, u32[]{:S(2)}, u32[]{:S(2)}) %collective-permute-start.5) | collective-permute-done | bytes 32800 | tf_op jit(solution)/shard_map/ppermute | solution.py:147
  23.1 0.0 collective-permute-done.6
  23.1 0.0 collective-permute-done.7
  23.1 0.0 collective-permute-done.8
  23.1 0.6 %add_bitcast_fusion = f32[256,32]{0,1:T(8,128)} fusion(f32[32,256]{1,0:T(8,128)S(1)} %shard_map.38, f32[32,256]{1,0:T(8,128)S(1)} %get-tuple-element.14, f32[32,256]{1,0:T(8,128)S(1)} %collective-permute-done.8, f32[32,256]{1,0:T(8,128)S(1)} %collective-permute-done.7, f32[32,256]{1,0:T(8,128)S(1)} %collective-permute-done.5, ...), kind=kLoop, calls=%fused_computation.1 | loop fusion | flops 40960 | bytes 229376 | tf_op jit(solution)/shard_map/transpose | solution.py:169
Async XLA Ops:
  0.9 6.9 %collective-permute-start = (bf16[288,256]{1,0:T(8,128)(2,1)S(1)}, bf16[288,256]{1,0:T(8,128)(2,1)S(1)}, u32[]{:S(2)}, u32[]{:S(2)}) collective-permute-start(bf16[288,256]{1,0:T(8,128)(2,1)S(1)} %pad_maximum_fusion.refs_0_.refs_4_), channel_id=1, source_target_pairs={{0,2},{1,3},{2,0},{3,1},{4,6},{5,7},{6,4},{7,5},{8,10},{9,11},{10,... | collective-permute-start | bytes 442376 | tf_op jit(solution)/shard_map/ppermute | solution.py:150
  4.0 9.5 %collective-permute-start.4 = (bf16[288,256]{1,0:T(8,128)(2,1)S(1)}, bf16[288,256]{1,0:T(8,128)(2,1)S(1)}, u32[]{:S(2)}, u32[]{:S(2)}) collective-permute-start(bf16[288,256]{1,0:T(8,128)(2,1)S(1)} %pad_maximum_fusion.refs_0_.refs_4_), channel_id=1, source_target_pairs={{12,4},{13,5},{14,6},{15,7},{4,8},{5,9},{6,10},{7,11},{8,0},{9,1},... | collective-permute-start | bytes 442376 | tf_op jit(solution)/shard_map/ppermute | solution.py:147
  7.6 5.9 %collective-permute-start.3 = (bf16[288,256]{1,0:T(8,128)(2,1)S(1)}, bf16[288,256]{1,0:T(8,128)(2,1)S(1)}, u32[]{:S(2)}, u32[]{:S(2)}) collective-permute-start(bf16[288,256]{1,0:T(8,128)(2,1)S(1)} %pad_maximum_fusion.refs_0_.refs_4_), channel_id=1, source_target_pairs={{0,1},{1,0},{2,3},{3,2},{4,5},{5,4},{6,7},{7,6},{8,9},{9,8},{10,11... | collective-permute-start | bytes 442376 | tf_op jit(solution)/shard_map/ppermute | solution.py:150
  7.6 7.9 %collective-permute-start.2 = (bf16[288,256]{1,0:T(8,128)(2,1)S(1)}, bf16[288,256]{1,0:T(8,128)(2,1)S(1)}, u32[]{:S(2)}, u32[]{:S(2)}) collective-permute-start(bf16[288,256]{1,0:T(8,128)(2,1)S(1)} %pad_maximum_fusion.refs_0_.refs_4_), channel_id=1, source_target_pairs={{12,8},{13,9},{14,10},{15,11},{4,0},{5,1},{6,2},{7,3},{8,12},{9,13... | collective-permute-start | bytes 442376 | tf_op jit(solution)/shard_map/ppermute | solution.py:147
  7.8 7.7 %collective-permute-start.1 = (bf16[288,256]{1,0:T(8,128)(2,1)S(1)}, bf16[288,256]{1,0:T(8,128)(2,1)S(1)}, u32[]{:S(2)}, u32[]{:S(2)}) collective-permute-start(bf16[288,256]{1,0:T(8,128)(2,1)S(1)} %collective-permute-done.refs_5_.refs_2_), channel_id=1, source_target_pairs={{0,1},{1,0},{2,3},{3,2},{4,5},{5,4},{6,7},{7,6},{8,9},{9,8},{10,11... | collective-permute-start | bytes 442376 | tf_op jit(solution)/shard_map/ppermute | solution.py:150
  17.3 5.7 %collective-permute-start.5 = (f32[32,256]{1,0:T(8,128)S(1)}, f32[32,256]{1,0:T(8,128)S(1)}, u32[]{:S(2)}, u32[]{:S(2)}) collective-permute-start(f32[32,256]{1,0:T(8,128)S(1)} %get-tuple-element.10), channel_id=1, source_target_pairs={{4,12},{5,13},{6,14},{7,15},{8,4},{9,5},{10,6},{11,7},{0,8},{1,9},... | collective-permute-start | bytes 98312 | tf_op jit(solution)/shard_map/ppermute | solution.py:147
  17.3 5.7 %collective-permute-start.6 = (f32[32,256]{1,0:T(8,128)S(1)}, f32[32,256]{1,0:T(8,128)S(1)}, u32[]{:S(2)}, u32[]{:S(2)}) collective-permute-start(f32[32,256]{1,0:T(8,128)S(1)} %get-tuple-element.11), channel_id=1, source_target_pairs={{0,3},{1,2},{2,1},{3,0},{4,7},{5,6},{6,5},{7,4},{8,11},{9,10},{10,... | collective-permute-start | bytes 98312 | tf_op jit(solution)/shard_map/ppermute | solution.py:150
  17.4 5.7 %collective-permute-start.7 = (f32[32,256]{1,0:T(8,128)S(1)}, f32[32,256]{1,0:T(8,128)S(1)}, u32[]{:S(2)}, u32[]{:S(2)}) collective-permute-start(f32[32,256]{1,0:T(8,128)S(1)} %get-tuple-element.12), channel_id=1, source_target_pairs={{0,2},{1,3},{2,0},{3,1},{4,6},{5,7},{6,4},{7,5},{8,10},{9,11},{10,... | collective-permute-start | bytes 98312 | tf_op jit(solution)/shard_map/ppermute | solution.py:150
  18.9 0.7 %copy-start = (f32[256]{0:T(256)S(1)}, f32[256]{0:T(256)}, u32[]{:S(2)}) copy-start(f32[256]{0:T(256)} %param.5) | copy-start | bytes 3076
  18.9 4.2 %collective-permute-start.8 = (f32[32,256]{1,0:T(8,128)S(1)}, f32[32,256]{1,0:T(8,128)S(1)}, u32[]{:S(2)}, u32[]{:S(2)}) collective-permute-start(f32[32,256]{1,0:T(8,128)S(1)} %get-tuple-element.13), channel_id=1, source_target_pairs={{0,1},{1,0},{2,3},{3,2},{4,5},{5,4},{6,7},{7,6},{8,9},{9,8},{10,11... | collective-permute-start | bytes 98312 | tf_op jit(solution)/shard_map/ppermute | solution.py:150

commit v13 on v9

--- a/solution.py
+++ b/solution.py
@@ -100,7 +100,7 @@
         ref[...] = sums[name]
 
 
-def tile(rows, cols, order, pairs, sums, shard, vectors, noise=(), waits=1):
+def tile(rows, cols, order, pairs, sums, shard, vectors, noise=()):
     blocks = [*rows, *cols]
     args = [*[blocks[place] for place in order], *noise, *sums.values()]
     elements = len(pairs) * shard * shard
@@ -116,7 +116,7 @@
         out_specs=[whole] * len(names),
         compiler_params=pltpu.CompilerParams(vmem_limit_bytes=32 * 1024 * 1024),
         cost_estimate=pl.CostEstimate(
-            flops=2 * elements * (width + 2 * vectors) * waits,
+            flops=2 * elements * (width + 2 * vectors),
             bytes_accessed=2 * width * shard * len(blocks),
             transcendentals=2 * elements,
         ),
@@ -124,29 +124,13 @@
     return dict(zip(names, found))
 
 
-def copy_kernel(from_ref, to_ref):
-    to_ref[...] = from_ref[0 : to_ref.shape[0], :]
-
-
-def copy_rows(value, rows):
-    whole = pl.BlockSpec(memory_space=pltpu.VMEM)
-    return pl.pallas_call(
-        copy_kernel,
-        out_shape=jax.ShapeDtypeStruct((rows, value.shape[1]), value.dtype),
-        in_specs=[whole],
-        out_specs=whole,
-    )(value)
-
-
 def on_device(features, probes, noise_level):
     count = lax.axis_size("blk")
     inner = group_size(count)
     outer = count // inner
-    shard, width = features.shape
+    shard = features.shape[0]
     vectors = probes.shape[1]
-    spare = jnp.zeros((16, width), features.dtype)
-    longer = jnp.concatenate([features, probes.T, spare], axis=0)
-    packed = copy_rows(longer, shard + vectors)
+    packed = jnp.concatenate([features, probes.T], axis=0)
 
     def along_outer(value, edges):
         return lax.ppermute(value, "blk", [(s * inner + b, t * inner + b) for s, t in edges for b in range(inner)])
@@ -158,7 +142,7 @@
         return [(plane_target(b, step, inner), b) for b in range(inner)]
 
     one_way, exchanges = outer_maps(outer)
-    cols = [along_outer(longer, edges) for edges in one_way] + [along_outer(packed, edges) for edges in exchanges]
+    cols = [along_outer(packed, edges) for edges in one_way + exchanges]
     kinds = [("rows", "back")] * len(one_way) + [("rows",)] * len(exchanges)
     blocks = plane_blocks(packed, inner, in_plane)
     direct = [step for step in range(inner) if step & (step - 1) == 0]
@@ -166,7 +150,7 @@
 
     early = [(row, col, kinds[col]) for col in range(len(one_way)) for row in range(len(direct))]
     order = [0, 1] + list(range(len(direct), len(direct) + len(one_way))) + list(range(2, len(direct)))
-    sums = tile([blocks[step] for step in direct], cols[: len(one_way)], order, early, {}, shard, vectors, waits=1000)
+    sums = tile([blocks[step] for step in direct], cols[: len(one_way)], order, early, {}, shard, vectors)
     sums = {(part, direct[place] if part == "rows" else place): value for (part, place), value in sums.items()}
     late = [(row, col, kinds[col]) for col in range(len(cols)) for row in range(inner) if col >= len(one_way) or row in passed]
     sums = tile(blocks, cols, range(inner + len(cols)), late, sums, shard, vectors)

time: 25.8 us -> 25.1 us (0.973)
  waiting for transfers between devices: 4.5 us -> 7.75 us
  Pallas kernels: 4.55 us -> 2.97 us
  starting transfers between devices: 13.6 us -> 12.3 us
  local copies, waits for them, and re-layouts: 1.23 us -> 0.24 us
    ppermute x3, waiting for transfers between devices: 0.72 us -> 6.39 us  [along_outer(): lax.ppermute(value, 'blk', [(s * inner + b, t * inner + b) for s, t in ed...]
    ppermute x3, starting transfers between devices: 10.2 us -> 7.45 us  [along_outer(): lax.ppermute(value, 'blk', [(s * inner + b, t * inner + b) for s, t in ed...]
    ppermute x6, waiting for transfers between devices: 3.77 us -> 1.36 us  [in_plane(): lax.ppermute(value, 'blk', [(a * inner + s, a * inner + t) for a in range...]
    pallas_call x1 -> x0, Pallas kernels: 1.57 us -> none  [copy_rows(): pl.pallas_call(copy_kernel, out_shape=jax.ShapeDtypeStruct((rows, value.s...]
    ppermute x6, starting transfers between devices: 3.39 us -> 4.9 us  [in_plane(): lax.ppermute(value, 'blk', [(a * inner + s, a * inner + t) for a in range...]
    unnamed x8 -> x2, local copies, waits for them, and re-layouts: 1.15 us -> 0.24 us
  transfers between devices with their start and end apart: 9 -> 9, of which waited for: 4 -> 4; matrix products, arithmetic and copies ran while one was open for 0% -> 0% of each run, Pallas kernels for 13% -> 7%
where the time goes in v13:
time: 25.1 us; the launch traced here: 24.9 us
  starting transfers between devices  12.3 us (49%)
  waiting for transfers between devices  7.75 us (31%)
  Pallas kernels  2.97 us (12%)
  other arithmetic  1.56 us (6%)
    ppermute x3, starting transfers between devices, along_outer(): lax.ppermute(value, 'blk', [(s * inner + b, t * inner + b) for s, t in ed...  7.45 us
    ppermute x3, waiting for transfers between devices, along_outer(): lax.ppermute(value, 'blk', [(s * inner + b, t * inner + b) for s, t in ed...  6.39 us
    ppermute x6, starting transfers between devices, in_plane(): lax.ppermute(value, 'blk', [(a * inner + s, a * inner + t) for a in range...  4.9 us
    pallas_call x3, Pallas kernels, tile(): pl.pallas_call(functools.partial(tile_kernel, list(order), tuple(pairs),...  2.97 us
    ppermute x6, waiting for transfers between devices, in_plane(): lax.ppermute(value, 'blk', [(a * inner + s, a * inner + t) for a in range...  1.36 us
    concatenate x1, other arithmetic, on_device(): packed = jnp.concatenate([features, probes.T], axis=0)  0.93 us
    transpose x1, other arithmetic, on_device(): functools.reduce(lambda total, term: total + term, total + [sums['rows',...  0.63 us
  transfers between devices with their start and end apart: 9, of which 4 were waited for; matrix products, arithmetic and copies ran while one was open for 0% of the time, Pallas kernels for 7%

profile of v13, /device:TPU:0, one launch (start us, length us, event | category | flops | bytes accessed | tf_op | source)
XLA Modules:
  0.0 24.9 jit_solution(15926971960835771926)
XLA Ops:
  0.0 0.9 %pad_maximum_fusion.refs_0_.refs_4_ = bf16[288,256]{1,0:T(8,128)(2,1)S(1)} fusion(bf16[32,256]{1,0:T(8,128)(2,1)} %bitcast.5, bf16[256,256]{1,0:T(8,128)(2,1)} %param.3), kind=kLoop, calls=%fused_computation | loop fusion | flops 294912 | bytes 294912 | tf_op jit(solution)/shard_map/concatenate | solution.py:133
  0.9 3.0 %collective-permute-start.1 = (bf16[288,256]{1,0:T(8,128)(2,1)S(1)}, bf16[288,256]{1,0:T(8,128)(2,1)S(1)}, u32[]{:S(2)}, u32[]{:S(2)}) collective-permute-start(bf16[288,256]{1,0:T(8,128)(2,1)S(1)} %pad_maximum_fusion.refs_0_.refs_4_), channel_id=1, source_target_pairs={{0,2},{1,3},{2,0},{3,1},{4,6},{5,7},{6,4},{7,5},{8,10},{9,11},{10,... | collective-permute-start | bytes 442376 | tf_op jit(solution)/shard_map/ppermute | solution.py:139
  4.0 0.0 collective-permute-start
  4.0 2.6 %collective-permute-start.3 = (bf16[288,256]{1,0:T(8,128)(2,1)S(1)}, bf16[288,256]{1,0:T(8,128)(2,1)S(1)}, u32[]{:S(2)}, u32[]{:S(2)}) collective-permute-start(bf16[288,256]{1,0:T(8,128)(2,1)S(1)} %pad_maximum_fusion.refs_0_.refs_4_), channel_id=1, source_target_pairs={{0,8},{1,9},{2,10},{3,11},{8,4},{9,5},{10,6},{11,7},{4,12},{5,13},... | collective-permute-start | bytes 442376 | tf_op jit(solution)/shard_map/ppermute | solution.py:136
  6.6 1.6 %collective-permute-start.4 = (bf16[288,256]{1,0:T(8,128)(2,1)S(1)}, bf16[288,256]{1,0:T(8,128)(2,1)S(1)}, u32[]{:S(2)}, u32[]{:S(2)}) collective-permute-start(bf16[288,256]{1,0:T(8,128)(2,1)S(1)} %pad_maximum_fusion.refs_0_.refs_4_), channel_id=1, source_target_pairs={{0,4},{1,5},{2,6},{3,7},{8,12},{9,13},{10,14},{11,15},{4,0},{5,1},... | collective-permute-start | bytes 442376 | tf_op jit(solution)/shard_map/ppermute | solution.py:136
  8.1 0.0 collective-permute-done.1.refs_3_.refs_2_
  8.1 0.0 collective-permute-start.2
  8.1 0.0 collective-permute-done.refs_1_
  8.2 4.3 %collective-permute-done.3.refs_2_.refs_4_ = bf16[288,256]{1,0:T(8,128)(2,1)S(1)} collective-permute-done((bf16[288,256]{1,0:T(8,128)(2,1)S(1)}, bf16[288,256]{1,0:T(8,128)(2,1)S(1)}, u32[]{:S(2)}, u32[]{:S(2)}) %collective-permute-start.3) | collective-permute-done | bytes 147488 | tf_op jit(solution)/shard_map/ppermute | solution.py:136
  12.5 0.8 %shard_map.37 = (f32[32,256]{1,0:T(8,128)S(1)}, f32[32,256]{1,0:T(8,128)S(1)}, f32[32,256]{1,0:T(8,128)S(1)}, f32[32,256]{1,0:T(8,128)S(1)}) custom-call(bf16[288,256]{1,0:T(8,128)(2,1)S(1)} %pad_maximum_fusion.refs_0_.refs_4_, bf16[288,256]{1,0:T(8,128)(2,1)S(1)} %collective-permute-done.refs_1_, ...), custom_call_target="tpu_custom_call" | custom-call | flops 125829120 | bytes 524288 | tf_op jit(solution)/shard_map/pallas_call | solution.py:110
  13.3 2.1 %collective-permute-done.4.refs_5_ = bf16[288,256]{1,0:T(8,128)(2,1)S(1)} collective-permute-done((bf16[288,256]{1,0:T(8,128)(2,1)S(1)}, bf16[288,256]{1,0:T(8,128)(2,1)S(1)}, u32[]{:S(2)}, u32[]{:S(2)}) %collective-permute-start.4) | collective-permute-done | bytes 147488 | tf_op jit(solution)/shard_map/ppermute | solution.py:136
  15.4 0.0 collective-permute-done.2.refs_3_
  15.4 1.3 %shard_map.38 = (f32[32,256]{1,0:T(8,128)S(1)}, f32[32,256]{1,0:T(8,128)S(1)}, f32[32,256]{1,0:T(8,128)S(1)}, f32[32,256]{1,0:T(8,128)S(1)}, f32[32,256]{1,0:T(8,128)S(1)}) custom-call(bf16[288,256]{1,0:T(8,128)(2,1)S(1)} %pad_maximum_fusion.refs_0_.refs_4_, bf16[288,256]{1,0:T(8,128)(2,1)S(1)} %collective-permute-done.refs_1_, ...), custom_call_target="tpu_custom_call" | custom-call | flops 209715200 | bytes 786432 | tf_op jit(solution)/shard_map/pallas_call | solution.py:110
  16.6 3.3 %collective-permute-start.5 = (f32[32,256]{1,0:T(8,128)S(1)}, f32[32,256]{1,0:T(8,128)S(1)}, u32[]{:S(2)}, u32[]{:S(2)}) collective-permute-start(f32[32,256]{1,0:T(8,128)S(1)} %get-tuple-element.18), channel_id=1, source_target_pairs={{8,0},{9,1},{10,2},{11,3},{4,8},{5,9},{6,10},{7,11},{12,4},{13,5},... | collective-permute-start | bytes 98312 | tf_op jit(solution)/shard_map/ppermute | solution.py:136
  19.9 0.0 collective-permute-start.6
  19.9 1.4 %collective-permute-start.7 = (f32[32,256]{1,0:T(8,128)S(1)}, f32[32,256]{1,0:T(8,128)S(1)}, u32[]{:S(2)}, u32[]{:S(2)}) collective-permute-start(f32[32,256]{1,0:T(8,128)S(1)} %get-tuple-element.20), channel_id=1, source_target_pairs={{0,2},{1,3},{2,0},{3,1},{4,6},{5,7},{6,4},{7,5},{8,10},{9,11},{10,... | collective-permute-start | bytes 98312 | tf_op jit(solution)/shard_map/ppermute | solution.py:139
  21.4 0.4 %collective-permute-start.8 = (f32[32,256]{1,0:T(8,128)S(1)}, f32[32,256]{1,0:T(8,128)S(1)}, u32[]{:S(2)}, u32[]{:S(2)}) collective-permute-start(f32[32,256]{1,0:T(8,128)S(1)} %get-tuple-element.21), channel_id=1, source_target_pairs={{0,1},{1,0},{2,3},{3,2},{4,5},{5,4},{6,7},{7,6},{8,9},{9,8},{10,11... | collective-permute-start | bytes 98312 | tf_op jit(solution)/shard_map/ppermute | solution.py:139
  21.8 0.2 copy-done
  22.0 0.9 %shard_map.39 = f32[32,256]{1,0:T(8,128)S(1)} custom-call(bf16[288,256]{1,0:T(8,128)(2,1)S(1)} %pad_maximum_fusion.refs_0_.refs_4_, bf16[288,256]{1,0:T(8,128)(2,1)S(1)} %collective-permute-done.refs_1_, bf16[288,256]{1,0:T(8,128)(2,1)S(1)} %collective-permute-done.1.refs_3_.refs_2_, bf16[288,256]{1,0:T(8,128)(2,1)S(1)} %collective-permute-done.2.refs_3_, ...), custom_call_target="tpu_custom_call" | custom-call | flops 167772160 | bytes 655360 | tf_op jit(solution)/shard_map/pallas_call | solution.py:110
  22.9 0.0 collective-permute-done.5
  22.9 0.7 %collective-permute-done.6 = f32[32,256]{1,0:T(8,128)S(1)} collective-permute-done((f32[32,256]{1,0:T(8,128)S(1)}, f32[32,256]{1,0:T(8,128)S(1)}, u32[]{:S(2)}, u32[]{:S(2)}) %collective-permute-start.6) | collective-permute-done | bytes 32800 | tf_op jit(solution)/shard_map/ppermute | solution.py:139
  23.6 0.6 %collective-permute-done.7 = f32[32,256]{1,0:T(8,128)S(1)} collective-permute-done((f32[32,256]{1,0:T(8,128)S(1)}, f32[32,256]{1,0:T(8,128)S(1)}, u32[]{:S(2)}, u32[]{:S(2)}) %collective-permute-start.7) | collective-permute-done | bytes 32800 | tf_op jit(solution)/shard_map/ppermute | solution.py:139
  24.3 0.0 collective-permute-done.8
  24.3 0.6 %add_bitcast_fusion = f32[256,32]{0,1:T(8,128)} fusion(f32[32,256]{1,0:T(8,128)S(1)} %shard_map.39, f32[32,256]{1,0:T(8,128)S(1)} %get-tuple-element.22, f32[32,256]{1,0:T(8,128)S(1)} %collective-permute-done.8, f32[32,256]{1,0:T(8,128)S(1)} %collective-permute-done.7, f32[32,256]{1,0:T(8,128)S(1)} %collective-permute-done.5, ...), kind=kLoop, calls=%fused_computation.1 | loop fusion | flops 40960 | bytes 229376 | tf_op jit(solution)/shard_map/transpose | solution.py:162
  (1 shorter events, 0.0 us)
Async XLA Ops:
  0.9 7.2 %collective-permute-start.1 = (bf16[288,256]{1,0:T(8,128)(2,1)S(1)}, bf16[288,256]{1,0:T(8,128)(2,1)S(1)}, u32[]{:S(2)}, u32[]{:S(2)}) collective-permute-start(bf16[288,256]{1,0:T(8,128)(2,1)S(1)} %pad_maximum_fusion.refs_0_.refs_4_), channel_id=1, source_target_pairs={{0,2},{1,3},{2,0},{3,1},{4,6},{5,7},{6,4},{7,5},{8,10},{9,11},{10,... | collective-permute-start | bytes 442376 | tf_op jit(solution)/shard_map/ppermute | solution.py:139
  4.0 4.2 %collective-permute-start = (bf16[288,256]{1,0:T(8,128)(2,1)S(1)}, bf16[288,256]{1,0:T(8,128)(2,1)S(1)}, u32[]{:S(2)}, u32[]{:S(2)}) collective-permute-start(bf16[288,256]{1,0:T(8,128)(2,1)S(1)} %pad_maximum_fusion.refs_0_.refs_4_), channel_id=1, source_target_pairs={{0,1},{1,0},{2,3},{3,2},{4,5},{5,4},{6,7},{7,6},{8,9},{9,8},{10,11... | collective-permute-start | bytes 442376 | tf_op jit(solution)/shard_map/ppermute | solution.py:139
  4.0 8.5 %collective-permute-start.3 = (bf16[288,256]{1,0:T(8,128)(2,1)S(1)}, bf16[288,256]{1,0:T(8,128)(2,1)S(1)}, u32[]{:S(2)}, u32[]{:S(2)}) collective-permute-start(bf16[288,256]{1,0:T(8,128)(2,1)S(1)} %pad_maximum_fusion.refs_0_.refs_4_), channel_id=1, source_target_pairs={{0,8},{1,9},{2,10},{3,11},{8,4},{9,5},{10,6},{11,7},{4,12},{5,13},... | collective-permute-start | bytes 442376 | tf_op jit(solution)/shard_map/ppermute | solution.py:136
  6.6 8.8 %collective-permute-start.4 = (bf16[288,256]{1,0:T(8,128)(2,1)S(1)}, bf16[288,256]{1,0:T(8,128)(2,1)S(1)}, u32[]{:S(2)}, u32[]{:S(2)}) collective-permute-start(bf16[288,256]{1,0:T(8,128)(2,1)S(1)} %pad_maximum_fusion.refs_0_.refs_4_), channel_id=1, source_target_pairs={{0,4},{1,5},{2,6},{3,7},{8,12},{9,13},{10,14},{11,15},{4,0},{5,1},... | collective-permute-start | bytes 442376 | tf_op jit(solution)/shard_map/ppermute | solution.py:136
  8.1 7.2 %collective-permute-start.2 = (bf16[288,256]{1,0:T(8,128)(2,1)S(1)}, bf16[288,256]{1,0:T(8,128)(2,1)S(1)}, u32[]{:S(2)}, u32[]{:S(2)}) collective-permute-start(bf16[288,256]{1,0:T(8,128)(2,1)S(1)} %collective-permute-done.1.refs_3_.refs_2_), channel_id=1, source_target_pairs={{0,1},{1,0},{2,3},{3,2},{4,5},{5,4},{6,7},{7,6},{8,9},{9,8},{10,11... | collective-permute-start | bytes 442376 | tf_op jit(solution)/shard_map/ppermute | solution.py:139
  16.6 6.3 %collective-permute-start.5 = (f32[32,256]{1,0:T(8,128)S(1)}, f32[32,256]{1,0:T(8,128)S(1)}, u32[]{:S(2)}, u32[]{:S(2)}) collective-permute-start(f32[32,256]{1,0:T(8,128)S(1)} %get-tuple-element.18), channel_id=1, source_target_pairs={{8,0},{9,1},{10,2},{11,3},{4,8},{5,9},{6,10},{7,11},{12,4},{13,5},... | collective-permute-start | bytes 98312 | tf_op jit(solution)/shard_map/ppermute | solution.py:136
  19.9 3.7 %collective-permute-start.6 = (f32[32,256]{1,0:T(8,128)S(1)}, f32[32,256]{1,0:T(8,128)S(1)}, u32[]{:S(2)}, u32[]{:S(2)}) collective-permute-start(f32[32,256]{1,0:T(8,128)S(1)} %get-tuple-element.19), channel_id=1, source_target_pairs={{0,3},{1,2},{2,1},{3,0},{4,7},{5,6},{6,5},{7,4},{8,11},{9,10},{10,... | collective-permute-start | bytes 98312 | tf_op jit(solution)/shard_map/ppermute | solution.py:139
  19.9 4.3 %collective-permute-start.7 = (f32[32,256]{1,0:T(8,128)S(1)}, f32[32,256]{1,0:T(8,128)S(1)}, u32[]{:S(2)}, u32[]{:S(2)}) collective-permute-start(f32[32,256]{1,0:T(8,128)S(1)} %get-tuple-element.20), channel_id=1, source_target_pairs={{0,2},{1,3},{2,0},{3,1},{4,6},{5,7},{6,4},{7,5},{8,10},{9,11},{10,... | collective-permute-start | bytes 98312 | tf_op jit(solution)/shard_map/ppermute | solution.py:139
  21.4 0.7 %copy-start = (f32[256]{0:T(256)S(1)}, f32[256]{0:T(256)}, u32[]{:S(2)}) copy-start(f32[256]{0:T(256)} %param.5) | copy-start | bytes 3076
  21.4 2.9 %collective-permute-start.8 = (f32[32,256]{1,0:T(8,128)S(1)}, f32[32,256]{1,0:T(8,128)S(1)}, u32[]{:S(2)}, u32[]{:S(2)}) collective-permute-start(f32[32,256]{1,0:T(8,128)S(1)} %get-tuple-element.21), channel_id=1, source_target_pairs={{0,1},{1,0},{2,3},{3,2},{4,5},{5,4},{6,7},{7,6},{8,9},{9,8},{10,11... | collective-permute-start | bytes 98312 | tf_op jit(solution)/shard_map/ppermute | solution.py:139

commit v14 on v8

--- a/solution.py
+++ b/solution.py
@@ -163,9 +163,9 @@
     last = [inner + place for place in range(len(one_way), len(cols))]
     order = [0] + passed + last + direct[:1] + first + direct[1:]
     backs, terms = tile(blocks, cols, order, kinds, shard)
-    sums = [along_outer(back, [(t, s) for s, t in edges]) for back, edges in zip(backs, one_way)]
-    sums += [in_plane(terms[step], [(t, s) for s, t in near(step)]) for step in range(inner - 1, 0, -1)]
     (own,), _ = tile(blocks, [packed], range(inner + 1), [("back",)], shard, noise=[noise_level[None, :]])
+    sums = [in_plane(terms[step], [(t, s) for s, t in near(step)]) for step in range(inner - 1, 0, -1)]
+    sums += [along_outer(back, [(t, s) for s, t in edges]) for back, edges in zip(backs, one_way)]
     return functools.reduce(lambda total, term: total + term, sums + list(terms[:1]) + [own]).T
 
 

time: 24 us -> 24.1 us (level)
    ppermute x3, waiting for transfers between devices: 6.03 us -> 7.34 us  [along_outer(): lax.ppermute(value, 'blk', [(s * inner + b, t * inner + b) for s, t in ed...]
    ppermute x6, waiting for transfers between devices: 1.17 us -> 0.04 us  [in_plane(): lax.ppermute(value, 'blk', [(a * inner + s, a * inner + t) for a in range...]
  transfers between devices with their start and end apart: 9 -> 9, of which waited for: 4 -> 3; matrix products, arithmetic and copies ran while one was open for 0% -> 0% of each run, Pallas kernels for 4% -> 4%
where the time goes in v14:
time: 24.1 us; the launch traced here: 23.9 us
  starting transfers between devices  12.1 us (50%)
  waiting for transfers between devices  7.37 us (31%)
  Pallas kernels  2.82 us (12%)
  other arithmetic  1.56 us (6%)
    ppermute x3, waiting for transfers between devices, along_outer(): lax.ppermute(value, 'blk', [(s * inner + b, t * inner + b) for s, t in ed...  7.34 us
    ppermute x3, starting transfers between devices, along_outer(): lax.ppermute(value, 'blk', [(s * inner + b, t * inner + b) for s, t in ed...  6.96 us
    ppermute x6, starting transfers between devices, in_plane(): lax.ppermute(value, 'blk', [(a * inner + s, a * inner + t) for a in range...  5.16 us
    pallas_call x2, Pallas kernels, tile(): pl.pallas_call(functools.partial(tile_kernel, (len(rows), len(cols)), [li...  2.82 us
    concatenate x1, other arithmetic, on_device(): packed = jnp.concatenate([features, probes.T], axis=0)  0.93 us
    transpose x1, other arithmetic, on_device(): functools.reduce(lambda total, term: total + term, sums + list(terms[:1])...  0.63 us
  transfers between devices with their start and end apart: 9, of which 3 were waited for; matrix products, arithmetic and copies ran while one was open for 0% of the time, Pallas kernels for 4%

profile of v14, /device:TPU:0, one launch (start us, length us, event | category | flops | bytes accessed | tf_op | source)
XLA Modules:
  0.0 23.9 jit_solution(10656250101687729553)
XLA Ops:
  0.0 0.9 %pad_maximum_fusion.refs_0_.refs_4_ = bf16[288,256]{1,0:T(8,128)(2,1)S(1)} fusion(bf16[32,256]{1,0:T(8,128)(2,1)} %bitcast.5, bf16[256,256]{1,0:T(8,128)(2,1)} %param.3), kind=kLoop, calls=%fused_computation | loop fusion | flops 294912 | bytes 294912 | tf_op jit(solution)/shard_map/concatenate | solution.py:144
  0.9 3.0 %collective-permute-start = (bf16[288,256]{1,0:T(8,128)(2,1)S(1)}, bf16[288,256]{1,0:T(8,128)(2,1)S(1)}, u32[]{:S(2)}, u32[]{:S(2)}) collective-permute-start(bf16[288,256]{1,0:T(8,128)(2,1)S(1)} %pad_maximum_fusion.refs_0_.refs_4_), channel_id=1, source_target_pairs={{0,2},{1,3},{2,0},{3,1},{4,6},{5,7},{6,4},{7,5},{8,10},{9,11},{10,... | collective-permute-start | bytes 442376 | tf_op jit(solution)/shard_map/ppermute | solution.py:150
  4.0 2.6 %collective-permute-start.4 = (bf16[288,256]{1,0:T(8,128)(2,1)S(1)}, bf16[288,256]{1,0:T(8,128)(2,1)S(1)}, u32[]{:S(2)}, u32[]{:S(2)}) collective-permute-start(bf16[288,256]{1,0:T(8,128)(2,1)S(1)} %pad_maximum_fusion.refs_0_.refs_4_), channel_id=1, source_target_pairs={{0,8},{1,9},{2,10},{3,11},{8,4},{9,5},{10,6},{11,7},{4,12},{5,13},... | collective-permute-start | bytes 442376 | tf_op jit(solution)/shard_map/ppermute | solution.py:147
  6.6 0.0 collective-permute-start.3
  6.6 1.6 %collective-permute-start.2 = (bf16[288,256]{1,0:T(8,128)(2,1)S(1)}, bf16[288,256]{1,0:T(8,128)(2,1)S(1)}, u32[]{:S(2)}, u32[]{:S(2)}) collective-permute-start(bf16[288,256]{1,0:T(8,128)(2,1)S(1)} %pad_maximum_fusion.refs_0_.refs_4_), channel_id=1, source_target_pairs={{0,4},{1,5},{2,6},{3,7},{8,12},{9,13},{10,14},{11,15},{4,0},{5,1},... | collective-permute-start | bytes 442376 | tf_op jit(solution)/shard_map/ppermute | solution.py:147
  8.1 0.0 collective-permute-done.refs_5_.refs_2_
  8.1 0.2 collective-permute-start.1
  8.4 4.2 %collective-permute-done.4.refs_4_ = bf16[288,256]{1,0:T(8,128)(2,1)S(1)} collective-permute-done((bf16[288,256]{1,0:T(8,128)(2,1)S(1)}, bf16[288,256]{1,0:T(8,128)(2,1)S(1)}, u32[]{:S(2)}, u32[]{:S(2)}) %collective-permute-start.4) | collective-permute-done | bytes 147488 | tf_op jit(solution)/shard_map/ppermute | solution.py:147
  12.5 0.0 collective-permute-done.3.refs_3_.refs_1_
  12.5 1.9 %collective-permute-done.2.refs_2_ = bf16[288,256]{1,0:T(8,128)(2,1)S(1)} collective-permute-done((bf16[288,256]{1,0:T(8,128)(2,1)S(1)}, bf16[288,256]{1,0:T(8,128)(2,1)S(1)}, u32[]{:S(2)}, u32[]{:S(2)}) %collective-permute-start.2) | collective-permute-done | bytes 147488 | tf_op jit(solution)/shard_map/ppermute | solution.py:147
  14.4 0.0 collective-permute-done.1.refs_1_.refs_3_
  14.4 1.8 %shard_map.37 = (f32[32,256]{1,0:T(8,128)S(1)}, f32[32,256]{1,0:T(8,128)S(1)}, f32[32,256]{1,0:T(8,128)S(1)}, f32[32,256]{1,0:T(8,128)S(1)}, f32[32,256]{1,0:T(8,128)S(1)}) custom-call(bf16[288,256]{1,0:T(8,128)(2,1)S(1)} %pad_maximum_fusion.refs_0_.refs_4_, bf16[288,256]{1,0:T(8,128)(2,1)S(1)} %collective-permute-done.1.refs_1_.refs_3_, ...), custom_call_target="tpu_custom_call" | custom-call | flops 335544320 | bytes 786432 | tf_op jit(solution)/shard_map/pallas_call | solution.py:117
  16.2 0.2 collective-permute-start.5
  16.4 1.5 %collective-permute-start.6 = (f32[32,256]{1,0:T(8,128)S(1)}, f32[32,256]{1,0:T(8,128)S(1)}, u32[]{:S(2)}, u32[]{:S(2)}) collective-permute-start(f32[32,256]{1,0:T(8,128)S(1)} %get-tuple-element.11), channel_id=1, source_target_pairs={{0,2},{1,3},{2,0},{3,1},{4,6},{5,7},{6,4},{7,5},{8,10},{9,11},{10,... | collective-permute-start | bytes 98312 | tf_op jit(solution)/shard_map/ppermute | solution.py:150
  17.9 0.2 collective-permute-start.7
  18.1 0.0 copy-start
  18.1 2.8 %collective-permute-start.8 = (f32[32,256]{1,0:T(8,128)S(1)}, f32[32,256]{1,0:T(8,128)S(1)}, u32[]{:S(2)}, u32[]{:S(2)}) collective-permute-start(f32[32,256]{1,0:T(8,128)S(1)} %get-tuple-element.13), channel_id=1, source_target_pairs={{8,0},{9,1},{10,2},{11,3},{4,8},{5,9},{6,10},{7,11},{12,4},{13,5},... | collective-permute-start | bytes 98312 | tf_op jit(solution)/shard_map/ppermute | solution.py:147
  20.9 0.0 copy-done
  20.9 1.0 %shard_map.38 = f32[32,256]{1,0:T(8,128)S(1)} custom-call(bf16[288,256]{1,0:T(8,128)(2,1)S(1)} %pad_maximum_fusion.refs_0_.refs_4_, bf16[288,256]{1,0:T(8,128)(2,1)S(1)} %collective-permute-done.3.refs_3_.refs_1_, bf16[288,256]{1,0:T(8,128)(2,1)S(1)} %collective-permute-done.refs_5_.refs_2_, bf16[288,256]{1,0:T(8,128)(2,1)S(1)} %collective-permute-done.1.refs_1_.refs_3_, ...), custom_call_target="tpu_custom_call" | custom-call | flops 167772160 | bytes 655360 | tf_op jit(solution)/shard_map/pallas_call | solution.py:117
  21.9 0.0 collective-permute-done.5
  21.9 0.0 collective-permute-done.6
  22.0 0.0 collective-permute-done.7
  22.0 1.3 %collective-permute-done.8 = f32[32,256]{1,0:T(8,128)S(1)} collective-permute-done((f32[32,256]{1,0:T(8,128)S(1)}, f32[32,256]{1,0:T(8,128)S(1)}, u32[]{:S(2)}, u32[]{:S(2)}) %collective-permute-start.8) | collective-permute-done | bytes 32800 | tf_op jit(solution)/shard_map/ppermute | solution.py:147
  23.3 0.6 %add_bitcast_fusion = f32[256,32]{0,1:T(8,128)} fusion(f32[32,256]{1,0:T(8,128)S(1)} %shard_map.38, f32[32,256]{1,0:T(8,128)S(1)} %get-tuple-element.14, f32[32,256]{1,0:T(8,128)S(1)} %collective-permute-done.8, f32[32,256]{1,0:T(8,128)S(1)} %collective-permute-done.7, f32[32,256]{1,0:T(8,128)S(1)} %collective-permute-done.5, ...), kind=kLoop, calls=%fused_computation.1 | loop fusion | flops 40960 | bytes 229376 | tf_op jit(solution)/shard_map/transpose | solution.py:169
Async XLA Ops:
  0.9 7.2 %collective-permute-start = (bf16[288,256]{1,0:T(8,128)(2,1)S(1)}, bf16[288,256]{1,0:T(8,128)(2,1)S(1)}, u32[]{:S(2)}, u32[]{:S(2)}) collective-permute-start(bf16[288,256]{1,0:T(8,128)(2,1)S(1)} %pad_maximum_fusion.refs_0_.refs_4_), channel_id=1, source_target_pairs={{0,2},{1,3},{2,0},{3,1},{4,6},{5,7},{6,4},{7,5},{8,10},{9,11},{10,... | collective-permute-start | bytes 442376 | tf_op jit(solution)/shard_map/ppermute | solution.py:150
  4.0 8.6 %collective-permute-start.4 = (bf16[288,256]{1,0:T(8,128)(2,1)S(1)}, bf16[288,256]{1,0:T(8,128)(2,1)S(1)}, u32[]{:S(2)}, u32[]{:S(2)}) collective-permute-start(bf16[288,256]{1,0:T(8,128)(2,1)S(1)} %pad_maximum_fusion.refs_0_.refs_4_), channel_id=1, source_target_pairs={{0,8},{1,9},{2,10},{3,11},{8,4},{9,5},{10,6},{11,7},{4,12},{5,13},... | collective-permute-start | bytes 442376 | tf_op jit(solution)/shard_map/ppermute | solution.py:147
  6.6 6.0 %collective-permute-start.3 = (bf16[288,256]{1,0:T(8,128)(2,1)S(1)}, bf16[288,256]{1,0:T(8,128)(2,1)S(1)}, u32[]{:S(2)}, u32[]{:S(2)}) collective-permute-start(bf16[288,256]{1,0:T(8,128)(2,1)S(1)} %pad_maximum_fusion.refs_0_.refs_4_), channel_id=1, source_target_pairs={{0,1},{1,0},{2,3},{3,2},{4,5},{5,4},{6,7},{7,6},{8,9},{9,8},{10,11... | collective-permute-start | bytes 442376 | tf_op jit(solution)/shard_map/ppermute | solution.py:150
  6.6 7.8 %collective-permute-start.2 = (bf16[288,256]{1,0:T(8,128)(2,1)S(1)}, bf16[288,256]{1,0:T(8,128)(2,1)S(1)}, u32[]{:S(2)}, u32[]{:S(2)}) collective-permute-start(bf16[288,256]{1,0:T(8,128)(2,1)S(1)} %pad_maximum_fusion.refs_0_.refs_4_), channel_id=1, source_target_pairs={{0,4},{1,5},{2,6},{3,7},{8,12},{9,13},{10,14},{11,15},{4,0},{5,1},... | collective-permute-start | bytes 442376 | tf_op jit(solution)/shard_map/ppermute | solution.py:147
  8.1 6.3 %collective-permute-start.1 = (bf16[288,256]{1,0:T(8,128)(2,1)S(1)}, bf16[288,256]{1,0:T(8,128)(2,1)S(1)}, u32[]{:S(2)}, u32[]{:S(2)}) collective-permute-start(bf16[288,256]{1,0:T(8,128)(2,1)S(1)} %collective-permute-done.refs_5_.refs_2_), channel_id=1, source_target_pairs={{0,1},{1,0},{2,3},{3,2},{4,5},{5,4},{6,7},{7,6},{8,9},{9,8},{10,11... | collective-permute-start | bytes 442376 | tf_op jit(solution)/shard_map/ppermute | solution.py:150
  16.2 5.7 %collective-permute-start.5 = (f32[32,256]{1,0:T(8,128)S(1)}, f32[32,256]{1,0:T(8,128)S(1)}, u32[]{:S(2)}, u32[]{:S(2)}) collective-permute-start(f32[32,256]{1,0:T(8,128)S(1)} %get-tuple-element.10), channel_id=1, source_target_pairs={{0,3},{1,2},{2,1},{3,0},{4,7},{5,6},{6,5},{7,4},{8,11},{9,10},{10,... | collective-permute-start | bytes 98312 | tf_op jit(solution)/shard_map/ppermute | solution.py:150
  16.4 5.5 %collective-permute-start.6 = (f32[32,256]{1,0:T(8,128)S(1)}, f32[32,256]{1,0:T(8,128)S(1)}, u32[]{:S(2)}, u32[]{:S(2)}) collective-permute-start(f32[32,256]{1,0:T(8,128)S(1)} %get-tuple-element.11), channel_id=1, source_target_pairs={{0,2},{1,3},{2,0},{3,1},{4,6},{5,7},{6,4},{7,5},{8,10},{9,11},{10,... | collective-permute-start | bytes 98312 | tf_op jit(solution)/shard_map/ppermute | solution.py:150
  17.9 4.1 %collective-permute-start.7 = (f32[32,256]{1,0:T(8,128)S(1)}, f32[32,256]{1,0:T(8,128)S(1)}, u32[]{:S(2)}, u32[]{:S(2)}) collective-permute-start(f32[32,256]{1,0:T(8,128)S(1)} %get-tuple-element.12), channel_id=1, source_target_pairs={{0,1},{1,0},{2,3},{3,2},{4,5},{5,4},{6,7},{7,6},{8,9},{9,8},{10,11... | collective-permute-start | bytes 98312 | tf_op jit(solution)/shard_map/ppermute | solution.py:150
  18.1 2.8 %copy-start = (f32[256]{0:T(256)S(1)}, f32[256]{0:T(256)}, u32[]{:S(2)}) copy-start(f32[256]{0:T(256)} %param.5) | copy-start | bytes 3076
  18.1 5.2 %collective-permute-start.8 = (f32[32,256]{1,0:T(8,128)S(1)}, f32[32,256]{1,0:T(8,128)S(1)}, u32[]{:S(2)}, u32[]{:S(2)}) collective-permute-start(f32[32,256]{1,0:T(8,128)S(1)} %get-tuple-element.13), channel_id=1, source_target_pairs={{8,0},{9,1},{10,2},{11,3},{4,8},{5,9},{6,10},{7,11},{12,4},{13,5},... | collective-permute-start | bytes 98312 | tf_op jit(solution)/shard_map/ppermute | solution.py:147

commit v15 on v11

--- a/solution.py
+++ b/solution.py
@@ -41,7 +41,7 @@
     bits = count.bit_length() - 1
     order = list(range(count))
     if count == 1 << bits:
-        order = [int(f"{a:0{bits}b}"[::-1], 2) if bits else a for a in order]
+        order = [int(f"{a:0{bits}b}"[::-1], 2) if bits else a for a in reversed(order)]
     shifts = [[(order[p], order[(p + step) % count]) for p in range(count)] for step in range(1, count // 2 + 1)]
     if count % 2:
         return shifts, []
@@ -100,7 +100,7 @@
         ref[...] = sums[name]
 
 
-def tile(rows, cols, order, pairs, sums, shard, vectors, noise=()):
+def tile(rows, cols, order, pairs, sums, shard, vectors, noise=(), work=1.0):
     blocks = [*rows, *cols]
     args = [*[blocks[place] for place in order], *noise, *sums.values()]
     elements = len(pairs) * shard * shard
@@ -116,12 +116,28 @@
         out_specs=[whole] * len(names),
         compiler_params=pltpu.CompilerParams(vmem_limit_bytes=32 * 1024 * 1024),
         cost_estimate=pl.CostEstimate(
-            flops=2 * elements * (width + 2 * vectors),
-            bytes_accessed=2 * width * shard * len(blocks),
-            transcendentals=2 * elements,
+            flops=int(work * 2 * elements * (width + 2 * vectors)),
+            bytes_accessed=int(work * 2 * width * shard * len(blocks)),
+            transcendentals=int(work * 2 * elements),
         ),
     )(*args)
     return dict(zip(names, found))
+
+
+def copy_kernel(from_ref, to_ref):
+    to_ref[0 : from_ref.shape[0], :] = from_ref[...]
+    to_ref[from_ref.shape[0] :, :] = jnp.zeros((to_ref.shape[0] - from_ref.shape[0], to_ref.shape[1]), to_ref.dtype)
+
+
+def copy_rows(value, rows):
+    whole = pl.BlockSpec(memory_space=pltpu.VMEM)
+    return pl.pallas_call(
+        copy_kernel,
+        out_shape=jax.ShapeDtypeStruct((rows, value.shape[1]), value.dtype),
+        in_specs=[whole],
+        out_specs=whole,
+        compiler_params=pltpu.CompilerParams(vmem_limit_bytes=32 * 1024 * 1024),
+    )(value)
 
 
 def on_device(features, probes, noise_level):
@@ -142,15 +158,16 @@
         return [(plane_target(b, step, inner), b) for b in range(inner)]
 
     one_way, exchanges = outer_maps(outer)
-    cols = [along_outer(packed, edges) for edges in one_way]
-    others = [along_outer(packed, edges) for edges in exchanges]
+    longer = copy_rows(packed, shard + vectors + 16)
+    cols = [along_outer(longer, edges) for edges in one_way]
+    others = [along_outer(longer, edges) for edges in exchanges]
     blocks = plane_blocks(packed, inner, in_plane)
     direct = [step for step in range(1, inner) if step & (step - 1) == 0]
     passed = [step for step in range(1, inner) if step & (step - 1)]
 
     order = [0] + passed + [inner + place for place in range(len(cols))] + direct
     pairs = [(row, col, ("rows", "back")) for col in range(len(cols)) for row in range(inner)]
-    sums = tile(blocks, cols, order, pairs, {}, shard, vectors)
+    sums = tile(blocks, cols, order, pairs, {}, shard, vectors, work=0.0)
     backs = [sums.pop(("back", place)) for place in range(len(cols))]
     pairs = [(row, col, ("rows",)) for col in range(len(others)) for row in range(inner)]
     sums = tile(blocks, others, range(inner + len(others)), pairs, sums, shard, vectors)
@@ -159,9 +176,8 @@
 
     total = [own["back", 0]]
     total += [in_plane(sums["rows", step], [(t, s) for s, t in near(step)]) for step in range(1, inner)]
-    total += [sums["rows", 0]]
     total += [along_outer(back, [(t, s) for s, t in edges]) for back, edges in zip(backs, one_way)]
-    return functools.reduce(lambda sofar, term: sofar + term, total).T
+    return functools.reduce(lambda sofar, term: sofar + term, total + [sums["rows", 0]]).T
 
 
 def solution(mesh):

time: 24.1 us -> 22.4 us (0.929)
  starting transfers between devices: 15 us -> 10.4 us
  waiting for transfers between devices: 4.3 us -> 7.19 us
    ppermute x3, starting transfers between devices: 10.1 us -> 5.2 us  [along_outer(): lax.ppermute(value, 'blk', [(s * inner + b, t * inner + b) for s, t in ed...]
    ppermute x3, waiting for transfers between devices: 1.66 us -> 5.38 us  [along_outer(): lax.ppermute(value, 'blk', [(s * inner + b, t * inner + b) for s, t in ed...]
    ppermute x6, waiting for transfers between devices: 2.65 us -> 1.82 us  [in_plane(): lax.ppermute(value, 'blk', [(a * inner + s, a * inner + t) for a in range...]
    ppermute x6, starting transfers between devices: 4.91 us -> 5.24 us  [in_plane(): lax.ppermute(value, 'blk', [(a * inner + s, a * inner + t) for a in range...]
  transfers between devices with their start and end apart: 9 -> 9, of which waited for: 4 -> 6; matrix products, arithmetic and copies ran while one was open for 0% -> 0% of each run, Pallas kernels for 12% -> 13%
where the time goes in v15:
time: 22.4 us; the launch traced here: 22.1 us
  starting transfers between devices  10.4 us (46%)
  waiting for transfers between devices  7.19 us (32%)
  Pallas kernels  2.91 us (13%)
  other arithmetic  1.56 us (7%)
    ppermute x3, waiting for transfers between devices, along_outer(): lax.ppermute(value, 'blk', [(s * inner + b, t * inner + b) for s, t in ed...  5.38 us
    ppermute x6, starting transfers between devices, in_plane(): lax.ppermute(value, 'blk', [(a * inner + s, a * inner + t) for a in range...  5.24 us
    ppermute x3, starting transfers between devices, along_outer(): lax.ppermute(value, 'blk', [(s * inner + b, t * inner + b) for s, t in ed...  5.2 us
    pallas_call x3, Pallas kernels, tile(): pl.pallas_call(functools.partial(tile_kernel, list(order), tuple(pairs),...  2.9 us
    ppermute x6, waiting for transfers between devices, in_plane(): lax.ppermute(value, 'blk', [(a * inner + s, a * inner + t) for a in range...  1.82 us
    concatenate x1, other arithmetic, on_device(): packed = jnp.concatenate([features, probes.T], axis=0)  0.93 us
    transpose x1, other arithmetic, on_device(): functools.reduce(lambda sofar, term: sofar + term, total + [sums['rows',...  0.63 us
  transfers between devices with their start and end apart: 9, of which 6 were waited for; matrix products, arithmetic and copies ran while one was open for 0% of the time, Pallas kernels for 13%

profile of v15, /device:TPU:0, one launch (start us, length us, event | category | flops | bytes accessed | tf_op | source)
XLA Modules:
  0.0 22.1 jit_solution(13630678505228955272)
XLA Ops:
  0.0 0.9 %pad_maximum_fusion.refs_0_.refs_4_.from_ref = bf16[288,256]{1,0:T(8,128)(2,1)S(1)} fusion(bf16[32,256]{1,0:T(8,128)(2,1)} %bitcast.5, bf16[256,256]{1,0:T(8,128)(2,1)} %param.3), kind=kLoop, calls=%fused_computation | loop fusion | flops 294912 | bytes 294912 | tf_op jit(solution)/shard_map/concatenate | solution.py:149
  0.9 3.0 %collective-permute-start.1 = (bf16[288,256]{1,0:T(8,128)(2,1)S(1)}, bf16[288,256]{1,0:T(8,128)(2,1)S(1)}, u32[]{:S(2)}, u32[]{:S(2)}) collective-permute-start(bf16[288,256]{1,0:T(8,128)(2,1)S(1)} %pad_maximum_fusion.refs_0_.refs_4_.from_ref), channel_id=1, source_target_pairs={{0,2},{1,3},{2,0},{3,1},{4,6},{5,7},{6,4},{7,5},{8,10},{9,11},{10,... | collective-permute-start | bytes 442376 | tf_op jit(solution)/shard_map/ppermute | solution.py:155
  4.0 3.7 %collective-permute-start.4 = (bf16[304,256]{1,0:T(8,128)(2,1)S(1)}, bf16[304,256]{1,0:T(8,128)(2,1)S(1)}, u32[]{:S(2)}, u32[]{:S(2)}) collective-permute-start(bf16[304,256]{1,0:T(8,128)(2,1)S(1)} %shard_map.38), channel_id=1, source_target_pairs={{12,4},{13,5},{14,6},{15,7},{4,8},{5,9},{6,10},{7,11},{8,0},{9,1},... | collective-permute-start | bytes 466952 | tf_op jit(solution)/shard_map/ppermute | solution.py:152
  7.6 0.0 collective-permute-start.3
  7.6 0.0 collective-permute-start
  7.6 0.2 collective-permute-done.1.refs_2_.refs_4_
  7.8 0.3 %collective-permute-start.2 = (bf16[288,256]{1,0:T(8,128)(2,1)S(1)}, bf16[288,256]{1,0:T(8,128)(2,1)S(1)}, u32[]{:S(2)}, u32[]{:S(2)}) collective-permute-start(bf16[288,256]{1,0:T(8,128)(2,1)S(1)} %collective-permute-done.1.refs_2_.refs_4_), channel_id=1, source_target_pairs={{0,1},{1,0},{2,3},{3,2},{4,5},{5,4},{6,7},{7,6},{8,9},{9,8},{10,11... | collective-permute-start | bytes 442376 | tf_op jit(solution)/shard_map/ppermute | solution.py:155
  8.2 0.9 %collective-permute-done.refs_1_.refs_3_ = bf16[288,256]{1,0:T(8,128)(2,1)S(1)} collective-permute-done((bf16[288,256]{1,0:T(8,128)(2,1)S(1)}, bf16[288,256]{1,0:T(8,128)(2,1)S(1)}, u32[]{:S(2)}, u32[]{:S(2)}) %collective-permute-start) | collective-permute-done | bytes 147488 | tf_op jit(solution)/shard_map/ppermute | solution.py:155
  9.0 4.8 %collective-permute-done.4.refs_2_ = bf16[304,256]{1,0:T(8,128)(2,1)S(1)} collective-permute-done((bf16[304,256]{1,0:T(8,128)(2,1)S(1)}, bf16[304,256]{1,0:T(8,128)(2,1)S(1)}, u32[]{:S(2)}, u32[]{:S(2)}) %collective-permute-start.4) | collective-permute-done | bytes 155680 | tf_op jit(solution)/shard_map/ppermute | solution.py:152
  13.9 0.0 collective-permute-done.2.refs_3_.refs_1_
  13.9 1.1 %shard_map.39 = (f32[32,256]{1,0:T(8,128)S(1)}, f32[32,256]{1,0:T(8,128)S(1)}, f32[32,256]{1,0:T(8,128)S(1)}, f32[32,256]{1,0:T(8,128)S(1)}, f32[32,256]{1,0:T(8,128)S(1)}) custom-call(bf16[288,256]{1,0:T(8,128)(2,1)S(1)} %pad_maximum_fusion.refs_0_.refs_4_.from_ref, bf16[288,256]{1,0:T(8,128)(2,1)S(1)} %collective-permute-done.2.refs_3_.refs_1_, ...), custom_call_target="tpu_custom_call" | custom-call | tf_op jit(solution)/shard_map/pallas_call | solution.py:110
  15.0 1.5 %collective-permute-start.8 = (f32[32,256]{1,0:T(8,128)S(1)}, f32[32,256]{1,0:T(8,128)S(1)}, u32[]{:S(2)}, u32[]{:S(2)}) collective-permute-start(f32[32,256]{1,0:T(8,128)S(1)} %get-tuple-element.21), channel_id=1, source_target_pairs={{4,12},{5,13},{6,14},{7,15},{8,4},{9,5},{10,6},{11,7},{0,8},{1,9},... | collective-permute-start | bytes 98312 | tf_op jit(solution)/shard_map/ppermute | solution.py:152
  16.5 0.0 collective-permute-done.3.refs_4_
  16.5 0.9 %shard_map.40 = (f32[32,256]{1,0:T(8,128)S(1)}, f32[32,256]{1,0:T(8,128)S(1)}, f32[32,256]{1,0:T(8,128)S(1)}, f32[32,256]{1,0:T(8,128)S(1)}) custom-call(bf16[288,256]{1,0:T(8,128)(2,1)S(1)} %pad_maximum_fusion.refs_0_.refs_4_.from_ref, bf16[288,256]{1,0:T(8,128)(2,1)S(1)} %collective-permute-done.refs_1_.refs_3_, ...), custom_call_target="tpu_custom_call" | custom-call | flops 167772160 | bytes 655360 | tf_op jit(solution)/shard_map/pallas_call | solution.py:110
  17.4 0.0 collective-permute-start.7
  17.5 0.6 %collective-permute-start.6 = (f32[32,256]{1,0:T(8,128)S(1)}, f32[32,256]{1,0:T(8,128)S(1)}, u32[]{:S(2)}, u32[]{:S(2)}) collective-permute-start(f32[32,256]{1,0:T(8,128)S(1)} %get-tuple-element.19), channel_id=1, source_target_pairs={{0,2},{1,3},{2,0},{3,1},{4,6},{5,7},{6,4},{7,5},{8,10},{9,11},{10,... | collective-permute-start | bytes 98312 | tf_op jit(solution)/shard_map/ppermute | solution.py:155
  18.0 1.3 %collective-permute-start.5 = (f32[32,256]{1,0:T(8,128)S(1)}, f32[32,256]{1,0:T(8,128)S(1)}, u32[]{:S(2)}, u32[]{:S(2)}) collective-permute-start(f32[32,256]{1,0:T(8,128)S(1)} %get-tuple-element.18), channel_id=1, source_target_pairs={{0,1},{1,0},{2,3},{3,2},{4,5},{5,4},{6,7},{7,6},{8,9},{9,8},{10,11... | collective-permute-start | bytes 98312 | tf_op jit(solution)/shard_map/ppermute | solution.py:155
  19.3 0.0 copy-done
  19.3 0.9 %shard_map.37 = f32[32,256]{1,0:T(8,128)S(1)} custom-call(bf16[288,256]{1,0:T(8,128)(2,1)S(1)} %pad_maximum_fusion.refs_0_.refs_4_.from_ref, bf16[288,256]{1,0:T(8,128)(2,1)S(1)} %collective-permute-done.refs_1_.refs_3_, bf16[288,256]{1,0:T(8,128)(2,1)S(1)} %collective-permute-done.1.refs_2_.refs_4_, ...), custom_call_target="tpu_custom_call" | custom-call | flops 167772160 | bytes 655360 | tf_op jit(solution)/shard_map/pallas_call | solution.py:110
  20.2 0.5 %collective-permute-done.8 = f32[32,256]{1,0:T(8,128)S(1)} collective-permute-done((f32[32,256]{1,0:T(8,128)S(1)}, f32[32,256]{1,0:T(8,128)S(1)}, u32[]{:S(2)}, u32[]{:S(2)}) %collective-permute-start.8) | collective-permute-done | bytes 32800 | tf_op jit(solution)/shard_map/ppermute | solution.py:152
  20.7 0.1 collective-permute-done.7
  20.8 0.7 %collective-permute-done.6 = f32[32,256]{1,0:T(8,128)S(1)} collective-permute-done((f32[32,256]{1,0:T(8,128)S(1)}, f32[32,256]{1,0:T(8,128)S(1)}, u32[]{:S(2)}, u32[]{:S(2)}) %collective-permute-start.6) | collective-permute-done | bytes 32800 | tf_op jit(solution)/shard_map/ppermute | solution.py:155
  21.5 0.0 collective-permute-done.5
  21.5 0.6 %add_bitcast_fusion = f32[256,32]{0,1:T(8,128)} fusion(f32[32,256]{1,0:T(8,128)S(1)} %get-tuple-element.22, f32[32,256]{1,0:T(8,128)S(1)} %collective-permute-done.8, f32[32,256]{1,0:T(8,128)S(1)} %collective-permute-done.7, f32[32,256]{1,0:T(8,128)S(1)} %collective-permute-done.6, f32[32,256]{1,0:T(8,128)S(1)} %shard_map.37, ...), kind=kLoop, calls=%fused_computation.1 | loop fusion | flops 40960 | bytes 229376 | tf_op jit(solution)/shard_map/transpose | solution.py:180
  (2 shorter events, 0.0 us)
Async XLA Ops:
  0.9 6.9 %collective-permute-start.1 = (bf16[288,256]{1,0:T(8,128)(2,1)S(1)}, bf16[288,256]{1,0:T(8,128)(2,1)S(1)}, u32[]{:S(2)}, u32[]{:S(2)}) collective-permute-start(bf16[288,256]{1,0:T(8,128)(2,1)S(1)} %pad_maximum_fusion.refs_0_.refs_4_.from_ref), channel_id=1, source_target_pairs={{0,2},{1,3},{2,0},{3,1},{4,6},{5,7},{6,4},{7,5},{8,10},{9,11},{10,... | collective-permute-start | bytes 442376 | tf_op jit(solution)/shard_map/ppermute | solution.py:155
  4.0 9.9 %collective-permute-start.4 = (bf16[304,256]{1,0:T(8,128)(2,1)S(1)}, bf16[304,256]{1,0:T(8,128)(2,1)S(1)}, u32[]{:S(2)}, u32[]{:S(2)}) collective-permute-start(bf16[304,256]{1,0:T(8,128)(2,1)S(1)} %shard_map.38), channel_id=1, source_target_pairs={{12,4},{13,5},{14,6},{15,7},{4,8},{5,9},{6,10},{7,11},{8,0},{9,1},... | collective-permute-start | bytes 466952 | tf_op jit(solution)/shard_map/ppermute | solution.py:152
  7.6 8.9 %collective-permute-start.3 = (bf16[304,256]{1,0:T(8,128)(2,1)S(1)}, bf16[304,256]{1,0:T(8,128)(2,1)S(1)}, u32[]{:S(2)}, u32[]{:S(2)}) collective-permute-start(bf16[304,256]{1,0:T(8,128)(2,1)S(1)} %shard_map.38), channel_id=1, source_target_pairs={{12,8},{13,9},{14,10},{15,11},{4,0},{5,1},{6,2},{7,3},{8,12},{9,13... | collective-permute-start | bytes 466952 | tf_op jit(solution)/shard_map/ppermute | solution.py:152
  7.6 1.4 %collective-permute-start = (bf16[288,256]{1,0:T(8,128)(2,1)S(1)}, bf16[288,256]{1,0:T(8,128)(2,1)S(1)}, u32[]{:S(2)}, u32[]{:S(2)}) collective-permute-start(bf16[288,256]{1,0:T(8,128)(2,1)S(1)} %pad_maximum_fusion.refs_0_.refs_4_.from_ref), channel_id=1, source_target_pairs={{0,1},{1,0},{2,3},{3,2},{4,5},{5,4},{6,7},{7,6},{8,9},{9,8},{10,11... | collective-permute-start | bytes 442376 | tf_op jit(solution)/shard_map/ppermute | solution.py:155
  7.8 6.0 %collective-permute-start.2 = (bf16[288,256]{1,0:T(8,128)(2,1)S(1)}, bf16[288,256]{1,0:T(8,128)(2,1)S(1)}, u32[]{:S(2)}, u32[]{:S(2)}) collective-permute-start(bf16[288,256]{1,0:T(8,128)(2,1)S(1)} %collective-permute-done.1.refs_2_.refs_4_), channel_id=1, source_target_pairs={{0,1},{1,0},{2,3},{3,2},{4,5},{5,4},{6,7},{7,6},{8,9},{9,8},{10,11... | collective-permute-start | bytes 442376 | tf_op jit(solution)/shard_map/ppermute | solution.py:155
  15.0 5.7 %collective-permute-start.8 = (f32[32,256]{1,0:T(8,128)S(1)}, f32[32,256]{1,0:T(8,128)S(1)}, u32[]{:S(2)}, u32[]{:S(2)}) collective-permute-start(f32[32,256]{1,0:T(8,128)S(1)} %get-tuple-element.21), channel_id=1, source_target_pairs={{4,12},{5,13},{6,14},{7,15},{8,4},{9,5},{10,6},{11,7},{0,8},{1,9},... | collective-permute-start | bytes 98312 | tf_op jit(solution)/shard_map/ppermute | solution.py:152
  17.4 3.4 %collective-permute-start.7 = (f32[32,256]{1,0:T(8,128)S(1)}, f32[32,256]{1,0:T(8,128)S(1)}, u32[]{:S(2)}, u32[]{:S(2)}) collective-permute-start(f32[32,256]{1,0:T(8,128)S(1)} %get-tuple-element.20), channel_id=1, source_target_pairs={{0,3},{1,2},{2,1},{3,0},{4,7},{5,6},{6,5},{7,4},{8,11},{9,10},{10,... | collective-permute-start | bytes 98312 | tf_op jit(solution)/shard_map/ppermute | solution.py:155
  17.5 4.0 %collective-permute-start.6 = (f32[32,256]{1,0:T(8,128)S(1)}, f32[32,256]{1,0:T(8,128)S(1)}, u32[]{:S(2)}, u32[]{:S(2)}) collective-permute-start(f32[32,256]{1,0:T(8,128)S(1)} %get-tuple-element.19), channel_id=1, source_target_pairs={{0,2},{1,3},{2,0},{3,1},{4,6},{5,7},{6,4},{7,5},{8,10},{9,11},{10,... | collective-permute-start | bytes 98312 | tf_op jit(solution)/shard_map/ppermute | solution.py:155
  18.0 1.3 %copy-start = (f32[256]{0:T(256)S(1)}, f32[256]{0:T(256)}, u32[]{:S(2)}) copy-start(f32[256]{0:T(256)} %param.5) | copy-start | bytes 3076
  18.0 3.5 %collective-permute-start.5 = (f32[32,256]{1,0:T(8,128)S(1)}, f32[32,256]{1,0:T(8,128)S(1)}, u32[]{:S(2)}, u32[]{:S(2)}) collective-permute-start(f32[32,256]{1,0:T(8,128)S(1)} %get-tuple-element.18), channel_id=1, source_target_pairs={{0,1},{1,0},{2,3},{3,2},{4,5},{5,4},{6,7},{7,6},{8,9},{9,8},{10,11... | collective-permute-start | bytes 98312 | tf_op jit(solution)/shard_map/ppermute | solution.py:155

commit v16 on v15

--- a/solution.py
+++ b/solution.py
@@ -97,10 +97,10 @@
         probes = cols[place][pl.ds(shard, vectors), :].astype(jnp.float32)
         sums["back", place] = sums["back", place] + noise[place][...] * probes
     for ref, name in zip(rest, sorted(sums)):
-        ref[...] = sums[name]
+        ref[...] = sums[name].astype(ref.dtype)
 
 
-def tile(rows, cols, order, pairs, sums, shard, vectors, noise=(), work=1.0):
+def tile(rows, cols, order, pairs, sums, shard, vectors, noise=(), work=1.0, sent=()):
     blocks = [*rows, *cols]
     args = [*[blocks[place] for place in order], *noise, *sums.values()]
     elements = len(pairs) * shard * shard
@@ -111,7 +111,9 @@
         functools.partial(
             tile_kernel, list(order), tuple(pairs), tuple(sums), (len(rows), len(cols), len(noise)), shard, vectors
         ),
-        out_shape=[jax.ShapeDtypeStruct((vectors, shard), jnp.float32)] * len(names),
+        out_shape=[
+            jax.ShapeDtypeStruct((vectors, shard), jnp.bfloat16 if name in sent else jnp.float32) for name in names
+        ],
         in_specs=[whole] * len(args),
         out_specs=[whole] * len(names),
         compiler_params=pltpu.CompilerParams(vmem_limit_bytes=32 * 1024 * 1024),
@@ -167,10 +169,12 @@
 
     order = [0] + passed + [inner + place for place in range(len(cols))] + direct
     pairs = [(row, col, ("rows", "back")) for col in range(len(cols)) for row in range(inner)]
-    sums = tile(blocks, cols, order, pairs, {}, shard, vectors, work=0.0)
-    backs = [sums.pop(("back", place)) for place in range(len(cols))]
+    returns = [("back", place) for place in range(len(cols))]
+    sums = tile(blocks, cols, order, pairs, {}, shard, vectors, work=0.0, sent=returns)
+    backs = [sums.pop(name) for name in returns]
     pairs = [(row, col, ("rows",)) for col in range(len(others)) for row in range(inner)]
-    sums = tile(blocks, others, range(inner + len(others)), pairs, sums, shard, vectors)
+    shares = [("rows", step) for step in range(1, inner)]
+    sums = tile(blocks, others, range(inner + len(others)), pairs, sums, shard, vectors, sent=shares)
     pairs = [(row, 0, ("back",)) for row in range(inner)]
     own = tile(blocks, [packed], range(inner + 1), pairs, {}, shard, vectors, noise=[noise_level[None, :]])
 

time: 22.4 us -> 24.3 us (1.085)
  waiting for transfers between devices: 7.19 us -> 9.1 us
    ppermute x3, waiting for transfers between devices: 5.38 us -> 8.06 us  [along_outer(): lax.ppermute(value, 'blk', [(s * inner + b, t * inner + b) for s, t in ed...]
    ppermute x6, waiting for transfers between devices: 1.82 us -> 1.04 us  [in_plane(): lax.ppermute(value, 'blk', [(a * inner + s, a * inner + t) for a in range...]
  transfers between devices with their start and end apart: 9 -> 9, of which waited for: 6 -> 5; matrix products, arithmetic and copies ran while one was open for 0% -> 0% of each run, Pallas kernels for 13% -> 8%
where the time goes in v16:
time: 24.3 us; the launch traced here: 24 us
  starting transfers between devices  10.4 us (43%)
  waiting for transfers between devices  9.1 us (37%)
  Pallas kernels  2.91 us (12%)
  other arithmetic  1.56 us (6%)
    ppermute x3, waiting for transfers between devices, along_outer(): lax.ppermute(value, 'blk', [(s * inner + b, t * inner + b) for s, t in ed...  8.06 us
    ppermute x6, starting transfers between devices, in_plane(): lax.ppermute(value, 'blk', [(a * inner + s, a * inner + t) for a in range...  5.24 us
    ppermute x3, starting transfers between devices, along_outer(): lax.ppermute(value, 'blk', [(s * inner + b, t * inner + b) for s, t in ed...  5.14 us
    pallas_call x3, Pallas kernels, tile(): pl.pallas_call(functools.partial(tile_kernel, list(order), tuple(pairs),...  2.9 us
    ppermute x6, waiting for transfers between devices, in_plane(): lax.ppermute(value, 'blk', [(a * inner + s, a * inner + t) for a in range...  1.04 us
    concatenate x1, other arithmetic, on_device(): packed = jnp.concatenate([features, probes.T], axis=0)  0.93 us
    transpose x1, other arithmetic, on_device(): functools.reduce(lambda sofar, term: sofar + term, total + [sums['rows',...  0.63 us
  transfers between devices with their start and end apart: 9, of which 5 were waited for; matrix products, arithmetic and copies ran while one was open for 0% of the time, Pallas kernels for 8%

profile of v16, /device:TPU:0, one launch (start us, length us, event | category | flops | bytes accessed | tf_op | source)
XLA Modules:
  0.0 24.0 jit_solution(9335294930255229105)
XLA Ops:
  0.0 0.9 %pad_maximum_fusion.refs_0_.refs_4_.from_ref = bf16[288,256]{1,0:T(8,128)(2,1)S(1)} fusion(bf16[32,256]{1,0:T(8,128)(2,1)} %bitcast.5, bf16[256,256]{1,0:T(8,128)(2,1)} %param.3), kind=kLoop, calls=%fused_computation | loop fusion | flops 294912 | bytes 294912 | tf_op jit(solution)/shard_map/concatenate | solution.py:151
  0.9 3.0 %collective-permute-start.1 = (bf16[288,256]{1,0:T(8,128)(2,1)S(1)}, bf16[288,256]{1,0:T(8,128)(2,1)S(1)}, u32[]{:S(2)}, u32[]{:S(2)}) collective-permute-start(bf16[288,256]{1,0:T(8,128)(2,1)S(1)} %pad_maximum_fusion.refs_0_.refs_4_.from_ref), channel_id=1, source_target_pairs={{0,2},{1,3},{2,0},{3,1},{4,6},{5,7},{6,4},{7,5},{8,10},{9,11},{10,... | collective-permute-start | bytes 442376 | tf_op jit(solution)/shard_map/ppermute | solution.py:157
  4.0 3.7 %collective-permute-start.4 = (bf16[304,256]{1,0:T(8,128)(2,1)S(1)}, bf16[304,256]{1,0:T(8,128)(2,1)S(1)}, u32[]{:S(2)}, u32[]{:S(2)}) collective-permute-start(bf16[304,256]{1,0:T(8,128)(2,1)S(1)} %shard_map.38), channel_id=1, source_target_pairs={{12,4},{13,5},{14,6},{15,7},{4,8},{5,9},{6,10},{7,11},{8,0},{9,1},... | collective-permute-start | bytes 466952 | tf_op jit(solution)/shard_map/ppermute | solution.py:154
  7.6 0.0 collective-permute-start.3
  7.6 0.0 collective-permute-start
  7.6 0.2 collective-permute-done.1.refs_2_.refs_4_
  7.8 0.3 %collective-permute-start.2 = (bf16[288,256]{1,0:T(8,128)(2,1)S(1)}, bf16[288,256]{1,0:T(8,128)(2,1)S(1)}, u32[]{:S(2)}, u32[]{:S(2)}) collective-permute-start(bf16[288,256]{1,0:T(8,128)(2,1)S(1)} %collective-permute-done.1.refs_2_.refs_4_), channel_id=1, source_target_pairs={{0,1},{1,0},{2,3},{3,2},{4,5},{5,4},{6,7},{7,6},{8,9},{9,8},{10,11... | collective-permute-start | bytes 442376 | tf_op jit(solution)/shard_map/ppermute | solution.py:157
  8.2 0.9 %collective-permute-done.refs_1_.refs_3_ = bf16[288,256]{1,0:T(8,128)(2,1)S(1)} collective-permute-done((bf16[288,256]{1,0:T(8,128)(2,1)S(1)}, bf16[288,256]{1,0:T(8,128)(2,1)S(1)}, u32[]{:S(2)}, u32[]{:S(2)}) %collective-permute-start) | collective-permute-done | bytes 147488 | tf_op jit(solution)/shard_map/ppermute | solution.py:157
  9.0 4.8 %collective-permute-done.4.refs_2_ = bf16[304,256]{1,0:T(8,128)(2,1)S(1)} collective-permute-done((bf16[304,256]{1,0:T(8,128)(2,1)S(1)}, bf16[304,256]{1,0:T(8,128)(2,1)S(1)}, u32[]{:S(2)}, u32[]{:S(2)}) %collective-permute-start.4) | collective-permute-done | bytes 155680 | tf_op jit(solution)/shard_map/ppermute | solution.py:154
  13.9 0.0 collective-permute-done.2.refs_3_.refs_1_
  13.9 1.1 %shard_map.39 = (bf16[32,256]{1,0:T(8,128)(2,1)S(1)}, f32[32,256]{1,0:T(8,128)S(1)}, f32[32,256]{1,0:T(8,128)S(1)}, f32[32,256]{1,0:T(8,128)S(1)}, f32[32,256]{1,0:T(8,128)S(1)}) custom-call(bf16[288,256]{1,0:T(8,128)(2,1)S(1)} %pad_maximum_fusion.refs_0_.refs_4_.from_ref, bf16[288,256]{1,0:T(8,128)(2,1)S(1)} %collective-permute-done.2.refs_3_.refs_1_, ...), custom_call_target="tpu_custom_call" | custom-call | tf_op jit(solution)/shard_map/pallas_call | solution.py:110
  15.0 0.1 collective-permute-done.3.refs_4_
  15.1 0.9 %shard_map.40 = (f32[32,256]{1,0:T(8,128)S(1)}, bf16[32,256]{1,0:T(8,128)(2,1)S(1)}, bf16[32,256]{1,0:T(8,128)(2,1)S(1)}, bf16[32,256]{1,0:T(8,128)(2,1)S(1)}) custom-call(bf16[288,256]{1,0:T(8,128)(2,1)S(1)} %pad_maximum_fusion.refs_0_.refs_4_.from_ref, bf16[288,256]{1,0:T(8,128)(2,1)S(1)} %collective-permute-done.refs_1_.refs_3_, ...), custom_call_target="tpu_custom_call" | custom-call | flops 167772160 | bytes 655360 | tf_op jit(solution)/shard_map/pallas_call | solution.py:110
  16.0 0.0 collective-permute-start.5
  16.0 0.5 %collective-permute-start.6 = (bf16[32,256]{1,0:T(8,128)(2,1)S(1)}, bf16[32,256]{1,0:T(8,128)(2,1)S(1)}, u32[]{:S(2)}, u32[]{:S(2)}) collective-permute-start(bf16[32,256]{1,0:T(8,128)(2,1)S(1)} %get-tuple-element.19), channel_id=1, source_target_pairs={{0,2},{1,3},{2,0},{3,1},{4,6},{5,7},{6,4},{7,5},{8,10},{9,11},{10,... | collective-permute-start | bytes 49160 | tf_op jit(solution)/shard_map/ppermute | solution.py:157
  16.5 1.3 %collective-permute-start.7 = (bf16[32,256]{1,0:T(8,128)(2,1)S(1)}, bf16[32,256]{1,0:T(8,128)(2,1)S(1)}, u32[]{:S(2)}, u32[]{:S(2)}) collective-permute-start(bf16[32,256]{1,0:T(8,128)(2,1)S(1)} %get-tuple-element.20), channel_id=1, source_target_pairs={{0,3},{1,2},{2,1},{3,0},{4,7},{5,6},{6,5},{7,4},{8,11},{9,10},{10,... | collective-permute-start | bytes 49160 | tf_op jit(solution)/shard_map/ppermute | solution.py:157
  17.9 1.5 %collective-permute-start.8 = (bf16[32,256]{1,0:T(8,128)(2,1)S(1)}, bf16[32,256]{1,0:T(8,128)(2,1)S(1)}, u32[]{:S(2)}, u32[]{:S(2)}) collective-permute-start(bf16[32,256]{1,0:T(8,128)(2,1)S(1)} %get-tuple-element.21), channel_id=1, source_target_pairs={{4,12},{5,13},{6,14},{7,15},{8,4},{9,5},{10,6},{11,7},{0,8},{1,9},... | collective-permute-start | bytes 49160 | tf_op jit(solution)/shard_map/ppermute | solution.py:154
  19.3 0.0 copy-done
  19.3 0.9 %shard_map.37 = f32[32,256]{1,0:T(8,128)S(1)} custom-call(bf16[288,256]{1,0:T(8,128)(2,1)S(1)} %pad_maximum_fusion.refs_0_.refs_4_.from_ref, bf16[288,256]{1,0:T(8,128)(2,1)S(1)} %collective-permute-done.refs_1_.refs_3_, bf16[288,256]{1,0:T(8,128)(2,1)S(1)} %collective-permute-done.1.refs_2_.refs_4_, ...), custom_call_target="tpu_custom_call" | custom-call | flops 167772160 | bytes 655360 | tf_op jit(solution)/shard_map/pallas_call | solution.py:110
  20.2 0.0 collective-permute-done.5
  20.2 0.0 collective-permute-done.6
  20.2 0.0 collective-permute-done.7
  20.2 3.1 %collective-permute-done.8 = bf16[32,256]{1,0:T(8,128)(2,1)S(1)} collective-permute-done((bf16[32,256]{1,0:T(8,128)(2,1)S(1)}, bf16[32,256]{1,0:T(8,128)(2,1)S(1)}, u32[]{:S(2)}, u32[]{:S(2)}) %collective-permute-start.8) | collective-permute-done | bytes 16416 | tf_op jit(solution)/shard_map/ppermute | solution.py:154
  23.4 0.6 %add_bitcast_fusion = f32[256,32]{0,1:T(8,128)} fusion(f32[32,256]{1,0:T(8,128)S(1)} %get-tuple-element.22, bf16[32,256]{1,0:T(8,128)(2,1)S(1)} %collective-permute-done.8, bf16[32,256]{1,0:T(8,128)(2,1)S(1)} %collective-permute-done.7, bf16[32,256]{1,0:T(8,128)(2,1)S(1)} %collective-permute-done.6, f32[32,256]{1,0:T(8,128)S(1)} %shard_map.37, ...), kind=kLoop, calls=%fused_computation.1 | loop fusion | flops 73728 | bytes 163840 | tf_op jit(solution)/shard_map/transpose | solution.py:184
  (2 shorter events, 0.0 us)
Async XLA Ops:
  0.9 6.9 %collective-permute-start.1 = (bf16[288,256]{1,0:T(8,128)(2,1)S(1)}, bf16[288,256]{1,0:T(8,128)(2,1)S(1)}, u32[]{:S(2)}, u32[]{:S(2)}) collective-permute-start(bf16[288,256]{1,0:T(8,128)(2,1)S(1)} %pad_maximum_fusion.refs_0_.refs_4_.from_ref), channel_id=1, source_target_pairs={{0,2},{1,3},{2,0},{3,1},{4,6},{5,7},{6,4},{7,5},{8,10},{9,11},{10,... | collective-permute-start | bytes 442376 | tf_op jit(solution)/shard_map/ppermute | solution.py:157
  4.0 9.9 %collective-permute-start.4 = (bf16[304,256]{1,0:T(8,128)(2,1)S(1)}, bf16[304,256]{1,0:T(8,128)(2,1)S(1)}, u32[]{:S(2)}, u32[]{:S(2)}) collective-permute-start(bf16[304,256]{1,0:T(8,128)(2,1)S(1)} %shard_map.38), channel_id=1, source_target_pairs={{12,4},{13,5},{14,6},{15,7},{4,8},{5,9},{6,10},{7,11},{8,0},{9,1},... | collective-permute-start | bytes 466952 | tf_op jit(solution)/shard_map/ppermute | solution.py:154
  7.6 7.4 %collective-permute-start.3 = (bf16[304,256]{1,0:T(8,128)(2,1)S(1)}, bf16[304,256]{1,0:T(8,128)(2,1)S(1)}, u32[]{:S(2)}, u32[]{:S(2)}) collective-permute-start(bf16[304,256]{1,0:T(8,128)(2,1)S(1)} %shard_map.38), channel_id=1, source_target_pairs={{12,8},{13,9},{14,10},{15,11},{4,0},{5,1},{6,2},{7,3},{8,12},{9,13... | collective-permute-start | bytes 466952 | tf_op jit(solution)/shard_map/ppermute | solution.py:154
  7.6 1.4 %collective-permute-start = (bf16[288,256]{1,0:T(8,128)(2,1)S(1)}, bf16[288,256]{1,0:T(8,128)(2,1)S(1)}, u32[]{:S(2)}, u32[]{:S(2)}) collective-permute-start(bf16[288,256]{1,0:T(8,128)(2,1)S(1)} %pad_maximum_fusion.refs_0_.refs_4_.from_ref), channel_id=1, source_target_pairs={{0,1},{1,0},{2,3},{3,2},{4,5},{5,4},{6,7},{7,6},{8,9},{9,8},{10,11... | collective-permute-start | bytes 442376 | tf_op jit(solution)/shard_map/ppermute | solution.py:157
  7.8 6.0 %collective-permute-start.2 = (bf16[288,256]{1,0:T(8,128)(2,1)S(1)}, bf16[288,256]{1,0:T(8,128)(2,1)S(1)}, u32[]{:S(2)}, u32[]{:S(2)}) collective-permute-start(bf16[288,256]{1,0:T(8,128)(2,1)S(1)} %collective-permute-done.1.refs_2_.refs_4_), channel_id=1, source_target_pairs={{0,1},{1,0},{2,3},{3,2},{4,5},{5,4},{6,7},{7,6},{8,9},{9,8},{10,11... | collective-permute-start | bytes 442376 | tf_op jit(solution)/shard_map/ppermute | solution.py:157
  16.0 4.2 %collective-permute-start.5 = (bf16[32,256]{1,0:T(8,128)(2,1)S(1)}, bf16[32,256]{1,0:T(8,128)(2,1)S(1)}, u32[]{:S(2)}, u32[]{:S(2)}) collective-permute-start(bf16[32,256]{1,0:T(8,128)(2,1)S(1)} %get-tuple-element.18), channel_id=1, source_target_pairs={{0,1},{1,0},{2,3},{3,2},{4,5},{5,4},{6,7},{7,6},{8,9},{9,8},{10,11... | collective-permute-start | bytes 49160 | tf_op jit(solution)/shard_map/ppermute | solution.py:157
  16.0 4.2 %collective-permute-start.6 = (bf16[32,256]{1,0:T(8,128)(2,1)S(1)}, bf16[32,256]{1,0:T(8,128)(2,1)S(1)}, u32[]{:S(2)}, u32[]{:S(2)}) collective-permute-start(bf16[32,256]{1,0:T(8,128)(2,1)S(1)} %get-tuple-element.19), channel_id=1, source_target_pairs={{0,2},{1,3},{2,0},{3,1},{4,6},{5,7},{6,4},{7,5},{8,10},{9,11},{10,... | collective-permute-start | bytes 49160 | tf_op jit(solution)/shard_map/ppermute | solution.py:157
  16.5 3.7 %collective-permute-start.7 = (bf16[32,256]{1,0:T(8,128)(2,1)S(1)}, bf16[32,256]{1,0:T(8,128)(2,1)S(1)}, u32[]{:S(2)}, u32[]{:S(2)}) collective-permute-start(bf16[32,256]{1,0:T(8,128)(2,1)S(1)} %get-tuple-element.20), channel_id=1, source_target_pairs={{0,3},{1,2},{2,1},{3,0},{4,7},{5,6},{6,5},{7,4},{8,11},{9,10},{10,... | collective-permute-start | bytes 49160 | tf_op jit(solution)/shard_map/ppermute | solution.py:157
  17.8 1.5 %copy-start = (f32[256]{0:T(256)S(1)}, f32[256]{0:T(256)}, u32[]{:S(2)}) copy-start(f32[256]{0:T(256)} %param.5) | copy-start | bytes 3076
  17.9 5.5 %collective-permute-start.8 = (bf16[32,256]{1,0:T(8,128)(2,1)S(1)}, bf16[32,256]{1,0:T(8,128)(2,1)S(1)}, u32[]{:S(2)}, u32[]{:S(2)}) collective-permute-start(bf16[32,256]{1,0:T(8,128)(2,1)S(1)} %get-tuple-element.21), channel_id=1, source_target_pairs={{4,12},{5,13},{6,14},{7,15},{8,4},{9,5},{10,6},{11,7},{0,8},{1,9},... | collective-permute-start | bytes 49160 | tf_op jit(solution)/shard_map/ppermute | solution.py:154

commit v17 on v16

--- a/solution.py
+++ b/solution.py
@@ -170,7 +170,7 @@
     order = [0] + passed + [inner + place for place in range(len(cols))] + direct
     pairs = [(row, col, ("rows", "back")) for col in range(len(cols)) for row in range(inner)]
     returns = [("back", place) for place in range(len(cols))]
-    sums = tile(blocks, cols, order, pairs, {}, shard, vectors, work=0.0, sent=returns)
+    sums = tile(blocks, cols, order, pairs, {}, shard, vectors, work=0.0)
     backs = [sums.pop(name) for name in returns]
     pairs = [(row, col, ("rows",)) for col in range(len(others)) for row in range(inner)]
     shares = [("rows", step) for step in range(1, inner)]

time: 24.3 us -> 22.1 us (0.909)
  waiting for transfers between devices: 9.1 us -> 6.96 us
    ppermute x3, waiting for transfers between devices: 8.06 us -> 4.85 us  [along_outer(): lax.ppermute(value, 'blk', [(s * inner + b, t * inner + b) for s, t in ed...]
    ppermute x6, waiting for transfers between devices: 1.04 us -> 2.11 us  [in_plane(): lax.ppermute(value, 'blk', [(a * inner + s, a * inner + t) for a in range...]
  transfers between devices with their start and end apart: 9 -> 9, of which waited for: 5 -> 5; matrix products, arithmetic and copies ran while one was open for 0% -> 0% of each run, Pallas kernels for 8% -> 13%
where the time goes in v17:
time: 22.1 us; the launch traced here: 21.9 us
  starting transfers between devices  10.4 us (47%)
  waiting for transfers between devices  6.96 us (31%)
  Pallas kernels  2.92 us (13%)
  other arithmetic  1.56 us (7%)
    ppermute x6, starting transfers between devices, in_plane(): lax.ppermute(value, 'blk', [(a * inner + s, a * inner + t) for a in range...  5.24 us
    ppermute x3, starting transfers between devices, along_outer(): lax.ppermute(value, 'blk', [(s * inner + b, t * inner + b) for s, t in ed...  5.2 us
    ppermute x3, waiting for transfers between devices, along_outer(): lax.ppermute(value, 'blk', [(s * inner + b, t * inner + b) for s, t in ed...  4.85 us
    pallas_call x3, Pallas kernels, tile(): pl.pallas_call(functools.partial(tile_kernel, list(order), tuple(pairs),...  2.9 us
    ppermute x6, waiting for transfers between devices, in_plane(): lax.ppermute(value, 'blk', [(a * inner + s, a * inner + t) for a in range...  2.11 us
    concatenate x1, other arithmetic, on_device(): packed = jnp.concatenate([features, probes.T], axis=0)  0.93 us
    transpose x1, other arithmetic, on_device(): functools.reduce(lambda sofar, term: sofar + term, total + [sums['rows',...  0.63 us
  transfers between devices with their start and end apart: 9, of which 5 were waited for; matrix products, arithmetic and copies ran while one was open for 0% of the time, Pallas kernels for 13%

profile of v17, /device:TPU:0, one launch (start us, length us, event | category | flops | bytes accessed | tf_op | source)
XLA Modules:
  0.0 21.9 jit_solution(5024198896115258395)
XLA Ops:
  0.0 0.9 %pad_maximum_fusion.refs_0_.refs_4_.from_ref = bf16[288,256]{1,0:T(8,128)(2,1)S(1)} fusion(bf16[32,256]{1,0:T(8,128)(2,1)} %bitcast.5, bf16[256,256]{1,0:T(8,128)(2,1)} %param.3), kind=kLoop, calls=%fused_computation | loop fusion | flops 294912 | bytes 294912 | tf_op jit(solution)/shard_map/concatenate | solution.py:151
  0.9 3.0 %collective-permute-start.1 = (bf16[288,256]{1,0:T(8,128)(2,1)S(1)}, bf16[288,256]{1,0:T(8,128)(2,1)S(1)}, u32[]{:S(2)}, u32[]{:S(2)}) collective-permute-start(bf16[288,256]{1,0:T(8,128)(2,1)S(1)} %pad_maximum_fusion.refs_0_.refs_4_.from_ref), channel_id=1, source_target_pairs={{0,2},{1,3},{2,0},{3,1},{4,6},{5,7},{6,4},{7,5},{8,10},{9,11},{10,... | collective-permute-start | bytes 442376 | tf_op jit(solution)/shard_map/ppermute | solution.py:157
  4.0 3.7 %collective-permute-start.4 = (bf16[304,256]{1,0:T(8,128)(2,1)S(1)}, bf16[304,256]{1,0:T(8,128)(2,1)S(1)}, u32[]{:S(2)}, u32[]{:S(2)}) collective-permute-start(bf16[304,256]{1,0:T(8,128)(2,1)S(1)} %shard_map.38), channel_id=1, source_target_pairs={{12,4},{13,5},{14,6},{15,7},{4,8},{5,9},{6,10},{7,11},{8,0},{9,1},... | collective-permute-start | bytes 466952 | tf_op jit(solution)/shard_map/ppermute | solution.py:154
  7.6 0.0 collective-permute-start.3
  7.6 0.0 collective-permute-start
  7.6 0.2 collective-permute-done.1.refs_2_.refs_4_
  7.8 0.3 %collective-permute-start.2 = (bf16[288,256]{1,0:T(8,128)(2,1)S(1)}, bf16[288,256]{1,0:T(8,128)(2,1)S(1)}, u32[]{:S(2)}, u32[]{:S(2)}) collective-permute-start(bf16[288,256]{1,0:T(8,128)(2,1)S(1)} %collective-permute-done.1.refs_2_.refs_4_), channel_id=1, source_target_pairs={{0,1},{1,0},{2,3},{3,2},{4,5},{5,4},{6,7},{7,6},{8,9},{9,8},{10,11... | collective-permute-start | bytes 442376 | tf_op jit(solution)/shard_map/ppermute | solution.py:157
  8.2 0.9 %collective-permute-done.refs_1_.refs_3_ = bf16[288,256]{1,0:T(8,128)(2,1)S(1)} collective-permute-done((bf16[288,256]{1,0:T(8,128)(2,1)S(1)}, bf16[288,256]{1,0:T(8,128)(2,1)S(1)}, u32[]{:S(2)}, u32[]{:S(2)}) %collective-permute-start) | collective-permute-done | bytes 147488 | tf_op jit(solution)/shard_map/ppermute | solution.py:157
  9.0 4.8 %collective-permute-done.4.refs_2_ = bf16[304,256]{1,0:T(8,128)(2,1)S(1)} collective-permute-done((bf16[304,256]{1,0:T(8,128)(2,1)S(1)}, bf16[304,256]{1,0:T(8,128)(2,1)S(1)}, u32[]{:S(2)}, u32[]{:S(2)}) %collective-permute-start.4) | collective-permute-done | bytes 155680 | tf_op jit(solution)/shard_map/ppermute | solution.py:154
  13.9 0.0 collective-permute-done.2.refs_3_.refs_1_
  13.9 1.1 %shard_map.39 = (f32[32,256]{1,0:T(8,128)S(1)}, f32[32,256]{1,0:T(8,128)S(1)}, f32[32,256]{1,0:T(8,128)S(1)}, f32[32,256]{1,0:T(8,128)S(1)}, f32[32,256]{1,0:T(8,128)S(1)}) custom-call(bf16[288,256]{1,0:T(8,128)(2,1)S(1)} %pad_maximum_fusion.refs_0_.refs_4_.from_ref, bf16[288,256]{1,0:T(8,128)(2,1)S(1)} %collective-permute-done.2.refs_3_.refs_1_, ...), custom_call_target="tpu_custom_call" | custom-call | tf_op jit(solution)/shard_map/pallas_call | solution.py:110
  15.0 1.5 %collective-permute-start.8 = (f32[32,256]{1,0:T(8,128)S(1)}, f32[32,256]{1,0:T(8,128)S(1)}, u32[]{:S(2)}, u32[]{:S(2)}) collective-permute-start(f32[32,256]{1,0:T(8,128)S(1)} %get-tuple-element.21), channel_id=1, source_target_pairs={{4,12},{5,13},{6,14},{7,15},{8,4},{9,5},{10,6},{11,7},{0,8},{1,9},... | collective-permute-start | bytes 98312 | tf_op jit(solution)/shard_map/ppermute | solution.py:154
  16.5 0.0 collective-permute-done.3.refs_4_
  16.5 0.9 %shard_map.40 = (f32[32,256]{1,0:T(8,128)S(1)}, bf16[32,256]{1,0:T(8,128)(2,1)S(1)}, bf16[32,256]{1,0:T(8,128)(2,1)S(1)}, bf16[32,256]{1,0:T(8,128)(2,1)S(1)}) custom-call(bf16[288,256]{1,0:T(8,128)(2,1)S(1)} %pad_maximum_fusion.refs_0_.refs_4_.from_ref, bf16[288,256]{1,0:T(8,128)(2,1)S(1)} %collective-permute-done.refs_1_.refs_3_, ...), custom_call_target="tpu_custom_call" | custom-call | flops 167772160 | bytes 655360 | tf_op jit(solution)/shard_map/pallas_call | solution.py:110
  17.5 0.0 collective-permute-start.7
  17.5 0.6 %collective-permute-start.6 = (bf16[32,256]{1,0:T(8,128)(2,1)S(1)}, bf16[32,256]{1,0:T(8,128)(2,1)S(1)}, u32[]{:S(2)}, u32[]{:S(2)}) collective-permute-start(bf16[32,256]{1,0:T(8,128)(2,1)S(1)} %get-tuple-element.19), channel_id=1, source_target_pairs={{0,2},{1,3},{2,0},{3,1},{4,6},{5,7},{6,4},{7,5},{8,10},{9,11},{10,... | collective-permute-start | bytes 49160 | tf_op jit(solution)/shard_map/ppermute | solution.py:157
  18.0 1.3 %collective-permute-start.5 = (bf16[32,256]{1,0:T(8,128)(2,1)S(1)}, bf16[32,256]{1,0:T(8,128)(2,1)S(1)}, u32[]{:S(2)}, u32[]{:S(2)}) collective-permute-start(bf16[32,256]{1,0:T(8,128)(2,1)S(1)} %get-tuple-element.18), channel_id=1, source_target_pairs={{0,1},{1,0},{2,3},{3,2},{4,5},{5,4},{6,7},{7,6},{8,9},{9,8},{10,11... | collective-permute-start | bytes 49160 | tf_op jit(solution)/shard_map/ppermute | solution.py:157
  19.3 0.0 copy-done
  19.3 0.9 %shard_map.37 = f32[32,256]{1,0:T(8,128)S(1)} custom-call(bf16[288,256]{1,0:T(8,128)(2,1)S(1)} %pad_maximum_fusion.refs_0_.refs_4_.from_ref, bf16[288,256]{1,0:T(8,128)(2,1)S(1)} %collective-permute-done.refs_1_.refs_3_, bf16[288,256]{1,0:T(8,128)(2,1)S(1)} %collective-permute-done.1.refs_2_.refs_4_, ...), custom_call_target="tpu_custom_call" | custom-call | flops 167772160 | bytes 655360 | tf_op jit(solution)/shard_map/pallas_call | solution.py:110
  20.2 0.4 %collective-permute-done.7 = bf16[32,256]{1,0:T(8,128)(2,1)S(1)} collective-permute-done((bf16[32,256]{1,0:T(8,128)(2,1)S(1)}, bf16[32,256]{1,0:T(8,128)(2,1)S(1)}, u32[]{:S(2)}, u32[]{:S(2)}) %collective-permute-start.7) | collective-permute-done | bytes 16416 | tf_op jit(solution)/shard_map/ppermute | solution.py:157
  20.6 0.6 %collective-permute-done.6 = bf16[32,256]{1,0:T(8,128)(2,1)S(1)} collective-permute-done((bf16[32,256]{1,0:T(8,128)(2,1)S(1)}, bf16[32,256]{1,0:T(8,128)(2,1)S(1)}, u32[]{:S(2)}, u32[]{:S(2)}) %collective-permute-start.6) | collective-permute-done | bytes 16416 | tf_op jit(solution)/shard_map/ppermute | solution.py:157
  21.3 0.0 collective-permute-done.5
  21.3 0.0 collective-permute-done.8
  21.3 0.6 %add_bitcast_fusion = f32[256,32]{0,1:T(8,128)} fusion(f32[32,256]{1,0:T(8,128)S(1)} %get-tuple-element.22, f32[32,256]{1,0:T(8,128)S(1)} %collective-permute-done.8, bf16[32,256]{1,0:T(8,128)(2,1)S(1)} %collective-permute-done.7, bf16[32,256]{1,0:T(8,128)(2,1)S(1)} %collective-permute-done.6, f32[32,256]{1,0:T(8,128)S(1)} %shard_map.37, ...), kind=kLoop, calls=%fused_computation.1 | loop fusion | flops 65536 | bytes 180224 | tf_op jit(solution)/shard_map/transpose | solution.py:184
  (2 shorter events, 0.0 us)
Async XLA Ops:
  0.9 6.9 %collective-permute-start.1 = (bf16[288,256]{1,0:T(8,128)(2,1)S(1)}, bf16[288,256]{1,0:T(8,128)(2,1)S(1)}, u32[]{:S(2)}, u32[]{:S(2)}) collective-permute-start(bf16[288,256]{1,0:T(8,128)(2,1)S(1)} %pad_maximum_fusion.refs_0_.refs_4_.from_ref), channel_id=1, source_target_pairs={{0,2},{1,3},{2,0},{3,1},{4,6},{5,7},{6,4},{7,5},{8,10},{9,11},{10,... | collective-permute-start | bytes 442376 | tf_op jit(solution)/shard_map/ppermute | solution.py:157
  4.0 9.9 %collective-permute-start.4 = (bf16[304,256]{1,0:T(8,128)(2,1)S(1)}, bf16[304,256]{1,0:T(8,128)(2,1)S(1)}, u32[]{:S(2)}, u32[]{:S(2)}) collective-permute-start(bf16[304,256]{1,0:T(8,128)(2,1)S(1)} %shard_map.38), channel_id=1, source_target_pairs={{12,4},{13,5},{14,6},{15,7},{4,8},{5,9},{6,10},{7,11},{8,0},{9,1},... | collective-permute-start | bytes 466952 | tf_op jit(solution)/shard_map/ppermute | solution.py:154
  7.6 8.9 %collective-permute-start.3 = (bf16[304,256]{1,0:T(8,128)(2,1)S(1)}, bf16[304,256]{1,0:T(8,128)(2,1)S(1)}, u32[]{:S(2)}, u32[]{:S(2)}) collective-permute-start(bf16[304,256]{1,0:T(8,128)(2,1)S(1)} %shard_map.38), channel_id=1, source_target_pairs={{12,8},{13,9},{14,10},{15,11},{4,0},{5,1},{6,2},{7,3},{8,12},{9,13... | collective-permute-start | bytes 466952 | tf_op jit(solution)/shard_map/ppermute | solution.py:154
  7.6 1.4 %collective-permute-start = (bf16[288,256]{1,0:T(8,128)(2,1)S(1)}, bf16[288,256]{1,0:T(8,128)(2,1)S(1)}, u32[]{:S(2)}, u32[]{:S(2)}) collective-permute-start(bf16[288,256]{1,0:T(8,128)(2,1)S(1)} %pad_maximum_fusion.refs_0_.refs_4_.from_ref), channel_id=1, source_target_pairs={{0,1},{1,0},{2,3},{3,2},{4,5},{5,4},{6,7},{7,6},{8,9},{9,8},{10,11... | collective-permute-start | bytes 442376 | tf_op jit(solution)/shard_map/ppermute | solution.py:157
  7.8 6.0 %collective-permute-start.2 = (bf16[288,256]{1,0:T(8,128)(2,1)S(1)}, bf16[288,256]{1,0:T(8,128)(2,1)S(1)}, u32[]{:S(2)}, u32[]{:S(2)}) collective-permute-start(bf16[288,256]{1,0:T(8,128)(2,1)S(1)} %collective-permute-done.1.refs_2_.refs_4_), channel_id=1, source_target_pairs={{0,1},{1,0},{2,3},{3,2},{4,5},{5,4},{6,7},{7,6},{8,9},{9,8},{10,11... | collective-permute-start | bytes 442376 | tf_op jit(solution)/shard_map/ppermute | solution.py:157
  15.0 6.3 %collective-permute-start.8 = (f32[32,256]{1,0:T(8,128)S(1)}, f32[32,256]{1,0:T(8,128)S(1)}, u32[]{:S(2)}, u32[]{:S(2)}) collective-permute-start(f32[32,256]{1,0:T(8,128)S(1)} %get-tuple-element.21), channel_id=1, source_target_pairs={{4,12},{5,13},{6,14},{7,15},{8,4},{9,5},{10,6},{11,7},{0,8},{1,9},... | collective-permute-start | bytes 98312 | tf_op jit(solution)/shard_map/ppermute | solution.py:154
  17.5 3.2 %collective-permute-start.7 = (bf16[32,256]{1,0:T(8,128)(2,1)S(1)}, bf16[32,256]{1,0:T(8,128)(2,1)S(1)}, u32[]{:S(2)}, u32[]{:S(2)}) collective-permute-start(bf16[32,256]{1,0:T(8,128)(2,1)S(1)} %get-tuple-element.20), channel_id=1, source_target_pairs={{0,3},{1,2},{2,1},{3,0},{4,7},{5,6},{6,5},{7,4},{8,11},{9,10},{10,... | collective-permute-start | bytes 49160 | tf_op jit(solution)/shard_map/ppermute | solution.py:157
  17.5 3.8 %collective-permute-start.6 = (bf16[32,256]{1,0:T(8,128)(2,1)S(1)}, bf16[32,256]{1,0:T(8,128)(2,1)S(1)}, u32[]{:S(2)}, u32[]{:S(2)}) collective-permute-start(bf16[32,256]{1,0:T(8,128)(2,1)S(1)} %get-tuple-element.19), channel_id=1, source_target_pairs={{0,2},{1,3},{2,0},{3,1},{4,6},{5,7},{6,4},{7,5},{8,10},{9,11},{10,... | collective-permute-start | bytes 49160 | tf_op jit(solution)/shard_map/ppermute | solution.py:157
  18.0 1.3 %copy-start = (f32[256]{0:T(256)S(1)}, f32[256]{0:T(256)}, u32[]{:S(2)}) copy-start(f32[256]{0:T(256)} %param.5) | copy-start | bytes 3076
  18.0 3.2 %collective-permute-start.5 = (bf16[32,256]{1,0:T(8,128)(2,1)S(1)}, bf16[32,256]{1,0:T(8,128)(2,1)S(1)}, u32[]{:S(2)}, u32[]{:S(2)}) collective-permute-start(bf16[32,256]{1,0:T(8,128)(2,1)S(1)} %get-tuple-element.18), channel_id=1, source_target_pairs={{0,1},{1,0},{2,3},{3,2},{4,5},{5,4},{6,7},{7,6},{8,9},{9,8},{10,11... | collective-permute-start | bytes 49160 | tf_op jit(solution)/shard_map/ppermute | solution.py:157

commit v18 on v15

--- a/solution.py
+++ b/solution.py
@@ -20,15 +20,17 @@
     return size
 
 
-def plane_blocks(value, count, send):
+def plane_blocks(value, halves, count, send):
     if count & (count - 1):
         maps = {step: [(b, (b - step) % count) for b in range(count)] for step in range(1, count)}
-        return [value] + [send(value, maps[step]) for step in range(1, count)]
-    blocks = {0: value}
+        return [(value,)] + [(send(value, maps[step]),) for step in range(1, count)]
+    blocks = {0: (value,)}
     bit = count // 2
     while bit:
+        hops = [(b, b ^ bit) for b in range(count)]
         for known in list(blocks):
-            blocks[known | bit] = send(blocks[known], [(b, b ^ bit) for b in range(count)])
+            parts = halves if known == 0 and bit == count // 2 and bit > 1 else blocks[known]
+            blocks[known | bit] = tuple(send(part, hops) for part in parts)
         bit //= 2
     return [blocks[distance] for distance in range(count)]
 
@@ -66,23 +68,31 @@
     return total[0:1, :]
 
 
+def joined(refs, shard, vectors):
+    points, some = shard // len(refs), vectors // len(refs)
+    features = [ref[0:points, :] for ref in refs]
+    probes = [ref[pl.ds(points, some), :] for ref in refs]
+    return (jnp.concatenate(features), jnp.concatenate(probes)) if len(refs) > 1 else (features[0], probes[0])
+
+
 def tile_kernel(order, pairs, known, counts, shard, vectors, *refs):
-    rows_in, cols_in, noise_in = counts
-    blocks = [refs[order.index(place)] for place in range(rows_in + cols_in)]
-    rows, cols = blocks[:rows_in], blocks[rows_in:]
-    rest = list(refs[rows_in + cols_in :])
+    parts, cols_in, noise_in = counts
+    rest = list(refs)
+    blocks = {place: [rest.pop(0) for _ in range((*parts, *[1] * cols_in)[place])] for place in order}
+    rows = [joined(blocks[place], shard, vectors) for place in range(len(parts))]
+    cols = [blocks[len(parts) + place][0] for place in range(cols_in)]
     noise = [rest.pop(0) for _ in range(noise_in)]
     sums = {name: rest.pop(0)[...] for name in known}
     ready_rows, ready_cols = {}, {}
     for row, col, kind in pairs:
         if row not in ready_rows:
-            wide = rows[row][0:shard, :].astype(jnp.float32)
+            wide = rows[row][0].astype(jnp.float32)
             ready_rows[row] = jnp.sum(wide * wide, axis=1, keepdims=True)
         if col not in ready_cols:
             block = cols[col][0:shard, :]
             ready_cols[col] = block * jnp.asarray(-2.0, block.dtype), lane_squares(block)
         scaled, col_squares = ready_cols[col]
-        row_block, row_probes = rows[row][0:shard, :], rows[row][pl.ds(shard, vectors), :]
+        row_block, row_probes = rows[row]
         cross = lax.dot_general(row_block, scaled, ROWS_BY_ROWS, preferred_element_type=jnp.float32)
         kernel = matern((ready_rows[row] + col_squares) + cross)
         found = {}
@@ -101,15 +111,15 @@
 
 
 def tile(rows, cols, order, pairs, sums, shard, vectors, noise=(), work=1.0):
-    blocks = [*rows, *cols]
-    args = [*[blocks[place] for place in order], *noise, *sums.values()]
+    blocks = [*rows, *[(col,) for col in cols]]
+    args = [*[part for place in order for part in blocks[place]], *noise, *sums.values()]
     elements = len(pairs) * shard * shard
-    width = rows[0].shape[1]
+    width = cols[0].shape[1]
     names = sorted({(part, col if part == "back" else row) for row, col, kind in pairs for part in kind} | set(sums))
     whole = pl.BlockSpec(memory_space=pltpu.VMEM)
     found = pl.pallas_call(
         functools.partial(
-            tile_kernel, list(order), tuple(pairs), tuple(sums), (len(rows), len(cols), len(noise)), shard, vectors
+            tile_kernel, list(order), tuple(pairs), tuple(sums), (tuple(map(len, rows)), len(cols), len(noise)), shard, vectors
         ),
         out_shape=[jax.ShapeDtypeStruct((vectors, shard), jnp.float32)] * len(names),
         in_specs=[whole] * len(args),
@@ -124,20 +134,24 @@
     return dict(zip(names, found))
 
 
-def copy_kernel(from_ref, to_ref):
-    to_ref[0 : from_ref.shape[0], :] = from_ref[...]
-    to_ref[from_ref.shape[0] :, :] = jnp.zeros((to_ref.shape[0] - from_ref.shape[0], to_ref.shape[1]), to_ref.dtype)
-
-
-def copy_rows(value, rows):
+def split_kernel(shard, vectors, longer_ref, whole_ref, *halves):
+    whole_ref[...] = longer_ref[0 : shard + vectors, :]
+    points, some = shard // 2, vectors // 2
+    for place, half in enumerate(halves):
+        half[0:points, :] = longer_ref[pl.ds(place * points, points), :]
+        half[points:, :] = longer_ref[pl.ds(shard + place * some, some), :]
+
+
+def split(longer, shard, vectors):
     whole = pl.BlockSpec(memory_space=pltpu.VMEM)
+    rows = [shard + vectors, (shard + vectors) // 2, (shard + vectors) // 2]
     return pl.pallas_call(
-        copy_kernel,
-        out_shape=jax.ShapeDtypeStruct((rows, value.shape[1]), value.dtype),
+        functools.partial(split_kernel, shard, vectors),
+        out_shape=[jax.ShapeDtypeStruct((count, longer.shape[1]), longer.dtype) for count in rows],
         in_specs=[whole],
-        out_specs=whole,
+        out_specs=[whole] * 3,
         compiler_params=pltpu.CompilerParams(vmem_limit_bytes=32 * 1024 * 1024),
-    )(value)
+    )(longer)
 
 
 def on_device(features, probes, noise_level):
@@ -146,7 +160,9 @@
     outer = count // inner
     shard = features.shape[0]
     vectors = probes.shape[1]
-    packed = jnp.concatenate([features, probes.T], axis=0)
+    spare = jnp.zeros((16, features.shape[1]), features.dtype)
+    longer = jnp.concatenate([features, probes.T, spare], axis=0)
+    packed, *halves = split(longer, shard, vectors)
 
     def along_outer(value, edges):
         return lax.ppermute(value, "blk", [(s * inner + b, t * inner + b) for s, t in edges for b in range(inner)])
@@ -158,14 +174,13 @@
         return [(plane_target(b, step, inner), b) for b in range(inner)]
 
     one_way, exchanges = outer_maps(outer)
-    longer = copy_rows(packed, shard + vectors + 16)
     cols = [along_outer(longer, edges) for edges in one_way]
-    others = [along_outer(longer, edges) for edges in exchanges]
-    blocks = plane_blocks(packed, inner, in_plane)
+    others = [along_outer(packed, edges) for edges in exchanges]
+    blocks = plane_blocks(packed, halves, inner, in_plane)
     direct = [step for step in range(1, inner) if step & (step - 1) == 0]
     passed = [step for step in range(1, inner) if step & (step - 1)]
 
-    order = [0] + passed + [inner + place for place in range(len(cols))] + direct
+    order = [0] + passed + direct + [inner + place for place in range(len(cols))]
     pairs = [(row, col, ("rows", "back")) for col in range(len(cols)) for row in range(inner)]
     sums = tile(blocks, cols, order, pairs, {}, shard, vectors, work=0.0)
     backs = [sums.pop(("back", place)) for place in range(len(cols))]
@@ -174,10 +189,10 @@
     pairs = [(row, 0, ("back",)) for row in range(inner)]
     own = tile(blocks, [packed], range(inner + 1), pairs, {}, shard, vectors, noise=[noise_level[None, :]])
 
-    total = [own["back", 0]]
+    total = [sums["rows", 0], own["back", 0]]
     total += [in_plane(sums["rows", step], [(t, s) for s, t in near(step)]) for step in range(1, inner)]
     total += [along_outer(back, [(t, s) for s, t in edges]) for back, edges in zip(backs, one_way)]
-    return functools.reduce(lambda sofar, term: sofar + term, total + [sums["rows", 0]]).T
+    return functools.reduce(lambda sofar, term: sofar + term, total).T
 
 
 def solution(mesh):

time: 22.4 us -> 22.7 us (1.013)
  local copies, waits for them, and re-layouts: 0.01 us -> 0.6 us
  starting transfers between devices: 10.4 us -> 9.94 us
    ppermute x6 -> x8, waiting for transfers between devices: 1.82 us -> 6.59 us  [in_plane(): lax.ppermute(value, 'blk', [(a * inner + s, a * inner + t) for a in range...]
    ppermute x3, waiting for transfers between devices: 5.38 us -> 0.7 us  [along_outer(): lax.ppermute(value, 'blk', [(s * inner + b, t * inner + b) for s, t in ed...]
    ppermute x6 -> x8, starting transfers between devices: 5.24 us -> 3.97 us  [in_plane(): lax.ppermute(value, 'blk', [(a * inner + s, a * inner + t) for a in range...]
    ppermute x3, starting transfers between devices: 5.2 us -> 5.96 us  [along_outer(): lax.ppermute(value, 'blk', [(s * inner + b, t * inner + b) for s, t in ed...]
    unnamed x2, local copies, waits for them, and re-layouts: 0.01 us -> 0.52 us
  transfers between devices with their start and end apart: 9 -> 11, of which waited for: 6 -> 7; matrix products, arithmetic and copies ran while one was open for 0% -> 0% of each run, Pallas kernels for 13% -> 13%
where the time goes in v18:
time: 22.7 us; the launch traced here: 22.4 us
  starting transfers between devices  9.94 us (44%)
  waiting for transfers between devices  7.3 us (32%)
  Pallas kernels  2.92 us (13%)
  other arithmetic  1.66 us (7%)
  local copies, waits for them, and re-layouts  0.6 us (3%)
    ppermute x8, waiting for transfers between devices, in_plane(): lax.ppermute(value, 'blk', [(a * inner + s, a * inner + t) for a in range...  6.59 us
    ppermute x3, starting transfers between devices, along_outer(): lax.ppermute(value, 'blk', [(s * inner + b, t * inner + b) for s, t in ed...  5.96 us
    ppermute x8, starting transfers between devices, in_plane(): lax.ppermute(value, 'blk', [(a * inner + s, a * inner + t) for a in range...  3.97 us
    pallas_call x3, Pallas kernels, tile(): pl.pallas_call(functools.partial(tile_kernel, list(order), tuple(pairs),...  2.9 us
    concatenate x1, other arithmetic, on_device(): longer = jnp.concatenate([features, probes.T, spare], axis=0)  1.03 us
    ppermute x3, waiting for transfers between devices, along_outer(): lax.ppermute(value, 'blk', [(s * inner + b, t * inner + b) for s, t in ed...  0.7 us
    transpose x1, other arithmetic, on_device(): return functools.reduce(lambda sofar, term: sofar + term, total).T  0.63 us
    unnamed x2, local copies, waits for them, and re-layouts  0.52 us
  transfers between devices with their start and end apart: 11, of which 7 were waited for; matrix products, arithmetic and copies ran while one was open for 0% of the time, Pallas kernels for 13%

profile of v18, /device:TPU:0, one launch (start us, length us, event | category | flops | bytes accessed | tf_op | source)
XLA Modules:
  0.0 22.4 jit_solution(9935135761797092693)
XLA Ops:
  0.0 0.1 pad.2.clone
  0.1 1.0 %maximum_maximum_fusion.longer_ref = bf16[304,256]{1,0:T(8,128)(2,1)S(1)} fusion(bf16[32,256]{1,0:T(8,128)(2,1)} %bitcast.5, bf16[256,256]{1,0:T(8,128)(2,1)} %param.3, bf16[304]{0:T(512)(128)(2,1)S(1)} %pad.2.clone), kind=kLoop, calls=%fused_computation | loop fusion | flops 466944 | bytes 303712 | tf_op jit(solution)/shard_map/concatenate | solution.py:164
  1.1 5.1 %collective-permute-start.6 = (bf16[304,256]{1,0:T(8,128)(2,1)S(1)}, bf16[304,256]{1,0:T(8,128)(2,1)S(1)}, u32[]{:S(2)}, u32[]{:S(2)}) collective-permute-start(bf16[304,256]{1,0:T(8,128)(2,1)S(1)} %maximum_maximum_fusion.longer_ref), channel_id=1, source_target_pairs={{12,4},{13,5},{14,6},{15,7},{4,8},{5,9},{6,10},{7,11},{8,0},{9,1},... | collective-permute-start | bytes 466952 | tf_op jit(solution)/shard_map/ppermute | solution.py:168
  6.2 1.6 %collective-permute-start.1 = (bf16[144,256]{1,0:T(8,128)(2,1)S(1)}, bf16[144,256]{1,0:T(8,128)(2,1)S(1)}, u32[]{:S(2)}, u32[]{:S(2)}) collective-permute-start(bf16[144,256]{1,0:T(8,128)(2,1)S(1)} %get-tuple-element.18), channel_id=1, source_target_pairs={{0,2},{1,3},{2,0},{3,1},{4,6},{5,7},{6,4},{7,5},{8,10},{9,11},{10,... | collective-permute-start | bytes 221192 | tf_op jit(solution)/shard_map/ppermute | solution.py:171
  7.8 0.5 %collective-permute-start.2 = (bf16[144,256]{1,0:T(8,128)(2,1)S(1)}, bf16[144,256]{1,0:T(8,128)(2,1)S(1)}, u32[]{:S(2)}, u32[]{:S(2)}) collective-permute-start(bf16[144,256]{1,0:T(8,128)(2,1)S(1)} %get-tuple-element.19), channel_id=1, source_target_pairs={{0,2},{1,3},{2,0},{3,1},{4,6},{5,7},{6,4},{7,5},{8,10},{9,11},{10,... | collective-permute-start | bytes 221192 | tf_op jit(solution)/shard_map/ppermute | solution.py:171
  8.3 0.0 collective-permute-start
  8.3 0.0 collective-permute-start.5
  8.3 2.9 %collective-permute-done.1.refs_4_.refs_2_ = bf16[144,256]{1,0:T(8,128)(2,1)S(1)} collective-permute-done((bf16[144,256]{1,0:T(8,128)(2,1)S(1)}, bf16[144,256]{1,0:T(8,128)(2,1)S(1)}, u32[]{:S(2)}, u32[]{:S(2)}) %collective-permute-start.1) | collective-permute-done | bytes 73760 | tf_op jit(solution)/shard_map/ppermute | solution.py:171
  11.3 0.0 collective-permute-start.3
  11.3 0.9 %collective-permute-done.2.refs_5_.refs_3_ = bf16[144,256]{1,0:T(8,128)(2,1)S(1)} collective-permute-done((bf16[144,256]{1,0:T(8,128)(2,1)S(1)}, bf16[144,256]{1,0:T(8,128)(2,1)S(1)}, u32[]{:S(2)}, u32[]{:S(2)}) %collective-permute-start.2) | collective-permute-done | bytes 73760 | tf_op jit(solution)/shard_map/ppermute | solution.py:171
  12.2 0.4 %collective-permute-done.3.refs_1_.refs_4_ = bf16[144,256]{1,0:T(8,128)(2,1)S(1)} collective-permute-done((bf16[144,256]{1,0:T(8,128)(2,1)S(1)}, bf16[144,256]{1,0:T(8,128)(2,1)S(1)}, u32[]{:S(2)}, u32[]{:S(2)}) %collective-permute-start.3) | collective-permute-done | bytes 73760 | tf_op jit(solution)/shard_map/ppermute | solution.py:171
  12.5 0.9 %collective-permute-done.4.refs_2_.refs_5_ = bf16[144,256]{1,0:T(8,128)(2,1)S(1)} collective-permute-done((bf16[144,256]{1,0:T(8,128)(2,1)S(1)}, bf16[144,256]{1,0:T(8,128)(2,1)S(1)}, u32[]{:S(2)}, u32[]{:S(2)}) %collective-permute-start.4) | collective-permute-done | bytes 73760 | tf_op jit(solution)/shard_map/ppermute | solution.py:171
  13.5 1.1 %shard_map.38 = (f32[32,256]{1,0:T(8,128)S(1)}, f32[32,256]{1,0:T(8,128)S(1)}, f32[32,256]{1,0:T(8,128)S(1)}, f32[32,256]{1,0:T(8,128)S(1)}, f32[32,256]{1,0:T(8,128)S(1)}) custom-call(bf16[288,256]{1,0:T(8,128)(2,1)S(1)} %get-tuple-element.17.refs_0_.refs_6_, bf16[144,256]{1,0:T(8,128)(2,1)S(1)} %collective-permute-done.3.refs_1_.refs_4_, ...), custom_call_target="tpu_custom_call" | custom-call | tf_op jit(solution)/shard_map/pallas_call | solution.py:120
  14.6 0.9 %collective-permute-start.10 = (f32[32,256]{1,0:T(8,128)S(1)}, f32[32,256]{1,0:T(8,128)S(1)}, u32[]{:S(2)}, u32[]{:S(2)}) collective-permute-start(f32[32,256]{1,0:T(8,128)S(1)} %get-tuple-element.28), channel_id=1, source_target_pairs={{4,12},{5,13},{6,14},{7,15},{8,4},{9,5},{10,6},{11,7},{0,8},{1,9},... | collective-permute-start | bytes 98312 | tf_op jit(solution)/shard_map/ppermute | solution.py:168
  15.4 0.3 %collective-permute-done.5.refs_6_ = bf16[288,256]{1,0:T(8,128)(2,1)S(1)} collective-permute-done((bf16[288,256]{1,0:T(8,128)(2,1)S(1)}, bf16[288,256]{1,0:T(8,128)(2,1)S(1)}, u32[]{:S(2)}, u32[]{:S(2)}) %collective-permute-start.5) | collective-permute-done | bytes 147488 | tf_op jit(solution)/shard_map/ppermute | solution.py:168
  15.7 0.9 %shard_map.39 = (f32[32,256]{1,0:T(8,128)S(1)}, f32[32,256]{1,0:T(8,128)S(1)}, f32[32,256]{1,0:T(8,128)S(1)}, f32[32,256]{1,0:T(8,128)S(1)}) custom-call(bf16[288,256]{1,0:T(8,128)(2,1)S(1)} %get-tuple-element.17.refs_0_.refs_6_, bf16[288,256]{1,0:T(8,128)(2,1)S(1)} %collective-permute-done.refs_3_.refs_1_, ...), custom_call_target="tpu_custom_call" | custom-call | flops 167772160 | bytes 655360 | tf_op jit(solution)/shard_map/pallas_call | solution.py:120
  16.6 1.3 %collective-permute-start.9 = (f32[32,256]{1,0:T(8,128)S(1)}, f32[32,256]{1,0:T(8,128)S(1)}, u32[]{:S(2)}, u32[]{:S(2)}) collective-permute-start(f32[32,256]{1,0:T(8,128)S(1)} %get-tuple-element.27), channel_id=1, source_target_pairs={{0,3},{1,2},{2,1},{3,0},{4,7},{5,6},{6,5},{7,4},{8,11},{9,10},{10,... | collective-permute-start | bytes 98312 | tf_op jit(solution)/shard_map/ppermute | solution.py:171
  17.9 0.5 %collective-permute-start.8 = (f32[32,256]{1,0:T(8,128)S(1)}, f32[32,256]{1,0:T(8,128)S(1)}, u32[]{:S(2)}, u32[]{:S(2)}) collective-permute-start(f32[32,256]{1,0:T(8,128)S(1)} %get-tuple-element.26), channel_id=1, source_target_pairs={{0,2},{1,3},{2,0},{3,1},{4,6},{5,7},{6,4},{7,5},{8,10},{9,11},{10,... | collective-permute-start | bytes 98312 | tf_op jit(solution)/shard_map/ppermute | solution.py:171
  18.3 0.2 collective-permute-start.7
  18.5 0.5 %copy-done = f32[256]{0:T(256)S(1)} copy-done((f32[256]{0:T(256)S(1)}, f32[256]{0:T(256)}, u32[]{:S(2)}) %copy-start) | copy-done | bytes 1048
  19.0 0.9 %shard_map.40 = f32[32,256]{1,0:T(8,128)S(1)} custom-call(bf16[288,256]{1,0:T(8,128)(2,1)S(1)} %get-tuple-element.17.refs_0_.refs_6_, bf16[288,256]{1,0:T(8,128)(2,1)S(1)} %collective-permute-done.refs_3_.refs_1_, bf16[144,256]{1,0:T(8,128)(2,1)S(1)} %collective-permute-done.1.refs_4_.refs_2_, bf16[144,256]{1,0:T(8,128)(2,1)S(1)} %collective-permute-done.2.refs_5_.refs_3_, ...), custom_call_target="tpu_custom_call" | custom-call | flops 167772160 | bytes 655360 | tf_op jit(solution)/shard_map/pallas_call | solution.py:120
  19.9 0.4 %collective-permute-done.10 = f32[32,256]{1,0:T(8,128)S(1)} collective-permute-done((f32[32,256]{1,0:T(8,128)S(1)}, f32[32,256]{1,0:T(8,128)S(1)}, u32[]{:S(2)}, u32[]{:S(2)}) %collective-permute-start.10) | collective-permute-done | bytes 32800 | tf_op jit(solution)/shard_map/ppermute | solution.py:168
  20.3 1.5 %collective-permute-done.8 = f32[32,256]{1,0:T(8,128)S(1)} collective-permute-done((f32[32,256]{1,0:T(8,128)S(1)}, f32[32,256]{1,0:T(8,128)S(1)}, u32[]{:S(2)}, u32[]{:S(2)}) %collective-permute-start.8) | collective-permute-done | bytes 32800 | tf_op jit(solution)/shard_map/ppermute | solution.py:171
  21.8 0.6 %add_bitcast_fusion = f32[256,32]{0,1:T(8,128)} fusion(f32[32,256]{1,0:T(8,128)S(1)} %collective-permute-done.10, f32[32,256]{1,0:T(8,128)S(1)} %collective-permute-done.9, f32[32,256]{1,0:T(8,128)S(1)} %collective-permute-done.8, f32[32,256]{1,0:T(8,128)S(1)} %collective-permute-done.7, f32[32,256]{1,0:T(8,128)S(1)} %get-tuple-element.24, ...), kind=kLoop, calls=%fused_computation.1 | loop fusion | flops 40960 | bytes 229376 | tf_op jit(solution)/shard_map/transpose | solution.py:195
  (8 shorter events, 0.0 us)
Async XLA Ops:
  1.1 12.3 %collective-permute-start.6 = (bf16[304,256]{1,0:T(8,128)(2,1)S(1)}, bf16[304,256]{1,0:T(8,128)(2,1)S(1)}, u32[]{:S(2)}, u32[]{:S(2)}) collective-permute-start(bf16[304,256]{1,0:T(8,128)(2,1)S(1)} %maximum_maximum_fusion.longer_ref), channel_id=1, source_target_pairs={{12,4},{13,5},{14,6},{15,7},{4,8},{5,9},{6,10},{7,11},{8,0},{9,1},... | collective-permute-start | bytes 466952 | tf_op jit(solution)/shard_map/ppermute | solution.py:168
  6.2 5.0 %collective-permute-start.1 = (bf16[144,256]{1,0:T(8,128)(2,1)S(1)}, bf16[144,256]{1,0:T(8,128)(2,1)S(1)}, u32[]{:S(2)}, u32[]{:S(2)}) collective-permute-start(bf16[144,256]{1,0:T(8,128)(2,1)S(1)} %get-tuple-element.18), channel_id=1, source_target_pairs={{0,2},{1,3},{2,0},{3,1},{4,6},{5,7},{6,4},{7,5},{8,10},{9,11},{10,... | collective-permute-start | bytes 221192 | tf_op jit(solution)/shard_map/ppermute | solution.py:171
  7.8 4.4 %collective-permute-start.2 = (bf16[144,256]{1,0:T(8,128)(2,1)S(1)}, bf16[144,256]{1,0:T(8,128)(2,1)S(1)}, u32[]{:S(2)}, u32[]{:S(2)}) collective-permute-start(bf16[144,256]{1,0:T(8,128)(2,1)S(1)} %get-tuple-element.19), channel_id=1, source_target_pairs={{0,2},{1,3},{2,0},{3,1},{4,6},{5,7},{6,4},{7,5},{8,10},{9,11},{10,... | collective-permute-start | bytes 221192 | tf_op jit(solution)/shard_map/ppermute | solution.py:171
  8.3 5.1 %collective-permute-start = (bf16[288,256]{1,0:T(8,128)(2,1)S(1)}, bf16[288,256]{1,0:T(8,128)(2,1)S(1)}, u32[]{:S(2)}, u32[]{:S(2)}) collective-permute-start(bf16[288,256]{1,0:T(8,128)(2,1)S(1)} %get-tuple-element.17.refs_0_.refs_6_), channel_id=1, source_target_pairs={{0,1},{1,0},{2,3},{3,2},{4,5},{5,4},{6,7},{7,6},{8,9},{9,8},{10,11... | collective-permute-start | bytes 442376 | tf_op jit(solution)/shard_map/ppermute | solution.py:171
  8.3 7.4 %collective-permute-start.5 = (bf16[288,256]{1,0:T(8,128)(2,1)S(1)}, bf16[288,256]{1,0:T(8,128)(2,1)S(1)}, u32[]{:S(2)}, u32[]{:S(2)}) collective-permute-start(bf16[288,256]{1,0:T(8,128)(2,1)S(1)} %get-tuple-element.17.refs_0_.refs_6_), channel_id=1, source_target_pairs={{12,8},{13,9},{14,10},{15,11},{4,0},{5,1},{6,2},{7,3},{8,12},{9,13... | collective-permute-start | bytes 442376 | tf_op jit(solution)/shard_map/ppermute | solution.py:168
  11.3 1.3 %collective-permute-start.3 = (bf16[144,256]{1,0:T(8,128)(2,1)S(1)}, bf16[144,256]{1,0:T(8,128)(2,1)S(1)}, u32[]{:S(2)}, u32[]{:S(2)}) collective-permute-start(bf16[144,256]{1,0:T(8,128)(2,1)S(1)} %collective-permute-done.1.refs_4_.refs_2_), channel_id=1, source_target_pairs={{0,1},{1,0},{2,3},{3,2},{4,5},{5,4},{6,7},{7,6},{8,9},{9,8},{10,11... | collective-permute-start | bytes 221192 | tf_op jit(solution)/shard_map/ppermute | solution.py:171
  12.2 1.3 %collective-permute-start.4 = (bf16[144,256]{1,0:T(8,128)(2,1)S(1)}, bf16[144,256]{1,0:T(8,128)(2,1)S(1)}, u32[]{:S(2)}, u32[]{:S(2)}) collective-permute-start(bf16[144,256]{1,0:T(8,128)(2,1)S(1)} %collective-permute-done.2.refs_5_.refs_3_), channel_id=1, source_target_pairs={{0,1},{1,0},{2,3},{3,2},{4,5},{5,4},{6,7},{7,6},{8,9},{9,8},{10,11... | collective-permute-start | bytes 221192 | tf_op jit(solution)/shard_map/ppermute | solution.py:171
  14.6 5.7 %collective-permute-start.10 = (f32[32,256]{1,0:T(8,128)S(1)}, f32[32,256]{1,0:T(8,128)S(1)}, u32[]{:S(2)}, u32[]{:S(2)}) collective-permute-start(f32[32,256]{1,0:T(8,128)S(1)} %get-tuple-element.28), channel_id=1, source_target_pairs={{4,12},{5,13},{6,14},{7,15},{8,4},{9,5},{10,6},{11,7},{0,8},{1,9},... | collective-permute-start | bytes 98312 | tf_op jit(solution)/shard_map/ppermute | solution.py:168
  16.6 3.7 %collective-permute-start.9 = (f32[32,256]{1,0:T(8,128)S(1)}, f32[32,256]{1,0:T(8,128)S(1)}, u32[]{:S(2)}, u32[]{:S(2)}) collective-permute-start(f32[32,256]{1,0:T(8,128)S(1)} %get-tuple-element.27), channel_id=1, source_target_pairs={{0,3},{1,2},{2,1},{3,0},{4,7},{5,6},{6,5},{7,4},{8,11},{9,10},{10,... | collective-permute-start | bytes 98312 | tf_op jit(solution)/shard_map/ppermute | solution.py:171
  17.9 3.9 %collective-permute-start.8 = (f32[32,256]{1,0:T(8,128)S(1)}, f32[32,256]{1,0:T(8,128)S(1)}, u32[]{:S(2)}, u32[]{:S(2)}) collective-permute-start(f32[32,256]{1,0:T(8,128)S(1)} %get-tuple-element.26), channel_id=1, source_target_pairs={{0,2},{1,3},{2,0},{3,1},{4,6},{5,7},{6,4},{7,5},{8,10},{9,11},{10,... | collective-permute-start | bytes 98312 | tf_op jit(solution)/shard_map/ppermute | solution.py:171
  18.3 0.7 %copy-start = (f32[256]{0:T(256)S(1)}, f32[256]{0:T(256)}, u32[]{:S(2)}) copy-start(f32[256]{0:T(256)} %param.5) | copy-start | bytes 3076
  18.3 3.5 %collective-permute-start.7 = (f32[32,256]{1,0:T(8,128)S(1)}, f32[32,256]{1,0:T(8,128)S(1)}, u32[]{:S(2)}, u32[]{:S(2)}) collective-permute-start(f32[32,256]{1,0:T(8,128)S(1)} %get-tuple-element.25), channel_id=1, source_target_pairs={{0,1},{1,0},{2,3},{3,2},{4,5},{5,4},{6,7},{7,6},{8,9},{9,8},{10,11... | collective-permute-start | bytes 98312 | tf_op jit(solution)/shard_map/ppermute | solution.py:171

commit v19 on v15

--- a/solution.py
+++ b/solution.py
@@ -73,24 +73,28 @@
     rest = list(refs[rows_in + cols_in :])
     noise = [rest.pop(0) for _ in range(noise_in)]
     sums = {name: rest.pop(0)[...] for name in known}
-    ready_rows, ready_cols = {}, {}
-    for row, col, kind in pairs:
-        if row not in ready_rows:
-            wide = rows[row][0:shard, :].astype(jnp.float32)
-            ready_rows[row] = jnp.sum(wide * wide, axis=1, keepdims=True)
-        if col not in ready_cols:
-            block = cols[col][0:shard, :]
-            ready_cols[col] = block * jnp.asarray(-2.0, block.dtype), lane_squares(block)
-        scaled, col_squares = ready_cols[col]
-        row_block, row_probes = rows[row][0:shard, :], rows[row][pl.ds(shard, vectors), :]
-        cross = lax.dot_general(row_block, scaled, ROWS_BY_ROWS, preferred_element_type=jnp.float32)
-        kernel = matern((ready_rows[row] + col_squares) + cross)
+    squares = {}
+    for col in sorted({col for _, col, _ in pairs}):
+        kind = next(kind for _, place, kind in pairs if place == col)
+        members = [row for row, place, _ in pairs if place == col]
+        for row in members:
+            if row not in squares:
+                wide = rows[row][0:shard, :].astype(jnp.float32)
+                squares[row] = jnp.sum(wide * wide, axis=1, keepdims=True)
+        block = cols[col][0:shard, :]
+        scaled, col_squares = block * jnp.asarray(-2.0, block.dtype), lane_squares(block)
+        joined = jnp.concatenate([rows[row][0:shard, :] for row in members])
+        cross = lax.dot_general(joined, scaled, ROWS_BY_ROWS, preferred_element_type=jnp.float32)
+        kernel = matern((jnp.concatenate([squares[row] for row in members]) + col_squares) + cross)
         found = {}
         if "back" in kind:
-            found["back", col] = jnp.dot(row_probes, kernel, preferred_element_type=jnp.float32)
+            probes = jnp.concatenate([rows[row][pl.ds(shard, vectors), :] for row in members], axis=1)
+            found["back", col] = jnp.dot(probes, kernel, preferred_element_type=jnp.float32)
         if "rows" in kind:
             col_probes = cols[col][pl.ds(shard, vectors), :]
-            found["rows", row] = lax.dot_general(col_probes, kernel, ROWS_BY_ROWS, preferred_element_type=jnp.float32)
+            terms = lax.dot_general(col_probes, kernel, ROWS_BY_ROWS, preferred_element_type=jnp.float32)
+            for place, row in enumerate(members):
+                found["rows", row] = terms[:, place * shard : (place + 1) * shard]
         for name, value in found.items():
             sums[name] = sums[name] + value if name in sums else value
     for place in range(noise_in):

time: 22.4 us -> 22.4 us (level)
  no operation moved by 1% of the time
where the time goes in v19:
time: 22.4 us; the launch traced here: 22.1 us
  starting transfers between devices  10.5 us (47%)
  waiting for transfers between devices  7.17 us (32%)
  Pallas kernels  2.85 us (13%)
  other arithmetic  1.56 us (7%)
    ppermute x6, starting transfers between devices, in_plane(): lax.ppermute(value, 'blk', [(a * inner + s, a * inner + t) for a in range...  5.29 us
    ppermute x3, waiting for transfers between devices, along_outer(): lax.ppermute(value, 'blk', [(s * inner + b, t * inner + b) for s, t in ed...  5.29 us
    ppermute x3, starting transfers between devices, along_outer(): lax.ppermute(value, 'blk', [(s * inner + b, t * inner + b) for s, t in ed...  5.21 us
    pallas_call x3, Pallas kernels, tile(): pl.pallas_call(functools.partial(tile_kernel, list(order), tuple(pairs),...  2.83 us
    ppermute x6, waiting for transfers between devices, in_plane(): lax.ppermute(value, 'blk', [(a * inner + s, a * inner + t) for a in range...  1.88 us
    concatenate x1, other arithmetic, on_device(): packed = jnp.concatenate([features, probes.T], axis=0)  0.93 us
    transpose x1, other arithmetic, on_device(): functools.reduce(lambda sofar, term: sofar + term, total + [sums['rows',...  0.63 us
  transfers between devices with their start and end apart: 9, of which 6 were waited for; matrix products, arithmetic and copies ran while one was open for 0% of the time, Pallas kernels for 13%

profile of v19, /device:TPU:0, one launch (start us, length us, event | category | flops | bytes accessed | tf_op | source)
XLA Modules:
  0.0 22.1 jit_solution(3372295564839148436)
XLA Ops:
  0.0 0.9 %pad_maximum_fusion.refs_0_.refs_4_.from_ref = bf16[288,256]{1,0:T(8,128)(2,1)S(1)} fusion(bf16[32,256]{1,0:T(8,128)(2,1)} %bitcast.5, bf16[256,256]{1,0:T(8,128)(2,1)} %param.3), kind=kLoop, calls=%fused_computation | loop fusion | flops 294912 | bytes 294912 | tf_op jit(solution)/shard_map/concatenate | solution.py:153
  0.9 3.0 %collective-permute-start.1 = (bf16[288,256]{1,0:T(8,128)(2,1)S(1)}, bf16[288,256]{1,0:T(8,128)(2,1)S(1)}, u32[]{:S(2)}, u32[]{:S(2)}) collective-permute-start(bf16[288,256]{1,0:T(8,128)(2,1)S(1)} %pad_maximum_fusion.refs_0_.refs_4_.from_ref), channel_id=1, source_target_pairs={{0,2},{1,3},{2,0},{3,1},{4,6},{5,7},{6,4},{7,5},{8,10},{9,11},{10,... | collective-permute-start | bytes 442376 | tf_op jit(solution)/shard_map/ppermute | solution.py:159
  4.0 3.7 %collective-permute-start.4 = (bf16[304,256]{1,0:T(8,128)(2,1)S(1)}, bf16[304,256]{1,0:T(8,128)(2,1)S(1)}, u32[]{:S(2)}, u32[]{:S(2)}) collective-permute-start(bf16[304,256]{1,0:T(8,128)(2,1)S(1)} %shard_map.38), channel_id=1, source_target_pairs={{12,4},{13,5},{14,6},{15,7},{4,8},{5,9},{6,10},{7,11},{8,0},{9,1},... | collective-permute-start | bytes 466952 | tf_op jit(solution)/shard_map/ppermute | solution.py:156
  7.6 0.0 collective-permute-start.3
  7.6 0.0 collective-permute-start
  7.6 0.2 collective-permute-done.1.refs_2_.refs_4_
  7.8 0.3 %collective-permute-start.2 = (bf16[288,256]{1,0:T(8,128)(2,1)S(1)}, bf16[288,256]{1,0:T(8,128)(2,1)S(1)}, u32[]{:S(2)}, u32[]{:S(2)}) collective-permute-start(bf16[288,256]{1,0:T(8,128)(2,1)S(1)} %collective-permute-done.1.refs_2_.refs_4_), channel_id=1, source_target_pairs={{0,1},{1,0},{2,3},{3,2},{4,5},{5,4},{6,7},{7,6},{8,9},{9,8},{10,11... | collective-permute-start | bytes 442376 | tf_op jit(solution)/shard_map/ppermute | solution.py:159
  8.2 0.9 %collective-permute-done.refs_1_.refs_3_ = bf16[288,256]{1,0:T(8,128)(2,1)S(1)} collective-permute-done((bf16[288,256]{1,0:T(8,128)(2,1)S(1)}, bf16[288,256]{1,0:T(8,128)(2,1)S(1)}, u32[]{:S(2)}, u32[]{:S(2)}) %collective-permute-start) | collective-permute-done | bytes 147488 | tf_op jit(solution)/shard_map/ppermute | solution.py:159
  9.0 4.8 %collective-permute-done.4.refs_2_ = bf16[304,256]{1,0:T(8,128)(2,1)S(1)} collective-permute-done((bf16[304,256]{1,0:T(8,128)(2,1)S(1)}, bf16[304,256]{1,0:T(8,128)(2,1)S(1)}, u32[]{:S(2)}, u32[]{:S(2)}) %collective-permute-start.4) | collective-permute-done | bytes 155680 | tf_op jit(solution)/shard_map/ppermute | solution.py:156
  13.9 0.0 collective-permute-done.2.refs_3_.refs_1_
  13.9 1.0 %shard_map.39 = (f32[32,256]{1,0:T(8,128)S(1)}, f32[32,256]{1,0:T(8,128)S(1)}, f32[32,256]{1,0:T(8,128)S(1)}, f32[32,256]{1,0:T(8,128)S(1)}, f32[32,256]{1,0:T(8,128)S(1)}) custom-call(bf16[288,256]{1,0:T(8,128)(2,1)S(1)} %pad_maximum_fusion.refs_0_.refs_4_.from_ref, bf16[288,256]{1,0:T(8,128)(2,1)S(1)} %collective-permute-done.2.refs_3_.refs_1_, ...), custom_call_target="tpu_custom_call" | custom-call | tf_op jit(solution)/shard_map/pallas_call | solution.py:114
  14.9 1.6 %collective-permute-start.8 = (f32[32,256]{1,0:T(8,128)S(1)}, f32[32,256]{1,0:T(8,128)S(1)}, u32[]{:S(2)}, u32[]{:S(2)}) collective-permute-start(f32[32,256]{1,0:T(8,128)S(1)} %get-tuple-element.21), channel_id=1, source_target_pairs={{4,12},{5,13},{6,14},{7,15},{8,4},{9,5},{10,6},{11,7},{0,8},{1,9},... | collective-permute-start | bytes 98312 | tf_op jit(solution)/shard_map/ppermute | solution.py:156
  16.5 0.0 collective-permute-done.3.refs_4_
  16.5 0.9 %shard_map.40 = (f32[32,256]{1,0:T(8,128)S(1)}, f32[32,256]{1,0:T(8,128)S(1)}, f32[32,256]{1,0:T(8,128)S(1)}, f32[32,256]{1,0:T(8,128)S(1)}) custom-call(bf16[288,256]{1,0:T(8,128)(2,1)S(1)} %pad_maximum_fusion.refs_0_.refs_4_.from_ref, bf16[288,256]{1,0:T(8,128)(2,1)S(1)} %collective-permute-done.refs_1_.refs_3_, ...), custom_call_target="tpu_custom_call" | custom-call | flops 167772160 | bytes 655360 | tf_op jit(solution)/shard_map/pallas_call | solution.py:114
  17.4 0.1 collective-permute-start.7
  17.5 0.6 %collective-permute-start.6 = (f32[32,256]{1,0:T(8,128)S(1)}, f32[32,256]{1,0:T(8,128)S(1)}, u32[]{:S(2)}, u32[]{:S(2)}) collective-permute-start(f32[32,256]{1,0:T(8,128)S(1)} %get-tuple-element.19), channel_id=1, source_target_pairs={{0,2},{1,3},{2,0},{3,1},{4,6},{5,7},{6,4},{7,5},{8,10},{9,11},{10,... | collective-permute-start | bytes 98312 | tf_op jit(solution)/shard_map/ppermute | solution.py:159
  18.0 1.3 %collective-permute-start.5 = (f32[32,256]{1,0:T(8,128)S(1)}, f32[32,256]{1,0:T(8,128)S(1)}, u32[]{:S(2)}, u32[]{:S(2)}) collective-permute-start(f32[32,256]{1,0:T(8,128)S(1)} %get-tuple-element.18), channel_id=1, source_target_pairs={{0,1},{1,0},{2,3},{3,2},{4,5},{5,4},{6,7},{7,6},{8,9},{9,8},{10,11... | collective-permute-start | bytes 98312 | tf_op jit(solution)/shard_map/ppermute | solution.py:159
  19.3 0.0 copy-done
  19.3 0.9 %shard_map.37 = f32[32,256]{1,0:T(8,128)S(1)} custom-call(bf16[288,256]{1,0:T(8,128)(2,1)S(1)} %pad_maximum_fusion.refs_0_.refs_4_.from_ref, bf16[288,256]{1,0:T(8,128)(2,1)S(1)} %collective-permute-done.refs_1_.refs_3_, bf16[288,256]{1,0:T(8,128)(2,1)S(1)} %collective-permute-done.1.refs_2_.refs_4_, ...), custom_call_target="tpu_custom_call" | custom-call | flops 167772160 | bytes 655360 | tf_op jit(solution)/shard_map/pallas_call | solution.py:114
  20.2 0.4 %collective-permute-done.8 = f32[32,256]{1,0:T(8,128)S(1)} collective-permute-done((f32[32,256]{1,0:T(8,128)S(1)}, f32[32,256]{1,0:T(8,128)S(1)}, u32[]{:S(2)}, u32[]{:S(2)}) %collective-permute-start.8) | collective-permute-done | bytes 32800 | tf_op jit(solution)/shard_map/ppermute | solution.py:156
  20.6 0.1 collective-permute-done.7
  20.8 0.7 %collective-permute-done.6 = f32[32,256]{1,0:T(8,128)S(1)} collective-permute-done((f32[32,256]{1,0:T(8,128)S(1)}, f32[32,256]{1,0:T(8,128)S(1)}, u32[]{:S(2)}, u32[]{:S(2)}) %collective-permute-start.6) | collective-permute-done | bytes 32800 | tf_op jit(solution)/shard_map/ppermute | solution.py:159
  21.5 0.0 collective-permute-done.5
  21.5 0.6 %add_bitcast_fusion = f32[256,32]{0,1:T(8,128)} fusion(f32[32,256]{1,0:T(8,128)S(1)} %get-tuple-element.22, f32[32,256]{1,0:T(8,128)S(1)} %collective-permute-done.8, f32[32,256]{1,0:T(8,128)S(1)} %collective-permute-done.7, f32[32,256]{1,0:T(8,128)S(1)} %collective-permute-done.6, f32[32,256]{1,0:T(8,128)S(1)} %shard_map.37, ...), kind=kLoop, calls=%fused_computation.1 | loop fusion | flops 40960 | bytes 229376 | tf_op jit(solution)/shard_map/transpose | solution.py:184
  (2 shorter events, 0.0 us)
Async XLA Ops:
  0.9 6.9 %collective-permute-start.1 = (bf16[288,256]{1,0:T(8,128)(2,1)S(1)}, bf16[288,256]{1,0:T(8,128)(2,1)S(1)}, u32[]{:S(2)}, u32[]{:S(2)}) collective-permute-start(bf16[288,256]{1,0:T(8,128)(2,1)S(1)} %pad_maximum_fusion.refs_0_.refs_4_.from_ref), channel_id=1, source_target_pairs={{0,2},{1,3},{2,0},{3,1},{4,6},{5,7},{6,4},{7,5},{8,10},{9,11},{10,... | collective-permute-start | bytes 442376 | tf_op jit(solution)/shard_map/ppermute | solution.py:159
  4.0 9.9 %collective-permute-start.4 = (bf16[304,256]{1,0:T(8,128)(2,1)S(1)}, bf16[304,256]{1,0:T(8,128)(2,1)S(1)}, u32[]{:S(2)}, u32[]{:S(2)}) collective-permute-start(bf16[304,256]{1,0:T(8,128)(2,1)S(1)} %shard_map.38), channel_id=1, source_target_pairs={{12,4},{13,5},{14,6},{15,7},{4,8},{5,9},{6,10},{7,11},{8,0},{9,1},... | collective-permute-start | bytes 466952 | tf_op jit(solution)/shard_map/ppermute | solution.py:156
  7.6 8.8 %collective-permute-start.3 = (bf16[304,256]{1,0:T(8,128)(2,1)S(1)}, bf16[304,256]{1,0:T(8,128)(2,1)S(1)}, u32[]{:S(2)}, u32[]{:S(2)}) collective-permute-start(bf16[304,256]{1,0:T(8,128)(2,1)S(1)} %shard_map.38), channel_id=1, source_target_pairs={{12,8},{13,9},{14,10},{15,11},{4,0},{5,1},{6,2},{7,3},{8,12},{9,13... | collective-permute-start | bytes 466952 | tf_op jit(solution)/shard_map/ppermute | solution.py:156
  7.6 1.4 %collective-permute-start = (bf16[288,256]{1,0:T(8,128)(2,1)S(1)}, bf16[288,256]{1,0:T(8,128)(2,1)S(1)}, u32[]{:S(2)}, u32[]{:S(2)}) collective-permute-start(bf16[288,256]{1,0:T(8,128)(2,1)S(1)} %pad_maximum_fusion.refs_0_.refs_4_.from_ref), channel_id=1, source_target_pairs={{0,1},{1,0},{2,3},{3,2},{4,5},{5,4},{6,7},{7,6},{8,9},{9,8},{10,11... | collective-permute-start | bytes 442376 | tf_op jit(solution)/shard_map/ppermute | solution.py:159
  7.8 6.0 %collective-permute-start.2 = (bf16[288,256]{1,0:T(8,128)(2,1)S(1)}, bf16[288,256]{1,0:T(8,128)(2,1)S(1)}, u32[]{:S(2)}, u32[]{:S(2)}) collective-permute-start(bf16[288,256]{1,0:T(8,128)(2,1)S(1)} %collective-permute-done.1.refs_2_.refs_4_), channel_id=1, source_target_pairs={{0,1},{1,0},{2,3},{3,2},{4,5},{5,4},{6,7},{7,6},{8,9},{9,8},{10,11... | collective-permute-start | bytes 442376 | tf_op jit(solution)/shard_map/ppermute | solution.py:159
  14.9 5.7 %collective-permute-start.8 = (f32[32,256]{1,0:T(8,128)S(1)}, f32[32,256]{1,0:T(8,128)S(1)}, u32[]{:S(2)}, u32[]{:S(2)}) collective-permute-start(f32[32,256]{1,0:T(8,128)S(1)} %get-tuple-element.21), channel_id=1, source_target_pairs={{4,12},{5,13},{6,14},{7,15},{8,4},{9,5},{10,6},{11,7},{0,8},{1,9},... | collective-permute-start | bytes 98312 | tf_op jit(solution)/shard_map/ppermute | solution.py:156
  17.4 3.4 %collective-permute-start.7 = (f32[32,256]{1,0:T(8,128)S(1)}, f32[32,256]{1,0:T(8,128)S(1)}, u32[]{:S(2)}, u32[]{:S(2)}) collective-permute-start(f32[32,256]{1,0:T(8,128)S(1)} %get-tuple-element.20), channel_id=1, source_target_pairs={{0,3},{1,2},{2,1},{3,0},{4,7},{5,6},{6,5},{7,4},{8,11},{9,10},{10,... | collective-permute-start | bytes 98312 | tf_op jit(solution)/shard_map/ppermute | solution.py:159
  17.5 4.0 %collective-permute-start.6 = (f32[32,256]{1,0:T(8,128)S(1)}, f32[32,256]{1,0:T(8,128)S(1)}, u32[]{:S(2)}, u32[]{:S(2)}) collective-permute-start(f32[32,256]{1,0:T(8,128)S(1)} %get-tuple-element.19), channel_id=1, source_target_pairs={{0,2},{1,3},{2,0},{3,1},{4,6},{5,7},{6,4},{7,5},{8,10},{9,11},{10,... | collective-permute-start | bytes 98312 | tf_op jit(solution)/shard_map/ppermute | solution.py:159
  18.0 1.3 %copy-start = (f32[256]{0:T(256)S(1)}, f32[256]{0:T(256)}, u32[]{:S(2)}) copy-start(f32[256]{0:T(256)} %param.5) | copy-start | bytes 3076
  18.0 3.5 %collective-permute-start.5 = (f32[32,256]{1,0:T(8,128)S(1)}, f32[32,256]{1,0:T(8,128)S(1)}, u32[]{:S(2)}, u32[]{:S(2)}) collective-permute-start(f32[32,256]{1,0:T(8,128)S(1)} %get-tuple-element.18), channel_id=1, source_target_pairs={{0,1},{1,0},{2,3},{3,2},{4,5},{5,4},{6,7},{7,6},{8,9},{9,8},{10,11... | collective-permute-start | bytes 98312 | tf_op jit(solution)/shard_map/ppermute | solution.py:159

commit v20 on v18

--- a/solution.py
+++ b/solution.py
@@ -20,7 +20,7 @@
     return size
 
 
-def plane_blocks(value, halves, count, send):
+def plane_blocks(value, count, send, cut):
     if count & (count - 1):
         maps = {step: [(b, (b - step) % count) for b in range(count)] for step in range(1, count)}
         return [(value,)] + [(send(value, maps[step]),) for step in range(1, count)]
@@ -29,7 +29,7 @@
     while bit:
         hops = [(b, b ^ bit) for b in range(count)]
         for known in list(blocks):
-            parts = halves if known == 0 and bit == count // 2 and bit > 1 else blocks[known]
+            parts = blocks[known] if known == 0 or len(blocks[known]) > 1 else cut(*blocks[known])
             blocks[known | bit] = tuple(send(part, hops) for part in parts)
         bit //= 2
     return [blocks[distance] for distance in range(count)]
@@ -83,24 +83,28 @@
     cols = [blocks[len(parts) + place][0] for place in range(cols_in)]
     noise = [rest.pop(0) for _ in range(noise_in)]
     sums = {name: rest.pop(0)[...] for name in known}
-    ready_rows, ready_cols = {}, {}
-    for row, col, kind in pairs:
-        if row not in ready_rows:
-            wide = rows[row][0].astype(jnp.float32)
-            ready_rows[row] = jnp.sum(wide * wide, axis=1, keepdims=True)
-        if col not in ready_cols:
-            block = cols[col][0:shard, :]
-            ready_cols[col] = block * jnp.asarray(-2.0, block.dtype), lane_squares(block)
-        scaled, col_squares = ready_cols[col]
-        row_block, row_probes = rows[row]
-        cross = lax.dot_general(row_block, scaled, ROWS_BY_ROWS, preferred_element_type=jnp.float32)
-        kernel = matern((ready_rows[row] + col_squares) + cross)
+    squares = {}
+    for col in sorted({col for _, col, _ in pairs}):
+        kind = next(kind for _, place, kind in pairs if place == col)
+        members = [row for row, place, _ in pairs if place == col]
+        for row in members:
+            if row not in squares:
+                wide = rows[row][0].astype(jnp.float32)
+                squares[row] = jnp.sum(wide * wide, axis=1, keepdims=True)
+        block = cols[col][0:shard, :]
+        scaled, col_squares = block * jnp.asarray(-2.0, block.dtype), lane_squares(block)
+        left = jnp.concatenate([rows[row][0] for row in members])
+        cross = lax.dot_general(left, scaled, ROWS_BY_ROWS, preferred_element_type=jnp.float32)
+        kernel = matern((jnp.concatenate([squares[row] for row in members]) + col_squares) + cross)
         found = {}
         if "back" in kind:
-            found["back", col] = jnp.dot(row_probes, kernel, preferred_element_type=jnp.float32)
+            probes = jnp.concatenate([rows[row][1] for row in members], axis=1)
+            found["back", col] = jnp.dot(probes, kernel, preferred_element_type=jnp.float32)
         if "rows" in kind:
             col_probes = cols[col][pl.ds(shard, vectors), :]
-            found["rows", row] = lax.dot_general(col_probes, kernel, ROWS_BY_ROWS, preferred_element_type=jnp.float32)
+            terms = lax.dot_general(col_probes, kernel, ROWS_BY_ROWS, preferred_element_type=jnp.float32)
+            for place, row in enumerate(members):
+                found["rows", row] = terms[:, place * shard : (place + 1) * shard]
         for name, value in found.items():
             sums[name] = sums[name] + value if name in sums else value
     for place in range(noise_in):
@@ -134,24 +138,24 @@
     return dict(zip(names, found))
 
 
-def split_kernel(shard, vectors, longer_ref, whole_ref, *halves):
-    whole_ref[...] = longer_ref[0 : shard + vectors, :]
+def halve_kernel(shard, vectors, from_ref, *halves):
     points, some = shard // 2, vectors // 2
     for place, half in enumerate(halves):
-        half[0:points, :] = longer_ref[pl.ds(place * points, points), :]
-        half[points:, :] = longer_ref[pl.ds(shard + place * some, some), :]
-
-
-def split(longer, shard, vectors):
+        half[0:points, :] = from_ref[pl.ds(place * points, points), :]
+        half[points:, :] = from_ref[pl.ds(shard + place * some, some), :]
+
+
+def halve(value, shard, vectors):
     whole = pl.BlockSpec(memory_space=pltpu.VMEM)
-    rows = [shard + vectors, (shard + vectors) // 2, (shard + vectors) // 2]
+    half = jax.ShapeDtypeStruct(((shard + vectors) // 2, value.shape[1]), value.dtype)
     return pl.pallas_call(
-        functools.partial(split_kernel, shard, vectors),
-        out_shape=[jax.ShapeDtypeStruct((count, longer.shape[1]), longer.dtype) for count in rows],
+        functools.partial(halve_kernel, shard, vectors),
+        out_shape=[half, half],
         in_specs=[whole],
-        out_specs=[whole] * 3,
+        out_specs=[whole, whole],
         compiler_params=pltpu.CompilerParams(vmem_limit_bytes=32 * 1024 * 1024),
-    )(longer)
+        cost_estimate=pl.CostEstimate(flops=0, bytes_accessed=0, transcendentals=0),
+    )(value)
 
 
 def on_device(features, probes, noise_level):
@@ -160,9 +164,7 @@
     outer = count // inner
     shard = features.shape[0]
     vectors = probes.shape[1]
-    spare = jnp.zeros((16, features.shape[1]), features.dtype)
-    longer = jnp.concatenate([features, probes.T, spare], axis=0)
-    packed, *halves = split(longer, shard, vectors)
+    packed = jnp.concatenate([features, probes.T], axis=0)
 
     def along_outer(value, edges):
         return lax.ppermute(value, "blk", [(s * inner + b, t * inner + b) for s, t in edges for b in range(inner)])
@@ -174,13 +176,13 @@
         return [(plane_target(b, step, inner), b) for b in range(inner)]
 
     one_way, exchanges = outer_maps(outer)
-    cols = [along_outer(longer, edges) for edges in one_way]
+    cols = [along_outer(packed, edges) for edges in one_way]
     others = [along_outer(packed, edges) for edges in exchanges]
-    blocks = plane_blocks(packed, halves, inner, in_plane)
+    blocks = plane_blocks(packed, inner, in_plane, lambda block: halve(block, shard, vectors))
     direct = [step for step in range(1, inner) if step & (step - 1) == 0]
     passed = [step for step in range(1, inner) if step & (step - 1)]
 
-    order = [0] + passed + direct + [inner + place for place in range(len(cols))]
+    order = [0] + passed + [inner + place for place in range(len(cols))] + direct
     pairs = [(row, col, ("rows", "back")) for col in range(len(cols)) for row in range(inner)]
     sums = tile(blocks, cols, order, pairs, {}, shard, vectors, work=0.0)
     backs = [sums.pop(("back", place)) for place in range(len(cols))]

time: 22.7 us -> 21.8 us (0.960)
  waiting for transfers between devices: 7.3 us -> 6.6 us
  local copies, waits for them, and re-layouts: 0.6 us -> 0.01 us
  starting transfers between devices: 9.94 us -> 10.5 us
    ppermute x8 -> x7, waiting for transfers between devices: 6.59 us -> 0.95 us  [in_plane(): lax.ppermute(value, 'blk', [(a * inner + s, a * inner + t) for a in range...]
    ppermute x3, waiting for transfers between devices: 0.7 us -> 5.65 us  [along_outer(): lax.ppermute(value, 'blk', [(s * inner + b, t * inner + b) for s, t in ed...]
    ppermute x8 -> x7, starting transfers between devices: 3.97 us -> 5.53 us  [in_plane(): lax.ppermute(value, 'blk', [(a * inner + s, a * inner + t) for a in range...]
    ppermute x3, starting transfers between devices: 5.96 us -> 4.98 us  [along_outer(): lax.ppermute(value, 'blk', [(s * inner + b, t * inner + b) for s, t in ed...]
    unnamed x2, local copies, waits for them, and re-layouts: 0.52 us -> 0.01 us
  transfers between devices with their start and end apart: 11 -> 10, of which waited for: 7 -> 4; matrix products, arithmetic and copies ran while one was open for 0% -> 0% of each run, Pallas kernels for 13% -> 13%
where the time goes in v20:
time: 21.8 us; the launch traced here: 21.6 us
  starting transfers between devices  10.5 us (48%)
  waiting for transfers between devices  6.6 us (30%)
  Pallas kernels  2.85 us (13%)
  other arithmetic  1.56 us (7%)
    ppermute x3, waiting for transfers between devices, along_outer(): lax.ppermute(value, 'blk', [(s * inner + b, t * inner + b) for s, t in ed...  5.65 us
    ppermute x7, starting transfers between devices, in_plane(): lax.ppermute(value, 'blk', [(a * inner + s, a * inner + t) for a in range...  5.53 us
    ppermute x3, starting transfers between devices, along_outer(): lax.ppermute(value, 'blk', [(s * inner + b, t * inner + b) for s, t in ed...  4.98 us
    pallas_call x3, Pallas kernels, tile(): pl.pallas_call(functools.partial(tile_kernel, list(order), tuple(pairs),...  2.84 us
    ppermute x7, waiting for transfers between devices, in_plane(): lax.ppermute(value, 'blk', [(a * inner + s, a * inner + t) for a in range...  0.95 us
    concatenate x1, other arithmetic, on_device(): packed = jnp.concatenate([features, probes.T], axis=0)  0.93 us
    transpose x1, other arithmetic, on_device(): return functools.reduce(lambda sofar, term: sofar + term, total).T  0.63 us
  transfers between devices with their start and end apart: 10, of which 4 were waited for; matrix products, arithmetic and copies ran while one was open for 0% of the time, Pallas kernels for 13%

profile of v20, /device:TPU:0, one launch (start us, length us, event | category | flops | bytes accessed | tf_op | source)
XLA Modules:
  0.0 21.6 jit_solution(372771339821041598)
XLA Ops:
  0.0 0.9 %pad_maximum_fusion.refs_0_.refs_5_ = bf16[288,256]{1,0:T(8,128)(2,1)S(1)} fusion(bf16[32,256]{1,0:T(8,128)(2,1)} %bitcast.5, bf16[256,256]{1,0:T(8,128)(2,1)} %param.3), kind=kLoop, calls=%fused_computation | loop fusion | flops 294912 | bytes 294912 | tf_op jit(solution)/shard_map/concatenate | solution.py:167
  0.9 3.0 %collective-permute-start.1 = (bf16[288,256]{1,0:T(8,128)(2,1)S(1)}, bf16[288,256]{1,0:T(8,128)(2,1)S(1)}, u32[]{:S(2)}, u32[]{:S(2)}) collective-permute-start(bf16[288,256]{1,0:T(8,128)(2,1)S(1)} %pad_maximum_fusion.refs_0_.refs_5_), channel_id=1, source_target_pairs={{0,2},{1,3},{2,0},{3,1},{4,6},{5,7},{6,4},{7,5},{8,10},{9,11},{10,... | collective-permute-start | bytes 442376 | tf_op jit(solution)/shard_map/ppermute | solution.py:173
  4.0 3.6 %collective-permute-start.5 = (bf16[288,256]{1,0:T(8,128)(2,1)S(1)}, bf16[288,256]{1,0:T(8,128)(2,1)S(1)}, u32[]{:S(2)}, u32[]{:S(2)}) collective-permute-start(bf16[288,256]{1,0:T(8,128)(2,1)S(1)} %pad_maximum_fusion.refs_0_.refs_5_), channel_id=1, source_target_pairs={{12,4},{13,5},{14,6},{15,7},{4,8},{5,9},{6,10},{7,11},{8,0},{9,1},... | collective-permute-start | bytes 442376 | tf_op jit(solution)/shard_map/ppermute | solution.py:170
  7.6 0.0 collective-permute-start
  7.6 0.0 collective-permute-start.4
  7.6 0.2 %collective-permute-done.1.from_ref.refs_5_.refs_2_ = bf16[288,256]{1,0:T(8,128)(2,1)S(1)} collective-permute-done((bf16[288,256]{1,0:T(8,128)(2,1)S(1)}, bf16[288,256]{1,0:T(8,128)(2,1)S(1)}, u32[]{:S(2)}, u32[]{:S(2)}) %collective-permute-start.1) | collective-permute-done | bytes 147488 | tf_op jit(solution)/shard_map/ppermute | solution.py:173
  7.8 0.3 %collective-permute-start.2 = (bf16[144,256]{1,0:T(8,128)(2,1)S(1)}, bf16[144,256]{1,0:T(8,128)(2,1)S(1)}, u32[]{:S(2)}, u32[]{:S(2)}) collective-permute-start(bf16[144,256]{1,0:T(8,128)(2,1)S(1)} %get-tuple-element.16), channel_id=1, source_target_pairs={{0,1},{1,0},{2,3},{3,2},{4,5},{5,4},{6,7},{7,6},{8,9},{9,8},{10,11... | collective-permute-start | bytes 221192 | tf_op jit(solution)/shard_map/ppermute | solution.py:173
  8.2 0.2 %collective-permute-start.3 = (bf16[144,256]{1,0:T(8,128)(2,1)S(1)}, bf16[144,256]{1,0:T(8,128)(2,1)S(1)}, u32[]{:S(2)}, u32[]{:S(2)}) collective-permute-start(bf16[144,256]{1,0:T(8,128)(2,1)S(1)} %get-tuple-element.17), channel_id=1, source_target_pairs={{0,1},{1,0},{2,3},{3,2},{4,5},{5,4},{6,7},{7,6},{8,9},{9,8},{10,11... | collective-permute-start | bytes 221192 | tf_op jit(solution)/shard_map/ppermute | solution.py:173
  8.4 5.0 %collective-permute-done.5.refs_3_ = bf16[288,256]{1,0:T(8,128)(2,1)S(1)} collective-permute-done((bf16[288,256]{1,0:T(8,128)(2,1)S(1)}, bf16[288,256]{1,0:T(8,128)(2,1)S(1)}, u32[]{:S(2)}, u32[]{:S(2)}) %collective-permute-start.5) | collective-permute-done | bytes 147488 | tf_op jit(solution)/shard_map/ppermute | solution.py:170
  13.4 0.0 collective-permute-done.refs_4_.refs_1_
  13.4 0.0 collective-permute-done.2.refs_1_.refs_3_
  13.4 0.0 collective-permute-done.3.refs_2_.refs_4_
  13.5 1.0 %shard_map.38 = (f32[32,256]{1,0:T(8,128)S(1)}, f32[32,256]{1,0:T(8,128)S(1)}, f32[32,256]{1,0:T(8,128)S(1)}, f32[32,256]{1,0:T(8,128)S(1)}, f32[32,256]{1,0:T(8,128)S(1)}) custom-call(bf16[288,256]{1,0:T(8,128)(2,1)S(1)} %pad_maximum_fusion.refs_0_.refs_5_, bf16[144,256]{1,0:T(8,128)(2,1)S(1)} %collective-permute-done.2.refs_1_.refs_3_, ...), custom_call_target="tpu_custom_call" | custom-call | tf_op jit(solution)/shard_map/pallas_call | solution.py:124
  14.5 1.4 %collective-permute-start.9 = (f32[32,256]{1,0:T(8,128)S(1)}, f32[32,256]{1,0:T(8,128)S(1)}, u32[]{:S(2)}, u32[]{:S(2)}) collective-permute-start(f32[32,256]{1,0:T(8,128)S(1)} %get-tuple-element.26), channel_id=1, source_target_pairs={{4,12},{5,13},{6,14},{7,15},{8,4},{9,5},{10,6},{11,7},{0,8},{1,9},... | collective-permute-start | bytes 98312 | tf_op jit(solution)/shard_map/ppermute | solution.py:170
  15.9 0.0 collective-permute-done.4.refs_5_
  15.9 0.9 %shard_map.39 = (f32[32,256]{1,0:T(8,128)S(1)}, f32[32,256]{1,0:T(8,128)S(1)}, f32[32,256]{1,0:T(8,128)S(1)}, f32[32,256]{1,0:T(8,128)S(1)}) custom-call(bf16[288,256]{1,0:T(8,128)(2,1)S(1)} %pad_maximum_fusion.refs_0_.refs_5_, bf16[288,256]{1,0:T(8,128)(2,1)S(1)} %collective-permute-done.refs_4_.refs_1_, ...), custom_call_target="tpu_custom_call" | custom-call | flops 167772160 | bytes 655360 | tf_op jit(solution)/shard_map/pallas_call | solution.py:124
  16.8 0.1 collective-permute-start.8
  16.9 1.1 %collective-permute-start.7 = (f32[32,256]{1,0:T(8,128)S(1)}, f32[32,256]{1,0:T(8,128)S(1)}, u32[]{:S(2)}, u32[]{:S(2)}) collective-permute-start(f32[32,256]{1,0:T(8,128)S(1)} %get-tuple-element.24), channel_id=1, source_target_pairs={{0,2},{1,3},{2,0},{3,1},{4,6},{5,7},{6,4},{7,5},{8,10},{9,11},{10,... | collective-permute-start | bytes 98312 | tf_op jit(solution)/shard_map/ppermute | solution.py:173
  18.0 0.7 %collective-permute-start.6 = (f32[32,256]{1,0:T(8,128)S(1)}, f32[32,256]{1,0:T(8,128)S(1)}, u32[]{:S(2)}, u32[]{:S(2)}) collective-permute-start(f32[32,256]{1,0:T(8,128)S(1)} %get-tuple-element.23), channel_id=1, source_target_pairs={{0,1},{1,0},{2,3},{3,2},{4,5},{5,4},{6,7},{7,6},{8,9},{9,8},{10,11... | collective-permute-start | bytes 98312 | tf_op jit(solution)/shard_map/ppermute | solution.py:173
  18.7 0.9 %shard_map.40 = f32[32,256]{1,0:T(8,128)S(1)} custom-call(bf16[288,256]{1,0:T(8,128)(2,1)S(1)} %pad_maximum_fusion.refs_0_.refs_5_, bf16[288,256]{1,0:T(8,128)(2,1)S(1)} %collective-permute-done.refs_4_.refs_1_, bf16[288,256]{1,0:T(8,128)(2,1)S(1)} %collective-permute-done.1.from_ref.refs_5_.refs_2_, ...), custom_call_target="tpu_custom_call" | custom-call | flops 167772160 | bytes 655360 | tf_op jit(solution)/shard_map/pallas_call | solution.py:124
  19.6 0.6 %collective-permute-done.9 = f32[32,256]{1,0:T(8,128)S(1)} collective-permute-done((f32[32,256]{1,0:T(8,128)S(1)}, f32[32,256]{1,0:T(8,128)S(1)}, u32[]{:S(2)}, u32[]{:S(2)}) %collective-permute-start.9) | collective-permute-done | bytes 32800 | tf_op jit(solution)/shard_map/ppermute | solution.py:170
  20.2 0.7 %collective-permute-done.7 = f32[32,256]{1,0:T(8,128)S(1)} collective-permute-done((f32[32,256]{1,0:T(8,128)S(1)}, f32[32,256]{1,0:T(8,128)S(1)}, u32[]{:S(2)}, u32[]{:S(2)}) %collective-permute-start.7) | collective-permute-done | bytes 32800 | tf_op jit(solution)/shard_map/ppermute | solution.py:173
  20.9 0.0 collective-permute-done.6
  20.9 0.6 %add_bitcast_fusion = f32[256,32]{0,1:T(8,128)} fusion(f32[32,256]{1,0:T(8,128)S(1)} %collective-permute-done.9, f32[32,256]{1,0:T(8,128)S(1)} %collective-permute-done.8, f32[32,256]{1,0:T(8,128)S(1)} %collective-permute-done.7, f32[32,256]{1,0:T(8,128)S(1)} %collective-permute-done.6, f32[32,256]{1,0:T(8,128)S(1)} %get-tuple-element.22, ...), kind=kLoop, calls=%fused_computation.1 | loop fusion | flops 40960 | bytes 229376 | tf_op jit(solution)/shard_map/transpose | solution.py:197
  (4 shorter events, 0.0 us)
Async XLA Ops:
  0.9 6.9 %collective-permute-start.1 = (bf16[288,256]{1,0:T(8,128)(2,1)S(1)}, bf16[288,256]{1,0:T(8,128)(2,1)S(1)}, u32[]{:S(2)}, u32[]{:S(2)}) collective-permute-start(bf16[288,256]{1,0:T(8,128)(2,1)S(1)} %pad_maximum_fusion.refs_0_.refs_5_), channel_id=1, source_target_pairs={{0,2},{1,3},{2,0},{3,1},{4,6},{5,7},{6,4},{7,5},{8,10},{9,11},{10,... | collective-permute-start | bytes 442376 | tf_op jit(solution)/shard_map/ppermute | solution.py:173
  4.0 9.5 %collective-permute-start.5 = (bf16[288,256]{1,0:T(8,128)(2,1)S(1)}, bf16[288,256]{1,0:T(8,128)(2,1)S(1)}, u32[]{:S(2)}, u32[]{:S(2)}) collective-permute-start(bf16[288,256]{1,0:T(8,128)(2,1)S(1)} %pad_maximum_fusion.refs_0_.refs_5_), channel_id=1, source_target_pairs={{12,4},{13,5},{14,6},{15,7},{4,8},{5,9},{6,10},{7,11},{8,0},{9,1},... | collective-permute-start | bytes 442376 | tf_op jit(solution)/shard_map/ppermute | solution.py:170
  7.6 5.9 %collective-permute-start = (bf16[288,256]{1,0:T(8,128)(2,1)S(1)}, bf16[288,256]{1,0:T(8,128)(2,1)S(1)}, u32[]{:S(2)}, u32[]{:S(2)}) collective-permute-start(bf16[288,256]{1,0:T(8,128)(2,1)S(1)} %pad_maximum_fusion.refs_0_.refs_5_), channel_id=1, source_target_pairs={{0,1},{1,0},{2,3},{3,2},{4,5},{5,4},{6,7},{7,6},{8,9},{9,8},{10,11... | collective-permute-start | bytes 442376 | tf_op jit(solution)/shard_map/ppermute | solution.py:173
  7.6 8.3 %collective-permute-start.4 = (bf16[288,256]{1,0:T(8,128)(2,1)S(1)}, bf16[288,256]{1,0:T(8,128)(2,1)S(1)}, u32[]{:S(2)}, u32[]{:S(2)}) collective-permute-start(bf16[288,256]{1,0:T(8,128)(2,1)S(1)} %pad_maximum_fusion.refs_0_.refs_5_), channel_id=1, source_target_pairs={{12,8},{13,9},{14,10},{15,11},{4,0},{5,1},{6,2},{7,3},{8,12},{9,13... | collective-permute-start | bytes 442376 | tf_op jit(solution)/shard_map/ppermute | solution.py:170
  7.8 5.6 %collective-permute-start.2 = (bf16[144,256]{1,0:T(8,128)(2,1)S(1)}, bf16[144,256]{1,0:T(8,128)(2,1)S(1)}, u32[]{:S(2)}, u32[]{:S(2)}) collective-permute-start(bf16[144,256]{1,0:T(8,128)(2,1)S(1)} %get-tuple-element.16), channel_id=1, source_target_pairs={{0,1},{1,0},{2,3},{3,2},{4,5},{5,4},{6,7},{7,6},{8,9},{9,8},{10,11... | collective-permute-start | bytes 221192 | tf_op jit(solution)/shard_map/ppermute | solution.py:173
  8.2 5.3 %collective-permute-start.3 = (bf16[144,256]{1,0:T(8,128)(2,1)S(1)}, bf16[144,256]{1,0:T(8,128)(2,1)S(1)}, u32[]{:S(2)}, u32[]{:S(2)}) collective-permute-start(bf16[144,256]{1,0:T(8,128)(2,1)S(1)} %get-tuple-element.17), channel_id=1, source_target_pairs={{0,1},{1,0},{2,3},{3,2},{4,5},{5,4},{6,7},{7,6},{8,9},{9,8},{10,11... | collective-permute-start | bytes 221192 | tf_op jit(solution)/shard_map/ppermute | solution.py:173
  14.5 5.7 %collective-permute-start.9 = (f32[32,256]{1,0:T(8,128)S(1)}, f32[32,256]{1,0:T(8,128)S(1)}, u32[]{:S(2)}, u32[]{:S(2)}) collective-permute-start(f32[32,256]{1,0:T(8,128)S(1)} %get-tuple-element.26), channel_id=1, source_target_pairs={{4,12},{5,13},{6,14},{7,15},{8,4},{9,5},{10,6},{11,7},{0,8},{1,9},... | collective-permute-start | bytes 98312 | tf_op jit(solution)/shard_map/ppermute | solution.py:170
  16.8 3.4 %collective-permute-start.8 = (f32[32,256]{1,0:T(8,128)S(1)}, f32[32,256]{1,0:T(8,128)S(1)}, u32[]{:S(2)}, u32[]{:S(2)}) collective-permute-start(f32[32,256]{1,0:T(8,128)S(1)} %get-tuple-element.25), channel_id=1, source_target_pairs={{0,3},{1,2},{2,1},{3,0},{4,7},{5,6},{6,5},{7,4},{8,11},{9,10},{10,... | collective-permute-start | bytes 98312 | tf_op jit(solution)/shard_map/ppermute | solution.py:173
  16.9 4.1 %collective-permute-start.7 = (f32[32,256]{1,0:T(8,128)S(1)}, f32[32,256]{1,0:T(8,128)S(1)}, u32[]{:S(2)}, u32[]{:S(2)}) collective-permute-start(f32[32,256]{1,0:T(8,128)S(1)} %get-tuple-element.24), channel_id=1, source_target_pairs={{0,2},{1,3},{2,0},{3,1},{4,6},{5,7},{6,4},{7,5},{8,10},{9,11},{10,... | collective-permute-start | bytes 98312 | tf_op jit(solution)/shard_map/ppermute | solution.py:173
  18.0 0.7 %copy-start = (f32[256]{0:T(256)S(1)}, f32[256]{0:T(256)}, u32[]{:S(2)}) copy-start(f32[256]{0:T(256)} %param.5) | copy-start | bytes 3076
  18.0 2.9 %collective-permute-start.6 = (f32[32,256]{1,0:T(8,128)S(1)}, f32[32,256]{1,0:T(8,128)S(1)}, u32[]{:S(2)}, u32[]{:S(2)}) collective-permute-start(f32[32,256]{1,0:T(8,128)S(1)} %get-tuple-element.23), channel_id=1, source_target_pairs={{0,1},{1,0},{2,3},{3,2},{4,5},{5,4},{6,7},{7,6},{8,9},{9,8},{10,11... | collective-permute-start | bytes 98312 | tf_op jit(solution)/shard_map/ppermute | solution.py:173

commit v21 on v20

--- a/solution.py
+++ b/solution.py
@@ -29,7 +29,8 @@
     while bit:
         hops = [(b, b ^ bit) for b in range(count)]
         for known in list(blocks):
-            parts = blocks[known] if known == 0 or len(blocks[known]) > 1 else cut(*blocks[known])
+            whole = len(blocks[known]) == 1 and (known or bit < count // 2)
+            parts = cut(*blocks[known]) if whole else blocks[known]
             blocks[known | bit] = tuple(send(part, hops) for part in parts)
         bit //= 2
     return [blocks[distance] for distance in range(count)]
@@ -182,19 +183,17 @@
     direct = [step for step in range(1, inner) if step & (step - 1) == 0]
     passed = [step for step in range(1, inner) if step & (step - 1)]
 
-    order = [0] + passed + [inner + place for place in range(len(cols))] + direct
+    pairs = [(row, col, ("rows",)) for col in range(len(others)) for row in range(inner)]
+    sums = tile(blocks, others, [0] + passed + direct + [inner + place for place in range(len(others))], pairs, {}, shard, vectors, work=0.0)
     pairs = [(row, col, ("rows", "back")) for col in range(len(cols)) for row in range(inner)]
-    sums = tile(blocks, cols, order, pairs, {}, shard, vectors, work=0.0)
-    backs = [sums.pop(("back", place)) for place in range(len(cols))]
-    pairs = [(row, col, ("rows",)) for col in range(len(others)) for row in range(inner)]
-    sums = tile(blocks, others, range(inner + len(others)), pairs, sums, shard, vectors)
+    sums = tile(blocks, cols, [0] + passed + direct + [inner + place for place in range(len(cols))], pairs, sums, shard, vectors)
+    backs = [sums["back", place] for place in range(len(cols))]
     pairs = [(row, 0, ("back",)) for row in range(inner)]
     own = tile(blocks, [packed], range(inner + 1), pairs, {}, shard, vectors, noise=[noise_level[None, :]])
 
-    total = [sums["rows", 0], own["back", 0]]
-    total += [in_plane(sums["rows", step], [(t, s) for s, t in near(step)]) for step in range(1, inner)]
-    total += [along_outer(back, [(t, s) for s, t in edges]) for back, edges in zip(backs, one_way)]
-    return functools.reduce(lambda sofar, term: sofar + term, total).T
+    total = [along_outer(back, [(t, s) for s, t in edges]) for back, edges in zip(backs, one_way)]
+    total += [in_plane(sums["rows", step], [(t, s) for s, t in near(step)]) for step in range(inner - 1, 0, -1)]
+    return functools.reduce(lambda sofar, term: sofar + term, total + [own["back", 0], sums["rows", 0]]).T
 
 
 def solution(mesh):

time: 21.8 us -> 23.6 us (1.083)
  starting transfers between devices: 10.5 us -> 11.5 us
  waiting for transfers between devices: 6.6 us -> 7.39 us
    ppermute x3, starting transfers between devices: 4.98 us -> 5.81 us  [along_outer(): lax.ppermute(value, 'blk', [(s * inner + b, t * inner + b) for s, t in ed...]
    ppermute x3, waiting for transfers between devices: 5.65 us -> 6.27 us  [along_outer(): lax.ppermute(value, 'blk', [(s * inner + b, t * inner + b) for s, t in ed...]
    ppermute x7 -> x8, starting transfers between devices: 5.53 us -> 5.7 us  [in_plane(): lax.ppermute(value, 'blk', [(a * inner + s, a * inner + t) for a in range...]
    ppermute x7 -> x8, waiting for transfers between devices: 0.95 us -> 1.12 us  [in_plane(): lax.ppermute(value, 'blk', [(a * inner + s, a * inner + t) for a in range...]
  transfers between devices with their start and end apart: 10 -> 11, of which waited for: 4 -> 5; matrix products, arithmetic and copies ran while one was open for 0% -> 0% of each run, Pallas kernels for 13% -> 8%
where the time goes in v21:
time: 23.6 us; the launch traced here: 23.4 us
  starting transfers between devices  11.5 us (49%)
  waiting for transfers between devices  7.39 us (31%)
  Pallas kernels  2.87 us (12%)
  other arithmetic  1.56 us (7%)
    ppermute x3, waiting for transfers between devices, along_outer(): lax.ppermute(value, 'blk', [(s * inner + b, t * inner + b) for s, t in ed...  6.27 us
    ppermute x3, starting transfers between devices, along_outer(): lax.ppermute(value, 'blk', [(s * inner + b, t * inner + b) for s, t in ed...  5.81 us
    ppermute x8, starting transfers between devices, in_plane(): lax.ppermute(value, 'blk', [(a * inner + s, a * inner + t) for a in range...  5.7 us
    pallas_call x3, Pallas kernels, tile(): pl.pallas_call(functools.partial(tile_kernel, list(order), tuple(pairs),...  2.85 us
    ppermute x8, waiting for transfers between devices, in_plane(): lax.ppermute(value, 'blk', [(a * inner + s, a * inner + t) for a in range...  1.12 us
    concatenate x1, other arithmetic, on_device(): packed = jnp.concatenate([features, probes.T], axis=0)  0.93 us
    transpose x1, other arithmetic, on_device(): functools.reduce(lambda sofar, term: sofar + term, total + [own['back', 0...  0.63 us
  transfers between devices with their start and end apart: 11, of which 5 were waited for; matrix products, arithmetic and copies ran while one was open for 0% of the time, Pallas kernels for 8%

profile of v21, /device:TPU:0, one launch (start us, length us, event | category | flops | bytes accessed | tf_op | source)
XLA Modules:
  0.0 23.4 jit_solution(12430498818939045287)
XLA Ops:
  0.0 0.9 %pad_maximum_fusion.from_ref.refs_0_.refs_6_ = bf16[288,256]{1,0:T(8,128)(2,1)S(1)} fusion(bf16[32,256]{1,0:T(8,128)(2,1)} %bitcast.5, bf16[256,256]{1,0:T(8,128)(2,1)} %param.3), kind=kLoop, calls=%fused_computation | loop fusion | flops 294912 | bytes 294912 | tf_op jit(solution)/shard_map/concatenate | solution.py:168
  0.9 3.0 %collective-permute-start = (bf16[288,256]{1,0:T(8,128)(2,1)S(1)}, bf16[288,256]{1,0:T(8,128)(2,1)S(1)}, u32[]{:S(2)}, u32[]{:S(2)}) collective-permute-start(bf16[288,256]{1,0:T(8,128)(2,1)S(1)} %pad_maximum_fusion.from_ref.refs_0_.refs_6_), channel_id=1, source_target_pairs={{0,2},{1,3},{2,0},{3,1},{4,6},{5,7},{6,4},{7,5},{8,10},{9,11},{10,... | collective-permute-start | bytes 442376 | tf_op jit(solution)/shard_map/ppermute | solution.py:174
  4.0 1.6 %collective-permute-start.6 = (bf16[288,256]{1,0:T(8,128)(2,1)S(1)}, bf16[288,256]{1,0:T(8,128)(2,1)S(1)}, u32[]{:S(2)}, u32[]{:S(2)}) collective-permute-start(bf16[288,256]{1,0:T(8,128)(2,1)S(1)} %pad_maximum_fusion.from_ref.refs_0_.refs_6_), channel_id=1, source_target_pairs={{12,8},{13,9},{14,10},{15,11},{4,0},{5,1},{6,2},{7,3},{8,12},{9,13... | collective-permute-start | bytes 442376 | tf_op jit(solution)/shard_map/ppermute | solution.py:171
  5.6 0.1 collective-permute-start.3
  5.6 2.5 %collective-permute-start.5 = (bf16[288,256]{1,0:T(8,128)(2,1)S(1)}, bf16[288,256]{1,0:T(8,128)(2,1)S(1)}, u32[]{:S(2)}, u32[]{:S(2)}) collective-permute-start(bf16[288,256]{1,0:T(8,128)(2,1)S(1)} %pad_maximum_fusion.from_ref.refs_0_.refs_6_), channel_id=1, source_target_pairs={{12,4},{13,5},{14,6},{15,7},{4,8},{5,9},{6,10},{7,11},{8,0},{9,1},... | collective-permute-start | bytes 442376 | tf_op jit(solution)/shard_map/ppermute | solution.py:171
  8.2 0.2 collective-permute-start.4
  8.3 0.0 collective-permute-done.from_ref.refs_5_.refs_3_
  8.3 0.4 %collective-permute-start.1 = (bf16[144,256]{1,0:T(8,128)(2,1)S(1)}, bf16[144,256]{1,0:T(8,128)(2,1)S(1)}, u32[]{:S(2)}, u32[]{:S(2)}) collective-permute-start(bf16[144,256]{1,0:T(8,128)(2,1)S(1)} %get-tuple-element.18), channel_id=1, source_target_pairs={{0,1},{1,0},{2,3},{3,2},{4,5},{5,4},{6,7},{7,6},{8,9},{9,8},{10,11... | collective-permute-start | bytes 221192 | tf_op jit(solution)/shard_map/ppermute | solution.py:174
  8.8 0.0 collective-permute-done.3.refs_3_.refs_1_
  8.8 0.2 collective-permute-start.2
  8.9 0.5 %collective-permute-done.4.refs_4_.refs_2_ = bf16[144,256]{1,0:T(8,128)(2,1)S(1)} collective-permute-done((bf16[144,256]{1,0:T(8,128)(2,1)S(1)}, bf16[144,256]{1,0:T(8,128)(2,1)S(1)}, u32[]{:S(2)}, u32[]{:S(2)}) %collective-permute-start.4) | collective-permute-done | bytes 73760 | tf_op jit(solution)/shard_map/ppermute | solution.py:174
  9.4 0.0 collective-permute-done.6.refs_6_
  9.4 0.2 %collective-permute-done.1.refs_1_.refs_4_ = bf16[144,256]{1,0:T(8,128)(2,1)S(1)} collective-permute-done((bf16[144,256]{1,0:T(8,128)(2,1)S(1)}, bf16[144,256]{1,0:T(8,128)(2,1)S(1)}, u32[]{:S(2)}, u32[]{:S(2)}) %collective-permute-start.1) | collective-permute-done | bytes 73760 | tf_op jit(solution)/shard_map/ppermute | solution.py:174
  9.7 0.3 %collective-permute-done.2.refs_2_.refs_5_ = bf16[144,256]{1,0:T(8,128)(2,1)S(1)} collective-permute-done((bf16[144,256]{1,0:T(8,128)(2,1)S(1)}, bf16[144,256]{1,0:T(8,128)(2,1)S(1)}, u32[]{:S(2)}, u32[]{:S(2)}) %collective-permute-start.2) | collective-permute-done | bytes 73760 | tf_op jit(solution)/shard_map/ppermute | solution.py:174
  10.0 0.9 %shard_map.39 = (f32[32,256]{1,0:T(8,128)S(1)}, f32[32,256]{1,0:T(8,128)S(1)}, f32[32,256]{1,0:T(8,128)S(1)}, f32[32,256]{1,0:T(8,128)S(1)}) custom-call(bf16[288,256]{1,0:T(8,128)(2,1)S(1)} %pad_maximum_fusion.from_ref.refs_0_.refs_6_, bf16[144,256]{1,0:T(8,128)(2,1)S(1)} %collective-permute-done.1.refs_1_.refs_4_, ...), custom_call_target="tpu_custom_call" | custom-call | tf_op jit(solution)/shard_map/pallas_call | solution.py:125
  10.9 5.0 %collective-permute-done.5.refs_6_ = bf16[288,256]{1,0:T(8,128)(2,1)S(1)} collective-permute-done((bf16[288,256]{1,0:T(8,128)(2,1)S(1)}, bf16[288,256]{1,0:T(8,128)(2,1)S(1)}, u32[]{:S(2)}, u32[]{:S(2)}) %collective-permute-start.5) | collective-permute-done | bytes 147488 | tf_op jit(solution)/shard_map/ppermute | solution.py:171
  15.9 1.0 %shard_map.40 = (f32[32,256]{1,0:T(8,128)S(1)}, f32[32,256]{1,0:T(8,128)S(1)}, f32[32,256]{1,0:T(8,128)S(1)}, f32[32,256]{1,0:T(8,128)S(1)}, f32[32,256]{1,0:T(8,128)S(1)}) custom-call(bf16[288,256]{1,0:T(8,128)(2,1)S(1)} %pad_maximum_fusion.from_ref.refs_0_.refs_6_, bf16[144,256]{1,0:T(8,128)(2,1)S(1)} %collective-permute-done.1.refs_1_.refs_4_, ...), custom_call_target="tpu_custom_call" | custom-call | flops 167772160 | bytes 655360 | tf_op jit(solution)/shard_map/pallas_call | solution.py:125
  17.0 1.7 %collective-permute-start.7 = (f32[32,256]{1,0:T(8,128)S(1)}, f32[32,256]{1,0:T(8,128)S(1)}, u32[]{:S(2)}, u32[]{:S(2)}) collective-permute-start(f32[32,256]{1,0:T(8,128)S(1)} %get-tuple-element.26), channel_id=1, source_target_pairs={{4,12},{5,13},{6,14},{7,15},{8,4},{9,5},{10,6},{11,7},{0,8},{1,9},... | collective-permute-start | bytes 98312 | tf_op jit(solution)/shard_map/ppermute | solution.py:171
  18.7 1.0 %collective-permute-start.9 = (f32[32,256]{1,0:T(8,128)S(1)}, f32[32,256]{1,0:T(8,128)S(1)}, u32[]{:S(2)}, u32[]{:S(2)}) collective-permute-start(f32[32,256]{1,0:T(8,128)S(1)} %get-tuple-element.28), channel_id=1, source_target_pairs={{0,2},{1,3},{2,0},{3,1},{4,6},{5,7},{6,4},{7,5},{8,10},{9,11},{10,... | collective-permute-start | bytes 98312 | tf_op jit(solution)/shard_map/ppermute | solution.py:174
  19.7 0.9 %collective-permute-start.10 = (f32[32,256]{1,0:T(8,128)S(1)}, f32[32,256]{1,0:T(8,128)S(1)}, u32[]{:S(2)}, u32[]{:S(2)}) collective-permute-start(f32[32,256]{1,0:T(8,128)S(1)} %get-tuple-element.29), channel_id=1, source_target_pairs={{0,1},{1,0},{2,3},{3,2},{4,5},{5,4},{6,7},{7,6},{8,9},{9,8},{10,11... | collective-permute-start | bytes 98312 | tf_op jit(solution)/shard_map/ppermute | solution.py:174
  20.6 0.9 %shard_map.41 = f32[32,256]{1,0:T(8,128)S(1)} custom-call(bf16[288,256]{1,0:T(8,128)(2,1)S(1)} %pad_maximum_fusion.from_ref.refs_0_.refs_6_, bf16[144,256]{1,0:T(8,128)(2,1)S(1)} %collective-permute-done.3.refs_3_.refs_1_, bf16[144,256]{1,0:T(8,128)(2,1)S(1)} %collective-permute-done.4.refs_4_.refs_2_, ...), custom_call_target="tpu_custom_call" | custom-call | flops 167772160 | bytes 655360 | tf_op jit(solution)/shard_map/pallas_call | solution.py:125
  21.5 1.3 %collective-permute-done.7 = f32[32,256]{1,0:T(8,128)S(1)} collective-permute-done((f32[32,256]{1,0:T(8,128)S(1)}, f32[32,256]{1,0:T(8,128)S(1)}, u32[]{:S(2)}, u32[]{:S(2)}) %collective-permute-start.7) | collective-permute-done | bytes 32800 | tf_op jit(solution)/shard_map/ppermute | solution.py:171
  22.7 0.0 collective-permute-done.9
  22.7 0.6 %add_bitcast_fusion = f32[256,32]{0,1:T(8,128)} fusion(f32[32,256]{1,0:T(8,128)S(1)} %get-tuple-element.30, f32[32,256]{1,0:T(8,128)S(1)} %shard_map.41, f32[32,256]{1,0:T(8,128)S(1)} %collective-permute-done.10, f32[32,256]{1,0:T(8,128)S(1)} %collective-permute-done.9, f32[32,256]{1,0:T(8,128)S(1)} %collective-permute-done.7, ...), kind=kLoop, calls=%fused_computation.1 | loop fusion | flops 40960 | bytes 229376 | tf_op jit(solution)/shard_map/transpose | solution.py:196
  (7 shorter events, 0.0 us)
Async XLA Ops:
  0.9 7.4 %collective-permute-start = (bf16[288,256]{1,0:T(8,128)(2,1)S(1)}, bf16[288,256]{1,0:T(8,128)(2,1)S(1)}, u32[]{:S(2)}, u32[]{:S(2)}) collective-permute-start(bf16[288,256]{1,0:T(8,128)(2,1)S(1)} %pad_maximum_fusion.from_ref.refs_0_.refs_6_), channel_id=1, source_target_pairs={{0,2},{1,3},{2,0},{3,1},{4,6},{5,7},{6,4},{7,5},{8,10},{9,11},{10,... | collective-permute-start | bytes 442376 | tf_op jit(solution)/shard_map/ppermute | solution.py:174
  4.0 5.5 %collective-permute-start.6 = (bf16[288,256]{1,0:T(8,128)(2,1)S(1)}, bf16[288,256]{1,0:T(8,128)(2,1)S(1)}, u32[]{:S(2)}, u32[]{:S(2)}) collective-permute-start(bf16[288,256]{1,0:T(8,128)(2,1)S(1)} %pad_maximum_fusion.from_ref.refs_0_.refs_6_), channel_id=1, source_target_pairs={{12,8},{13,9},{14,10},{15,11},{4,0},{5,1},{6,2},{7,3},{8,12},{9,13... | collective-permute-start | bytes 442376 | tf_op jit(solution)/shard_map/ppermute | solution.py:171
  5.6 3.2 %collective-permute-start.3 = (bf16[144,256]{1,0:T(8,128)(2,1)S(1)}, bf16[144,256]{1,0:T(8,128)(2,1)S(1)}, u32[]{:S(2)}, u32[]{:S(2)}) collective-permute-start(bf16[144,256]{1,0:T(8,128)(2,1)S(1)} %get-tuple-element.20), channel_id=1, source_target_pairs={{0,1},{1,0},{2,3},{3,2},{4,5},{5,4},{6,7},{7,6},{8,9},{9,8},{10,11... | collective-permute-start | bytes 221192 | tf_op jit(solution)/shard_map/ppermute | solution.py:174
  5.6 10.3 %collective-permute-start.5 = (bf16[288,256]{1,0:T(8,128)(2,1)S(1)}, bf16[288,256]{1,0:T(8,128)(2,1)S(1)}, u32[]{:S(2)}, u32[]{:S(2)}) collective-permute-start(bf16[288,256]{1,0:T(8,128)(2,1)S(1)} %pad_maximum_fusion.from_ref.refs_0_.refs_6_), channel_id=1, source_target_pairs={{12,4},{13,5},{14,6},{15,7},{4,8},{5,9},{6,10},{7,11},{8,0},{9,1},... | collective-permute-start | bytes 442376 | tf_op jit(solution)/shard_map/ppermute | solution.py:171
  8.2 1.3 %collective-permute-start.4 = (bf16[144,256]{1,0:T(8,128)(2,1)S(1)}, bf16[144,256]{1,0:T(8,128)(2,1)S(1)}, u32[]{:S(2)}, u32[]{:S(2)}) collective-permute-start(bf16[144,256]{1,0:T(8,128)(2,1)S(1)} %get-tuple-element.21), channel_id=1, source_target_pairs={{0,1},{1,0},{2,3},{3,2},{4,5},{5,4},{6,7},{7,6},{8,9},{9,8},{10,11... | collective-permute-start | bytes 221192 | tf_op jit(solution)/shard_map/ppermute | solution.py:174
  8.3 1.3 %collective-permute-start.1 = (bf16[144,256]{1,0:T(8,128)(2,1)S(1)}, bf16[144,256]{1,0:T(8,128)(2,1)S(1)}, u32[]{:S(2)}, u32[]{:S(2)}) collective-permute-start(bf16[144,256]{1,0:T(8,128)(2,1)S(1)} %get-tuple-element.18), channel_id=1, source_target_pairs={{0,1},{1,0},{2,3},{3,2},{4,5},{5,4},{6,7},{7,6},{8,9},{9,8},{10,11... | collective-permute-start | bytes 221192 | tf_op jit(solution)/shard_map/ppermute | solution.py:174
  8.8 1.3 %collective-permute-start.2 = (bf16[144,256]{1,0:T(8,128)(2,1)S(1)}, bf16[144,256]{1,0:T(8,128)(2,1)S(1)}, u32[]{:S(2)}, u32[]{:S(2)}) collective-permute-start(bf16[144,256]{1,0:T(8,128)(2,1)S(1)} %get-tuple-element.19), channel_id=1, source_target_pairs={{0,1},{1,0},{2,3},{3,2},{4,5},{5,4},{6,7},{7,6},{8,9},{9,8},{10,11... | collective-permute-start | bytes 221192 | tf_op jit(solution)/shard_map/ppermute | solution.py:174
  17.0 5.7 %collective-permute-start.7 = (f32[32,256]{1,0:T(8,128)S(1)}, f32[32,256]{1,0:T(8,128)S(1)}, u32[]{:S(2)}, u32[]{:S(2)}) collective-permute-start(f32[32,256]{1,0:T(8,128)S(1)} %get-tuple-element.26), channel_id=1, source_target_pairs={{4,12},{5,13},{6,14},{7,15},{8,4},{9,5},{10,6},{11,7},{0,8},{1,9},... | collective-permute-start | bytes 98312 | tf_op jit(solution)/shard_map/ppermute | solution.py:171
  18.7 4.0 %collective-permute-start.8 = (f32[32,256]{1,0:T(8,128)S(1)}, f32[32,256]{1,0:T(8,128)S(1)}, u32[]{:S(2)}, u32[]{:S(2)}) collective-permute-start(f32[32,256]{1,0:T(8,128)S(1)} %get-tuple-element.27), channel_id=1, source_target_pairs={{0,3},{1,2},{2,1},{3,0},{4,7},{5,6},{6,5},{7,4},{8,11},{9,10},{10,... | collective-permute-start | bytes 98312 | tf_op jit(solution)/shard_map/ppermute | solution.py:174
  18.7 4.0 %collective-permute-start.9 = (f32[32,256]{1,0:T(8,128)S(1)}, f32[32,256]{1,0:T(8,128)S(1)}, u32[]{:S(2)}, u32[]{:S(2)}) collective-permute-start(f32[32,256]{1,0:T(8,128)S(1)} %get-tuple-element.28), channel_id=1, source_target_pairs={{0,2},{1,3},{2,0},{3,1},{4,6},{5,7},{6,4},{7,5},{8,10},{9,11},{10,... | collective-permute-start | bytes 98312 | tf_op jit(solution)/shard_map/ppermute | solution.py:174
  19.7 0.9 %copy-start = (f32[256]{0:T(256)S(1)}, f32[256]{0:T(256)}, u32[]{:S(2)}) copy-start(f32[256]{0:T(256)} %param.5) | copy-start | bytes 3076
  19.7 3.0 %collective-permute-start.10 = (f32[32,256]{1,0:T(8,128)S(1)}, f32[32,256]{1,0:T(8,128)S(1)}, u32[]{:S(2)}, u32[]{:S(2)}) collective-permute-start(f32[32,256]{1,0:T(8,128)S(1)} %get-tuple-element.29), channel_id=1, source_target_pairs={{0,1},{1,0},{2,3},{3,2},{4,5},{5,4},{6,7},{7,6},{8,9},{9,8},{10,11... | collective-permute-start | bytes 98312 | tf_op jit(solution)/shard_map/ppermute | solution.py:174

commit v22 on v20

--- a/solution.py
+++ b/solution.py
@@ -186,8 +186,13 @@
     pairs = [(row, col, ("rows", "back")) for col in range(len(cols)) for row in range(inner)]
     sums = tile(blocks, cols, order, pairs, {}, shard, vectors, work=0.0)
     backs = [sums.pop(("back", place)) for place in range(len(cols))]
-    pairs = [(row, col, ("rows",)) for col in range(len(others)) for row in range(inner)]
-    sums = tile(blocks, others, range(inner + len(others)), pairs, sums, shard, vectors)
+    half = inner // 2
+    far, near_by = list(range(half, inner)), list(range(half))
+    for rows in (far, near_by):
+        pairs = [(place, col, ("rows",)) for col in range(len(others)) for place in range(len(rows))]
+        known = {("rows", place): sums[("rows", row)] for place, row in enumerate(rows)}
+        found = tile([blocks[row] for row in rows], others, range(len(rows) + len(others)), pairs, known, shard, vectors)
+        sums.update({("rows", row): found[("rows", place)] for place, row in enumerate(rows)})
     pairs = [(row, 0, ("back",)) for row in range(inner)]
     own = tile(blocks, [packed], range(inner + 1), pairs, {}, shard, vectors, noise=[noise_level[None, :]])
 

time: 21.8 us -> 21.5 us (0.986)
  waiting for transfers between devices: 6.6 us -> 5.85 us
  Pallas kernels: 2.85 us -> 3.29 us
    ppermute x3, waiting for transfers between devices: 5.65 us -> 5.17 us  [along_outer(): lax.ppermute(value, 'blk', [(s * inner + b, t * inner + b) for s, t in ed...]
    pallas_call x3 -> x4, Pallas kernels: 2.84 us -> 3.28 us  [tile(): pl.pallas_call(functools.partial(tile_kernel, list(order), tuple(pairs),...]
    ppermute x7, waiting for transfers between devices: 0.95 us -> 0.68 us  [in_plane(): lax.ppermute(value, 'blk', [(a * inner + s, a * inner + t) for a in range...]
  transfers between devices with their start and end apart: 10 -> 10, of which waited for: 4 -> 4; matrix products, arithmetic and copies ran while one was open for 0% -> 0% of each run, Pallas kernels for 13% -> 15%
where the time goes in v22:
time: 21.5 us; the launch traced here: 21.3 us
  starting transfers between devices  10.5 us (49%)
  waiting for transfers between devices  5.85 us (27%)
  Pallas kernels  3.29 us (15%)
  other arithmetic  1.56 us (7%)
    ppermute x7, starting transfers between devices, in_plane(): lax.ppermute(value, 'blk', [(a * inner + s, a * inner + t) for a in range...  5.55 us
    ppermute x3, waiting for transfers between devices, along_outer(): lax.ppermute(value, 'blk', [(s * inner + b, t * inner + b) for s, t in ed...  5.17 us
    ppermute x3, starting transfers between devices, along_outer(): lax.ppermute(value, 'blk', [(s * inner + b, t * inner + b) for s, t in ed...  4.99 us
    pallas_call x4, Pallas kernels, tile(): pl.pallas_call(functools.partial(tile_kernel, list(order), tuple(pairs),...  3.28 us
    concatenate x1, other arithmetic, on_device(): packed = jnp.concatenate([features, probes.T], axis=0)  0.93 us
    ppermute x7, waiting for transfers between devices, in_plane(): lax.ppermute(value, 'blk', [(a * inner + s, a * inner + t) for a in range...  0.68 us
    transpose x1, other arithmetic, on_device(): return functools.reduce(lambda sofar, term: sofar + term, total).T  0.63 us
  transfers between devices with their start and end apart: 10, of which 4 were waited for; matrix products, arithmetic and copies ran while one was open for 0% of the time, Pallas kernels for 15%

profile of v22, /device:TPU:0, one launch (start us, length us, event | category | flops | bytes accessed | tf_op | source)
XLA Modules:
  0.0 21.3 jit_solution(749001703391383411)
XLA Ops:
  0.0 0.9 %pad_maximum_fusion.refs_0_.refs_5_ = bf16[288,256]{1,0:T(8,128)(2,1)S(1)} fusion(bf16[32,256]{1,0:T(8,128)(2,1)} %bitcast.5, bf16[256,256]{1,0:T(8,128)(2,1)} %param.3), kind=kLoop, calls=%fused_computation | loop fusion | flops 294912 | bytes 294912 | tf_op jit(solution)/shard_map/concatenate | solution.py:167
  0.9 3.0 %collective-permute-start.2 = (bf16[288,256]{1,0:T(8,128)(2,1)S(1)}, bf16[288,256]{1,0:T(8,128)(2,1)S(1)}, u32[]{:S(2)}, u32[]{:S(2)}) collective-permute-start(bf16[288,256]{1,0:T(8,128)(2,1)S(1)} %pad_maximum_fusion.refs_0_.refs_5_), channel_id=1, source_target_pairs={{0,2},{1,3},{2,0},{3,1},{4,6},{5,7},{6,4},{7,5},{8,10},{9,11},{10,... | collective-permute-start | bytes 442376 | tf_op jit(solution)/shard_map/ppermute | solution.py:173
  4.0 3.6 %collective-permute-start.5 = (bf16[288,256]{1,0:T(8,128)(2,1)S(1)}, bf16[288,256]{1,0:T(8,128)(2,1)S(1)}, u32[]{:S(2)}, u32[]{:S(2)}) collective-permute-start(bf16[288,256]{1,0:T(8,128)(2,1)S(1)} %pad_maximum_fusion.refs_0_.refs_5_), channel_id=1, source_target_pairs={{12,4},{13,5},{14,6},{15,7},{4,8},{5,9},{6,10},{7,11},{8,0},{9,1},... | collective-permute-start | bytes 442376 | tf_op jit(solution)/shard_map/ppermute | solution.py:170
  7.6 0.2 %collective-permute-done.2.from_ref.refs_5_.refs_2_.refs_0_ = bf16[288,256]{1,0:T(8,128)(2,1)S(1)} collective-permute-done((bf16[288,256]{1,0:T(8,128)(2,1)S(1)}, bf16[288,256]{1,0:T(8,128)(2,1)S(1)}, u32[]{:S(2)}, u32[]{:S(2)}) %collective-permute-start.2) | collective-permute-done | bytes 147488 | tf_op jit(solution)/shard_map/ppermute | solution.py:173
  7.8 0.3 %collective-permute-start.3 = (bf16[144,256]{1,0:T(8,128)(2,1)S(1)}, bf16[144,256]{1,0:T(8,128)(2,1)S(1)}, u32[]{:S(2)}, u32[]{:S(2)}) collective-permute-start(bf16[144,256]{1,0:T(8,128)(2,1)S(1)} %get-tuple-element.16), channel_id=1, source_target_pairs={{0,1},{1,0},{2,3},{3,2},{4,5},{5,4},{6,7},{7,6},{8,9},{9,8},{10,11... | collective-permute-start | bytes 221192 | tf_op jit(solution)/shard_map/ppermute | solution.py:173
  8.2 0.2 %collective-permute-start.4 = (bf16[144,256]{1,0:T(8,128)(2,1)S(1)}, bf16[144,256]{1,0:T(8,128)(2,1)S(1)}, u32[]{:S(2)}, u32[]{:S(2)}) collective-permute-start(bf16[144,256]{1,0:T(8,128)(2,1)S(1)} %get-tuple-element.17), channel_id=1, source_target_pairs={{0,1},{1,0},{2,3},{3,2},{4,5},{5,4},{6,7},{7,6},{8,9},{9,8},{10,11... | collective-permute-start | bytes 221192 | tf_op jit(solution)/shard_map/ppermute | solution.py:173
  8.4 5.0 %collective-permute-done.5.refs_3_ = bf16[288,256]{1,0:T(8,128)(2,1)S(1)} collective-permute-done((bf16[288,256]{1,0:T(8,128)(2,1)S(1)}, bf16[288,256]{1,0:T(8,128)(2,1)S(1)}, u32[]{:S(2)}, u32[]{:S(2)}) %collective-permute-start.5) | collective-permute-done | bytes 147488 | tf_op jit(solution)/shard_map/ppermute | solution.py:170
  13.4 0.0 collective-permute-done.refs_4_.refs_1_
  13.4 0.0 collective-permute-done.3.refs_1_.refs_3_
  13.4 0.0 collective-permute-done.4.refs_2_.refs_4_
  13.5 1.0 %shard_map.38 = (f32[32,256]{1,0:T(8,128)S(1)}, f32[32,256]{1,0:T(8,128)S(1)}, f32[32,256]{1,0:T(8,128)S(1)}, f32[32,256]{1,0:T(8,128)S(1)}, f32[32,256]{1,0:T(8,128)S(1)}) custom-call(bf16[288,256]{1,0:T(8,128)(2,1)S(1)} %pad_maximum_fusion.refs_0_.refs_5_, bf16[144,256]{1,0:T(8,128)(2,1)S(1)} %collective-permute-done.3.refs_1_.refs_3_, ...), custom_call_target="tpu_custom_call" | custom-call | tf_op jit(solution)/shard_map/pallas_call | solution.py:124
  14.5 1.4 %collective-permute-start.9 = (f32[32,256]{1,0:T(8,128)S(1)}, f32[32,256]{1,0:T(8,128)S(1)}, u32[]{:S(2)}, u32[]{:S(2)}) collective-permute-start(f32[32,256]{1,0:T(8,128)S(1)} %get-tuple-element.26), channel_id=1, source_target_pairs={{4,12},{5,13},{6,14},{7,15},{8,4},{9,5},{10,6},{11,7},{0,8},{1,9},... | collective-permute-start | bytes 98312 | tf_op jit(solution)/shard_map/ppermute | solution.py:170
  15.9 0.7 %shard_map.41 = (f32[32,256]{1,0:T(8,128)S(1)}, f32[32,256]{1,0:T(8,128)S(1)}) custom-call(bf16[288,256]{1,0:T(8,128)(2,1)S(1)} %collective-permute-done.2.from_ref.refs_5_.refs_2_.refs_0_, bf16[144,256]{1,0:T(8,128)(2,1)S(1)} %collective-permute-done.3.refs_1_.refs_3_, bf16[144,256]{1,0:T(8,128)(2,1)S(1)} %collective-permute-done.4.refs_2_.refs_4_, ...), custom_call_target="tpu_custom_call" | custom-call | flops 83886080 | bytes 393216 | tf_op jit(solution)/shard_map/pallas_call | solution.py:124
  16.5 0.0 collective-permute-start.8
  16.6 1.1 %collective-permute-start.7 = (f32[32,256]{1,0:T(8,128)S(1)}, f32[32,256]{1,0:T(8,128)S(1)}, u32[]{:S(2)}, u32[]{:S(2)}) collective-permute-start(f32[32,256]{1,0:T(8,128)S(1)} %get-tuple-element.24), channel_id=1, source_target_pairs={{0,2},{1,3},{2,0},{3,1},{4,6},{5,7},{6,4},{7,5},{8,10},{9,11},{10,... | collective-permute-start | bytes 98312 | tf_op jit(solution)/shard_map/ppermute | solution.py:173
  17.7 0.7 %shard_map.39 = (f32[32,256]{1,0:T(8,128)S(1)}, f32[32,256]{1,0:T(8,128)S(1)}) custom-call(bf16[288,256]{1,0:T(8,128)(2,1)S(1)} %pad_maximum_fusion.refs_0_.refs_5_, bf16[288,256]{1,0:T(8,128)(2,1)S(1)} %collective-permute-done.refs_4_.refs_1_, bf16[288,256]{1,0:T(8,128)(2,1)S(1)} %collective-permute-done.1.refs_2_.refs_3_, ...), custom_call_target="tpu_custom_call" | custom-call | flops 83886080 | bytes 393216 | tf_op jit(solution)/shard_map/pallas_call | solution.py:124
  18.4 0.0 copy-start
  18.4 0.8 %collective-permute-start.6 = (f32[32,256]{1,0:T(8,128)S(1)}, f32[32,256]{1,0:T(8,128)S(1)}, u32[]{:S(2)}, u32[]{:S(2)}) collective-permute-start(f32[32,256]{1,0:T(8,128)S(1)} %get-tuple-element.21), channel_id=1, source_target_pairs={{0,1},{1,0},{2,3},{3,2},{4,5},{5,4},{6,7},{7,6},{8,9},{9,8},{10,11... | collective-permute-start | bytes 98312 | tf_op jit(solution)/shard_map/ppermute | solution.py:173
  19.2 0.9 %shard_map.40 = f32[32,256]{1,0:T(8,128)S(1)} custom-call(bf16[288,256]{1,0:T(8,128)(2,1)S(1)} %pad_maximum_fusion.refs_0_.refs_5_, bf16[288,256]{1,0:T(8,128)(2,1)S(1)} %collective-permute-done.refs_4_.refs_1_, bf16[288,256]{1,0:T(8,128)(2,1)S(1)} %collective-permute-done.2.from_ref.refs_5_.refs_2_.refs_0_, ...), custom_call_target="tpu_custom_call" | custom-call | flops 167772160 | bytes 655360 | tf_op jit(solution)/shard_map/pallas_call | solution.py:124
  20.1 0.1 collective-permute-done.9
  20.2 0.0 collective-permute-done.8
  20.2 0.4 %collective-permute-done.7 = f32[32,256]{1,0:T(8,128)S(1)} collective-permute-done((f32[32,256]{1,0:T(8,128)S(1)}, f32[32,256]{1,0:T(8,128)S(1)}, u32[]{:S(2)}, u32[]{:S(2)}) %collective-permute-start.7) | collective-permute-done | bytes 32800 | tf_op jit(solution)/shard_map/ppermute | solution.py:173
  20.7 0.0 collective-permute-done.6
  20.7 0.6 %add_bitcast_fusion = f32[256,32]{0,1:T(8,128)} fusion(f32[32,256]{1,0:T(8,128)S(1)} %collective-permute-done.9, f32[32,256]{1,0:T(8,128)S(1)} %collective-permute-done.8, f32[32,256]{1,0:T(8,128)S(1)} %collective-permute-done.7, f32[32,256]{1,0:T(8,128)S(1)} %collective-permute-done.6, f32[32,256]{1,0:T(8,128)S(1)} %get-tuple-element.20, ...), kind=kLoop, calls=%fused_computation.1 | loop fusion | flops 40960 | bytes 229376 | tf_op jit(solution)/shard_map/transpose | solution.py:202
  (5 shorter events, 0.0 us)
Async XLA Ops:
  0.9 6.9 %collective-permute-start.2 = (bf16[288,256]{1,0:T(8,128)(2,1)S(1)}, bf16[288,256]{1,0:T(8,128)(2,1)S(1)}, u32[]{:S(2)}, u32[]{:S(2)}) collective-permute-start(bf16[288,256]{1,0:T(8,128)(2,1)S(1)} %pad_maximum_fusion.refs_0_.refs_5_), channel_id=1, source_target_pairs={{0,2},{1,3},{2,0},{3,1},{4,6},{5,7},{6,4},{7,5},{8,10},{9,11},{10,... | collective-permute-start | bytes 442376 | tf_op jit(solution)/shard_map/ppermute | solution.py:173
  4.0 9.5 %collective-permute-start.5 = (bf16[288,256]{1,0:T(8,128)(2,1)S(1)}, bf16[288,256]{1,0:T(8,128)(2,1)S(1)}, u32[]{:S(2)}, u32[]{:S(2)}) collective-permute-start(bf16[288,256]{1,0:T(8,128)(2,1)S(1)} %pad_maximum_fusion.refs_0_.refs_5_), channel_id=1, source_target_pairs={{12,4},{13,5},{14,6},{15,7},{4,8},{5,9},{6,10},{7,11},{8,0},{9,1},... | collective-permute-start | bytes 442376 | tf_op jit(solution)/shard_map/ppermute | solution.py:170
  7.6 5.9 %collective-permute-start = (bf16[288,256]{1,0:T(8,128)(2,1)S(1)}, bf16[288,256]{1,0:T(8,128)(2,1)S(1)}, u32[]{:S(2)}, u32[]{:S(2)}) collective-permute-start(bf16[288,256]{1,0:T(8,128)(2,1)S(1)} %pad_maximum_fusion.refs_0_.refs_5_), channel_id=1, source_target_pairs={{0,1},{1,0},{2,3},{3,2},{4,5},{5,4},{6,7},{7,6},{8,9},{9,8},{10,11... | collective-permute-start | bytes 442376 | tf_op jit(solution)/shard_map/ppermute | solution.py:173
  7.6 8.3 %collective-permute-start.1 = (bf16[288,256]{1,0:T(8,128)(2,1)S(1)}, bf16[288,256]{1,0:T(8,128)(2,1)S(1)}, u32[]{:S(2)}, u32[]{:S(2)}) collective-permute-start(bf16[288,256]{1,0:T(8,128)(2,1)S(1)} %pad_maximum_fusion.refs_0_.refs_5_), channel_id=1, source_target_pairs={{12,8},{13,9},{14,10},{15,11},{4,0},{5,1},{6,2},{7,3},{8,12},{9,13... | collective-permute-start | bytes 442376 | tf_op jit(solution)/shard_map/ppermute | solution.py:170
  7.8 5.6 %collective-permute-start.3 = (bf16[144,256]{1,0:T(8,128)(2,1)S(1)}, bf16[144,256]{1,0:T(8,128)(2,1)S(1)}, u32[]{:S(2)}, u32[]{:S(2)}) collective-permute-start(bf16[144,256]{1,0:T(8,128)(2,1)S(1)} %get-tuple-element.16), channel_id=1, source_target_pairs={{0,1},{1,0},{2,3},{3,2},{4,5},{5,4},{6,7},{7,6},{8,9},{9,8},{10,11... | collective-permute-start | bytes 221192 | tf_op jit(solution)/shard_map/ppermute | solution.py:173
  8.2 5.3 %collective-permute-start.4 = (bf16[144,256]{1,0:T(8,128)(2,1)S(1)}, bf16[144,256]{1,0:T(8,128)(2,1)S(1)}, u32[]{:S(2)}, u32[]{:S(2)}) collective-permute-start(bf16[144,256]{1,0:T(8,128)(2,1)S(1)} %get-tuple-element.17), channel_id=1, source_target_pairs={{0,1},{1,0},{2,3},{3,2},{4,5},{5,4},{6,7},{7,6},{8,9},{9,8},{10,11... | collective-permute-start | bytes 221192 | tf_op jit(solution)/shard_map/ppermute | solution.py:173
  14.5 5.7 %collective-permute-start.9 = (f32[32,256]{1,0:T(8,128)S(1)}, f32[32,256]{1,0:T(8,128)S(1)}, u32[]{:S(2)}, u32[]{:S(2)}) collective-permute-start(f32[32,256]{1,0:T(8,128)S(1)} %get-tuple-element.26), channel_id=1, source_target_pairs={{4,12},{5,13},{6,14},{7,15},{8,4},{9,5},{10,6},{11,7},{0,8},{1,9},... | collective-permute-start | bytes 98312 | tf_op jit(solution)/shard_map/ppermute | solution.py:170
  16.5 3.7 %collective-permute-start.8 = (f32[32,256]{1,0:T(8,128)S(1)}, f32[32,256]{1,0:T(8,128)S(1)}, u32[]{:S(2)}, u32[]{:S(2)}) collective-permute-start(f32[32,256]{1,0:T(8,128)S(1)} %get-tuple-element.25), channel_id=1, source_target_pairs={{0,3},{1,2},{2,1},{3,0},{4,7},{5,6},{6,5},{7,4},{8,11},{9,10},{10,... | collective-permute-start | bytes 98312 | tf_op jit(solution)/shard_map/ppermute | solution.py:173
  16.6 4.1 %collective-permute-start.7 = (f32[32,256]{1,0:T(8,128)S(1)}, f32[32,256]{1,0:T(8,128)S(1)}, u32[]{:S(2)}, u32[]{:S(2)}) collective-permute-start(f32[32,256]{1,0:T(8,128)S(1)} %get-tuple-element.24), channel_id=1, source_target_pairs={{0,2},{1,3},{2,0},{3,1},{4,6},{5,7},{6,4},{7,5},{8,10},{9,11},{10,... | collective-permute-start | bytes 98312 | tf_op jit(solution)/shard_map/ppermute | solution.py:173
  18.4 0.8 %copy-start = (f32[256]{0:T(256)S(1)}, f32[256]{0:T(256)}, u32[]{:S(2)}) copy-start(f32[256]{0:T(256)} %param.5) | copy-start | bytes 3076
  18.4 2.3 %collective-permute-start.6 = (f32[32,256]{1,0:T(8,128)S(1)}, f32[32,256]{1,0:T(8,128)S(1)}, u32[]{:S(2)}, u32[]{:S(2)}) collective-permute-start(f32[32,256]{1,0:T(8,128)S(1)} %get-tuple-element.21), channel_id=1, source_target_pairs={{0,1},{1,0},{2,3},{3,2},{4,5},{5,4},{6,7},{7,6},{8,9},{9,8},{10,11... | collective-permute-start | bytes 98312 | tf_op jit(solution)/shard_map/ppermute | solution.py:173

commit v23 on v22

--- a/solution.py
+++ b/solution.py
@@ -59,13 +59,8 @@
 
 def lane_squares(block):
     wide = block.astype(jnp.float32)
-    square = wide * wide
-    high = square.astype(jnp.bfloat16)
-    low = (square - high.astype(jnp.float32)).astype(jnp.bfloat16)
-    ones = jnp.ones((8, block.shape[1]), jnp.bfloat16)
-    total = lax.dot_general(ones, high, ROWS_BY_ROWS, preferred_element_type=jnp.float32)
-    total += lax.dot_general(ones, low, ROWS_BY_ROWS, preferred_element_type=jnp.float32)
-    return total[0:1, :]
+    sums = jnp.sum(wide * wide, axis=1, keepdims=True)
+    return jnp.transpose(jnp.broadcast_to(sums, (block.shape[0], 128)))[0:1, :]
 
 
 def joined(refs, shard, vectors):

time: 21.5 us -> 21.5 us (level)
  no operation moved by 1% of the time
where the time goes in v23:
time: 21.5 us; the launch traced here: 21.3 us
  starting transfers between devices  10.5 us (49%)
  waiting for transfers between devices  5.88 us (27%)
  Pallas kernels  3.23 us (15%)
  other arithmetic  1.56 us (7%)
    ppermute x7, starting transfers between devices, in_plane(): lax.ppermute(value, 'blk', [(a * inner + s, a * inner + t) for a in range...  5.54 us
    ppermute x3, waiting for transfers between devices, along_outer(): lax.ppermute(value, 'blk', [(s * inner + b, t * inner + b) for s, t in ed...  5.3 us
    ppermute x3, starting transfers between devices, along_outer(): lax.ppermute(value, 'blk', [(s * inner + b, t * inner + b) for s, t in ed...  4.99 us
    pallas_call x4, Pallas kernels, tile(): pl.pallas_call(functools.partial(tile_kernel, list(order), tuple(pairs),...  3.22 us
    concatenate x1, other arithmetic, on_device(): packed = jnp.concatenate([features, probes.T], axis=0)  0.93 us
    transpose x1, other arithmetic, on_device(): return functools.reduce(lambda sofar, term: sofar + term, total).T  0.63 us
    ppermute x7, waiting for transfers between devices, in_plane(): lax.ppermute(value, 'blk', [(a * inner + s, a * inner + t) for a in range...  0.58 us
  transfers between devices with their start and end apart: 10, of which 4 were waited for; matrix products, arithmetic and copies ran while one was open for 0% of the time, Pallas kernels for 15%

profile of v23, /device:TPU:0, one launch (start us, length us, event | category | flops | bytes accessed | tf_op | source)
XLA Modules:
  0.0 21.3 jit_solution(7087412245439121946)
XLA Ops:
  0.0 0.9 %pad_maximum_fusion.refs_0_.refs_5_ = bf16[288,256]{1,0:T(8,128)(2,1)S(1)} fusion(bf16[32,256]{1,0:T(8,128)(2,1)} %bitcast.5, bf16[256,256]{1,0:T(8,128)(2,1)} %param.3), kind=kLoop, calls=%fused_computation | loop fusion | flops 294912 | bytes 294912 | tf_op jit(solution)/shard_map/concatenate | solution.py:162
  0.9 3.0 %collective-permute-start.2 = (bf16[288,256]{1,0:T(8,128)(2,1)S(1)}, bf16[288,256]{1,0:T(8,128)(2,1)S(1)}, u32[]{:S(2)}, u32[]{:S(2)}) collective-permute-start(bf16[288,256]{1,0:T(8,128)(2,1)S(1)} %pad_maximum_fusion.refs_0_.refs_5_), channel_id=1, source_target_pairs={{0,2},{1,3},{2,0},{3,1},{4,6},{5,7},{6,4},{7,5},{8,10},{9,11},{10,... | collective-permute-start | bytes 442376 | tf_op jit(solution)/shard_map/ppermute | solution.py:168
  4.0 3.6 %collective-permute-start.5 = (bf16[288,256]{1,0:T(8,128)(2,1)S(1)}, bf16[288,256]{1,0:T(8,128)(2,1)S(1)}, u32[]{:S(2)}, u32[]{:S(2)}) collective-permute-start(bf16[288,256]{1,0:T(8,128)(2,1)S(1)} %pad_maximum_fusion.refs_0_.refs_5_), channel_id=1, source_target_pairs={{12,4},{13,5},{14,6},{15,7},{4,8},{5,9},{6,10},{7,11},{8,0},{9,1},... | collective-permute-start | bytes 442376 | tf_op jit(solution)/shard_map/ppermute | solution.py:165
  7.6 0.0 collective-permute-start
  7.6 0.0 collective-permute-start.1
  7.6 0.2 %collective-permute-done.2.from_ref.refs_5_.refs_2_.refs_0_ = bf16[288,256]{1,0:T(8,128)(2,1)S(1)} collective-permute-done((bf16[288,256]{1,0:T(8,128)(2,1)S(1)}, bf16[288,256]{1,0:T(8,128)(2,1)S(1)}, u32[]{:S(2)}, u32[]{:S(2)}) %collective-permute-start.2) | collective-permute-done | bytes 147488 | tf_op jit(solution)/shard_map/ppermute | solution.py:168
  7.8 0.3 %collective-permute-start.3 = (bf16[144,256]{1,0:T(8,128)(2,1)S(1)}, bf16[144,256]{1,0:T(8,128)(2,1)S(1)}, u32[]{:S(2)}, u32[]{:S(2)}) collective-permute-start(bf16[144,256]{1,0:T(8,128)(2,1)S(1)} %get-tuple-element.16), channel_id=1, source_target_pairs={{0,1},{1,0},{2,3},{3,2},{4,5},{5,4},{6,7},{7,6},{8,9},{9,8},{10,11... | collective-permute-start | bytes 221192 | tf_op jit(solution)/shard_map/ppermute | solution.py:168
  8.2 0.2 %collective-permute-start.4 = (bf16[144,256]{1,0:T(8,128)(2,1)S(1)}, bf16[144,256]{1,0:T(8,128)(2,1)S(1)}, u32[]{:S(2)}, u32[]{:S(2)}) collective-permute-start(bf16[144,256]{1,0:T(8,128)(2,1)S(1)} %get-tuple-element.17), channel_id=1, source_target_pairs={{0,1},{1,0},{2,3},{3,2},{4,5},{5,4},{6,7},{7,6},{8,9},{9,8},{10,11... | collective-permute-start | bytes 221192 | tf_op jit(solution)/shard_map/ppermute | solution.py:168
  8.4 5.0 %collective-permute-done.5.refs_3_ = bf16[288,256]{1,0:T(8,128)(2,1)S(1)} collective-permute-done((bf16[288,256]{1,0:T(8,128)(2,1)S(1)}, bf16[288,256]{1,0:T(8,128)(2,1)S(1)}, u32[]{:S(2)}, u32[]{:S(2)}) %collective-permute-start.5) | collective-permute-done | bytes 147488 | tf_op jit(solution)/shard_map/ppermute | solution.py:165
  13.4 0.0 collective-permute-done.refs_4_.refs_1_
  13.4 0.0 collective-permute-done.3.refs_1_.refs_3_
  13.4 0.0 collective-permute-done.4.refs_2_.refs_4_
  13.5 1.1 %shard_map.38 = (f32[32,256]{1,0:T(8,128)S(1)}, f32[32,256]{1,0:T(8,128)S(1)}, f32[32,256]{1,0:T(8,128)S(1)}, f32[32,256]{1,0:T(8,128)S(1)}, f32[32,256]{1,0:T(8,128)S(1)}) custom-call(bf16[288,256]{1,0:T(8,128)(2,1)S(1)} %pad_maximum_fusion.refs_0_.refs_5_, bf16[144,256]{1,0:T(8,128)(2,1)S(1)} %collective-permute-done.3.refs_1_.refs_3_, ...), custom_call_target="tpu_custom_call" | custom-call | tf_op jit(solution)/shard_map/pallas_call | solution.py:119
  14.6 1.4 %collective-permute-start.9 = (f32[32,256]{1,0:T(8,128)S(1)}, f32[32,256]{1,0:T(8,128)S(1)}, u32[]{:S(2)}, u32[]{:S(2)}) collective-permute-start(f32[32,256]{1,0:T(8,128)S(1)} %get-tuple-element.26), channel_id=1, source_target_pairs={{4,12},{5,13},{6,14},{7,15},{8,4},{9,5},{10,6},{11,7},{0,8},{1,9},... | collective-permute-start | bytes 98312 | tf_op jit(solution)/shard_map/ppermute | solution.py:165
  15.9 0.6 %shard_map.41 = (f32[32,256]{1,0:T(8,128)S(1)}, f32[32,256]{1,0:T(8,128)S(1)}) custom-call(bf16[288,256]{1,0:T(8,128)(2,1)S(1)} %collective-permute-done.2.from_ref.refs_5_.refs_2_.refs_0_, bf16[144,256]{1,0:T(8,128)(2,1)S(1)} %collective-permute-done.3.refs_1_.refs_3_, bf16[144,256]{1,0:T(8,128)(2,1)S(1)} %collective-permute-done.4.refs_2_.refs_4_, ...), custom_call_target="tpu_custom_call" | custom-call | flops 83886080 | bytes 393216 | tf_op jit(solution)/shard_map/pallas_call | solution.py:119
  16.6 0.0 collective-permute-start.8
  16.6 1.1 %collective-permute-start.7 = (f32[32,256]{1,0:T(8,128)S(1)}, f32[32,256]{1,0:T(8,128)S(1)}, u32[]{:S(2)}, u32[]{:S(2)}) collective-permute-start(f32[32,256]{1,0:T(8,128)S(1)} %get-tuple-element.24), channel_id=1, source_target_pairs={{0,2},{1,3},{2,0},{3,1},{4,6},{5,7},{6,4},{7,5},{8,10},{9,11},{10,... | collective-permute-start | bytes 98312 | tf_op jit(solution)/shard_map/ppermute | solution.py:168
  17.6 0.6 %shard_map.39 = (f32[32,256]{1,0:T(8,128)S(1)}, f32[32,256]{1,0:T(8,128)S(1)}) custom-call(bf16[288,256]{1,0:T(8,128)(2,1)S(1)} %pad_maximum_fusion.refs_0_.refs_5_, bf16[288,256]{1,0:T(8,128)(2,1)S(1)} %collective-permute-done.refs_4_.refs_1_, bf16[288,256]{1,0:T(8,128)(2,1)S(1)} %collective-permute-done.1.refs_2_.refs_3_, ...), custom_call_target="tpu_custom_call" | custom-call | flops 83886080 | bytes 393216 | tf_op jit(solution)/shard_map/pallas_call | solution.py:119
  18.3 0.9 %collective-permute-start.6 = (f32[32,256]{1,0:T(8,128)S(1)}, f32[32,256]{1,0:T(8,128)S(1)}, u32[]{:S(2)}, u32[]{:S(2)}) collective-permute-start(f32[32,256]{1,0:T(8,128)S(1)} %get-tuple-element.21), channel_id=1, source_target_pairs={{0,1},{1,0},{2,3},{3,2},{4,5},{5,4},{6,7},{7,6},{8,9},{9,8},{10,11... | collective-permute-start | bytes 98312 | tf_op jit(solution)/shard_map/ppermute | solution.py:168
  19.1 0.9 %shard_map.40 = f32[32,256]{1,0:T(8,128)S(1)} custom-call(bf16[288,256]{1,0:T(8,128)(2,1)S(1)} %pad_maximum_fusion.refs_0_.refs_5_, bf16[288,256]{1,0:T(8,128)(2,1)S(1)} %collective-permute-done.refs_4_.refs_1_, bf16[288,256]{1,0:T(8,128)(2,1)S(1)} %collective-permute-done.2.from_ref.refs_5_.refs_2_.refs_0_, ...), custom_call_target="tpu_custom_call" | custom-call | flops 167772160 | bytes 655360 | tf_op jit(solution)/shard_map/pallas_call | solution.py:119
  20.0 0.3 %collective-permute-done.9 = f32[32,256]{1,0:T(8,128)S(1)} collective-permute-done((f32[32,256]{1,0:T(8,128)S(1)}, f32[32,256]{1,0:T(8,128)S(1)}, u32[]{:S(2)}, u32[]{:S(2)}) %collective-permute-start.9) | collective-permute-done | bytes 32800 | tf_op jit(solution)/shard_map/ppermute | solution.py:165
  20.3 0.3 %collective-permute-done.7 = f32[32,256]{1,0:T(8,128)S(1)} collective-permute-done((f32[32,256]{1,0:T(8,128)S(1)}, f32[32,256]{1,0:T(8,128)S(1)}, u32[]{:S(2)}, u32[]{:S(2)}) %collective-permute-start.7) | collective-permute-done | bytes 32800 | tf_op jit(solution)/shard_map/ppermute | solution.py:168
  20.6 0.0 collective-permute-done.6
  20.6 0.6 %add_bitcast_fusion = f32[256,32]{0,1:T(8,128)} fusion(f32[32,256]{1,0:T(8,128)S(1)} %collective-permute-done.9, f32[32,256]{1,0:T(8,128)S(1)} %collective-permute-done.8, f32[32,256]{1,0:T(8,128)S(1)} %collective-permute-done.7, f32[32,256]{1,0:T(8,128)S(1)} %collective-permute-done.6, f32[32,256]{1,0:T(8,128)S(1)} %get-tuple-element.20, ...), kind=kLoop, calls=%fused_computation.1 | loop fusion | flops 40960 | bytes 229376 | tf_op jit(solution)/shard_map/transpose | solution.py:197
  (5 shorter events, 0.0 us)
Async XLA Ops:
  0.9 6.9 %collective-permute-start.2 = (bf16[288,256]{1,0:T(8,128)(2,1)S(1)}, bf16[288,256]{1,0:T(8,128)(2,1)S(1)}, u32[]{:S(2)}, u32[]{:S(2)}) collective-permute-start(bf16[288,256]{1,0:T(8,128)(2,1)S(1)} %pad_maximum_fusion.refs_0_.refs_5_), channel_id=1, source_target_pairs={{0,2},{1,3},{2,0},{3,1},{4,6},{5,7},{6,4},{7,5},{8,10},{9,11},{10,... | collective-permute-start | bytes 442376 | tf_op jit(solution)/shard_map/ppermute | solution.py:168
  4.0 9.5 %collective-permute-start.5 = (bf16[288,256]{1,0:T(8,128)(2,1)S(1)}, bf16[288,256]{1,0:T(8,128)(2,1)S(1)}, u32[]{:S(2)}, u32[]{:S(2)}) collective-permute-start(bf16[288,256]{1,0:T(8,128)(2,1)S(1)} %pad_maximum_fusion.refs_0_.refs_5_), channel_id=1, source_target_pairs={{12,4},{13,5},{14,6},{15,7},{4,8},{5,9},{6,10},{7,11},{8,0},{9,1},... | collective-permute-start | bytes 442376 | tf_op jit(solution)/shard_map/ppermute | solution.py:165
  7.6 5.9 %collective-permute-start = (bf16[288,256]{1,0:T(8,128)(2,1)S(1)}, bf16[288,256]{1,0:T(8,128)(2,1)S(1)}, u32[]{:S(2)}, u32[]{:S(2)}) collective-permute-start(bf16[288,256]{1,0:T(8,128)(2,1)S(1)} %pad_maximum_fusion.refs_0_.refs_5_), channel_id=1, source_target_pairs={{0,1},{1,0},{2,3},{3,2},{4,5},{5,4},{6,7},{7,6},{8,9},{9,8},{10,11... | collective-permute-start | bytes 442376 | tf_op jit(solution)/shard_map/ppermute | solution.py:168
  7.6 8.4 %collective-permute-start.1 = (bf16[288,256]{1,0:T(8,128)(2,1)S(1)}, bf16[288,256]{1,0:T(8,128)(2,1)S(1)}, u32[]{:S(2)}, u32[]{:S(2)}) collective-permute-start(bf16[288,256]{1,0:T(8,128)(2,1)S(1)} %pad_maximum_fusion.refs_0_.refs_5_), channel_id=1, source_target_pairs={{12,8},{13,9},{14,10},{15,11},{4,0},{5,1},{6,2},{7,3},{8,12},{9,13... | collective-permute-start | bytes 442376 | tf_op jit(solution)/shard_map/ppermute | solution.py:165
  7.8 5.6 %collective-permute-start.3 = (bf16[144,256]{1,0:T(8,128)(2,1)S(1)}, bf16[144,256]{1,0:T(8,128)(2,1)S(1)}, u32[]{:S(2)}, u32[]{:S(2)}) collective-permute-start(bf16[144,256]{1,0:T(8,128)(2,1)S(1)} %get-tuple-element.16), channel_id=1, source_target_pairs={{0,1},{1,0},{2,3},{3,2},{4,5},{5,4},{6,7},{7,6},{8,9},{9,8},{10,11... | collective-permute-start | bytes 221192 | tf_op jit(solution)/shard_map/ppermute | solution.py:168
  8.2 5.3 %collective-permute-start.4 = (bf16[144,256]{1,0:T(8,128)(2,1)S(1)}, bf16[144,256]{1,0:T(8,128)(2,1)S(1)}, u32[]{:S(2)}, u32[]{:S(2)}) collective-permute-start(bf16[144,256]{1,0:T(8,128)(2,1)S(1)} %get-tuple-element.17), channel_id=1, source_target_pairs={{0,1},{1,0},{2,3},{3,2},{4,5},{5,4},{6,7},{7,6},{8,9},{9,8},{10,11... | collective-permute-start | bytes 221192 | tf_op jit(solution)/shard_map/ppermute | solution.py:168
  14.6 5.7 %collective-permute-start.9 = (f32[32,256]{1,0:T(8,128)S(1)}, f32[32,256]{1,0:T(8,128)S(1)}, u32[]{:S(2)}, u32[]{:S(2)}) collective-permute-start(f32[32,256]{1,0:T(8,128)S(1)} %get-tuple-element.26), channel_id=1, source_target_pairs={{4,12},{5,13},{6,14},{7,15},{8,4},{9,5},{10,6},{11,7},{0,8},{1,9},... | collective-permute-start | bytes 98312 | tf_op jit(solution)/shard_map/ppermute | solution.py:165
  16.6 3.7 %collective-permute-start.8 = (f32[32,256]{1,0:T(8,128)S(1)}, f32[32,256]{1,0:T(8,128)S(1)}, u32[]{:S(2)}, u32[]{:S(2)}) collective-permute-start(f32[32,256]{1,0:T(8,128)S(1)} %get-tuple-element.25), channel_id=1, source_target_pairs={{0,3},{1,2},{2,1},{3,0},{4,7},{5,6},{6,5},{7,4},{8,11},{9,10},{10,... | collective-permute-start | bytes 98312 | tf_op jit(solution)/shard_map/ppermute | solution.py:168
  16.6 4.0 %collective-permute-start.7 = (f32[32,256]{1,0:T(8,128)S(1)}, f32[32,256]{1,0:T(8,128)S(1)}, u32[]{:S(2)}, u32[]{:S(2)}) collective-permute-start(f32[32,256]{1,0:T(8,128)S(1)} %get-tuple-element.24), channel_id=1, source_target_pairs={{0,2},{1,3},{2,0},{3,1},{4,6},{5,7},{6,4},{7,5},{8,10},{9,11},{10,... | collective-permute-start | bytes 98312 | tf_op jit(solution)/shard_map/ppermute | solution.py:168
  18.3 0.9 %copy-start = (f32[256]{0:T(256)S(1)}, f32[256]{0:T(256)}, u32[]{:S(2)}) copy-start(f32[256]{0:T(256)} %param.5) | copy-start | bytes 3076
  18.3 2.3 %collective-permute-start.6 = (f32[32,256]{1,0:T(8,128)S(1)}, f32[32,256]{1,0:T(8,128)S(1)}, u32[]{:S(2)}, u32[]{:S(2)}) collective-permute-start(f32[32,256]{1,0:T(8,128)S(1)} %get-tuple-element.21), channel_id=1, source_target_pairs={{0,1},{1,0},{2,3},{3,2},{4,5},{5,4},{6,7},{7,6},{8,9},{9,8},{10,11... | collective-permute-start | bytes 98312 | tf_op jit(solution)/shard_map/ppermute | solution.py:168

commit v24 on v23

--- a/solution.py
+++ b/solution.py
@@ -106,10 +106,10 @@
         probes = cols[place][pl.ds(shard, vectors), :].astype(jnp.float32)
         sums["back", place] = sums["back", place] + noise[place][...] * probes
     for ref, name in zip(rest, sorted(sums)):
-        ref[...] = sums[name]
-
-
-def tile(rows, cols, order, pairs, sums, shard, vectors, noise=(), work=1.0):
+        ref[...] = sums[name].astype(ref.dtype)
+
+
+def tile(rows, cols, order, pairs, sums, shard, vectors, noise=(), work=1.0, sent=()):
     blocks = [*rows, *[(col,) for col in cols]]
     args = [*[part for place in order for part in blocks[place]], *noise, *sums.values()]
     elements = len(pairs) * shard * shard
@@ -120,7 +120,9 @@
         functools.partial(
             tile_kernel, list(order), tuple(pairs), tuple(sums), (tuple(map(len, rows)), len(cols), len(noise)), shard, vectors
         ),
-        out_shape=[jax.ShapeDtypeStruct((vectors, shard), jnp.float32)] * len(names),
+        out_shape=[
+            jax.ShapeDtypeStruct((vectors, shard), jnp.bfloat16 if name in sent else jnp.float32) for name in names
+        ],
         in_specs=[whole] * len(args),
         out_specs=[whole] * len(names),
         compiler_params=pltpu.CompilerParams(vmem_limit_bytes=32 * 1024 * 1024),
@@ -186,7 +188,9 @@
     for rows in (far, near_by):
         pairs = [(place, col, ("rows",)) for col in range(len(others)) for place in range(len(rows))]
         known = {("rows", place): sums[("rows", row)] for place, row in enumerate(rows)}
-        found = tile([blocks[row] for row in rows], others, range(len(rows) + len(others)), pairs, known, shard, vectors)
+        sent = [("rows", place) for place, row in enumerate(rows) if row]
+        order = range(len(rows) + len(others))
+        found = tile([blocks[row] for row in rows], others, order, pairs, known, shard, vectors, sent=sent)
         sums.update({("rows", row): found[("rows", place)] for place, row in enumerate(rows)})
     pairs = [(row, 0, ("back",)) for row in range(inner)]
     own = tile(blocks, [packed], range(inner + 1), pairs, {}, shard, vectors, noise=[noise_level[None, :]])

time: 21.5 us -> 21.3 us (level)
  waiting for transfers between devices: 5.88 us -> 5.66 us
    ppermute x3, waiting for transfers between devices: 5.3 us -> 5.04 us  [along_outer(): lax.ppermute(value, 'blk', [(s * inner + b, t * inner + b) for s, t in ed...]
  transfers between devices with their start and end apart: 10 -> 10, of which waited for: 4 -> 3; matrix products, arithmetic and copies ran while one was open for 0% -> 0% of each run, Pallas kernels for 15% -> 15%
where the time goes in v24:
time: 21.3 us; the launch traced here: 21 us
  starting transfers between devices  10.5 us (49%)
  waiting for transfers between devices  5.66 us (27%)
  Pallas kernels  3.24 us (15%)
  other arithmetic  1.56 us (7%)
    ppermute x7, starting transfers between devices, in_plane(): lax.ppermute(value, 'blk', [(a * inner + s, a * inner + t) for a in range...  5.54 us
    ppermute x3, waiting for transfers between devices, along_outer(): lax.ppermute(value, 'blk', [(s * inner + b, t * inner + b) for s, t in ed...  5.04 us
    ppermute x3, starting transfers between devices, along_outer(): lax.ppermute(value, 'blk', [(s * inner + b, t * inner + b) for s, t in ed...  4.99 us
    pallas_call x4, Pallas kernels, tile(): pl.pallas_call(functools.partial(tile_kernel, list(order), tuple(pairs),...  3.22 us
    concatenate x1, other arithmetic, on_device(): packed = jnp.concatenate([features, probes.T], axis=0)  0.93 us
    transpose x1, other arithmetic, on_device(): return functools.reduce(lambda sofar, term: sofar + term, total).T  0.63 us
    ppermute x7, waiting for transfers between devices, in_plane(): lax.ppermute(value, 'blk', [(a * inner + s, a * inner + t) for a in range...  0.62 us
  transfers between devices with their start and end apart: 10, of which 3 were waited for; matrix products, arithmetic and copies ran while one was open for 0% of the time, Pallas kernels for 15%

profile of v24, /device:TPU:0, one launch (start us, length us, event | category | flops | bytes accessed | tf_op | source)
XLA Modules:
  0.0 21.0 jit_solution(3180207703686896335)
XLA Ops:
  0.0 0.9 %pad_maximum_fusion.refs_0_.refs_5_ = bf16[288,256]{1,0:T(8,128)(2,1)S(1)} fusion(bf16[32,256]{1,0:T(8,128)(2,1)} %bitcast.5, bf16[256,256]{1,0:T(8,128)(2,1)} %param.3), kind=kLoop, calls=%fused_computation | loop fusion | flops 294912 | bytes 294912 | tf_op jit(solution)/shard_map/concatenate | solution.py:164
  0.9 3.0 %collective-permute-start.2 = (bf16[288,256]{1,0:T(8,128)(2,1)S(1)}, bf16[288,256]{1,0:T(8,128)(2,1)S(1)}, u32[]{:S(2)}, u32[]{:S(2)}) collective-permute-start(bf16[288,256]{1,0:T(8,128)(2,1)S(1)} %pad_maximum_fusion.refs_0_.refs_5_), channel_id=1, source_target_pairs={{0,2},{1,3},{2,0},{3,1},{4,6},{5,7},{6,4},{7,5},{8,10},{9,11},{10,... | collective-permute-start | bytes 442376 | tf_op jit(solution)/shard_map/ppermute | solution.py:170
  4.0 3.6 %collective-permute-start.5 = (bf16[288,256]{1,0:T(8,128)(2,1)S(1)}, bf16[288,256]{1,0:T(8,128)(2,1)S(1)}, u32[]{:S(2)}, u32[]{:S(2)}) collective-permute-start(bf16[288,256]{1,0:T(8,128)(2,1)S(1)} %pad_maximum_fusion.refs_0_.refs_5_), channel_id=1, source_target_pairs={{12,4},{13,5},{14,6},{15,7},{4,8},{5,9},{6,10},{7,11},{8,0},{9,1},... | collective-permute-start | bytes 442376 | tf_op jit(solution)/shard_map/ppermute | solution.py:167
  7.6 0.0 collective-permute-start
  7.6 0.0 collective-permute-start.1
  7.6 0.2 %collective-permute-done.2.from_ref.refs_5_.refs_2_.refs_0_ = bf16[288,256]{1,0:T(8,128)(2,1)S(1)} collective-permute-done((bf16[288,256]{1,0:T(8,128)(2,1)S(1)}, bf16[288,256]{1,0:T(8,128)(2,1)S(1)}, u32[]{:S(2)}, u32[]{:S(2)}) %collective-permute-start.2) | collective-permute-done | bytes 147488 | tf_op jit(solution)/shard_map/ppermute | solution.py:170
  7.8 0.3 %collective-permute-start.3 = (bf16[144,256]{1,0:T(8,128)(2,1)S(1)}, bf16[144,256]{1,0:T(8,128)(2,1)S(1)}, u32[]{:S(2)}, u32[]{:S(2)}) collective-permute-start(bf16[144,256]{1,0:T(8,128)(2,1)S(1)} %get-tuple-element.16), channel_id=1, source_target_pairs={{0,1},{1,0},{2,3},{3,2},{4,5},{5,4},{6,7},{7,6},{8,9},{9,8},{10,11... | collective-permute-start | bytes 221192 | tf_op jit(solution)/shard_map/ppermute | solution.py:170
  8.2 0.2 %collective-permute-start.4 = (bf16[144,256]{1,0:T(8,128)(2,1)S(1)}, bf16[144,256]{1,0:T(8,128)(2,1)S(1)}, u32[]{:S(2)}, u32[]{:S(2)}) collective-permute-start(bf16[144,256]{1,0:T(8,128)(2,1)S(1)} %get-tuple-element.17), channel_id=1, source_target_pairs={{0,1},{1,0},{2,3},{3,2},{4,5},{5,4},{6,7},{7,6},{8,9},{9,8},{10,11... | collective-permute-start | bytes 221192 | tf_op jit(solution)/shard_map/ppermute | solution.py:170
  8.4 5.0 %collective-permute-done.5.refs_3_ = bf16[288,256]{1,0:T(8,128)(2,1)S(1)} collective-permute-done((bf16[288,256]{1,0:T(8,128)(2,1)S(1)}, bf16[288,256]{1,0:T(8,128)(2,1)S(1)}, u32[]{:S(2)}, u32[]{:S(2)}) %collective-permute-start.5) | collective-permute-done | bytes 147488 | tf_op jit(solution)/shard_map/ppermute | solution.py:167
  13.4 0.0 collective-permute-done.refs_4_.refs_1_
  13.5 1.1 %shard_map.38 = (f32[32,256]{1,0:T(8,128)S(1)}, f32[32,256]{1,0:T(8,128)S(1)}, f32[32,256]{1,0:T(8,128)S(1)}, f32[32,256]{1,0:T(8,128)S(1)}, f32[32,256]{1,0:T(8,128)S(1)}) custom-call(bf16[288,256]{1,0:T(8,128)(2,1)S(1)} %pad_maximum_fusion.refs_0_.refs_5_, bf16[144,256]{1,0:T(8,128)(2,1)S(1)} %collective-permute-done.3.refs_1_.refs_3_, ...), custom_call_target="tpu_custom_call" | custom-call | tf_op jit(solution)/shard_map/pallas_call | solution.py:119
  14.6 1.4 %collective-permute-start.9 = (f32[32,256]{1,0:T(8,128)S(1)}, f32[32,256]{1,0:T(8,128)S(1)}, u32[]{:S(2)}, u32[]{:S(2)}) collective-permute-start(f32[32,256]{1,0:T(8,128)S(1)} %get-tuple-element.26), channel_id=1, source_target_pairs={{4,12},{5,13},{6,14},{7,15},{8,4},{9,5},{10,6},{11,7},{0,8},{1,9},... | collective-permute-start | bytes 98312 | tf_op jit(solution)/shard_map/ppermute | solution.py:167
  15.9 0.0 collective-permute-done.1.refs_2_.refs_3_
  15.9 0.6 %shard_map.41 = (bf16[32,256]{1,0:T(8,128)(2,1)S(1)}, bf16[32,256]{1,0:T(8,128)(2,1)S(1)}) custom-call(bf16[288,256]{1,0:T(8,128)(2,1)S(1)} %collective-permute-done.2.from_ref.refs_5_.refs_2_.refs_0_, bf16[144,256]{1,0:T(8,128)(2,1)S(1)} %collective-permute-done.3.refs_1_.refs_3_, bf16[144,256]{1,0:T(8,128)(2,1)S(1)} %collective-permute-done.4.refs_2_.refs_4_, ...), custom_call_target="tpu_custom_call" | custom-call | flops 83886080 | bytes 393216 | tf_op jit(solution)/shard_map/pallas_call | solution.py:119
  16.6 0.0 collective-permute-start.8
  16.6 1.1 %collective-permute-start.7 = (bf16[32,256]{1,0:T(8,128)(2,1)S(1)}, bf16[32,256]{1,0:T(8,128)(2,1)S(1)}, u32[]{:S(2)}, u32[]{:S(2)}) collective-permute-start(bf16[32,256]{1,0:T(8,128)(2,1)S(1)} %get-tuple-element.24), channel_id=1, source_target_pairs={{0,2},{1,3},{2,0},{3,1},{4,6},{5,7},{6,4},{7,5},{8,10},{9,11},{10,... | collective-permute-start | bytes 49160 | tf_op jit(solution)/shard_map/ppermute | solution.py:170
  17.7 0.6 %shard_map.39 = (f32[32,256]{1,0:T(8,128)S(1)}, bf16[32,256]{1,0:T(8,128)(2,1)S(1)}) custom-call(bf16[288,256]{1,0:T(8,128)(2,1)S(1)} %pad_maximum_fusion.refs_0_.refs_5_, bf16[288,256]{1,0:T(8,128)(2,1)S(1)} %collective-permute-done.refs_4_.refs_1_, bf16[288,256]{1,0:T(8,128)(2,1)S(1)} %collective-permute-done.1.refs_2_.refs_3_, ...), custom_call_target="tpu_custom_call" | custom-call | flops 83886080 | bytes 393216 | tf_op jit(solution)/shard_map/pallas_call | solution.py:119
  18.3 0.9 %collective-permute-start.6 = (bf16[32,256]{1,0:T(8,128)(2,1)S(1)}, bf16[32,256]{1,0:T(8,128)(2,1)S(1)}, u32[]{:S(2)}, u32[]{:S(2)}) collective-permute-start(bf16[32,256]{1,0:T(8,128)(2,1)S(1)} %get-tuple-element.21), channel_id=1, source_target_pairs={{0,1},{1,0},{2,3},{3,2},{4,5},{5,4},{6,7},{7,6},{8,9},{9,8},{10,11... | collective-permute-start | bytes 49160 | tf_op jit(solution)/shard_map/ppermute | solution.py:170
  19.1 0.9 %shard_map.40 = f32[32,256]{1,0:T(8,128)S(1)} custom-call(bf16[288,256]{1,0:T(8,128)(2,1)S(1)} %pad_maximum_fusion.refs_0_.refs_5_, bf16[288,256]{1,0:T(8,128)(2,1)S(1)} %collective-permute-done.refs_4_.refs_1_, bf16[288,256]{1,0:T(8,128)(2,1)S(1)} %collective-permute-done.2.from_ref.refs_5_.refs_2_.refs_0_, ...), custom_call_target="tpu_custom_call" | custom-call | flops 167772160 | bytes 655360 | tf_op jit(solution)/shard_map/pallas_call | solution.py:119
  20.0 0.0 collective-permute-done.8
  20.0 0.4 %collective-permute-done.7 = bf16[32,256]{1,0:T(8,128)(2,1)S(1)} collective-permute-done((bf16[32,256]{1,0:T(8,128)(2,1)S(1)}, bf16[32,256]{1,0:T(8,128)(2,1)S(1)}, u32[]{:S(2)}, u32[]{:S(2)}) %collective-permute-start.7) | collective-permute-done | bytes 16416 | tf_op jit(solution)/shard_map/ppermute | solution.py:170
  20.4 0.0 collective-permute-done.6
  20.4 0.0 collective-permute-done.9
  20.4 0.6 %add_bitcast_fusion = f32[256,32]{0,1:T(8,128)} fusion(f32[32,256]{1,0:T(8,128)S(1)} %collective-permute-done.9, bf16[32,256]{1,0:T(8,128)(2,1)S(1)} %collective-permute-done.8, bf16[32,256]{1,0:T(8,128)(2,1)S(1)} %collective-permute-done.7, bf16[32,256]{1,0:T(8,128)(2,1)S(1)} %collective-permute-done.6, f32[32,256]{1,0:T(8,128)S(1)} %get-tuple-element.20, ...), kind=kLoop, calls=%fused_computation.1 | loop fusion | flops 65536 | bytes 180224 | tf_op jit(solution)/shard_map/transpose | solution.py:201
  (5 shorter events, 0.0 us)
Async XLA Ops:
  0.9 6.9 %collective-permute-start.2 = (bf16[288,256]{1,0:T(8,128)(2,1)S(1)}, bf16[288,256]{1,0:T(8,128)(2,1)S(1)}, u32[]{:S(2)}, u32[]{:S(2)}) collective-permute-start(bf16[288,256]{1,0:T(8,128)(2,1)S(1)} %pad_maximum_fusion.refs_0_.refs_5_), channel_id=1, source_target_pairs={{0,2},{1,3},{2,0},{3,1},{4,6},{5,7},{6,4},{7,5},{8,10},{9,11},{10,... | collective-permute-start | bytes 442376 | tf_op jit(solution)/shard_map/ppermute | solution.py:170
  4.0 9.5 %collective-permute-start.5 = (bf16[288,256]{1,0:T(8,128)(2,1)S(1)}, bf16[288,256]{1,0:T(8,128)(2,1)S(1)}, u32[]{:S(2)}, u32[]{:S(2)}) collective-permute-start(bf16[288,256]{1,0:T(8,128)(2,1)S(1)} %pad_maximum_fusion.refs_0_.refs_5_), channel_id=1, source_target_pairs={{12,4},{13,5},{14,6},{15,7},{4,8},{5,9},{6,10},{7,11},{8,0},{9,1},... | collective-permute-start | bytes 442376 | tf_op jit(solution)/shard_map/ppermute | solution.py:167
  7.6 5.9 %collective-permute-start = (bf16[288,256]{1,0:T(8,128)(2,1)S(1)}, bf16[288,256]{1,0:T(8,128)(2,1)S(1)}, u32[]{:S(2)}, u32[]{:S(2)}) collective-permute-start(bf16[288,256]{1,0:T(8,128)(2,1)S(1)} %pad_maximum_fusion.refs_0_.refs_5_), channel_id=1, source_target_pairs={{0,1},{1,0},{2,3},{3,2},{4,5},{5,4},{6,7},{7,6},{8,9},{9,8},{10,11... | collective-permute-start | bytes 442376 | tf_op jit(solution)/shard_map/ppermute | solution.py:170
  7.6 8.4 %collective-permute-start.1 = (bf16[288,256]{1,0:T(8,128)(2,1)S(1)}, bf16[288,256]{1,0:T(8,128)(2,1)S(1)}, u32[]{:S(2)}, u32[]{:S(2)}) collective-permute-start(bf16[288,256]{1,0:T(8,128)(2,1)S(1)} %pad_maximum_fusion.refs_0_.refs_5_), channel_id=1, source_target_pairs={{12,8},{13,9},{14,10},{15,11},{4,0},{5,1},{6,2},{7,3},{8,12},{9,13... | collective-permute-start | bytes 442376 | tf_op jit(solution)/shard_map/ppermute | solution.py:167
  7.8 5.6 %collective-permute-start.3 = (bf16[144,256]{1,0:T(8,128)(2,1)S(1)}, bf16[144,256]{1,0:T(8,128)(2,1)S(1)}, u32[]{:S(2)}, u32[]{:S(2)}) collective-permute-start(bf16[144,256]{1,0:T(8,128)(2,1)S(1)} %get-tuple-element.16), channel_id=1, source_target_pairs={{0,1},{1,0},{2,3},{3,2},{4,5},{5,4},{6,7},{7,6},{8,9},{9,8},{10,11... | collective-permute-start | bytes 221192 | tf_op jit(solution)/shard_map/ppermute | solution.py:170
  8.2 5.3 %collective-permute-start.4 = (bf16[144,256]{1,0:T(8,128)(2,1)S(1)}, bf16[144,256]{1,0:T(8,128)(2,1)S(1)}, u32[]{:S(2)}, u32[]{:S(2)}) collective-permute-start(bf16[144,256]{1,0:T(8,128)(2,1)S(1)} %get-tuple-element.17), channel_id=1, source_target_pairs={{0,1},{1,0},{2,3},{3,2},{4,5},{5,4},{6,7},{7,6},{8,9},{9,8},{10,11... | collective-permute-start | bytes 221192 | tf_op jit(solution)/shard_map/ppermute | solution.py:170
  14.6 5.8 %collective-permute-start.9 = (f32[32,256]{1,0:T(8,128)S(1)}, f32[32,256]{1,0:T(8,128)S(1)}, u32[]{:S(2)}, u32[]{:S(2)}) collective-permute-start(f32[32,256]{1,0:T(8,128)S(1)} %get-tuple-element.26), channel_id=1, source_target_pairs={{4,12},{5,13},{6,14},{7,15},{8,4},{9,5},{10,6},{11,7},{0,8},{1,9},... | collective-permute-start | bytes 98312 | tf_op jit(solution)/shard_map/ppermute | solution.py:167
  16.6 3.5 %collective-permute-start.8 = (bf16[32,256]{1,0:T(8,128)(2,1)S(1)}, bf16[32,256]{1,0:T(8,128)(2,1)S(1)}, u32[]{:S(2)}, u32[]{:S(2)}) collective-permute-start(bf16[32,256]{1,0:T(8,128)(2,1)S(1)} %get-tuple-element.25), channel_id=1, source_target_pairs={{0,3},{1,2},{2,1},{3,0},{4,7},{5,6},{6,5},{7,4},{8,11},{9,10},{10,... | collective-permute-start | bytes 49160 | tf_op jit(solution)/shard_map/ppermute | solution.py:170
  16.6 3.8 %collective-permute-start.7 = (bf16[32,256]{1,0:T(8,128)(2,1)S(1)}, bf16[32,256]{1,0:T(8,128)(2,1)S(1)}, u32[]{:S(2)}, u32[]{:S(2)}) collective-permute-start(bf16[32,256]{1,0:T(8,128)(2,1)S(1)} %get-tuple-element.24), channel_id=1, source_target_pairs={{0,2},{1,3},{2,0},{3,1},{4,6},{5,7},{6,4},{7,5},{8,10},{9,11},{10,... | collective-permute-start | bytes 49160 | tf_op jit(solution)/shard_map/ppermute | solution.py:170
  18.3 0.9 %copy-start = (f32[256]{0:T(256)S(1)}, f32[256]{0:T(256)}, u32[]{:S(2)}) copy-start(f32[256]{0:T(256)} %param.5) | copy-start | bytes 3076
  18.3 2.1 %collective-permute-start.6 = (bf16[32,256]{1,0:T(8,128)(2,1)S(1)}, bf16[32,256]{1,0:T(8,128)(2,1)S(1)}, u32[]{:S(2)}, u32[]{:S(2)}) collective-permute-start(bf16[32,256]{1,0:T(8,128)(2,1)S(1)} %get-tuple-element.21), channel_id=1, source_target_pairs={{0,1},{1,0},{2,3},{3,2},{4,5},{5,4},{6,7},{7,6},{8,9},{9,8},{10,11... | collective-permute-start | bytes 49160 | tf_op jit(solution)/shard_map/ppermute | solution.py:170

commit v25 on v24

--- a/solution.py
+++ b/solution.py
@@ -135,6 +135,60 @@
     return dict(zip(names, found))
 
 
+def features_of(rows):
+    left = jnp.concatenate([row[0] for row in rows])
+    wide = left.astype(jnp.float32)
+    return left, jnp.sum(wide * wide, axis=1, keepdims=True)
+
+
+def kernel_of(left, squares, col):
+    scaled = col * jnp.asarray(-2.0, col.dtype)
+    cross = lax.dot_general(left, scaled, ROWS_BY_ROWS, preferred_element_type=jnp.float32)
+    return matern((squares + lane_squares(col)) + cross)
+
+
+def cycle_kernel(order, parts, cols_in, shard, vectors, *refs):
+    rest = list(refs)
+    blocks = {place: [rest.pop(0) for _ in range((*parts, *[1] * cols_in)[place])] for place in order}
+    rows = [joined(blocks[place], shard, vectors) for place in range(len(parts))]
+    left, squares = features_of(rows)
+    probes = jnp.concatenate([row[1] for row in rows], axis=1)
+    for col in range(cols_in):
+        kernel = kernel_of(left, squares, blocks[len(parts) + col][0][0:shard, :])
+        rest[col][...] = jnp.dot(probes, kernel, preferred_element_type=jnp.float32)
+        rest[cols_in + col][...] = kernel
+
+
+def rows_kernel(parts, start, known, fresh, shard, vectors, *refs):
+    rest = list(refs)
+    rows = [joined([rest.pop(0) for _ in range(count)], shard, vectors) for count in parts]
+    cols, kernels, known_cols = ([rest.pop(0) for _ in range(n)] for n in (fresh, known, known))
+    left, squares = features_of(rows)
+    total = jnp.zeros((vectors, len(parts) * shard), jnp.float32)
+    for kernel, col in zip(kernels, known_cols):
+        some = kernel[start * shard : (start + len(parts)) * shard, :]
+        probes = col[pl.ds(shard, vectors), :]
+        total += lax.dot_general(probes, some, ROWS_BY_ROWS, preferred_element_type=jnp.float32)
+    for col in cols:
+        kernel = kernel_of(left, squares, col[0:shard, :])
+        probes = col[pl.ds(shard, vectors), :]
+        total += lax.dot_general(probes, kernel, ROWS_BY_ROWS, preferred_element_type=jnp.float32)
+    for place, ref in enumerate(rest):
+        ref[...] = total[:, place * shard : (place + 1) * shard].astype(ref.dtype)
+
+
+def call(body, args, outs, work):
+    whole = pl.BlockSpec(memory_space=pltpu.VMEM)
+    return pl.pallas_call(
+        body,
+        out_shape=outs,
+        in_specs=[whole] * len(args),
+        out_specs=[whole] * len(outs),
+        compiler_params=pltpu.CompilerParams(vmem_limit_bytes=32 * 1024 * 1024),
+        cost_estimate=pl.CostEstimate(flops=2 * work, bytes_accessed=0, transcendentals=0),
+    )(*args)
+
+
 def halve_kernel(shard, vectors, from_ref, *halves):
     points, some = shard // 2, vectors // 2
     for place, half in enumerate(halves):
@@ -180,18 +234,29 @@
     passed = [step for step in range(1, inner) if step & (step - 1)]
 
     order = [0] + passed + [inner + place for place in range(len(cols))] + direct
-    pairs = [(row, col, ("rows", "back")) for col in range(len(cols)) for row in range(inner)]
-    sums = tile(blocks, cols, order, pairs, {}, shard, vectors, work=0.0)
-    backs = [sums.pop(("back", place)) for place in range(len(cols))]
+    parts = tuple(map(len, blocks))
+    operands = [*blocks, *[(col,) for col in cols]]
+    flat = jax.ShapeDtypeStruct((vectors, shard), jnp.float32)
+    sent = jax.ShapeDtypeStruct((vectors, shard), jnp.bfloat16)
+    matrix = jax.ShapeDtypeStruct((inner * shard, shard), jnp.bfloat16)
+    found = call(
+        functools.partial(cycle_kernel, order, parts, len(cols), shard, vectors),
+        [part for place in order for part in operands[place]],
+        [flat] * len(cols) + [matrix] * len(cols),
+        0,
+    )
+    backs, kernels = found[: len(cols)], found[len(cols) :]
     half = inner // 2
-    far, near_by = list(range(half, inner)), list(range(half))
-    for rows in (far, near_by):
-        pairs = [(place, col, ("rows",)) for col in range(len(others)) for place in range(len(rows))]
-        known = {("rows", place): sums[("rows", row)] for place, row in enumerate(rows)}
-        sent = [("rows", place) for place, row in enumerate(rows) if row]
-        order = range(len(rows) + len(others))
-        found = tile([blocks[row] for row in rows], others, order, pairs, known, shard, vectors, sent=sent)
-        sums.update({("rows", row): found[("rows", place)] for place, row in enumerate(rows)})
+    sums = {}
+    for start, stop in ((half, inner), (0, half)):
+        some = blocks[start:stop]
+        found = call(
+            functools.partial(rows_kernel, parts[start:stop], start, len(cols), len(others), shard, vectors),
+            [*[part for block in some for part in block], *others, *kernels, *cols],
+            [sent if row else flat for row in range(start, stop)],
+            len(some) * len(others) * shard * shard * features.shape[1],
+        )
+        sums.update({("rows", start + place): value for place, value in enumerate(found)})
     pairs = [(row, 0, ("back",)) for row in range(inner)]
     own = tile(blocks, [packed], range(inner + 1), pairs, {}, shard, vectors, noise=[noise_level[None, :]])
 

time: 21.3 us -> 21.2 us (level)
  starting transfers between devices: 10.5 us -> 10.8 us
  waiting for transfers between devices: 5.66 us -> 5.36 us
    pallas_call x4 -> x1, Pallas kernels: 3.22 us -> 0.88 us  [tile(): pl.pallas_call(functools.partial(tile_kernel, list(order), tuple(pairs),...]
    pallas_call x0 -> x3, Pallas kernels: none -> 2.17 us  [call(): pl.pallas_call(body, out_shape=outs, in_specs=[whole] * len(args), out_sp...]
    ppermute x7, starting transfers between devices: 5.54 us -> 5.86 us  [in_plane(): lax.ppermute(value, 'blk', [(a * inner + s, a * inner + t) for a in range...]
    ppermute x7, waiting for transfers between devices: 0.62 us -> 0.32 us  [in_plane(): lax.ppermute(value, 'blk', [(a * inner + s, a * inner + t) for a in range...]
where the time goes in v25:
time: 21.2 us; the launch traced here: 20.9 us
  starting transfers between devices  10.8 us (51%)
  waiting for transfers between devices  5.36 us (25%)
  Pallas kernels  3.06 us (14%)
  other arithmetic  1.56 us (7%)
    ppermute x7, starting transfers between devices, in_plane(): lax.ppermute(value, 'blk', [(a * inner + s, a * inner + t) for a in range...  5.86 us
    ppermute x3, waiting for transfers between devices, along_outer(): lax.ppermute(value, 'blk', [(s * inner + b, t * inner + b) for s, t in ed...  5.04 us
    ppermute x3, starting transfers between devices, along_outer(): lax.ppermute(value, 'blk', [(s * inner + b, t * inner + b) for s, t in ed...  4.98 us
    pallas_call x3, Pallas kernels, call(): pl.pallas_call(body, out_shape=outs, in_specs=[whole] * len(args), out_sp...  2.17 us
    concatenate x1, other arithmetic, on_device(): packed = jnp.concatenate([features, probes.T], axis=0)  0.93 us
    pallas_call x1, Pallas kernels, tile(): pl.pallas_call(functools.partial(tile_kernel, list(order), tuple(pairs),...  0.88 us
    transpose x1, other arithmetic, on_device(): return functools.reduce(lambda sofar, term: sofar + term, total).T  0.63 us
  transfers between devices with their start and end apart: 10, of which 3 were waited for; matrix products, arithmetic and copies ran while one was open for 0% of the time, Pallas kernels for 15%

profile of v25, /device:TPU:0, one launch (start us, length us, event | category | flops | bytes accessed | tf_op | source)
XLA Modules:
  0.0 20.9 jit_solution(5442415376816269108)
XLA Ops:
  0.0 0.9 %pad_maximum_fusion.refs_0_.refs_5_ = bf16[288,256]{1,0:T(8,128)(2,1)S(1)} fusion(bf16[32,256]{1,0:T(8,128)(2,1)} %bitcast.5, bf16[256,256]{1,0:T(8,128)(2,1)} %param.3), kind=kLoop, calls=%fused_computation | loop fusion | flops 294912 | bytes 294912 | tf_op jit(solution)/shard_map/concatenate | solution.py:218
  0.9 3.0 %collective-permute-start.2 = (bf16[288,256]{1,0:T(8,128)(2,1)S(1)}, bf16[288,256]{1,0:T(8,128)(2,1)S(1)}, u32[]{:S(2)}, u32[]{:S(2)}) collective-permute-start(bf16[288,256]{1,0:T(8,128)(2,1)S(1)} %pad_maximum_fusion.refs_0_.refs_5_), channel_id=1, source_target_pairs={{0,2},{1,3},{2,0},{3,1},{4,6},{5,7},{6,4},{7,5},{8,10},{9,11},{10,... | collective-permute-start | bytes 442376 | tf_op jit(solution)/shard_map/ppermute | solution.py:224
  4.0 3.6 %collective-permute-start.5 = (bf16[288,256]{1,0:T(8,128)(2,1)S(1)}, bf16[288,256]{1,0:T(8,128)(2,1)S(1)}, u32[]{:S(2)}, u32[]{:S(2)}) collective-permute-start(bf16[288,256]{1,0:T(8,128)(2,1)S(1)} %pad_maximum_fusion.refs_0_.refs_5_), channel_id=1, source_target_pairs={{12,4},{13,5},{14,6},{15,7},{4,8},{5,9},{6,10},{7,11},{8,0},{9,1},... | collective-permute-start | bytes 442376 | tf_op jit(solution)/shard_map/ppermute | solution.py:221
  7.6 0.0 collective-permute-start
  7.6 0.0 collective-permute-start.1
  7.6 0.2 %collective-permute-done.2.from_ref.refs_5_.refs_2_.refs_0_ = bf16[288,256]{1,0:T(8,128)(2,1)S(1)} collective-permute-done((bf16[288,256]{1,0:T(8,128)(2,1)S(1)}, bf16[288,256]{1,0:T(8,128)(2,1)S(1)}, u32[]{:S(2)}, u32[]{:S(2)}) %collective-permute-start.2) | collective-permute-done | bytes 147488 | tf_op jit(solution)/shard_map/ppermute | solution.py:224
  7.8 0.3 %collective-permute-start.3 = (bf16[144,256]{1,0:T(8,128)(2,1)S(1)}, bf16[144,256]{1,0:T(8,128)(2,1)S(1)}, u32[]{:S(2)}, u32[]{:S(2)}) collective-permute-start(bf16[144,256]{1,0:T(8,128)(2,1)S(1)} %get-tuple-element.13), channel_id=1, source_target_pairs={{0,1},{1,0},{2,3},{3,2},{4,5},{5,4},{6,7},{7,6},{8,9},{9,8},{10,11... | collective-permute-start | bytes 221192 | tf_op jit(solution)/shard_map/ppermute | solution.py:224
  8.2 0.2 %collective-permute-start.4 = (bf16[144,256]{1,0:T(8,128)(2,1)S(1)}, bf16[144,256]{1,0:T(8,128)(2,1)S(1)}, u32[]{:S(2)}, u32[]{:S(2)}) collective-permute-start(bf16[144,256]{1,0:T(8,128)(2,1)S(1)} %get-tuple-element.14), channel_id=1, source_target_pairs={{0,1},{1,0},{2,3},{3,2},{4,5},{5,4},{6,7},{7,6},{8,9},{9,8},{10,11... | collective-permute-start | bytes 221192 | tf_op jit(solution)/shard_map/ppermute | solution.py:224
  8.4 5.0 %collective-permute-done.5.refs_3_.refs_4_.refs_5_ = bf16[288,256]{1,0:T(8,128)(2,1)S(1)} collective-permute-done((bf16[288,256]{1,0:T(8,128)(2,1)S(1)}, bf16[288,256]{1,0:T(8,128)(2,1)S(1)}, u32[]{:S(2)}, u32[]{:S(2)}) %collective-permute-start.5) | collective-permute-done | bytes 147488 | tf_op jit(solution)/shard_map/ppermute | solution.py:221
  13.4 0.0 collective-permute-done.refs_4_.refs_1_
  13.4 0.0 collective-permute-done.3.refs_1_.refs_3_
  13.4 0.0 collective-permute-done.4.refs_2_.refs_4_
  13.5 0.8 %shard_map.38 = (f32[32,256]{1,0:T(8,128)S(1)}, bf16[1024,256]{1,0:T(8,128)(2,1)S(1)}) custom-call(bf16[288,256]{1,0:T(8,128)(2,1)S(1)} %pad_maximum_fusion.refs_0_.refs_5_, bf16[144,256]{1,0:T(8,128)(2,1)S(1)} %collective-permute-done.3.refs_1_.refs_3_, bf16[144,256]{1,0:T(8,128)(2,1)S(1)} %collective-permute-done.4.refs_2_.refs_4_, ...), custom_call_target="tpu_custom_call" | custom-call | tf_op jit(solution)/shard_map/pallas_call | solution.py:182
  14.3 1.4 %collective-permute-start.9 = (f32[32,256]{1,0:T(8,128)S(1)}, f32[32,256]{1,0:T(8,128)S(1)}, u32[]{:S(2)}, u32[]{:S(2)}) collective-permute-start(f32[32,256]{1,0:T(8,128)S(1)} %get-tuple-element.20), channel_id=1, source_target_pairs={{4,12},{5,13},{6,14},{7,15},{8,4},{9,5},{10,6},{11,7},{0,8},{1,9},... | collective-permute-start | bytes 98312 | tf_op jit(solution)/shard_map/ppermute | solution.py:221
  15.6 0.0 collective-permute-done.1.refs_2_.refs_3_
  15.6 0.7 %shard_map.41 = (bf16[32,256]{1,0:T(8,128)(2,1)S(1)}, bf16[32,256]{1,0:T(8,128)(2,1)S(1)}) custom-call(bf16[288,256]{1,0:T(8,128)(2,1)S(1)} %collective-permute-done.2.from_ref.refs_5_.refs_2_.refs_0_, bf16[144,256]{1,0:T(8,128)(2,1)S(1)} %collective-permute-done.3.refs_1_.refs_3_, bf16[144,256]{1,0:T(8,128)(2,1)S(1)} %collective-permute-done.4.refs_2_.refs_4_, ...), custom_call_target="tpu_custom_call" | custom-call | flops 67108864 | tf_op jit(solution)/shard_map/pallas_call | solution.py:182
  16.3 0.5 %collective-permute-start.7 = (bf16[32,256]{1,0:T(8,128)(2,1)S(1)}, bf16[32,256]{1,0:T(8,128)(2,1)S(1)}, u32[]{:S(2)}, u32[]{:S(2)}) collective-permute-start(bf16[32,256]{1,0:T(8,128)(2,1)S(1)} %get-tuple-element.18), channel_id=1, source_target_pairs={{0,2},{1,3},{2,0},{3,1},{4,6},{5,7},{6,4},{7,5},{8,10},{9,11},{10,... | collective-permute-start | bytes 49160 | tf_op jit(solution)/shard_map/ppermute | solution.py:224
  16.9 0.6 %collective-permute-start.8 = (bf16[32,256]{1,0:T(8,128)(2,1)S(1)}, bf16[32,256]{1,0:T(8,128)(2,1)S(1)}, u32[]{:S(2)}, u32[]{:S(2)}) collective-permute-start(bf16[32,256]{1,0:T(8,128)(2,1)S(1)} %get-tuple-element.19), channel_id=1, source_target_pairs={{0,3},{1,2},{2,1},{3,0},{4,7},{5,6},{6,5},{7,4},{8,11},{9,10},{10,... | collective-permute-start | bytes 49160 | tf_op jit(solution)/shard_map/ppermute | solution.py:224
  17.5 0.7 %shard_map.39 = (f32[32,256]{1,0:T(8,128)S(1)}, bf16[32,256]{1,0:T(8,128)(2,1)S(1)}) custom-call(bf16[288,256]{1,0:T(8,128)(2,1)S(1)} %pad_maximum_fusion.refs_0_.refs_5_, bf16[288,256]{1,0:T(8,128)(2,1)S(1)} %collective-permute-done.refs_4_.refs_1_, bf16[288,256]{1,0:T(8,128)(2,1)S(1)} %collective-permute-done.1.refs_2_.refs_3_, ...), custom_call_target="tpu_custom_call" | custom-call | flops 67108864 | tf_op jit(solution)/shard_map/pallas_call | solution.py:182
  18.1 1.1 %collective-permute-start.6 = (bf16[32,256]{1,0:T(8,128)(2,1)S(1)}, bf16[32,256]{1,0:T(8,128)(2,1)S(1)}, u32[]{:S(2)}, u32[]{:S(2)}) collective-permute-start(bf16[32,256]{1,0:T(8,128)(2,1)S(1)} %get-tuple-element.17), channel_id=1, source_target_pairs={{0,1},{1,0},{2,3},{3,2},{4,5},{5,4},{6,7},{7,6},{8,9},{9,8},{10,11... | collective-permute-start | bytes 49160 | tf_op jit(solution)/shard_map/ppermute | solution.py:224
  19.3 0.9 %shard_map.40 = f32[32,256]{1,0:T(8,128)S(1)} custom-call(bf16[288,256]{1,0:T(8,128)(2,1)S(1)} %pad_maximum_fusion.refs_0_.refs_5_, bf16[288,256]{1,0:T(8,128)(2,1)S(1)} %collective-permute-done.refs_4_.refs_1_, bf16[288,256]{1,0:T(8,128)(2,1)S(1)} %collective-permute-done.2.from_ref.refs_5_.refs_2_.refs_0_, ...), custom_call_target="tpu_custom_call" | custom-call | flops 167772160 | bytes 655360 | tf_op jit(solution)/shard_map/pallas_call | solution.py:119
  20.1 0.1 collective-permute-done.7
  20.2 0.0 collective-permute-done.8
  20.2 0.6 %add_bitcast_fusion = f32[256,32]{0,1:T(8,128)} fusion(f32[32,256]{1,0:T(8,128)S(1)} %collective-permute-done.9, bf16[32,256]{1,0:T(8,128)(2,1)S(1)} %collective-permute-done.8, bf16[32,256]{1,0:T(8,128)(2,1)S(1)} %collective-permute-done.7, bf16[32,256]{1,0:T(8,128)(2,1)S(1)} %collective-permute-done.6, f32[32,256]{1,0:T(8,128)S(1)} %get-tuple-element.16, ...), kind=kLoop, calls=%fused_computation.1 | loop fusion | flops 65536 | bytes 180224 | tf_op jit(solution)/shard_map/transpose | solution.py:266
  (5 shorter events, 0.0 us)
Async XLA Ops:
  0.9 6.9 %collective-permute-start.2 = (bf16[288,256]{1,0:T(8,128)(2,1)S(1)}, bf16[288,256]{1,0:T(8,128)(2,1)S(1)}, u32[]{:S(2)}, u32[]{:S(2)}) collective-permute-start(bf16[288,256]{1,0:T(8,128)(2,1)S(1)} %pad_maximum_fusion.refs_0_.refs_5_), channel_id=1, source_target_pairs={{0,2},{1,3},{2,0},{3,1},{4,6},{5,7},{6,4},{7,5},{8,10},{9,11},{10,... | collective-permute-start | bytes 442376 | tf_op jit(solution)/shard_map/ppermute | solution.py:224
  4.0 9.5 %collective-permute-start.5 = (bf16[288,256]{1,0:T(8,128)(2,1)S(1)}, bf16[288,256]{1,0:T(8,128)(2,1)S(1)}, u32[]{:S(2)}, u32[]{:S(2)}) collective-permute-start(bf16[288,256]{1,0:T(8,128)(2,1)S(1)} %pad_maximum_fusion.refs_0_.refs_5_), channel_id=1, source_target_pairs={{12,4},{13,5},{14,6},{15,7},{4,8},{5,9},{6,10},{7,11},{8,0},{9,1},... | collective-permute-start | bytes 442376 | tf_op jit(solution)/shard_map/ppermute | solution.py:221
  7.6 5.9 %collective-permute-start = (bf16[288,256]{1,0:T(8,128)(2,1)S(1)}, bf16[288,256]{1,0:T(8,128)(2,1)S(1)}, u32[]{:S(2)}, u32[]{:S(2)}) collective-permute-start(bf16[288,256]{1,0:T(8,128)(2,1)S(1)} %pad_maximum_fusion.refs_0_.refs_5_), channel_id=1, source_target_pairs={{0,1},{1,0},{2,3},{3,2},{4,5},{5,4},{6,7},{7,6},{8,9},{9,8},{10,11... | collective-permute-start | bytes 442376 | tf_op jit(solution)/shard_map/ppermute | solution.py:224
  7.6 8.1 %collective-permute-start.1 = (bf16[288,256]{1,0:T(8,128)(2,1)S(1)}, bf16[288,256]{1,0:T(8,128)(2,1)S(1)}, u32[]{:S(2)}, u32[]{:S(2)}) collective-permute-start(bf16[288,256]{1,0:T(8,128)(2,1)S(1)} %pad_maximum_fusion.refs_0_.refs_5_), channel_id=1, source_target_pairs={{12,8},{13,9},{14,10},{15,11},{4,0},{5,1},{6,2},{7,3},{8,12},{9,13... | collective-permute-start | bytes 442376 | tf_op jit(solution)/shard_map/ppermute | solution.py:221
  7.8 5.6 %collective-permute-start.3 = (bf16[144,256]{1,0:T(8,128)(2,1)S(1)}, bf16[144,256]{1,0:T(8,128)(2,1)S(1)}, u32[]{:S(2)}, u32[]{:S(2)}) collective-permute-start(bf16[144,256]{1,0:T(8,128)(2,1)S(1)} %get-tuple-element.13), channel_id=1, source_target_pairs={{0,1},{1,0},{2,3},{3,2},{4,5},{5,4},{6,7},{7,6},{8,9},{9,8},{10,11... | collective-permute-start | bytes 221192 | tf_op jit(solution)/shard_map/ppermute | solution.py:224
  8.2 5.3 %collective-permute-start.4 = (bf16[144,256]{1,0:T(8,128)(2,1)S(1)}, bf16[144,256]{1,0:T(8,128)(2,1)S(1)}, u32[]{:S(2)}, u32[]{:S(2)}) collective-permute-start(bf16[144,256]{1,0:T(8,128)(2,1)S(1)} %get-tuple-element.14), channel_id=1, source_target_pairs={{0,1},{1,0},{2,3},{3,2},{4,5},{5,4},{6,7},{7,6},{8,9},{9,8},{10,11... | collective-permute-start | bytes 221192 | tf_op jit(solution)/shard_map/ppermute | solution.py:224
  14.3 6.0 %collective-permute-start.9 = (f32[32,256]{1,0:T(8,128)S(1)}, f32[32,256]{1,0:T(8,128)S(1)}, u32[]{:S(2)}, u32[]{:S(2)}) collective-permute-start(f32[32,256]{1,0:T(8,128)S(1)} %get-tuple-element.20), channel_id=1, source_target_pairs={{4,12},{5,13},{6,14},{7,15},{8,4},{9,5},{10,6},{11,7},{0,8},{1,9},... | collective-permute-start | bytes 98312 | tf_op jit(solution)/shard_map/ppermute | solution.py:221
  16.3 3.9 %collective-permute-start.7 = (bf16[32,256]{1,0:T(8,128)(2,1)S(1)}, bf16[32,256]{1,0:T(8,128)(2,1)S(1)}, u32[]{:S(2)}, u32[]{:S(2)}) collective-permute-start(bf16[32,256]{1,0:T(8,128)(2,1)S(1)} %get-tuple-element.18), channel_id=1, source_target_pairs={{0,2},{1,3},{2,0},{3,1},{4,6},{5,7},{6,4},{7,5},{8,10},{9,11},{10,... | collective-permute-start | bytes 49160 | tf_op jit(solution)/shard_map/ppermute | solution.py:224
  16.9 3.3 %collective-permute-start.8 = (bf16[32,256]{1,0:T(8,128)(2,1)S(1)}, bf16[32,256]{1,0:T(8,128)(2,1)S(1)}, u32[]{:S(2)}, u32[]{:S(2)}) collective-permute-start(bf16[32,256]{1,0:T(8,128)(2,1)S(1)} %get-tuple-element.19), channel_id=1, source_target_pairs={{0,3},{1,2},{2,1},{3,0},{4,7},{5,6},{6,5},{7,4},{8,11},{9,10},{10,... | collective-permute-start | bytes 49160 | tf_op jit(solution)/shard_map/ppermute | solution.py:224
  18.1 1.1 %copy-start = (f32[256]{0:T(256)S(1)}, f32[256]{0:T(256)}, u32[]{:S(2)}) copy-start(f32[256]{0:T(256)} %param.5) | copy-start | bytes 3076
  18.1 2.1 %collective-permute-start.6 = (bf16[32,256]{1,0:T(8,128)(2,1)S(1)}, bf16[32,256]{1,0:T(8,128)(2,1)S(1)}, u32[]{:S(2)}, u32[]{:S(2)}) collective-permute-start(bf16[32,256]{1,0:T(8,128)(2,1)S(1)} %get-tuple-element.17), channel_id=1, source_target_pairs={{0,1},{1,0},{2,3},{3,2},{4,5},{5,4},{6,7},{7,6},{8,9},{9,8},{10,11... | collective-permute-start | bytes 49160 | tf_op jit(solution)/shard_map/ppermute | solution.py:224

commit v26 on v25

--- a/solution.py
+++ b/solution.py
@@ -147,7 +147,7 @@
     return matern((squares + lane_squares(col)) + cross)
 
 
-def cycle_kernel(order, parts, cols_in, shard, vectors, *refs):
+def cycle_kernel(order, parts, cols_in, shard, vectors, own_ref, *refs):
     rest = list(refs)
     blocks = {place: [rest.pop(0) for _ in range((*parts, *[1] * cols_in)[place])] for place in order}
     rows = [joined(blocks[place], shard, vectors) for place in range(len(parts))]
@@ -157,6 +157,7 @@
         kernel = kernel_of(left, squares, blocks[len(parts) + col][0][0:shard, :])
         rest[col][...] = jnp.dot(probes, kernel, preferred_element_type=jnp.float32)
         rest[cols_in + col][...] = kernel
+    rest[2 * cols_in][...] = own_ref[...]
 
 
 def rows_kernel(parts, start, known, fresh, shard, vectors, *refs):
@@ -239,13 +240,26 @@
     flat = jax.ShapeDtypeStruct((vectors, shard), jnp.float32)
     sent = jax.ShapeDtypeStruct((vectors, shard), jnp.bfloat16)
     matrix = jax.ShapeDtypeStruct((inner * shard, shard), jnp.bfloat16)
+    early = sorted({0, inner // 2})
+    pairs = [(row, 0, ("back",)) for row in range(len(early))]
+    started = tile(
+        [blocks[row] for row in early],
+        [packed],
+        range(len(early) + 1),
+        pairs,
+        {},
+        shard,
+        vectors,
+        noise=[noise_level[None, :]],
+        work=0.0,
+    )
     found = call(
         functools.partial(cycle_kernel, order, parts, len(cols), shard, vectors),
-        [part for place in order for part in operands[place]],
-        [flat] * len(cols) + [matrix] * len(cols),
+        [started["back", 0], *[part for place in order for part in operands[place]]],
+        [flat] * len(cols) + [matrix] * len(cols) + [flat],
         0,
     )
-    backs, kernels = found[: len(cols)], found[len(cols) :]
+    backs, kernels, started = found[: len(cols)], found[len(cols) : -1], found[-1]
     half = inner // 2
     sums = {}
     for start, stop in ((half, inner), (0, half)):
@@ -257,8 +271,10 @@
             len(some) * len(others) * shard * shard * features.shape[1],
         )
         sums.update({("rows", start + place): value for place, value in enumerate(found)})
-    pairs = [(row, 0, ("back",)) for row in range(inner)]
-    own = tile(blocks, [packed], range(inner + 1), pairs, {}, shard, vectors, noise=[noise_level[None, :]])
+    later = [row for row in range(inner) if row not in early]
+    pairs = [(row, 0, ("back",)) for row in range(len(later))]
+    known = {("back", 0): started}
+    own = tile([blocks[row] for row in later], [packed], range(len(later) + 1), pairs, known, shard, vectors)
 
     total = [sums["rows", 0], own["back", 0]]
     total += [in_plane(sums["rows", step], [(t, s) for s, t in near(step)]) for step in range(1, inner)]

time: 21.2 us -> 21.1 us (level)
  waiting for transfers between devices: 5.36 us -> 4.54 us
  local copies, waits for them, and re-layouts: 0.01 us -> 0.44 us
  Pallas kernels: 3.06 us -> 3.47 us
    ppermute x3, waiting for transfers between devices: 5.04 us -> 3.95 us  [along_outer(): lax.ppermute(value, 'blk', [(s * inner + b, t * inner + b) for s, t in ed...]
    unnamed x2, local copies, waits for them, and re-layouts: 0.01 us -> 0.44 us
    pallas_call x1 -> x2, Pallas kernels: 0.88 us -> 1.29 us  [tile(): pl.pallas_call(functools.partial(tile_kernel, list(order), tuple(pairs),...]
    ppermute x7, waiting for transfers between devices: 0.32 us -> 0.59 us  [in_plane(): lax.ppermute(value, 'blk', [(a * inner + s, a * inner + t) for a in range...]
  transfers between devices with their start and end apart: 10 -> 10, of which waited for: 3 -> 3; matrix products, arithmetic and copies ran while one was open for 0% -> 0% of each run, Pallas kernels for 15% -> 17%
where the time goes in v26:
time: 21.1 us; the launch traced here: 20.9 us
  starting transfers between devices  10.8 us (51%)
  waiting for transfers between devices  4.54 us (22%)
  Pallas kernels  3.47 us (16%)
  other arithmetic  1.56 us (7%)
  local copies, waits for them, and re-layouts  0.44 us (2%)
    ppermute x7, starting transfers between devices, in_plane(): lax.ppermute(value, 'blk', [(a * inner + s, a * inner + t) for a in range...  5.83 us
    ppermute x3, starting transfers between devices, along_outer(): lax.ppermute(value, 'blk', [(s * inner + b, t * inner + b) for s, t in ed...  4.98 us
    ppermute x3, waiting for transfers between devices, along_outer(): lax.ppermute(value, 'blk', [(s * inner + b, t * inner + b) for s, t in ed...  3.95 us
    pallas_call x3, Pallas kernels, call(): pl.pallas_call(body, out_shape=outs, in_specs=[whole] * len(args), out_sp...  2.17 us
    pallas_call x2, Pallas kernels, tile(): pl.pallas_call(functools.partial(tile_kernel, list(order), tuple(pairs),...  1.29 us
    concatenate x1, other arithmetic, on_device(): packed = jnp.concatenate([features, probes.T], axis=0)  0.93 us
    transpose x1, other arithmetic, on_device(): return functools.reduce(lambda sofar, term: sofar + term, total).T  0.63 us
    ppermute x7, waiting for transfers between devices, in_plane(): lax.ppermute(value, 'blk', [(a * inner + s, a * inner + t) for a in range...  0.59 us
  transfers between devices with their start and end apart: 10, of which 3 were waited for; matrix products, arithmetic and copies ran while one was open for 0% of the time, Pallas kernels for 17%

profile of v26, /device:TPU:0, one launch (start us, length us, event | category | flops | bytes accessed | tf_op | source)
XLA Modules:
  0.0 20.9 jit_solution(11080783062836415627)
XLA Ops:
  0.0 0.9 %pad_maximum_fusion.refs_0_.refs_2_.refs_3_ = bf16[288,256]{1,0:T(8,128)(2,1)S(1)} fusion(bf16[32,256]{1,0:T(8,128)(2,1)} %bitcast.5, bf16[256,256]{1,0:T(8,128)(2,1)} %param.3), kind=kLoop, calls=%fused_computation | loop fusion | flops 294912 | bytes 294912 | tf_op jit(solution)/shard_map/concatenate | solution.py:219
  0.9 3.0 %collective-permute-start.2 = (bf16[288,256]{1,0:T(8,128)(2,1)S(1)}, bf16[288,256]{1,0:T(8,128)(2,1)S(1)}, u32[]{:S(2)}, u32[]{:S(2)}) collective-permute-start(bf16[288,256]{1,0:T(8,128)(2,1)S(1)} %pad_maximum_fusion.refs_0_.refs_2_.refs_3_), channel_id=1, source_target_pairs={{0,2},{1,3},{2,0},{3,1},{4,6},{5,7},{6,4},{7,5},{8,10},{9,11},{10,... | collective-permute-start | bytes 442376 | tf_op jit(solution)/shard_map/ppermute | solution.py:225
  4.0 3.6 %collective-permute-start.5 = (bf16[288,256]{1,0:T(8,128)(2,1)S(1)}, bf16[288,256]{1,0:T(8,128)(2,1)S(1)}, u32[]{:S(2)}, u32[]{:S(2)}) collective-permute-start(bf16[288,256]{1,0:T(8,128)(2,1)S(1)} %pad_maximum_fusion.refs_0_.refs_2_.refs_3_), channel_id=1, source_target_pairs={{12,4},{13,5},{14,6},{15,7},{4,8},{5,9},{6,10},{7,11},{8,0},{9,1},... | collective-permute-start | bytes 442376 | tf_op jit(solution)/shard_map/ppermute | solution.py:222
  7.6 0.0 collective-permute-start
  7.6 0.2 %collective-permute-done.2.refs_1_.from_ref.refs_5_.refs_0_ = bf16[288,256]{1,0:T(8,128)(2,1)S(1)} collective-permute-done((bf16[288,256]{1,0:T(8,128)(2,1)S(1)}, bf16[288,256]{1,0:T(8,128)(2,1)S(1)}, u32[]{:S(2)}, u32[]{:S(2)}) %collective-permute-start.2) | collective-permute-done | bytes 147488 | tf_op jit(solution)/shard_map/ppermute | solution.py:225
  7.8 0.3 %collective-permute-start.3 = (bf16[144,256]{1,0:T(8,128)(2,1)S(1)}, bf16[144,256]{1,0:T(8,128)(2,1)S(1)}, u32[]{:S(2)}, u32[]{:S(2)}) collective-permute-start(bf16[144,256]{1,0:T(8,128)(2,1)S(1)} %get-tuple-element.14), channel_id=1, source_target_pairs={{0,1},{1,0},{2,3},{3,2},{4,5},{5,4},{6,7},{7,6},{8,9},{9,8},{10,11... | collective-permute-start | bytes 221192 | tf_op jit(solution)/shard_map/ppermute | solution.py:225
  8.2 0.2 %collective-permute-start.4 = (bf16[144,256]{1,0:T(8,128)(2,1)S(1)}, bf16[144,256]{1,0:T(8,128)(2,1)S(1)}, u32[]{:S(2)}, u32[]{:S(2)}) collective-permute-start(bf16[144,256]{1,0:T(8,128)(2,1)S(1)} %get-tuple-element.15), channel_id=1, source_target_pairs={{0,1},{1,0},{2,3},{3,2},{4,5},{5,4},{6,7},{7,6},{8,9},{9,8},{10,11... | collective-permute-start | bytes 221192 | tf_op jit(solution)/shard_map/ppermute | solution.py:225
  8.4 0.4 %copy-done = f32[256]{0:T(256)S(1)} copy-done((f32[256]{0:T(256)S(1)}, f32[256]{0:T(256)}, u32[]{:S(2)}) %copy-start) | copy-done | bytes 1048
  8.8 0.6 %shard_map.37.own_ref = f32[32,256]{1,0:T(8,128)S(1)} custom-call(bf16[288,256]{1,0:T(8,128)(2,1)S(1)} %pad_maximum_fusion.refs_0_.refs_2_.refs_3_, bf16[288,256]{1,0:T(8,128)(2,1)S(1)} %collective-permute-done.2.refs_1_.from_ref.refs_5_.refs_0_, bf16[288,256]{1,0:T(8,128)(2,1)S(1)} %pad_maximum_fusion.refs_0_.refs_2_.refs_3_, f32[1,256]{1,0:T(1,128)S(1)} %bitcast.4), custom_call_target="tpu_custom_call" | custom-call | tf_op jit(solution)/shard_map/pallas_call | solution.py:119
  9.5 3.9 %collective-permute-done.5.refs_3_.refs_4_.refs_5_ = bf16[288,256]{1,0:T(8,128)(2,1)S(1)} collective-permute-done((bf16[288,256]{1,0:T(8,128)(2,1)S(1)}, bf16[288,256]{1,0:T(8,128)(2,1)S(1)}, u32[]{:S(2)}, u32[]{:S(2)}) %collective-permute-start.5) | collective-permute-done | bytes 147488 | tf_op jit(solution)/shard_map/ppermute | solution.py:222
  13.4 0.0 collective-permute-done.refs_4_.refs_1_.refs_0_
  13.4 0.0 collective-permute-done.3.refs_1_
  13.4 0.0 collective-permute-done.4.refs_2_
  13.5 0.8 %shard_map.39 = (f32[32,256]{1,0:T(8,128)S(1)}, bf16[1024,256]{1,0:T(8,128)(2,1)S(1)}, f32[32,256]{1,0:T(8,128)S(1)}) custom-call(f32[32,256]{1,0:T(8,128)S(1)} %shard_map.37.own_ref, bf16[288,256]{1,0:T(8,128)(2,1)S(1)} %pad_maximum_fusion.refs_0_.refs_2_.refs_3_, bf16[144,256]{1,0:T(8,128)(2,1)S(1)} %collective-permute-done.3.refs_1_, ...), custom_call_target="tpu_custom_call" | custom-call | tf_op jit(solution)/shard_map/pallas_call | solution.py:183
  14.3 1.4 %collective-permute-start.9 = (f32[32,256]{1,0:T(8,128)S(1)}, f32[32,256]{1,0:T(8,128)S(1)}, u32[]{:S(2)}, u32[]{:S(2)}) collective-permute-start(f32[32,256]{1,0:T(8,128)S(1)} %get-tuple-element.22), channel_id=1, source_target_pairs={{4,12},{5,13},{6,14},{7,15},{8,4},{9,5},{10,6},{11,7},{0,8},{1,9},... | collective-permute-start | bytes 98312 | tf_op jit(solution)/shard_map/ppermute | solution.py:222
  15.6 0.0 collective-permute-done.1.refs_2_.refs_3_
  15.6 0.7 %shard_map.42 = (bf16[32,256]{1,0:T(8,128)(2,1)S(1)}, bf16[32,256]{1,0:T(8,128)(2,1)S(1)}) custom-call(bf16[288,256]{1,0:T(8,128)(2,1)S(1)} %collective-permute-done.2.refs_1_.from_ref.refs_5_.refs_0_, bf16[144,256]{1,0:T(8,128)(2,1)S(1)} %collective-permute-done.3.refs_1_, bf16[144,256]{1,0:T(8,128)(2,1)S(1)} %collective-permute-done.4.refs_2_, ...), custom_call_target="tpu_custom_call" | custom-call | flops 67108864 | tf_op jit(solution)/shard_map/pallas_call | solution.py:183
  16.3 0.5 %collective-permute-start.7 = (bf16[32,256]{1,0:T(8,128)(2,1)S(1)}, bf16[32,256]{1,0:T(8,128)(2,1)S(1)}, u32[]{:S(2)}, u32[]{:S(2)}) collective-permute-start(bf16[32,256]{1,0:T(8,128)(2,1)S(1)} %get-tuple-element.20), channel_id=1, source_target_pairs={{0,2},{1,3},{2,0},{3,1},{4,6},{5,7},{6,4},{7,5},{8,10},{9,11},{10,... | collective-permute-start | bytes 49160 | tf_op jit(solution)/shard_map/ppermute | solution.py:225
  16.9 0.6 %collective-permute-start.8 = (bf16[32,256]{1,0:T(8,128)(2,1)S(1)}, bf16[32,256]{1,0:T(8,128)(2,1)S(1)}, u32[]{:S(2)}, u32[]{:S(2)}) collective-permute-start(bf16[32,256]{1,0:T(8,128)(2,1)S(1)} %get-tuple-element.21), channel_id=1, source_target_pairs={{0,3},{1,2},{2,1},{3,0},{4,7},{5,6},{6,5},{7,4},{8,11},{9,10},{10,... | collective-permute-start | bytes 49160 | tf_op jit(solution)/shard_map/ppermute | solution.py:225
  17.5 0.7 %shard_map.40 = (f32[32,256]{1,0:T(8,128)S(1)}, bf16[32,256]{1,0:T(8,128)(2,1)S(1)}) custom-call(bf16[288,256]{1,0:T(8,128)(2,1)S(1)} %pad_maximum_fusion.refs_0_.refs_2_.refs_3_, bf16[288,256]{1,0:T(8,128)(2,1)S(1)} %collective-permute-done.refs_4_.refs_1_.refs_0_, bf16[288,256]{1,0:T(8,128)(2,1)S(1)} %collective-permute-done.1.refs_2_.refs_3_, ...), custom_call_target="tpu_custom_call" | custom-call | flops 67108864 | tf_op jit(solution)/shard_map/pallas_call | solution.py:183
  18.1 1.1 %collective-permute-start.6 = (bf16[32,256]{1,0:T(8,128)(2,1)S(1)}, bf16[32,256]{1,0:T(8,128)(2,1)S(1)}, u32[]{:S(2)}, u32[]{:S(2)}) collective-permute-start(bf16[32,256]{1,0:T(8,128)(2,1)S(1)} %get-tuple-element.19), channel_id=1, source_target_pairs={{0,1},{1,0},{2,3},{3,2},{4,5},{5,4},{6,7},{7,6},{8,9},{9,8},{10,11... | collective-permute-start | bytes 49160 | tf_op jit(solution)/shard_map/ppermute | solution.py:225
  19.2 0.6 %shard_map.41 = f32[32,256]{1,0:T(8,128)S(1)} custom-call(bf16[288,256]{1,0:T(8,128)(2,1)S(1)} %collective-permute-done.refs_4_.refs_1_.refs_0_, bf16[144,256]{1,0:T(8,128)(2,1)S(1)} %collective-permute-done.3.refs_1_, bf16[144,256]{1,0:T(8,128)(2,1)S(1)} %collective-permute-done.4.refs_2_, bf16[288,256]{1,0:T(8,128)(2,1)S(1)} %pad_maximum_fusion.refs_0_.refs_2_.refs_3_, ...), custom_call_target="tpu_custom_call" | custom-call | flops 83886080 | bytes 393216 | tf_op jit(solution)/shard_map/pallas_call | solution.py:119
  19.9 0.3 %collective-permute-done.7 = bf16[32,256]{1,0:T(8,128)(2,1)S(1)} collective-permute-done((bf16[32,256]{1,0:T(8,128)(2,1)S(1)}, bf16[32,256]{1,0:T(8,128)(2,1)S(1)}, u32[]{:S(2)}, u32[]{:S(2)}) %collective-permute-start.7) | collective-permute-done | bytes 16416 | tf_op jit(solution)/shard_map/ppermute | solution.py:225
  20.2 0.6 %add_bitcast_fusion = f32[256,32]{0,1:T(8,128)} fusion(f32[32,256]{1,0:T(8,128)S(1)} %collective-permute-done.9, bf16[32,256]{1,0:T(8,128)(2,1)S(1)} %collective-permute-done.8, bf16[32,256]{1,0:T(8,128)(2,1)S(1)} %collective-permute-done.7, bf16[32,256]{1,0:T(8,128)(2,1)S(1)} %collective-permute-done.6, f32[32,256]{1,0:T(8,128)S(1)} %get-tuple-element.17, ...), kind=kLoop, calls=%fused_computation.1 | loop fusion | flops 65536 | bytes 180224 | tf_op jit(solution)/shard_map/transpose | solution.py:282
  (6 shorter events, 0.0 us)
Async XLA Ops:
  0.9 6.9 %collective-permute-start.2 = (bf16[288,256]{1,0:T(8,128)(2,1)S(1)}, bf16[288,256]{1,0:T(8,128)(2,1)S(1)}, u32[]{:S(2)}, u32[]{:S(2)}) collective-permute-start(bf16[288,256]{1,0:T(8,128)(2,1)S(1)} %pad_maximum_fusion.refs_0_.refs_2_.refs_3_), channel_id=1, source_target_pairs={{0,2},{1,3},{2,0},{3,1},{4,6},{5,7},{6,4},{7,5},{8,10},{9,11},{10,... | collective-permute-start | bytes 442376 | tf_op jit(solution)/shard_map/ppermute | solution.py:225
  4.0 9.5 %collective-permute-start.5 = (bf16[288,256]{1,0:T(8,128)(2,1)S(1)}, bf16[288,256]{1,0:T(8,128)(2,1)S(1)}, u32[]{:S(2)}, u32[]{:S(2)}) collective-permute-start(bf16[288,256]{1,0:T(8,128)(2,1)S(1)} %pad_maximum_fusion.refs_0_.refs_2_.refs_3_), channel_id=1, source_target_pairs={{12,4},{13,5},{14,6},{15,7},{4,8},{5,9},{6,10},{7,11},{8,0},{9,1},... | collective-permute-start | bytes 442376 | tf_op jit(solution)/shard_map/ppermute | solution.py:222
  7.6 5.9 %collective-permute-start = (bf16[288,256]{1,0:T(8,128)(2,1)S(1)}, bf16[288,256]{1,0:T(8,128)(2,1)S(1)}, u32[]{:S(2)}, u32[]{:S(2)}) collective-permute-start(bf16[288,256]{1,0:T(8,128)(2,1)S(1)} %pad_maximum_fusion.refs_0_.refs_2_.refs_3_), channel_id=1, source_target_pairs={{0,1},{1,0},{2,3},{3,2},{4,5},{5,4},{6,7},{7,6},{8,9},{9,8},{10,11... | collective-permute-start | bytes 442376 | tf_op jit(solution)/shard_map/ppermute | solution.py:225
  7.6 8.1 %collective-permute-start.1 = (bf16[288,256]{1,0:T(8,128)(2,1)S(1)}, bf16[288,256]{1,0:T(8,128)(2,1)S(1)}, u32[]{:S(2)}, u32[]{:S(2)}) collective-permute-start(bf16[288,256]{1,0:T(8,128)(2,1)S(1)} %pad_maximum_fusion.refs_0_.refs_2_.refs_3_), channel_id=1, source_target_pairs={{12,8},{13,9},{14,10},{15,11},{4,0},{5,1},{6,2},{7,3},{8,12},{9,13... | collective-permute-start | bytes 442376 | tf_op jit(solution)/shard_map/ppermute | solution.py:222
  7.8 5.6 %collective-permute-start.3 = (bf16[144,256]{1,0:T(8,128)(2,1)S(1)}, bf16[144,256]{1,0:T(8,128)(2,1)S(1)}, u32[]{:S(2)}, u32[]{:S(2)}) collective-permute-start(bf16[144,256]{1,0:T(8,128)(2,1)S(1)} %get-tuple-element.14), channel_id=1, source_target_pairs={{0,1},{1,0},{2,3},{3,2},{4,5},{5,4},{6,7},{7,6},{8,9},{9,8},{10,11... | collective-permute-start | bytes 221192 | tf_op jit(solution)/shard_map/ppermute | solution.py:225
  8.2 0.7 %copy-start = (f32[256]{0:T(256)S(1)}, f32[256]{0:T(256)}, u32[]{:S(2)}) copy-start(f32[256]{0:T(256)} %param.5) | copy-start | bytes 3076
  8.2 5.3 %collective-permute-start.4 = (bf16[144,256]{1,0:T(8,128)(2,1)S(1)}, bf16[144,256]{1,0:T(8,128)(2,1)S(1)}, u32[]{:S(2)}, u32[]{:S(2)}) collective-permute-start(bf16[144,256]{1,0:T(8,128)(2,1)S(1)} %get-tuple-element.15), channel_id=1, source_target_pairs={{0,1},{1,0},{2,3},{3,2},{4,5},{5,4},{6,7},{7,6},{8,9},{9,8},{10,11... | collective-permute-start | bytes 221192 | tf_op jit(solution)/shard_map/ppermute | solution.py:225
  14.3 6.0 %collective-permute-start.9 = (f32[32,256]{1,0:T(8,128)S(1)}, f32[32,256]{1,0:T(8,128)S(1)}, u32[]{:S(2)}, u32[]{:S(2)}) collective-permute-start(f32[32,256]{1,0:T(8,128)S(1)} %get-tuple-element.22), channel_id=1, source_target_pairs={{4,12},{5,13},{6,14},{7,15},{8,4},{9,5},{10,6},{11,7},{0,8},{1,9},... | collective-permute-start | bytes 98312 | tf_op jit(solution)/shard_map/ppermute | solution.py:222
  16.3 3.9 %collective-permute-start.7 = (bf16[32,256]{1,0:T(8,128)(2,1)S(1)}, bf16[32,256]{1,0:T(8,128)(2,1)S(1)}, u32[]{:S(2)}, u32[]{:S(2)}) collective-permute-start(bf16[32,256]{1,0:T(8,128)(2,1)S(1)} %get-tuple-element.20), channel_id=1, source_target_pairs={{0,2},{1,3},{2,0},{3,1},{4,6},{5,7},{6,4},{7,5},{8,10},{9,11},{10,... | collective-permute-start | bytes 49160 | tf_op jit(solution)/shard_map/ppermute | solution.py:225
  16.9 3.3 %collective-permute-start.8 = (bf16[32,256]{1,0:T(8,128)(2,1)S(1)}, bf16[32,256]{1,0:T(8,128)(2,1)S(1)}, u32[]{:S(2)}, u32[]{:S(2)}) collective-permute-start(bf16[32,256]{1,0:T(8,128)(2,1)S(1)} %get-tuple-element.21), channel_id=1, source_target_pairs={{0,3},{1,2},{2,1},{3,0},{4,7},{5,6},{6,5},{7,4},{8,11},{9,10},{10,... | collective-permute-start | bytes 49160 | tf_op jit(solution)/shard_map/ppermute | solution.py:225
  18.1 2.1 %collective-permute-start.6 = (bf16[32,256]{1,0:T(8,128)(2,1)S(1)}, bf16[32,256]{1,0:T(8,128)(2,1)S(1)}, u32[]{:S(2)}, u32[]{:S(2)}) collective-permute-start(bf16[32,256]{1,0:T(8,128)(2,1)S(1)} %get-tuple-element.19), channel_id=1, source_target_pairs={{0,1},{1,0},{2,3},{3,2},{4,5},{5,4},{6,7},{7,6},{8,9},{9,8},{10,11... | collective-permute-start | bytes 49160 | tf_op jit(solution)/shard_map/ppermute | solution.py:225

commit v27 on v25

--- a/solution.py
+++ b/solution.py
@@ -141,10 +141,21 @@
     return left, jnp.sum(wide * wide, axis=1, keepdims=True)
 
 
-def kernel_of(left, squares, col):
+def lane_squares_by_products(block):
+    wide = block.astype(jnp.float32)
+    square = wide * wide
+    high = square.astype(jnp.bfloat16)
+    low = (square - high.astype(jnp.float32)).astype(jnp.bfloat16)
+    ones = jnp.ones((8, block.shape[1]), jnp.bfloat16)
+    total = lax.dot_general(ones, high, ROWS_BY_ROWS, preferred_element_type=jnp.float32)
+    total += lax.dot_general(ones, low, ROWS_BY_ROWS, preferred_element_type=jnp.float32)
+    return total[0:1, :]
+
+
+def kernel_of(left, squares, col, lanes=lane_squares):
     scaled = col * jnp.asarray(-2.0, col.dtype)
     cross = lax.dot_general(left, scaled, ROWS_BY_ROWS, preferred_element_type=jnp.float32)
-    return matern((squares + lane_squares(col)) + cross)
+    return matern((squares + lanes(col)) + cross)
 
 
 def cycle_kernel(order, parts, cols_in, shard, vectors, *refs):
@@ -154,7 +165,7 @@
     left, squares = features_of(rows)
     probes = jnp.concatenate([row[1] for row in rows], axis=1)
     for col in range(cols_in):
-        kernel = kernel_of(left, squares, blocks[len(parts) + col][0][0:shard, :])
+        kernel = kernel_of(left, squares, blocks[len(parts) + col][0][0:shard, :], lane_squares_by_products)
         rest[col][...] = jnp.dot(probes, kernel, preferred_element_type=jnp.float32)
         rest[cols_in + col][...] = kernel
 

time: 21.2 us -> 21.4 us (level)
  no operation moved by 1% of the time
where the time goes in v27:
time: 21.4 us; the launch traced here: 21 us
  starting transfers between devices  10.8 us (50%)
  waiting for transfers between devices  5.36 us (25%)
  Pallas kernels  3.19 us (15%)
  other arithmetic  1.56 us (7%)
    ppermute x7, starting transfers between devices, in_plane(): lax.ppermute(value, 'blk', [(a * inner + s, a * inner + t) for a in range...  5.86 us
    ppermute x3, waiting for transfers between devices, along_outer(): lax.ppermute(value, 'blk', [(s * inner + b, t * inner + b) for s, t in ed...  5.04 us
    ppermute x3, starting transfers between devices, along_outer(): lax.ppermute(value, 'blk', [(s * inner + b, t * inner + b) for s, t in ed...  4.97 us
    pallas_call x3, Pallas kernels, call(): pl.pallas_call(body, out_shape=outs, in_specs=[whole] * len(args), out_sp...  2.29 us
    concatenate x1, other arithmetic, on_device(): packed = jnp.concatenate([features, probes.T], axis=0)  0.93 us
    pallas_call x1, Pallas kernels, tile(): pl.pallas_call(functools.partial(tile_kernel, list(order), tuple(pairs),...  0.88 us
    transpose x1, other arithmetic, on_device(): return functools.reduce(lambda sofar, term: sofar + term, total).T  0.63 us
  transfers between devices with their start and end apart: 10, of which 3 were waited for; matrix products, arithmetic and copies ran while one was open for 0% of the time, Pallas kernels for 15%

profile of v27, /device:TPU:0, one launch (start us, length us, event | category | flops | bytes accessed | tf_op | source)
XLA Modules:
  0.0 21.0 jit_solution(10584268580342564911)
XLA Ops:
  0.0 0.9 %pad_maximum_fusion.refs_0_.refs_5_ = bf16[288,256]{1,0:T(8,128)(2,1)S(1)} fusion(bf16[32,256]{1,0:T(8,128)(2,1)} %bitcast.5, bf16[256,256]{1,0:T(8,128)(2,1)} %param.3), kind=kLoop, calls=%fused_computation | loop fusion | flops 294912 | bytes 294912 | tf_op jit(solution)/shard_map/concatenate | solution.py:229
  0.9 3.0 %collective-permute-start.2 = (bf16[288,256]{1,0:T(8,128)(2,1)S(1)}, bf16[288,256]{1,0:T(8,128)(2,1)S(1)}, u32[]{:S(2)}, u32[]{:S(2)}) collective-permute-start(bf16[288,256]{1,0:T(8,128)(2,1)S(1)} %pad_maximum_fusion.refs_0_.refs_5_), channel_id=1, source_target_pairs={{0,2},{1,3},{2,0},{3,1},{4,6},{5,7},{6,4},{7,5},{8,10},{9,11},{10,... | collective-permute-start | bytes 442376 | tf_op jit(solution)/shard_map/ppermute | solution.py:235
  4.0 3.6 %collective-permute-start.5 = (bf16[288,256]{1,0:T(8,128)(2,1)S(1)}, bf16[288,256]{1,0:T(8,128)(2,1)S(1)}, u32[]{:S(2)}, u32[]{:S(2)}) collective-permute-start(bf16[288,256]{1,0:T(8,128)(2,1)S(1)} %pad_maximum_fusion.refs_0_.refs_5_), channel_id=1, source_target_pairs={{12,4},{13,5},{14,6},{15,7},{4,8},{5,9},{6,10},{7,11},{8,0},{9,1},... | collective-permute-start | bytes 442376 | tf_op jit(solution)/shard_map/ppermute | solution.py:232
  7.6 0.2 %collective-permute-done.2.from_ref.refs_5_.refs_2_.refs_0_ = bf16[288,256]{1,0:T(8,128)(2,1)S(1)} collective-permute-done((bf16[288,256]{1,0:T(8,128)(2,1)S(1)}, bf16[288,256]{1,0:T(8,128)(2,1)S(1)}, u32[]{:S(2)}, u32[]{:S(2)}) %collective-permute-start.2) | collective-permute-done | bytes 147488 | tf_op jit(solution)/shard_map/ppermute | solution.py:235
  7.8 0.3 %collective-permute-start.3 = (bf16[144,256]{1,0:T(8,128)(2,1)S(1)}, bf16[144,256]{1,0:T(8,128)(2,1)S(1)}, u32[]{:S(2)}, u32[]{:S(2)}) collective-permute-start(bf16[144,256]{1,0:T(8,128)(2,1)S(1)} %get-tuple-element.13), channel_id=1, source_target_pairs={{0,1},{1,0},{2,3},{3,2},{4,5},{5,4},{6,7},{7,6},{8,9},{9,8},{10,11... | collective-permute-start | bytes 221192 | tf_op jit(solution)/shard_map/ppermute | solution.py:235
  8.2 0.2 %collective-permute-start.4 = (bf16[144,256]{1,0:T(8,128)(2,1)S(1)}, bf16[144,256]{1,0:T(8,128)(2,1)S(1)}, u32[]{:S(2)}, u32[]{:S(2)}) collective-permute-start(bf16[144,256]{1,0:T(8,128)(2,1)S(1)} %get-tuple-element.14), channel_id=1, source_target_pairs={{0,1},{1,0},{2,3},{3,2},{4,5},{5,4},{6,7},{7,6},{8,9},{9,8},{10,11... | collective-permute-start | bytes 221192 | tf_op jit(solution)/shard_map/ppermute | solution.py:235
  8.4 5.0 %collective-permute-done.5.refs_3_.refs_4_.refs_5_ = bf16[288,256]{1,0:T(8,128)(2,1)S(1)} collective-permute-done((bf16[288,256]{1,0:T(8,128)(2,1)S(1)}, bf16[288,256]{1,0:T(8,128)(2,1)S(1)}, u32[]{:S(2)}, u32[]{:S(2)}) %collective-permute-start.5) | collective-permute-done | bytes 147488 | tf_op jit(solution)/shard_map/ppermute | solution.py:232
  13.4 0.0 collective-permute-done.refs_4_.refs_1_
  13.4 0.0 collective-permute-done.3.refs_1_.refs_3_
  13.4 0.0 collective-permute-done.4.refs_2_.refs_4_
  13.5 0.9 %shard_map.38 = (f32[32,256]{1,0:T(8,128)S(1)}, bf16[1024,256]{1,0:T(8,128)(2,1)S(1)}) custom-call(bf16[288,256]{1,0:T(8,128)(2,1)S(1)} %pad_maximum_fusion.refs_0_.refs_5_, bf16[144,256]{1,0:T(8,128)(2,1)S(1)} %collective-permute-done.3.refs_1_.refs_3_, bf16[144,256]{1,0:T(8,128)(2,1)S(1)} %collective-permute-done.4.refs_2_.refs_4_, ...), custom_call_target="tpu_custom_call" | custom-call | tf_op jit(solution)/shard_map/pallas_call | solution.py:193
  14.4 1.4 %collective-permute-start.9 = (f32[32,256]{1,0:T(8,128)S(1)}, f32[32,256]{1,0:T(8,128)S(1)}, u32[]{:S(2)}, u32[]{:S(2)}) collective-permute-start(f32[32,256]{1,0:T(8,128)S(1)} %get-tuple-element.20), channel_id=1, source_target_pairs={{4,12},{5,13},{6,14},{7,15},{8,4},{9,5},{10,6},{11,7},{0,8},{1,9},... | collective-permute-start | bytes 98312 | tf_op jit(solution)/shard_map/ppermute | solution.py:232
  15.8 0.0 collective-permute-done.1.refs_2_.refs_3_
  15.8 0.7 %shard_map.41 = (bf16[32,256]{1,0:T(8,128)(2,1)S(1)}, bf16[32,256]{1,0:T(8,128)(2,1)S(1)}) custom-call(bf16[288,256]{1,0:T(8,128)(2,1)S(1)} %collective-permute-done.2.from_ref.refs_5_.refs_2_.refs_0_, bf16[144,256]{1,0:T(8,128)(2,1)S(1)} %collective-permute-done.3.refs_1_.refs_3_, bf16[144,256]{1,0:T(8,128)(2,1)S(1)} %collective-permute-done.4.refs_2_.refs_4_, ...), custom_call_target="tpu_custom_call" | custom-call | flops 67108864 | tf_op jit(solution)/shard_map/pallas_call | solution.py:193
  16.4 0.5 %collective-permute-start.7 = (bf16[32,256]{1,0:T(8,128)(2,1)S(1)}, bf16[32,256]{1,0:T(8,128)(2,1)S(1)}, u32[]{:S(2)}, u32[]{:S(2)}) collective-permute-start(bf16[32,256]{1,0:T(8,128)(2,1)S(1)} %get-tuple-element.18), channel_id=1, source_target_pairs={{0,2},{1,3},{2,0},{3,1},{4,6},{5,7},{6,4},{7,5},{8,10},{9,11},{10,... | collective-permute-start | bytes 49160 | tf_op jit(solution)/shard_map/ppermute | solution.py:235
  17.0 0.5 %collective-permute-start.8 = (bf16[32,256]{1,0:T(8,128)(2,1)S(1)}, bf16[32,256]{1,0:T(8,128)(2,1)S(1)}, u32[]{:S(2)}, u32[]{:S(2)}) collective-permute-start(bf16[32,256]{1,0:T(8,128)(2,1)S(1)} %get-tuple-element.19), channel_id=1, source_target_pairs={{0,3},{1,2},{2,1},{3,0},{4,7},{5,6},{6,5},{7,4},{8,11},{9,10},{10,... | collective-permute-start | bytes 49160 | tf_op jit(solution)/shard_map/ppermute | solution.py:235
  17.5 0.7 %shard_map.39 = (f32[32,256]{1,0:T(8,128)S(1)}, bf16[32,256]{1,0:T(8,128)(2,1)S(1)}) custom-call(bf16[288,256]{1,0:T(8,128)(2,1)S(1)} %pad_maximum_fusion.refs_0_.refs_5_, bf16[288,256]{1,0:T(8,128)(2,1)S(1)} %collective-permute-done.refs_4_.refs_1_, bf16[288,256]{1,0:T(8,128)(2,1)S(1)} %collective-permute-done.1.refs_2_.refs_3_, ...), custom_call_target="tpu_custom_call" | custom-call | flops 67108864 | tf_op jit(solution)/shard_map/pallas_call | solution.py:193
  18.1 1.2 %collective-permute-start.6 = (bf16[32,256]{1,0:T(8,128)(2,1)S(1)}, bf16[32,256]{1,0:T(8,128)(2,1)S(1)}, u32[]{:S(2)}, u32[]{:S(2)}) collective-permute-start(bf16[32,256]{1,0:T(8,128)(2,1)S(1)} %get-tuple-element.17), channel_id=1, source_target_pairs={{0,1},{1,0},{2,3},{3,2},{4,5},{5,4},{6,7},{7,6},{8,9},{9,8},{10,11... | collective-permute-start | bytes 49160 | tf_op jit(solution)/shard_map/ppermute | solution.py:235
  19.4 0.9 %shard_map.40 = f32[32,256]{1,0:T(8,128)S(1)} custom-call(bf16[288,256]{1,0:T(8,128)(2,1)S(1)} %pad_maximum_fusion.refs_0_.refs_5_, bf16[288,256]{1,0:T(8,128)(2,1)S(1)} %collective-permute-done.refs_4_.refs_1_, bf16[288,256]{1,0:T(8,128)(2,1)S(1)} %collective-permute-done.2.from_ref.refs_5_.refs_2_.refs_0_, ...), custom_call_target="tpu_custom_call" | custom-call | flops 167772160 | bytes 655360 | tf_op jit(solution)/shard_map/pallas_call | solution.py:119
  20.3 0.1 collective-permute-done.7
  20.3 0.0 collective-permute-done.8
  20.3 0.0 collective-permute-done.6
  20.3 0.0 collective-permute-done.9
  20.3 0.6 %add_bitcast_fusion = f32[256,32]{0,1:T(8,128)} fusion(f32[32,256]{1,0:T(8,128)S(1)} %collective-permute-done.9, bf16[32,256]{1,0:T(8,128)(2,1)S(1)} %collective-permute-done.8, bf16[32,256]{1,0:T(8,128)(2,1)S(1)} %collective-permute-done.7, bf16[32,256]{1,0:T(8,128)(2,1)S(1)} %collective-permute-done.6, f32[32,256]{1,0:T(8,128)S(1)} %get-tuple-element.16, ...), kind=kLoop, calls=%fused_computation.1 | loop fusion | flops 65536 | bytes 180224 | tf_op jit(solution)/shard_map/transpose | solution.py:277
  (5 shorter events, 0.0 us)
Async XLA Ops:
  0.9 6.9 %collective-permute-start.2 = (bf16[288,256]{1,0:T(8,128)(2,1)S(1)}, bf16[288,256]{1,0:T(8,128)(2,1)S(1)}, u32[]{:S(2)}, u32[]{:S(2)}) collective-permute-start(bf16[288,256]{1,0:T(8,128)(2,1)S(1)} %pad_maximum_fusion.refs_0_.refs_5_), channel_id=1, source_target_pairs={{0,2},{1,3},{2,0},{3,1},{4,6},{5,7},{6,4},{7,5},{8,10},{9,11},{10,... | collective-permute-start | bytes 442376 | tf_op jit(solution)/shard_map/ppermute | solution.py:235
  4.0 9.5 %collective-permute-start.5 = (bf16[288,256]{1,0:T(8,128)(2,1)S(1)}, bf16[288,256]{1,0:T(8,128)(2,1)S(1)}, u32[]{:S(2)}, u32[]{:S(2)}) collective-permute-start(bf16[288,256]{1,0:T(8,128)(2,1)S(1)} %pad_maximum_fusion.refs_0_.refs_5_), channel_id=1, source_target_pairs={{12,4},{13,5},{14,6},{15,7},{4,8},{5,9},{6,10},{7,11},{8,0},{9,1},... | collective-permute-start | bytes 442376 | tf_op jit(solution)/shard_map/ppermute | solution.py:232
  7.6 5.9 %collective-permute-start = (bf16[288,256]{1,0:T(8,128)(2,1)S(1)}, bf16[288,256]{1,0:T(8,128)(2,1)S(1)}, u32[]{:S(2)}, u32[]{:S(2)}) collective-permute-start(bf16[288,256]{1,0:T(8,128)(2,1)S(1)} %pad_maximum_fusion.refs_0_.refs_5_), channel_id=1, source_target_pairs={{0,1},{1,0},{2,3},{3,2},{4,5},{5,4},{6,7},{7,6},{8,9},{9,8},{10,11... | collective-permute-start | bytes 442376 | tf_op jit(solution)/shard_map/ppermute | solution.py:235
  7.6 8.2 %collective-permute-start.1 = (bf16[288,256]{1,0:T(8,128)(2,1)S(1)}, bf16[288,256]{1,0:T(8,128)(2,1)S(1)}, u32[]{:S(2)}, u32[]{:S(2)}) collective-permute-start(bf16[288,256]{1,0:T(8,128)(2,1)S(1)} %pad_maximum_fusion.refs_0_.refs_5_), channel_id=1, source_target_pairs={{12,8},{13,9},{14,10},{15,11},{4,0},{5,1},{6,2},{7,3},{8,12},{9,13... | collective-permute-start | bytes 442376 | tf_op jit(solution)/shard_map/ppermute | solution.py:232
  7.8 5.6 %collective-permute-start.3 = (bf16[144,256]{1,0:T(8,128)(2,1)S(1)}, bf16[144,256]{1,0:T(8,128)(2,1)S(1)}, u32[]{:S(2)}, u32[]{:S(2)}) collective-permute-start(bf16[144,256]{1,0:T(8,128)(2,1)S(1)} %get-tuple-element.13), channel_id=1, source_target_pairs={{0,1},{1,0},{2,3},{3,2},{4,5},{5,4},{6,7},{7,6},{8,9},{9,8},{10,11... | collective-permute-start | bytes 221192 | tf_op jit(solution)/shard_map/ppermute | solution.py:235
  8.2 5.3 %collective-permute-start.4 = (bf16[144,256]{1,0:T(8,128)(2,1)S(1)}, bf16[144,256]{1,0:T(8,128)(2,1)S(1)}, u32[]{:S(2)}, u32[]{:S(2)}) collective-permute-start(bf16[144,256]{1,0:T(8,128)(2,1)S(1)} %get-tuple-element.14), channel_id=1, source_target_pairs={{0,1},{1,0},{2,3},{3,2},{4,5},{5,4},{6,7},{7,6},{8,9},{9,8},{10,11... | collective-permute-start | bytes 221192 | tf_op jit(solution)/shard_map/ppermute | solution.py:235
  14.4 6.0 %collective-permute-start.9 = (f32[32,256]{1,0:T(8,128)S(1)}, f32[32,256]{1,0:T(8,128)S(1)}, u32[]{:S(2)}, u32[]{:S(2)}) collective-permute-start(f32[32,256]{1,0:T(8,128)S(1)} %get-tuple-element.20), channel_id=1, source_target_pairs={{4,12},{5,13},{6,14},{7,15},{8,4},{9,5},{10,6},{11,7},{0,8},{1,9},... | collective-permute-start | bytes 98312 | tf_op jit(solution)/shard_map/ppermute | solution.py:232
  16.4 3.9 %collective-permute-start.7 = (bf16[32,256]{1,0:T(8,128)(2,1)S(1)}, bf16[32,256]{1,0:T(8,128)(2,1)S(1)}, u32[]{:S(2)}, u32[]{:S(2)}) collective-permute-start(bf16[32,256]{1,0:T(8,128)(2,1)S(1)} %get-tuple-element.18), channel_id=1, source_target_pairs={{0,2},{1,3},{2,0},{3,1},{4,6},{5,7},{6,4},{7,5},{8,10},{9,11},{10,... | collective-permute-start | bytes 49160 | tf_op jit(solution)/shard_map/ppermute | solution.py:235
  17.0 3.3 %collective-permute-start.8 = (bf16[32,256]{1,0:T(8,128)(2,1)S(1)}, bf16[32,256]{1,0:T(8,128)(2,1)S(1)}, u32[]{:S(2)}, u32[]{:S(2)}) collective-permute-start(bf16[32,256]{1,0:T(8,128)(2,1)S(1)} %get-tuple-element.19), channel_id=1, source_target_pairs={{0,3},{1,2},{2,1},{3,0},{4,7},{5,6},{6,5},{7,4},{8,11},{9,10},{10,... | collective-permute-start | bytes 49160 | tf_op jit(solution)/shard_map/ppermute | solution.py:235
  18.1 1.2 %copy-start = (f32[256]{0:T(256)S(1)}, f32[256]{0:T(256)}, u32[]{:S(2)}) copy-start(f32[256]{0:T(256)} %param.5) | copy-start | bytes 3076
  18.1 2.2 %collective-permute-start.6 = (bf16[32,256]{1,0:T(8,128)(2,1)S(1)}, bf16[32,256]{1,0:T(8,128)(2,1)S(1)}, u32[]{:S(2)}, u32[]{:S(2)}) collective-permute-start(bf16[32,256]{1,0:T(8,128)(2,1)S(1)} %get-tuple-element.17), channel_id=1, source_target_pairs={{0,1},{1,0},{2,3},{3,2},{4,5},{5,4},{6,7},{7,6},{8,9},{9,8},{10,11... | collective-permute-start | bytes 49160 | tf_op jit(solution)/shard_map/ppermute | solution.py:235

commit v28 on v25

--- a/solution.py
+++ b/solution.py
@@ -147,7 +147,7 @@
     return matern((squares + lane_squares(col)) + cross)
 
 
-def cycle_kernel(order, parts, cols_in, shard, vectors, *refs):
+def cycle_kernel(order, parts, cols_in, shard, vectors, noise_ref, *refs):
     rest = list(refs)
     blocks = {place: [rest.pop(0) for _ in range((*parts, *[1] * cols_in)[place])] for place in order}
     rows = [joined(blocks[place], shard, vectors) for place in range(len(parts))]
@@ -157,6 +157,7 @@
         kernel = kernel_of(left, squares, blocks[len(parts) + col][0][0:shard, :])
         rest[col][...] = jnp.dot(probes, kernel, preferred_element_type=jnp.float32)
         rest[cols_in + col][...] = kernel
+    rest[2 * cols_in][...] = noise_ref[...] * rows[0][1].astype(jnp.float32)
 
 
 def rows_kernel(parts, start, known, fresh, shard, vectors, *refs):
@@ -241,11 +242,11 @@
     matrix = jax.ShapeDtypeStruct((inner * shard, shard), jnp.bfloat16)
     found = call(
         functools.partial(cycle_kernel, order, parts, len(cols), shard, vectors),
-        [part for place in order for part in operands[place]],
-        [flat] * len(cols) + [matrix] * len(cols),
+        [noise_level[None, :], *[part for place in order for part in operands[place]]],
+        [flat] * len(cols) + [matrix] * len(cols) + [flat],
         0,
     )
-    backs, kernels = found[: len(cols)], found[len(cols) :]
+    backs, kernels, noise = found[: len(cols)], found[len(cols) : -1], found[-1]
     half = inner // 2
     sums = {}
     for start, stop in ((half, inner), (0, half)):
@@ -258,7 +259,7 @@
         )
         sums.update({("rows", start + place): value for place, value in enumerate(found)})
     pairs = [(row, 0, ("back",)) for row in range(inner)]
-    own = tile(blocks, [packed], range(inner + 1), pairs, {}, shard, vectors, noise=[noise_level[None, :]])
+    own = tile(blocks, [packed], range(inner + 1), pairs, {("back", 0): noise}, shard, vectors)
 
     total = [sums["rows", 0], own["back", 0]]
     total += [in_plane(sums["rows", step], [(t, s) for s, t in near(step)]) for step in range(1, inner)]

time: 21.2 us -> 21.1 us (level)
  no operation moved by 1% of the time
where the time goes in v28:
time: 21.1 us; the launch traced here: 20.9 us
  starting transfers between devices  10.8 us (51%)
  waiting for transfers between devices  5.39 us (26%)
  Pallas kernels  3.06 us (15%)
  other arithmetic  1.56 us (7%)
    ppermute x7, starting transfers between devices, in_plane(): lax.ppermute(value, 'blk', [(a * inner + s, a * inner + t) for a in range...  5.83 us
    ppermute x3, waiting for transfers between devices, along_outer(): lax.ppermute(value, 'blk', [(s * inner + b, t * inner + b) for s, t in ed...  5.04 us
    ppermute x3, starting transfers between devices, along_outer(): lax.ppermute(value, 'blk', [(s * inner + b, t * inner + b) for s, t in ed...  4.98 us
    pallas_call x3, Pallas kernels, call(): pl.pallas_call(body, out_shape=outs, in_specs=[whole] * len(args), out_sp...  2.17 us
    concatenate x1, other arithmetic, on_device(): packed = jnp.concatenate([features, probes.T], axis=0)  0.93 us
    pallas_call x1, Pallas kernels, tile(): pl.pallas_call(functools.partial(tile_kernel, list(order), tuple(pairs),...  0.88 us
    transpose x1, other arithmetic, on_device(): return functools.reduce(lambda sofar, term: sofar + term, total).T  0.63 us
  transfers between devices with their start and end apart: 10, of which 3 were waited for; matrix products, arithmetic and copies ran while one was open for 0% of the time, Pallas kernels for 15%

profile of v28, /device:TPU:0, one launch (start us, length us, event | category | flops | bytes accessed | tf_op | source)
XLA Modules:
  0.0 20.9 jit_solution(1665483198695004884)
XLA Ops:
  0.0 0.9 %pad_maximum_fusion.refs_0_.refs_5_ = bf16[288,256]{1,0:T(8,128)(2,1)S(1)} fusion(bf16[32,256]{1,0:T(8,128)(2,1)} %bitcast.5, bf16[256,256]{1,0:T(8,128)(2,1)} %param.3), kind=kLoop, calls=%fused_computation | loop fusion | flops 294912 | bytes 294912 | tf_op jit(solution)/shard_map/concatenate | solution.py:219
  0.9 3.0 %collective-permute-start.2 = (bf16[288,256]{1,0:T(8,128)(2,1)S(1)}, bf16[288,256]{1,0:T(8,128)(2,1)S(1)}, u32[]{:S(2)}, u32[]{:S(2)}) collective-permute-start(bf16[288,256]{1,0:T(8,128)(2,1)S(1)} %pad_maximum_fusion.refs_0_.refs_5_), channel_id=1, source_target_pairs={{0,2},{1,3},{2,0},{3,1},{4,6},{5,7},{6,4},{7,5},{8,10},{9,11},{10,... | collective-permute-start | bytes 442376 | tf_op jit(solution)/shard_map/ppermute | solution.py:225
  4.0 3.6 %collective-permute-start.5 = (bf16[288,256]{1,0:T(8,128)(2,1)S(1)}, bf16[288,256]{1,0:T(8,128)(2,1)S(1)}, u32[]{:S(2)}, u32[]{:S(2)}) collective-permute-start(bf16[288,256]{1,0:T(8,128)(2,1)S(1)} %pad_maximum_fusion.refs_0_.refs_5_), channel_id=1, source_target_pairs={{12,4},{13,5},{14,6},{15,7},{4,8},{5,9},{6,10},{7,11},{8,0},{9,1},... | collective-permute-start | bytes 442376 | tf_op jit(solution)/shard_map/ppermute | solution.py:222
  7.6 0.0 collective-permute-start
  7.6 0.0 collective-permute-start.1
  7.6 0.2 %collective-permute-done.2.from_ref.refs_5_.refs_2_.refs_0_ = bf16[288,256]{1,0:T(8,128)(2,1)S(1)} collective-permute-done((bf16[288,256]{1,0:T(8,128)(2,1)S(1)}, bf16[288,256]{1,0:T(8,128)(2,1)S(1)}, u32[]{:S(2)}, u32[]{:S(2)}) %collective-permute-start.2) | collective-permute-done | bytes 147488 | tf_op jit(solution)/shard_map/ppermute | solution.py:225
  7.8 0.3 %collective-permute-start.3 = (bf16[144,256]{1,0:T(8,128)(2,1)S(1)}, bf16[144,256]{1,0:T(8,128)(2,1)S(1)}, u32[]{:S(2)}, u32[]{:S(2)}) collective-permute-start(bf16[144,256]{1,0:T(8,128)(2,1)S(1)} %get-tuple-element.14), channel_id=1, source_target_pairs={{0,1},{1,0},{2,3},{3,2},{4,5},{5,4},{6,7},{7,6},{8,9},{9,8},{10,11... | collective-permute-start | bytes 221192 | tf_op jit(solution)/shard_map/ppermute | solution.py:225
  8.2 0.2 %collective-permute-start.4 = (bf16[144,256]{1,0:T(8,128)(2,1)S(1)}, bf16[144,256]{1,0:T(8,128)(2,1)S(1)}, u32[]{:S(2)}, u32[]{:S(2)}) collective-permute-start(bf16[144,256]{1,0:T(8,128)(2,1)S(1)} %get-tuple-element.15), channel_id=1, source_target_pairs={{0,1},{1,0},{2,3},{3,2},{4,5},{5,4},{6,7},{7,6},{8,9},{9,8},{10,11... | collective-permute-start | bytes 221192 | tf_op jit(solution)/shard_map/ppermute | solution.py:225
  8.4 5.0 %collective-permute-done.5.refs_3_.refs_4_.refs_5_ = bf16[288,256]{1,0:T(8,128)(2,1)S(1)} collective-permute-done((bf16[288,256]{1,0:T(8,128)(2,1)S(1)}, bf16[288,256]{1,0:T(8,128)(2,1)S(1)}, u32[]{:S(2)}, u32[]{:S(2)}) %collective-permute-start.5) | collective-permute-done | bytes 147488 | tf_op jit(solution)/shard_map/ppermute | solution.py:222
  13.4 0.0 collective-permute-done.refs_4_.refs_1_
  13.4 0.0 collective-permute-done.3.refs_1_.refs_3_
  13.4 0.0 collective-permute-done.4.refs_2_.refs_4_
  13.5 0.8 %shard_map.38 = (f32[32,256]{1,0:T(8,128)S(1)}, bf16[1024,256]{1,0:T(8,128)(2,1)S(1)}, f32[32,256]{1,0:T(8,128)S(1)}) custom-call(f32[1,256]{1,0:T(1,128)S(1)} %bitcast.4, bf16[288,256]{1,0:T(8,128)(2,1)S(1)} %pad_maximum_fusion.refs_0_.refs_5_, bf16[144,256]{1,0:T(8,128)(2,1)S(1)} %collective-permute-done.3.refs_1_.refs_3_, ...), custom_call_target="tpu_custom_call" | custom-call | tf_op jit(solution)/shard_map/pallas_call | solution.py:183
  14.3 1.4 %collective-permute-start.9 = (f32[32,256]{1,0:T(8,128)S(1)}, f32[32,256]{1,0:T(8,128)S(1)}, u32[]{:S(2)}, u32[]{:S(2)}) collective-permute-start(f32[32,256]{1,0:T(8,128)S(1)} %get-tuple-element.22), channel_id=1, source_target_pairs={{4,12},{5,13},{6,14},{7,15},{8,4},{9,5},{10,6},{11,7},{0,8},{1,9},... | collective-permute-start | bytes 98312 | tf_op jit(solution)/shard_map/ppermute | solution.py:222
  15.7 0.0 collective-permute-done.1.refs_2_.refs_3_
  15.7 0.7 %shard_map.41 = (bf16[32,256]{1,0:T(8,128)(2,1)S(1)}, bf16[32,256]{1,0:T(8,128)(2,1)S(1)}) custom-call(bf16[288,256]{1,0:T(8,128)(2,1)S(1)} %collective-permute-done.2.from_ref.refs_5_.refs_2_.refs_0_, bf16[144,256]{1,0:T(8,128)(2,1)S(1)} %collective-permute-done.3.refs_1_.refs_3_, bf16[144,256]{1,0:T(8,128)(2,1)S(1)} %collective-permute-done.4.refs_2_.refs_4_, ...), custom_call_target="tpu_custom_call" | custom-call | flops 67108864 | tf_op jit(solution)/shard_map/pallas_call | solution.py:183
  16.3 0.5 %collective-permute-start.7 = (bf16[32,256]{1,0:T(8,128)(2,1)S(1)}, bf16[32,256]{1,0:T(8,128)(2,1)S(1)}, u32[]{:S(2)}, u32[]{:S(2)}) collective-permute-start(bf16[32,256]{1,0:T(8,128)(2,1)S(1)} %get-tuple-element.20), channel_id=1, source_target_pairs={{0,2},{1,3},{2,0},{3,1},{4,6},{5,7},{6,4},{7,5},{8,10},{9,11},{10,... | collective-permute-start | bytes 49160 | tf_op jit(solution)/shard_map/ppermute | solution.py:225
  16.9 0.6 %collective-permute-start.8 = (bf16[32,256]{1,0:T(8,128)(2,1)S(1)}, bf16[32,256]{1,0:T(8,128)(2,1)S(1)}, u32[]{:S(2)}, u32[]{:S(2)}) collective-permute-start(bf16[32,256]{1,0:T(8,128)(2,1)S(1)} %get-tuple-element.21), channel_id=1, source_target_pairs={{0,3},{1,2},{2,1},{3,0},{4,7},{5,6},{6,5},{7,4},{8,11},{9,10},{10,... | collective-permute-start | bytes 49160 | tf_op jit(solution)/shard_map/ppermute | solution.py:225
  17.5 0.7 %shard_map.39 = (f32[32,256]{1,0:T(8,128)S(1)}, bf16[32,256]{1,0:T(8,128)(2,1)S(1)}) custom-call(bf16[288,256]{1,0:T(8,128)(2,1)S(1)} %pad_maximum_fusion.refs_0_.refs_5_, bf16[288,256]{1,0:T(8,128)(2,1)S(1)} %collective-permute-done.refs_4_.refs_1_, bf16[288,256]{1,0:T(8,128)(2,1)S(1)} %collective-permute-done.1.refs_2_.refs_3_, ...), custom_call_target="tpu_custom_call" | custom-call | flops 67108864 | tf_op jit(solution)/shard_map/pallas_call | solution.py:183
  18.1 1.1 %collective-permute-start.6 = (bf16[32,256]{1,0:T(8,128)(2,1)S(1)}, bf16[32,256]{1,0:T(8,128)(2,1)S(1)}, u32[]{:S(2)}, u32[]{:S(2)}) collective-permute-start(bf16[32,256]{1,0:T(8,128)(2,1)S(1)} %get-tuple-element.19), channel_id=1, source_target_pairs={{0,1},{1,0},{2,3},{3,2},{4,5},{5,4},{6,7},{7,6},{8,9},{9,8},{10,11... | collective-permute-start | bytes 49160 | tf_op jit(solution)/shard_map/ppermute | solution.py:225
  19.2 0.9 %shard_map.40 = f32[32,256]{1,0:T(8,128)S(1)} custom-call(bf16[288,256]{1,0:T(8,128)(2,1)S(1)} %pad_maximum_fusion.refs_0_.refs_5_, bf16[288,256]{1,0:T(8,128)(2,1)S(1)} %collective-permute-done.refs_4_.refs_1_, bf16[288,256]{1,0:T(8,128)(2,1)S(1)} %collective-permute-done.2.from_ref.refs_5_.refs_2_.refs_0_, ...), custom_call_target="tpu_custom_call" | custom-call | flops 167772160 | bytes 655360 | tf_op jit(solution)/shard_map/pallas_call | solution.py:119
  20.1 0.1 collective-permute-done.7
  20.2 0.0 collective-permute-done.8
  20.2 0.6 %add_bitcast_fusion = f32[256,32]{0,1:T(8,128)} fusion(f32[32,256]{1,0:T(8,128)S(1)} %collective-permute-done.9, bf16[32,256]{1,0:T(8,128)(2,1)S(1)} %collective-permute-done.8, bf16[32,256]{1,0:T(8,128)(2,1)S(1)} %collective-permute-done.7, bf16[32,256]{1,0:T(8,128)(2,1)S(1)} %collective-permute-done.6, f32[32,256]{1,0:T(8,128)S(1)} %get-tuple-element.17, ...), kind=kLoop, calls=%fused_computation.1 | loop fusion | flops 65536 | bytes 180224 | tf_op jit(solution)/shard_map/transpose | solution.py:267
  (5 shorter events, 0.0 us)
Async XLA Ops:
  0.9 6.9 %collective-permute-start.2 = (bf16[288,256]{1,0:T(8,128)(2,1)S(1)}, bf16[288,256]{1,0:T(8,128)(2,1)S(1)}, u32[]{:S(2)}, u32[]{:S(2)}) collective-permute-start(bf16[288,256]{1,0:T(8,128)(2,1)S(1)} %pad_maximum_fusion.refs_0_.refs_5_), channel_id=1, source_target_pairs={{0,2},{1,3},{2,0},{3,1},{4,6},{5,7},{6,4},{7,5},{8,10},{9,11},{10,... | collective-permute-start | bytes 442376 | tf_op jit(solution)/shard_map/ppermute | solution.py:225
  4.0 9.5 %collective-permute-start.5 = (bf16[288,256]{1,0:T(8,128)(2,1)S(1)}, bf16[288,256]{1,0:T(8,128)(2,1)S(1)}, u32[]{:S(2)}, u32[]{:S(2)}) collective-permute-start(bf16[288,256]{1,0:T(8,128)(2,1)S(1)} %pad_maximum_fusion.refs_0_.refs_5_), channel_id=1, source_target_pairs={{12,4},{13,5},{14,6},{15,7},{4,8},{5,9},{6,10},{7,11},{8,0},{9,1},... | collective-permute-start | bytes 442376 | tf_op jit(solution)/shard_map/ppermute | solution.py:222
  7.6 5.9 %collective-permute-start = (bf16[288,256]{1,0:T(8,128)(2,1)S(1)}, bf16[288,256]{1,0:T(8,128)(2,1)S(1)}, u32[]{:S(2)}, u32[]{:S(2)}) collective-permute-start(bf16[288,256]{1,0:T(8,128)(2,1)S(1)} %pad_maximum_fusion.refs_0_.refs_5_), channel_id=1, source_target_pairs={{0,1},{1,0},{2,3},{3,2},{4,5},{5,4},{6,7},{7,6},{8,9},{9,8},{10,11... | collective-permute-start | bytes 442376 | tf_op jit(solution)/shard_map/ppermute | solution.py:225
  7.6 8.1 %collective-permute-start.1 = (bf16[288,256]{1,0:T(8,128)(2,1)S(1)}, bf16[288,256]{1,0:T(8,128)(2,1)S(1)}, u32[]{:S(2)}, u32[]{:S(2)}) collective-permute-start(bf16[288,256]{1,0:T(8,128)(2,1)S(1)} %pad_maximum_fusion.refs_0_.refs_5_), channel_id=1, source_target_pairs={{12,8},{13,9},{14,10},{15,11},{4,0},{5,1},{6,2},{7,3},{8,12},{9,13... | collective-permute-start | bytes 442376 | tf_op jit(solution)/shard_map/ppermute | solution.py:222
  7.8 5.6 %collective-permute-start.3 = (bf16[144,256]{1,0:T(8,128)(2,1)S(1)}, bf16[144,256]{1,0:T(8,128)(2,1)S(1)}, u32[]{:S(2)}, u32[]{:S(2)}) collective-permute-start(bf16[144,256]{1,0:T(8,128)(2,1)S(1)} %get-tuple-element.14), channel_id=1, source_target_pairs={{0,1},{1,0},{2,3},{3,2},{4,5},{5,4},{6,7},{7,6},{8,9},{9,8},{10,11... | collective-permute-start | bytes 221192 | tf_op jit(solution)/shard_map/ppermute | solution.py:225
  8.2 5.3 %copy-start = (f32[256]{0:T(256)S(1)}, f32[256]{0:T(256)}, u32[]{:S(2)}) copy-start(f32[256]{0:T(256)} %param.5) | copy-start | bytes 3076
  8.2 5.3 %collective-permute-start.4 = (bf16[144,256]{1,0:T(8,128)(2,1)S(1)}, bf16[144,256]{1,0:T(8,128)(2,1)S(1)}, u32[]{:S(2)}, u32[]{:S(2)}) collective-permute-start(bf16[144,256]{1,0:T(8,128)(2,1)S(1)} %get-tuple-element.15), channel_id=1, source_target_pairs={{0,1},{1,0},{2,3},{3,2},{4,5},{5,4},{6,7},{7,6},{8,9},{9,8},{10,11... | collective-permute-start | bytes 221192 | tf_op jit(solution)/shard_map/ppermute | solution.py:225
  14.3 6.0 %collective-permute-start.9 = (f32[32,256]{1,0:T(8,128)S(1)}, f32[32,256]{1,0:T(8,128)S(1)}, u32[]{:S(2)}, u32[]{:S(2)}) collective-permute-start(f32[32,256]{1,0:T(8,128)S(1)} %get-tuple-element.22), channel_id=1, source_target_pairs={{4,12},{5,13},{6,14},{7,15},{8,4},{9,5},{10,6},{11,7},{0,8},{1,9},... | collective-permute-start | bytes 98312 | tf_op jit(solution)/shard_map/ppermute | solution.py:222
  16.3 3.9 %collective-permute-start.7 = (bf16[32,256]{1,0:T(8,128)(2,1)S(1)}, bf16[32,256]{1,0:T(8,128)(2,1)S(1)}, u32[]{:S(2)}, u32[]{:S(2)}) collective-permute-start(bf16[32,256]{1,0:T(8,128)(2,1)S(1)} %get-tuple-element.20), channel_id=1, source_target_pairs={{0,2},{1,3},{2,0},{3,1},{4,6},{5,7},{6,4},{7,5},{8,10},{9,11},{10,... | collective-permute-start | bytes 49160 | tf_op jit(solution)/shard_map/ppermute | solution.py:225
  16.9 3.3 %collective-permute-start.8 = (bf16[32,256]{1,0:T(8,128)(2,1)S(1)}, bf16[32,256]{1,0:T(8,128)(2,1)S(1)}, u32[]{:S(2)}, u32[]{:S(2)}) collective-permute-start(bf16[32,256]{1,0:T(8,128)(2,1)S(1)} %get-tuple-element.21), channel_id=1, source_target_pairs={{0,3},{1,2},{2,1},{3,0},{4,7},{5,6},{6,5},{7,4},{8,11},{9,10},{10,... | collective-permute-start | bytes 49160 | tf_op jit(solution)/shard_map/ppermute | solution.py:225
  18.1 2.1 %collective-permute-start.6 = (bf16[32,256]{1,0:T(8,128)(2,1)S(1)}, bf16[32,256]{1,0:T(8,128)(2,1)S(1)}, u32[]{:S(2)}, u32[]{:S(2)}) collective-permute-start(bf16[32,256]{1,0:T(8,128)(2,1)S(1)} %get-tuple-element.19), channel_id=1, source_target_pairs={{0,1},{1,0},{2,3},{3,2},{4,5},{5,4},{6,7},{7,6},{8,9},{9,8},{10,11... | collective-permute-start | bytes 49160 | tf_op jit(solution)/shard_map/ppermute | solution.py:225
